TPU v7x, 256 devices: a whole 4x4x8 slice. The times are simulated.
256 devices in a mesh: passage: 32 (over z, x), cell: 4 (over y), tm: 2 (over core).
Axes of the slice: x: 4, y: 4, z: 8, core: 2. Of those that a mesh axis runs over, the one named last changes fastest.
Arguments:
- adjoint_start: float32 [8, 5, 8, 1024, 256], P('tm', None, 'cell', 'passage'), may hold values from -6 to 6
- adjoint_source: float32 [8, 5, 8, 1024, 256], P('tm', None, 'cell', 'passage'), may hold values from -6 to 6
- jacobian: bfloat16 [2, 5, 5, 8, 1024, 256], P(None, None, None, 'cell', 'passage'), may hold values from -2.5 to 2.5
- pseudo_time: float32 [8, 1024, 256], P('cell', 'passage'), may hold values from 3 to 12
- dissipation: float32 [8, 1024, 256], P('cell', 'passage'), may hold values from 0.2 to 1
- surface_cells: int32 [4, 1024], P('cell'), may hold values from 0 to 1023, as said below
- surface_weights: float32 [8, 5, 4096], P('tm', None, 'cell'), may hold values from -1 to 1
Outputs:
- adjoint_final: float32 [8, 5, 8, 1024, 256], P('tm', None, 'cell', 'passage')
- diameter_modes: float32 [2, 16, 4096], P(None, None, 'cell')
Inputs may be any that keep to these rules, and one draw needn't show every extreme that they name: `surface_cells`: each row holds every value from 0 to 1023 exactly once, in a drawn order.
All inputs are finite; a program needn't handle non-finite values.
Results may differ from a plain program's by a relative error of at most 0.0025.
Values may be sent and summed in bfloat16 or wider, within the bound.
No kernel may reach another device: no remote copies, remote signals or barrier semaphores. Data moves between devices by JAX's collectives and lax.ppermute only.
A program may use at most 128 MiB of HBM per device.

v0:
```python
import jax
import jax.numpy as jnp
from jax import lax
from jax.sharding import PartitionSpec as P

PASSAGES = 16
CJ = 64
SWEEPS = 2


OMEGA = 1.0


def with_halo(array, sides, width):
    for axis, dim in sides:
        peers, length = (lax.axis_size(axis), array.shape[dim])
        up = [(i, (i + 1) % peers) for i in range(peers)]
        down = [(j, i) for i, j in up]
        last = lax.slice_in_dim(array, length - width, length, axis=dim)
        leading = lax.slice_in_dim(array, 0, width, axis=dim)
        before = lax.ppermute(last, axis, up)
        after = lax.ppermute(leading, axis, down)
        array = jnp.concatenate([before, array, after], axis=dim)
    return array


def spectral_matrix(total):
    index = jnp.arange(total, dtype=jnp.int32)
    offset = index[:, None] - index[None, :]
    parity = (1 - 2 * (offset % 2)).astype(jnp.float32)
    phase_arg = jnp.pi * offset.astype(jnp.float32) / total
    sine_safe = jnp.where(offset == 0, jnp.float32(1.0), jnp.sin(phase_arg))
    values = 0.5 * parity * jnp.cos(phase_arg) / sine_safe
    return jnp.where(offset == 0, jnp.float32(0.0), values)


def blade_table(passages):
    index = jnp.arange(passages, dtype=jnp.int32)
    product_mod = index[:, None] * index[None, :] % passages
    phase_arg = 2.0 * jnp.pi * product_mod.astype(jnp.float32) / passages
    factor = 1.0 / passages**0.5
    return jnp.stack([jnp.cos(phase_arg), -jnp.sin(phase_arg)]) * factor


def adjoint_operator(field, plus_i, minus_i, plus_j, minus_j, jacobian, sigma, damping):
    total_out = sigma * field + damping * (4.0 * field - plus_i - minus_i - plus_j - minus_j)
    variables = field.shape[1]
    flux_rows = []
    for target_var in range(variables):
        acc_flux = jnp.zeros_like(field[:, 0])
        for source_var in range(variables):
            acc_flux = acc_flux + jacobian[0, source_var, target_var].astype(jnp.float32) * (
                field[:, source_var] - plus_i[:, source_var]
            )
            acc_flux = acc_flux + jacobian[1, source_var, target_var].astype(jnp.float32) * (
                field[:, source_var] - plus_j[:, source_var]
            )
        flux_rows.append(acc_flux)
    return total_out + jnp.stack(flux_rows, axis=1)


def neighbours(field):
    stream_cells = field.shape[2]
    padded = with_halo(field, (("passage", 3), ("cell", 2)), 1)
    plus_i = padded[:, :, 2:, 1:-1]
    minus_i = padded[:, :, :-2, 1:-1]
    plus_j = padded[:, :, 1:-1, 2:]
    minus_j = padded[:, :, 1:-1, :-2]
    cell_pos = lax.axis_index("cell")
    last_pos = lax.axis_size("cell") - 1
    stream_ids = jnp.arange(stream_cells, dtype=jnp.int32)
    low_keep = jnp.where((stream_ids == 0) & (cell_pos == 0), 0.0, 1.0).astype(jnp.float32)
    high_keep = jnp.where(
        (stream_ids == stream_cells - 1) & (cell_pos == last_pos), 0.0, 1.0
    ).astype(jnp.float32)
    minus_i = minus_i * low_keep[None, None, :, None, None]
    plus_i = plus_i * high_keep[None, None, :, None, None]
    return (plus_i, minus_i, plus_j, minus_j)


def body(
    adjoint_start,
    adjoint_source,
    jacobian,
    pseudo_time,
    dissipation,
    surface_cells,
    surface_weights,
):
    local_times = adjoint_start.shape[0]
    all_times = local_times * lax.axis_size("tm")
    dmatrix = spectral_matrix(all_times)
    first_time = lax.axis_index("tm") * local_times
    start_rounded = adjoint_start.astype(jnp.bfloat16)
    own_columns = lax.dynamic_slice_in_dim(dmatrix, first_time, local_times, 1)
    spectral_term = OMEGA * jnp.einsum(
        "ab,avipk->bvipk",
        own_columns,
        lax.all_gather(start_rounded, "tm", axis=0, tiled=True).astype(jnp.float32),
        precision=lax.Precision.HIGHEST,
    )
    scaling = 1.0 / (pseudo_time + 4.0 * dissipation)
    field = adjoint_start
    for sweep_index in range(SWEEPS):
        plus_i, minus_i, plus_j, minus_j = neighbours(field)
        applied = adjoint_operator(
            field, plus_i, minus_i, plus_j, minus_j, jacobian, pseudo_time, dissipation
        )
        field = field + (adjoint_source - applied - spectral_term) * scaling
    variables = field.shape[1]
    stream_cells = field.shape[2]
    pitch_cells = field.shape[3]
    span_cells = field.shape[4]
    first_pitch = lax.axis_index("passage") * pitch_cells
    side_rows = (
        jnp.arange(PASSAGES, dtype=jnp.int32)[:, None] * CJ
        + jnp.arange(2, dtype=jnp.int32)[None, :] * (CJ - 1)
    ).reshape(2 * PASSAGES)
    local_rows = side_rows - first_pitch
    owned = (local_rows >= 0) & (local_rows < pitch_cells)
    clipped = jnp.clip(local_rows, 0, pitch_cells - 1)
    rows = jnp.take(field, clipped, axis=3)
    rows = jnp.where(owned[None, None, None, :, None], rows, jnp.float32(0.0))
    rows = rows.reshape(local_times, variables, stream_cells, PASSAGES, 2, span_cells)
    rows = rows.transpose(0, 1, 3, 4, 2, 5).reshape(
        local_times, variables, PASSAGES, 2 * stream_cells * span_cells
    )
    picked = jnp.take(rows, surface_cells[0], axis=3)
    partial_sens = jnp.einsum(
        "tvs,tvps->ps", surface_weights, picked, precision=lax.Precision.HIGHEST
    )
    table = blade_table(PASSAGES)
    mode_terms = jnp.einsum("cmp,ps->cms", table, partial_sens, precision=lax.Precision.HIGHEST)
    diameter_modes = lax.psum(mode_terms, ("passage", "tm"))
    return (field, diameter_modes)


def solution(mesh):
    in_specs = (
        P("tm", None, "cell", "passage", None),
        P("tm", None, "cell", "passage", None),
        P(None, None, None, "cell", "passage", None),
        P("cell", "passage", None),
        P("cell", "passage", None),
        P("cell", None),
        P("tm", None, "cell"),
    )
    out_specs = (P("tm", None, "cell", "passage", None), P(None, None, "cell"))
    return jax.shard_map(body, mesh=mesh, in_specs=in_specs, out_specs=out_specs, check_vma=False)
```

profile of v0, /device:TPU:8, one launch (start us, length us, event | category | flops | bytes accessed | tf_op | source)
XLA Modules:
  0.0 319.9 jit_solution(16755320663396980557)
XLA Ops:
  7.2 2.3 copy.78
  9.5 1.0 copy-done.1
  10.5 1.5 collective-permute-start
  12.0 6.6 %collective-permute-start.1 = (f32[4,5,2,1,256]{4,0,3,2,1:T(4,128)S(1)}, f32[4,5,2,1,256]{4,0,3,2,1:T(4,128)S(1)}, u32[]{:S(2)}, u32[]{:S(2)}) collective-permute-start(f32[4,5,2,1,256]{4,0,3,2,1:T(4,128)S(1)} %get-tuple-element.92), channel_id=1, source_target_pairs={{8,0},{16,8},{24,16},{32,24},{40,32},{48,40},{56,48},{64,56},{72,6... | collective-permute-start | bytes 122888 | tf_op jit(solution)/shard_map/ppermute | solution.py:22
  18.7 0.9 convert_element_type.678
  19.8 1.8 bitcast_convert_fusion
  21.6 0.7 add_divide_fusion
  22.2 0.6 compare_and_fusion.1
  22.9 0.6 and_select_fusion
  23.4 0.1 copy.82
  23.5 0.1 min.12
  23.6 1.1 constant_dynamic-update-slice_fusion.4
  24.8 0.2 fusion.73
  25.0 0.5 collective-permute-start.2
  25.6 0.6 fusion.62
  26.1 0.6 copy-done.4
  26.7 0.1 bitcast_convert_fusion.1
  27.0 0.1 bitcast_convert_fusion.9
  27.4 1.8 collective-permute-start.3
  29.2 13.0 %collective-permute-done.2 = f32[4,5,1,34,256]{4,0,3,2,1:T(4,128)S(1)} collective-permute-done((f32[4,5,1,34,256]{4,0,3,2,1:T(4,128)S(1)}, f32[4,5,1,34,256]{4,0,3,2,1:T(4,128)S(1)}, u32[]{:S(2)}, u32[]{:S(2)}) %collective-permute-start.2) | collective-permute-done | bytes 696352 | tf_op jit(solution)/shard_map/ppermute | solution.py:22
  42.3 1.2 fusion.21
  43.6 1.1 add_dynamic-update-slice_fusion.9
  44.8 0.6 add_dynamic-update-slice_fusion.8
  45.5 0.6 add_dynamic-update-slice_fusion.7
  46.2 0.6 add_dynamic-update-slice_fusion.6
  46.9 0.6 add_dynamic-update-slice_fusion.5
  47.6 1.1 copy-done.110
  48.6 8.3 %fusion.18 = (f32[4,5,2,32,256]{4,0,3,2,1:T(4,128)S(1)}, f32[4,5,2,32,256]{4,0,3,2,1:T(4,128)}) fusion(f32[4,5,2,32,256]{4,0,3,2,1:T(4,128)} %copy-done.1, f32[4,5,2,32,256]{4,0,3,2,1:T(4,128)} %copy-done.110, f32[4,5,2,1,256]{4,0,3,2,1:T(4,128)S(1)} %collective-permute-done, f32[4,5,2,33,256]{4,0,3,2,1:T(4,128)} %copy-done.3, ...), kind=kOutput, calls=%fused_computation.35 | convolution fusion | flops 37355520 | bytes 12199956 | tf_op jit(solution)/shard_map/ab,avipk->bvipk/dot_general | solution.py:96
  56.9 0.1 collective-permute-start.4
  57.0 5.3 %collective-permute-start.5 = (f32[4,5,2,1,256]{4,0,3,2,1:T(4,128)S(1)}, f32[4,5,2,1,256]{4,0,3,2,1:T(4,128)S(1)}, u32[]{:S(2)}, u32[]{:S(2)}) collective-permute-start(f32[4,5,2,1,256]{4,0,3,2,1:T(4,128)S(1)} %get-tuple-element.89), channel_id=1, source_target_pairs={{8,0},{16,8},{24,16},{32,24},{40,32},{48,40},{56,48},{64,56},{72,6... | collective-permute-start | bytes 122888 | tf_op jit(solution)/shard_map/ppermute | solution.py:22
  62.4 0.6 sine_negate_fusion
  63.0 1.3 collective-permute-done.4
  64.3 0.3 pad_maximum_fusion
  64.7 0.2 fusion.72
  65.0 1.1 collective-permute-start.6
  66.0 0.6 pad_clamp_fusion
  66.6 1.3 copy.80
  67.9 1.3 copy.81
  69.2 3.5 %copy.96 = f32[1024,4,5]{1,2,0:T(8,128)} copy(f32[1024,4,5]{0,1,2:T(4,128)} %bitcast.178) | data formatting | bytes 163840
  72.6 1.2 compare_and_fusion
  73.9 0.7 compare_select_fusion
  74.5 0.6 broadcast_clamp_fusion
  75.2 1.3 collective-permute-start.7
  76.6 3.6 %collective-permute-done.6 = f32[4,5,1,34,256]{4,0,3,2,1:T(4,128)S(1)} collective-permute-done((f32[4,5,1,34,256]{4,0,3,2,1:T(4,128)S(1)}, f32[4,5,1,34,256]{4,0,3,2,1:T(4,128)S(1)}, u32[]{:S(2)}, u32[]{:S(2)}) %collective-permute-start.6) | collective-permute-done | bytes 696352 | tf_op jit(solution)/shard_map/ppermute | solution.py:22
  80.1 1.0 fusion.10
  81.4 1.2 add_dynamic-update-slice_fusion.4
  82.8 0.5 add_dynamic-update-slice_fusion.3
  83.3 0.2 copy-done.48
  83.9 0.6 add_dynamic-update-slice_fusion.2
  84.4 0.2 copy-done.66
  85.0 0.5 add_dynamic-update-slice_fusion.1
  85.5 0.3 copy-done.30
  86.0 0.6 add_dynamic-update-slice_fusion
  86.6 5.6 %collective-permute-done.7 = f32[4,5,1,34,256]{4,0,3,2,1:T(4,128)S(1)} collective-permute-done((f32[4,5,1,34,256]{4,0,3,2,1:T(4,128)S(1)}, f32[4,5,1,34,256]{4,0,3,2,1:T(4,128)S(1)}, u32[]{:S(2)}, u32[]{:S(2)}) %collective-permute-start.7) | collective-permute-done | bytes 696352 | tf_op jit(solution)/shard_map/ppermute | solution.py:21
  92.2 3.2 %multiply_add_fusion = f32[4,5,2,32,256]{4,0,3,2,1:T(4,128)S(1)} fusion(f32[4,5,2,32,256]{4,0,3,2,1:T(4,128)S(1)} %get-tuple-element.97, f32[4,5,2,32,256]{4,0,3,2,1:T(4,128)S(1)} %copy-done.6, f32[4,5,2,32,256]{4,0,3,2,1:T(4,128)S(1)} %add_dynamic-update-slice_fusion, f32[4,5,2,1,256]{4,0,3,2,1:T(4,128)S(1)} %collective-permute-done.4, ...), kind=kLoop, calls=%fused_computation.47 | loop fusion | flops 7536640 | bytes 8224784 | tf_op jit(solution)/shard_map/add | solution.py:109
  95.5 1.5 gather_fusion
  97.0 2.1 fusion.23
  99.1 9.1 %copy.94 = f32[4,5,16,2,2,256]{2,0,5,4,3,1:T(4,128)} copy(f32[4,5,16,2,2,256]{5,4,3,2,1,0:T(2,128)} %fusion.23) | data formatting | bytes 2621440 | tf_op jit(solution)/shard_map/reshape | solution.py:125
  108.2 20.8 %gather_fusion.1 = f32[1024,4,5,16]{3,1,2,0:T(4,128)} fusion(f32[4,5,16,1024]{2,0,3,1:T(4,128)} %bitcast.176, s32[1024]{0:T(1024)S(1)} %copy-done.112), kind=kCustom, calls=%fused_computation.1 | custom fusion | bytes 2625536 | tf_op jit(solution)/shard_map/jit(_take)/gather | solution.py:128
  129.0 9.9 %multiply_reduce_fusion = f32[1024,16]{1,0:T(8,128)S(1)} fusion(f32[1024,4,5,16]{3,1,2,0:T(4,128)} %gather_fusion.1, f32[1024,4,5]{1,2,0:T(8,128)} %copy.96, pred[1024]{0:T(1024)(128)(4,1)S(1)} %copy-done.115), kind=kLoop, calls=%fused_computation.2 | loop fusion | flops 966656 | bytes 1459200
  138.9 1.3 fusion.26
  140.2 1.3 copy.85
  141.5 170.0 %all-reduce.2.cloned.1.call-done = f32[2,16,1024]{2,1,0:T(8,128)} async-done(((f32[2,16,1024]{2,1,0:T(8,128)}), f32[2,16,1024]{2,1,0:T(8,128)}) %all-reduce.2.cloned.1.call-update) | async-done | bytes 131088 | tf_op jit(solution)/shard_map/psum | solution.py:134
  311.5 1.6 copy.122
  (244 shorter events, 1.6 us)
Async XLA Ops:
  7.2 11.5 %copy-start = (f32[4,5,2,32,256]{4,3,2,1,0:T(8,128)S(1)}, f32[4,5,2,32,256]{4,3,2,1,0:T(8,128)}, u32[]{:S(2)}) copy-start(f32[4,5,2,32,256]{4,3,2,1,0:T(8,128)} %param.7) | copy-start | bytes 3932164
  7.2 41.5 %all-gather.2.cloned.1.call-start = ((), (), s32[]{:S(2)}) async-start(), calls=%async_computation | async-start | bytes 1966080 | tf_op jit(solution)/shard_map/all_gather | solution.py:99
  10.5 13.1 %collective-permute-start = (f32[4,5,2,1,256]{4,0,3,2,1:T(4,128)S(1)}, f32[4,5,2,1,256]{4,0,3,2,1:T(4,128)S(1)}, u32[]{:S(2)}, u32[]{:S(2)}) collective-permute-start(f32[4,5,2,1,256]{4,0,3,2,1:T(4,128)S(1)} %get-tuple-element.93), channel_id=1, source_target_pairs={{0,8},{8,16},{16,24},{24,32},{32,40},{40,48},{48,56},{56,64},{64,7... | collective-permute-start | bytes 122888 | tf_op jit(solution)/shard_map/ppermute | solution.py:21
  12.0 12.7 %collective-permute-start.1 = (f32[4,5,2,1,256]{4,0,3,2,1:T(4,128)S(1)}, f32[4,5,2,1,256]{4,0,3,2,1:T(4,128)S(1)}, u32[]{:S(2)}, u32[]{:S(2)}) collective-permute-start(f32[4,5,2,1,256]{4,0,3,2,1:T(4,128)S(1)} %get-tuple-element.92), channel_id=1, source_target_pairs={{8,0},{16,8},{24,16},{32,24},{40,32},{48,40},{56,48},{64,56},{72,6... | collective-permute-start | bytes 122888 | tf_op jit(solution)/shard_map/ppermute | solution.py:22
  19.6 291.8 %all-reduce.2.cloned.1.call-start = ((), (), s32[]{:S(2)}) async-start(), calls=%async_computation.1 | async-start | bytes 262144 | tf_op jit(solution)/shard_map/psum | solution.py:134
  24.8 18.7 %copy-start.3 = (f32[4,5,2,33,256]{4,0,3,2,1:T(4,128)}, f32[4,5,2,33,256]{4,0,3,2,1:T(4,128)S(1)}, u32[]{:S(2)}) copy-start(f32[4,5,2,33,256]{4,0,3,2,1:T(4,128)S(1)} %get-tuple-element.94) | copy-start | bytes 4055044
  25.0 17.1 %collective-permute-start.2 = (f32[4,5,1,34,256]{4,0,3,2,1:T(4,128)S(1)}, f32[4,5,1,34,256]{4,0,3,2,1:T(4,128)S(1)}, u32[]{:S(2)}, u32[]{:S(2)}) collective-permute-start(f32[4,5,1,34,256]{4,0,3,2,1:T(4,128)S(1)} %get-tuple-element.87), channel_id=1, source_target_pairs={{2,0},{4,2},{6,4},{0,6},{3,1},{5,3},{7,5},{1,7},{10,8},{12,10},{14... | collective-permute-start | bytes 2088968 | tf_op jit(solution)/shard_map/ppermute | solution.py:22
  26.9 17.8 %copy-start.85 = (f32[2,32,256]{2,1,0:T(8,128)}, f32[2,32,256]{2,1,0:T(8,128)S(1)}, u32[]{:S(2)}) copy-start(f32[2,32,256]{2,1,0:T(8,128)S(1)} %get-tuple-element.63) | copy-start | bytes 196612
  26.9 17.8 %copy-start.87 = (f32[2,32,256]{2,1,0:T(8,128)}, f32[2,32,256]{2,1,0:T(8,128)S(1)}, u32[]{:S(2)}) copy-start(f32[2,32,256]{2,1,0:T(8,128)S(1)} %get-tuple-element.64) | copy-start | bytes 196612
  26.9 17.8 %copy-start.89 = (f32[2,32,256]{2,1,0:T(8,128)}, f32[2,32,256]{2,1,0:T(8,128)S(1)}, u32[]{:S(2)}) copy-start(f32[2,32,256]{2,1,0:T(8,128)S(1)} %get-tuple-element.65) | copy-start | bytes 196612
  26.9 17.8 %copy-start.91 = (f32[2,32,256]{2,1,0:T(8,128)}, f32[2,32,256]{2,1,0:T(8,128)S(1)}, u32[]{:S(2)}) copy-start(f32[2,32,256]{2,1,0:T(8,128)S(1)} %get-tuple-element.66) | copy-start | bytes 196612
  26.9 17.8 %copy-start.93 = (f32[2,32,256]{2,1,0:T(8,128)}, f32[2,32,256]{2,1,0:T(8,128)S(1)}, u32[]{:S(2)}) copy-start(f32[2,32,256]{2,1,0:T(8,128)S(1)} %get-tuple-element.67) | copy-start | bytes 196612
  26.9 17.8 %copy-start.95 = (f32[2,32,256]{2,1,0:T(8,128)}, f32[2,32,256]{2,1,0:T(8,128)S(1)}, u32[]{:S(2)}) copy-start(f32[2,32,256]{2,1,0:T(8,128)S(1)} %get-tuple-element.68) | copy-start | bytes 196612
  26.9 17.8 %copy-start.97 = (f32[2,32,256]{2,1,0:T(8,128)}, f32[2,32,256]{2,1,0:T(8,128)S(1)}, u32[]{:S(2)}) copy-start(f32[2,32,256]{2,1,0:T(8,128)S(1)} %get-tuple-element.69) | copy-start | bytes 196612
  26.9 17.8 %copy-start.99 = (f32[2,32,256]{2,1,0:T(8,128)}, f32[2,32,256]{2,1,0:T(8,128)S(1)}, u32[]{:S(2)}) copy-start(f32[2,32,256]{2,1,0:T(8,128)S(1)} %get-tuple-element.70) | copy-start | bytes 196612
  26.9 17.8 %copy-start.101 = (f32[2,32,256]{2,1,0:T(8,128)}, f32[2,32,256]{2,1,0:T(8,128)S(1)}, u32[]{:S(2)}) copy-start(f32[2,32,256]{2,1,0:T(8,128)S(1)} %get-tuple-element.71) | copy-start | bytes 196612
  26.9 18.5 %copy-start.47 = (f32[2,32,256]{2,1,0:T(8,128)}, f32[2,32,256]{2,1,0:T(8,128)S(1)}, u32[]{:S(2)}) copy-start(f32[2,32,256]{2,1,0:T(8,128)S(1)} %get-tuple-element.54) | copy-start | bytes 196612
  27.0 18.5 %copy-start.49 = (f32[2,32,256]{2,1,0:T(8,128)}, f32[2,32,256]{2,1,0:T(8,128)S(1)}, u32[]{:S(2)}) copy-start(f32[2,32,256]{2,1,0:T(8,128)S(1)} %get-tuple-element.55) | copy-start | bytes 196612
  27.0 18.5 %copy-start.51 = (f32[2,32,256]{2,1,0:T(8,128)}, f32[2,32,256]{2,1,0:T(8,128)S(1)}, u32[]{:S(2)}) copy-start(f32[2,32,256]{2,1,0:T(8,128)S(1)} %get-tuple-element.56) | copy-start | bytes 196612
  27.0 18.5 %copy-start.53 = (f32[2,32,256]{2,1,0:T(8,128)}, f32[2,32,256]{2,1,0:T(8,128)S(1)}, u32[]{:S(2)}) copy-start(f32[2,32,256]{2,1,0:T(8,128)S(1)} %get-tuple-element.57) | copy-start | bytes 196612
  27.0 18.5 %copy-start.55 = (f32[2,32,256]{2,1,0:T(8,128)}, f32[2,32,256]{2,1,0:T(8,128)S(1)}, u32[]{:S(2)}) copy-start(f32[2,32,256]{2,1,0:T(8,128)S(1)} %get-tuple-element.58) | copy-start | bytes 196612
  27.0 18.5 %copy-start.57 = (f32[2,32,256]{2,1,0:T(8,128)}, f32[2,32,256]{2,1,0:T(8,128)S(1)}, u32[]{:S(2)}) copy-start(f32[2,32,256]{2,1,0:T(8,128)S(1)} %get-tuple-element.59) | copy-start | bytes 196612
  27.0 18.5 %copy-start.59 = (f32[2,32,256]{2,1,0:T(8,128)}, f32[2,32,256]{2,1,0:T(8,128)S(1)}, u32[]{:S(2)}) copy-start(f32[2,32,256]{2,1,0:T(8,128)S(1)} %get-tuple-element.60) | copy-start | bytes 196612
  27.0 18.5 %copy-start.61 = (f32[2,32,256]{2,1,0:T(8,128)}, f32[2,32,256]{2,1,0:T(8,128)S(1)}, u32[]{:S(2)}) copy-start(f32[2,32,256]{2,1,0:T(8,128)S(1)} %get-tuple-element.61) | copy-start | bytes 196612
  27.0 18.5 %copy-start.63 = (f32[2,32,256]{2,1,0:T(8,128)}, f32[2,32,256]{2,1,0:T(8,128)S(1)}, u32[]{:S(2)}) copy-start(f32[2,32,256]{2,1,0:T(8,128)S(1)} %get-tuple-element.62) | copy-start | bytes 196612
  27.0 19.8 %copy-start.29 = (f32[2,32,256]{2,1,0:T(8,128)}, f32[2,32,256]{2,1,0:T(8,128)S(1)}, u32[]{:S(2)}) copy-start(f32[2,32,256]{2,1,0:T(8,128)S(1)} %get-tuple-element.53) | copy-start | bytes 196612
  27.2 18.3 %copy-start.103 = (f32[2,32,256]{2,1,0:T(8,128)}, f32[2,32,256]{2,1,0:T(8,128)S(1)}, u32[]{:S(2)}) copy-start(f32[2,32,256]{2,1,0:T(8,128)S(1)} %get-tuple-element.52) | copy-start | bytes 196612
  27.2 18.9 %copy-start.65 = (f32[2,32,256]{2,1,0:T(8,128)}, f32[2,32,256]{2,1,0:T(8,128)S(1)}, u32[]{:S(2)}) copy-start(f32[2,32,256]{2,1,0:T(8,128)S(1)} %get-tuple-element.42) | copy-start | bytes 196612
  27.2 18.9 %copy-start.67 = (f32[2,32,256]{2,1,0:T(8,128)}, f32[2,32,256]{2,1,0:T(8,128)S(1)}, u32[]{:S(2)}) copy-start(f32[2,32,256]{2,1,0:T(8,128)S(1)} %get-tuple-element.43) | copy-start | bytes 196612
  27.2 18.9 %copy-start.69 = (f32[2,32,256]{2,1,0:T(8,128)}, f32[2,32,256]{2,1,0:T(8,128)S(1)}, u32[]{:S(2)}) copy-start(f32[2,32,256]{2,1,0:T(8,128)S(1)} %get-tuple-element.44) | copy-start | bytes 196612
  27.2 18.9 %copy-start.71 = (f32[2,32,256]{2,1,0:T(8,128)}, f32[2,32,256]{2,1,0:T(8,128)S(1)}, u32[]{:S(2)}) copy-start(f32[2,32,256]{2,1,0:T(8,128)S(1)} %get-tuple-element.45) | copy-start | bytes 196612
  27.2 18.9 %copy-start.73 = (f32[2,32,256]{2,1,0:T(8,128)}, f32[2,32,256]{2,1,0:T(8,128)S(1)}, u32[]{:S(2)}) copy-start(f32[2,32,256]{2,1,0:T(8,128)S(1)} %get-tuple-element.46) | copy-start | bytes 196612
  27.3 18.9 %copy-start.75 = (f32[2,32,256]{2,1,0:T(8,128)}, f32[2,32,256]{2,1,0:T(8,128)S(1)}, u32[]{:S(2)}) copy-start(f32[2,32,256]{2,1,0:T(8,128)S(1)} %get-tuple-element.47) | copy-start | bytes 196612
  27.3 18.9 %copy-start.77 = (f32[2,32,256]{2,1,0:T(8,128)}, f32[2,32,256]{2,1,0:T(8,128)S(1)}, u32[]{:S(2)}) copy-start(f32[2,32,256]{2,1,0:T(8,128)S(1)} %get-tuple-element.48) | copy-start | bytes 196612
  27.3 18.9 %copy-start.79 = (f32[2,32,256]{2,1,0:T(8,128)}, f32[2,32,256]{2,1,0:T(8,128)S(1)}, u32[]{:S(2)}) copy-start(f32[2,32,256]{2,1,0:T(8,128)S(1)} %get-tuple-element.49) | copy-start | bytes 196612
  27.3 18.9 %copy-start.81 = (f32[2,32,256]{2,1,0:T(8,128)}, f32[2,32,256]{2,1,0:T(8,128)S(1)}, u32[]{:S(2)}) copy-start(f32[2,32,256]{2,1,0:T(8,128)S(1)} %get-tuple-element.50) | copy-start | bytes 196612
  27.3 18.9 %copy-start.83 = (f32[2,32,256]{2,1,0:T(8,128)}, f32[2,32,256]{2,1,0:T(8,128)S(1)}, u32[]{:S(2)}) copy-start(f32[2,32,256]{2,1,0:T(8,128)S(1)} %get-tuple-element.51) | copy-start | bytes 196612
  27.3 19.5 %copy-start.31 = (f32[2,32,256]{2,1,0:T(8,128)}, f32[2,32,256]{2,1,0:T(8,128)S(1)}, u32[]{:S(2)}) copy-start(f32[2,32,256]{2,1,0:T(8,128)S(1)} %get-tuple-element.34) | copy-start | bytes 196612
  27.3 19.5 %copy-start.33 = (f32[2,32,256]{2,1,0:T(8,128)}, f32[2,32,256]{2,1,0:T(8,128)S(1)}, u32[]{:S(2)}) copy-start(f32[2,32,256]{2,1,0:T(8,128)S(1)} %get-tuple-element.35) | copy-start | bytes 196612
  27.3 19.5 %copy-start.35 = (f32[2,32,256]{2,1,0:T(8,128)}, f32[2,32,256]{2,1,0:T(8,128)S(1)}, u32[]{:S(2)}) copy-start(f32[2,32,256]{2,1,0:T(8,128)S(1)} %get-tuple-element.36) | copy-start | bytes 196612
  27.3 19.5 %copy-start.37 = (f32[2,32,256]{2,1,0:T(8,128)}, f32[2,32,256]{2,1,0:T(8,128)S(1)}, u32[]{:S(2)}) copy-start(f32[2,32,256]{2,1,0:T(8,128)S(1)} %get-tuple-element.37) | copy-start | bytes 196612
  27.3 19.5 %copy-start.39 = (f32[2,32,256]{2,1,0:T(8,128)}, f32[2,32,256]{2,1,0:T(8,128)S(1)}, u32[]{:S(2)}) copy-start(f32[2,32,256]{2,1,0:T(8,128)S(1)} %get-tuple-element.38) | copy-start | bytes 196612
  27.4 19.5 %copy-start.41 = (f32[2,32,256]{2,1,0:T(8,128)}, f32[2,32,256]{2,1,0:T(8,128)S(1)}, u32[]{:S(2)}) copy-start(f32[2,32,256]{2,1,0:T(8,128)S(1)} %get-tuple-element.39) | copy-start | bytes 196612
  27.4 19.5 %copy-start.43 = (f32[2,32,256]{2,1,0:T(8,128)}, f32[2,32,256]{2,1,0:T(8,128)S(1)}, u32[]{:S(2)}) copy-start(f32[2,32,256]{2,1,0:T(8,128)S(1)} %get-tuple-element.40) | copy-start | bytes 196612
  27.4 19.5 %copy-start.45 = (f32[2,32,256]{2,1,0:T(8,128)}, f32[2,32,256]{2,1,0:T(8,128)S(1)}, u32[]{:S(2)}) copy-start(f32[2,32,256]{2,1,0:T(8,128)S(1)} %get-tuple-element.41) | copy-start | bytes 196612
  27.4 21.2 %collective-permute-start.3 = (f32[4,5,1,34,256]{4,0,3,2,1:T(4,128)S(1)}, f32[4,5,1,34,256]{4,0,3,2,1:T(4,128)}, u32[]{:S(2)}, u32[]{:S(2)}) collective-permute-start(f32[4,5,1,34,256]{4,0,3,2,1:T(4,128)S(1)} %get-tuple-element.86), channel_id=1, source_target_pairs={{0,2},{2,4},{4,6},{6,0},{1,3},{3,5},{5,7},{7,1},{8,10},{10,12},{12... | collective-permute-start | bytes 2088968 | tf_op jit(solution)/shard_map/ppermute | solution.py:21
  56.9 7.4 %collective-permute-start.4 = (f32[4,5,2,1,256]{4,0,3,2,1:T(4,128)S(1)}, f32[4,5,2,1,256]{4,0,3,2,1:T(4,128)S(1)}, u32[]{:S(2)}, u32[]{:S(2)}) collective-permute-start(f32[4,5,2,1,256]{4,0,3,2,1:T(4,128)S(1)} %get-tuple-element.88), channel_id=1, source_target_pairs={{0,8},{8,16},{16,24},{24,32},{32,40},{40,48},{48,56},{56,64},{64,7... | collective-permute-start | bytes 122888 | tf_op jit(solution)/shard_map/ppermute | solution.py:21
  57.0 7.3 %collective-permute-start.5 = (f32[4,5,2,1,256]{4,0,3,2,1:T(4,128)S(1)}, f32[4,5,2,1,256]{4,0,3,2,1:T(4,128)S(1)}, u32[]{:S(2)}, u32[]{:S(2)}) collective-permute-start(f32[4,5,2,1,256]{4,0,3,2,1:T(4,128)S(1)} %get-tuple-element.89), channel_id=1, source_target_pairs={{8,0},{16,8},{24,16},{32,24},{40,32},{48,40},{56,48},{64,56},{72,6... | collective-permute-start | bytes 122888 | tf_op jit(solution)/shard_map/ppermute | solution.py:22
  65.0 15.2 %collective-permute-start.6 = (f32[4,5,1,34,256]{4,0,3,2,1:T(4,128)S(1)}, f32[4,5,1,34,256]{4,0,3,2,1:T(4,128)S(1)}, u32[]{:S(2)}, u32[]{:S(2)}) collective-permute-start(f32[4,5,1,34,256]{4,0,3,2,1:T(4,128)S(1)} %get-tuple-element.85), channel_id=1, source_target_pairs={{2,0},{4,2},{6,4},{0,6},{3,1},{5,3},{7,5},{1,7},{10,8},{12,10},{14... | collective-permute-start | bytes 2088968 | tf_op jit(solution)/shard_map/ppermute | solution.py:22
  75.2 6.1 %copy-start.18 = (f32[2,32,256]{2,1,0:T(8,128)S(1)}, f32[2,32,256]{2,1,0:T(8,128)}, u32[]{:S(2)}) copy-start(f32[2,32,256]{2,1,0:T(8,128)} %get-tuple-element.78) | copy-start | bytes 196612
  75.2 6.1 %copy-start.20 = (f32[2,32,256]{2,1,0:T(8,128)S(1)}, f32[2,32,256]{2,1,0:T(8,128)}, u32[]{:S(2)}) copy-start(f32[2,32,256]{2,1,0:T(8,128)} %get-tuple-element.79) | copy-start | bytes 196612
  75.2 6.1 %copy-start.22 = (f32[2,32,256]{2,1,0:T(8,128)S(1)}, f32[2,32,256]{2,1,0:T(8,128)}, u32[]{:S(2)}) copy-start(f32[2,32,256]{2,1,0:T(8,128)} %get-tuple-element.80) | copy-start | bytes 196612
  75.2 6.1 %copy-start.24 = (f32[2,32,256]{2,1,0:T(8,128)S(1)}, f32[2,32,256]{2,1,0:T(8,128)}, u32[]{:S(2)}) copy-start(f32[2,32,256]{2,1,0:T(8,128)} %get-tuple-element.81) | copy-start | bytes 196612
  75.2 6.1 %copy-start.26 = (f32[2,32,256]{2,1,0:T(8,128)S(1)}, f32[2,32,256]{2,1,0:T(8,128)}, u32[]{:S(2)}) copy-start(f32[2,32,256]{2,1,0:T(8,128)} %get-tuple-element.82) | copy-start | bytes 196612
  75.2 6.1 %copy-start.28 = (f32[2,32,256]{2,1,0:T(8,128)S(1)}, f32[2,32,256]{2,1,0:T(8,128)}, u32[]{:S(2)}) copy-start(f32[2,32,256]{2,1,0:T(8,128)} %get-tuple-element.83) | copy-start | bytes 196612
  75.2 17.0 %collective-permute-start.7 = (f32[4,5,1,34,256]{4,0,3,2,1:T(4,128)S(1)}, f32[4,5,1,34,256]{4,0,3,2,1:T(4,128)S(1)}, u32[]{:S(2)}, u32[]{:S(2)}) collective-permute-start(f32[4,5,1,34,256]{4,0,3,2,1:T(4,128)S(1)} %get-tuple-element.84), channel_id=1, source_target_pairs={{0,2},{2,4},{4,6},{6,0},{1,3},{3,5},{5,7},{7,1},{8,10},{10,12},{12... | collective-permute-start | bytes 2088968 | tf_op jit(solution)/shard_map/ppermute | solution.py:21
  86.0 6.2 %copy-start.5 = (f32[4,5,2,32,256]{4,3,2,1,0:T(8,128)S(1)}, f32[4,5,2,32,256]{4,3,2,1,0:T(8,128)}, u32[]{:S(2)}) copy-start(f32[4,5,2,32,256]{4,3,2,1,0:T(8,128)} %param.8) | copy-start | bytes 3932164
  86.0 6.2 %copy-start.6 = (f32[4,5,2,32,256]{4,0,3,2,1:T(4,128)S(1)}, f32[4,5,2,32,256]{4,0,3,2,1:T(4,128)}, u32[]{:S(2)}) copy-start(f32[4,5,2,32,256]{4,0,3,2,1:T(4,128)} %get-tuple-element.98) | copy-start | bytes 3932164
  86.0 6.2 %copy-start.106 = (f32[2,32,256]{2,1,0:T(8,128)S(1)}, f32[2,32,256]{2,1,0:T(8,128)}, u32[]{:S(2)}) copy-start(f32[2,32,256]{2,1,0:T(8,128)} %param.10) | copy-start | bytes 196612
  86.0 6.2 %copy-start.108 = (f32[2,32,256]{2,1,0:T(8,128)S(1)}, f32[2,32,256]{2,1,0:T(8,128)}, u32[]{:S(2)}) copy-start(f32[2,32,256]{2,1,0:T(8,128)} %param.11) | copy-start | bytes 196612
  86.0 6.2 %copy-start.109 = (f32[2,32,256]{2,1,0:T(8,128)S(1)}, f32[2,32,256]{2,1,0:T(8,128)}, u32[]{:S(2)}) copy-start(f32[2,32,256]{2,1,0:T(8,128)} %add_divide_fusion) | copy-start | bytes 196612
  99.1 9.1 %copy-start.112 = (s32[1024]{0:T(1024)S(1)}, s32[1024]{0:T(1024)}, u32[]{:S(2)}) copy-start(s32[1024]{0:T(1024)} %broadcast_clamp_fusion) | copy-start | bytes 12292
  108.2 20.8 %copy-start.115 = (pred[1024]{0:T(1024)(128)(4,1)S(1)}, pred[1024]{0:T(1024)(128)(4,1)}, u32[]{:S(2)}) copy-start(pred[1024]{0:T(1024)(128)(4,1)} %compare_and_fusion) | copy-start | bytes 3076
  129.0 9.9 %copy-start.111 = (f32[1,16,16]{2,1,0:T(8,128)S(1)}, f32[1,16,16]{2,1,0:T(8,128)}, u32[]{:S(2)}) copy-start(f32[1,16,16]{2,1,0:T(8,128)} %get-tuple-element.102) | copy-start | bytes 3076
  (63 other events, 92.9 us)
Sparse Core Ops, SparseCore 0:
  19.8 12.3 all-gather.1
  140.3 171.1 all-reduce.1
where the time goes:
time: 323 us; the launch traced here: 320 us
  waiting for transfers between devices  194 us (60%)
  local copies, waits for them, and re-layouts  49 us (15%)
  other arithmetic  33.8 us (10%)
  starting transfers between devices  18.4 us (6%)
  between operations  15.6 us (5%)
  matrix products  9.57 us (3%)
    psum x1, waiting for transfers between devices, body(): diameter_modes = lax.psum(mode_terms, ('passage', 'tm'))  170 us
    gather x1, local copies, waits for them, and re-layouts, body(): picked = jnp.take(rows, surface_cells[0], axis=3)  20.8 us
    ppermute x4, waiting for transfers between devices, with_halo(): after = lax.ppermute(leading, axis, down)  16.6 us
    unnamed x9, other arithmetic  15.6 us
    unnamed x240, local copies, waits for them, and re-layouts  14.4 us
    ppermute x4, starting transfers between devices, with_halo(): after = lax.ppermute(leading, axis, down)  13.6 us
    reshape x1, local copies, waits for them, and re-layouts, body(): rows.transpose(0, 1, 3, 4, 2, 5)  9.08 us
    dot_general x1, matrix products, body(): jnp.einsum('ab,avipk->bvipk', own_columns, lax.all_gather(start_rounded,...  8.3 us
  transfers between devices with their start and end apart: 10, of which 5 were waited for; matrix products, arithmetic and copies ran while one was open for 8% of the time, Pallas kernels for 0%

commit v1 on v0

v1 whole, which is shorter than its diff:
```python
import functools
import math

import jax
import jax.numpy as jnp
from jax import lax
from jax.experimental import pallas as pl
from jax.experimental.pallas import tpu as pltpu
from jax.sharding import PartitionSpec as P

PASSAGES = 16
SWEEPS = 2
NT = 8
F32 = jnp.float32
BF16 = jnp.bfloat16
VMEM = pl.BlockSpec(memory_space=pltpu.VMEM)
SMEM = pl.BlockSpec(memory_space=pltpu.SMEM)


def derivative(offset):
    offset = offset % NT
    if offset in (0, NT // 2):
        return 0.0
    angle = math.pi * offset / NT
    return 0.5 * (-1) ** offset * math.cos(angle) / math.sin(angle)


def call(kernel, outs, args, specs, mib, flops, name):
    nbytes = sum(a.size * a.dtype.itemsize for a in args) + sum(
        math.prod(o.shape) * o.dtype.itemsize for o in outs
    )
    return pl.pallas_call(
        kernel,
        out_shape=outs,
        in_specs=specs,
        out_specs=[VMEM] * len(outs),
        compiler_params=pltpu.CompilerParams(vmem_limit_bytes=mib << 20),
        cost_estimate=pl.CostEstimate(
            flops=flops, bytes_accessed=nbytes, transcendentals=0
        ),
        name=name,
    )(*args)


def by_parity(ids_ref, run):
    @pl.when(ids_ref[0] == 0)
    def _():
        run(1, 0)

    @pl.when(ids_ref[0] != 0)
    def _():
        run(0, 1)


def pack_layers(f_ref, a_ref, b_ref, low_ref, high_ref, layer_a, layer_b):
    nt, nv, ni, nj, nk = f_ref.shape
    for t in range(nt):
        for v in range(nv):
            a_ref[t, v] = f_ref[t, v, layer_a].astype(BF16)
            b_ref[t, v] = f_ref[t, v, layer_b].astype(BF16)
            for i in range(ni):
                row = (t * nv + v) * ni + i
                low_ref[row : row + 1, :] = f_ref[t, v, i, 0:1, :]
                high_ref[row : row + 1, :] = f_ref[t, v, i, nj - 1 : nj, :]


def prepare_kernel(ids_ref, f_ref, a_ref, b_ref, low_ref, high_ref):
    by_parity(
        ids_ref,
        lambda la, lb: pack_layers(f_ref, a_ref, b_ref, low_ref, high_ref, la, lb),
    )


def rhs_kernel(ids_ref, f_ref, src_ref, pa_ref, pb_ref, out_ref):
    nt, nv, ni, nj, nk = f_ref.shape

    def run(layer_a, layer_b):
        for layer, other in ((layer_a, pa_ref), (layer_b, pb_ref)):

            def one(v, carry):
                for j in range(0, nj, 16):
                    rows = slice(j, j + 16)
                    own = [
                        f_ref[t, v, layer, rows, :].astype(BF16).astype(F32)
                        for t in range(nt)
                    ]
                    far = [other[t, v, rows, :].astype(F32) for t in range(nt)]
                    times = own + far
                    for b in range(nt):
                        total = src_ref[b, v, layer, rows, :]
                        for n in range(1, NT // 2):
                            diff = times[(b + n) % NT] - times[(b - n) % NT]
                            total = total - derivative(n) * diff
                        out_ref[b, v, layer, rows, :] = total
                return carry

            lax.fori_loop(0, nv, one, 0)

    by_parity(ids_ref, run)


def shifted(f_ref, t, u, i, j, lanes, low_ref, high_ref, row, rows_id):
    nj = f_ref.shape[3]
    here = f_ref[t, u, i, j : j + 8, lanes]
    if j + 8 < nj:
        after = f_ref[t, u, i, j + 8 : j + 16, lanes]
        plus = jnp.where(rows_id == 7, pltpu.roll(after, 7, 0), pltpu.roll(here, 7, 0))
    else:
        edge = jnp.broadcast_to(high_ref[row : row + 1, lanes], here.shape)
        plus = jnp.where(rows_id == 7, edge, pltpu.roll(here, 7, 0))
    if j > 0:
        before = f_ref[t, u, i, j - 8 : j, lanes]
        minus = jnp.where(
            rows_id == 0, pltpu.roll(before, 1, 0), pltpu.roll(here, 1, 0)
        )
    else:
        edge = jnp.broadcast_to(low_ref[row : row + 1, lanes], here.shape)
        minus = jnp.where(rows_id == 0, edge, pltpu.roll(here, 1, 0))
    return here, plus, minus


def sweep_tile(refs, out_ref, halo_of, i, j, lanes):
    f_ref, rhs_ref, jac_ref, sig_ref, dmp_ref, low_ref, high_ref = refs
    nt, nv, ni = f_ref.shape[:3]
    pair = slice(j // 16 * 16, j // 16 * 16 + 16)
    half = slice(j % 16, j % 16 + 8)
    halo = halo_of[i]
    sigma = sig_ref[i, j : j + 8, lanes]
    damping = dmp_ref[i, j : j + 8, lanes]
    scaling = 1.0 / (sigma + 4.0 * damping)
    rows_id = lax.broadcasted_iota(jnp.int32, sigma.shape, 0)
    acc = [[None] * nv for _ in range(nt)]
    for u in range(nv):
        jac = [
            [jac_ref[d, u, v, i, pair, lanes].astype(F32)[half] for v in range(nv)]
            for d in range(2)
        ]
        for t in range(nt):
            row = (t * nv + u) * ni + i
            here, plus_j, minus_j = shifted(
                f_ref, t, u, i, j, lanes, low_ref, high_ref, row, rows_id
            )
            outer = halo[t, u, pair, lanes].astype(F32)[half]
            inner = f_ref[t, u, 1 - i, j : j + 8, lanes]
            plus_i, minus_i = (outer, inner) if i else (inner, outer)
            diff_i, diff_j = here - plus_i, here - plus_j
            both = diff_i + diff_j + ((here - minus_i) + (here - minus_j))
            own = sigma * here + damping * both
            for v in range(nv):
                term = jac[0][v] * diff_i + jac[1][v] * diff_j
                if v == u:
                    term = term + own
                acc[t][v] = term if acc[t][v] is None else acc[t][v] + term
    for t in range(nt):
        for v in range(nv):
            spot = (t, v, i, slice(j, j + 8), lanes)
            out_ref[spot] = f_ref[spot] + (rhs_ref[spot] - acc[t][v]) * scaling


def sweep_all(refs, out_ref, halo_of):
    nt, nv, ni, nj, nk = out_ref.shape

    def one(k, carry):
        lanes = pl.ds(pl.multiple_of(k * 128, 128), 128)
        for i in range(ni):
            for j in range(0, nj, 8):
                sweep_tile(refs, out_ref, halo_of, i, j, lanes)
        return carry

    lax.fori_loop(0, nk // 128, one, 0)


def first_kernel(ids_ref, *refs):
    ins, ha_ref, hb_ref = refs[:7], refs[7], refs[8]
    out_ref, a_ref, b_ref, low_ref, high_ref = refs[9:]

    def run(layer_a, layer_b):
        sweep_all(ins, out_ref, {layer_a: ha_ref, layer_b: hb_ref})
        pack_layers(out_ref, a_ref, b_ref, low_ref, high_ref, layer_a, layer_b)

    by_parity(ids_ref, run)


def second_kernel(ids_ref, *refs):
    ins, ha_ref, hb_ref, w_ref = refs[:7], refs[7], refs[8], refs[9]
    out_ref, sens_ref = refs[10:]
    nt, nv, ni, nj, nk = out_ref.shape

    def run(layer_a, layer_b):
        sweep_all(ins, out_ref, {layer_a: ha_ref, layer_b: hb_ref})

    by_parity(ids_ref, run)
    side = ids_ref[1]
    start = pl.multiple_of(side * (nj - 8), 8)
    mask = lax.broadcasted_iota(jnp.int32, (8, nk), 0) == side * 7
    for i in range(ni):
        total = jnp.zeros((8, nk), F32)
        for t in range(nt):
            for v in range(nv):
                weight = w_ref[t * nv + v : t * nv + v + 1, i * nk : (i + 1) * nk]
                total = total + out_ref[t, v, i, pl.ds(start, 8), :] * weight
        value = jnp.sum(jnp.where(mask, total, 0.0), axis=0, keepdims=True)
        for c in range(nk // 128):
            sens_ref[:, i * (nk // 128) + c, :] = jnp.broadcast_to(
                value[:, c * 128 : (c + 1) * 128], (sens_ref.shape[0], 128)
            )


def split3(x):
    one = x.astype(BF16)
    rest = x - one.astype(F32)
    two = rest.astype(BF16)
    three = (rest - two.astype(F32)).astype(BF16)
    return one, two, three


def one_hot(cells_ref, first, rows):
    cells = cells_ref.shape[1]
    index = lax.broadcasted_iota(jnp.int32, (rows, cells), 0) + first
    return jnp.where(cells_ref[0:1, :] == index, 1.0, 0.0).astype(BF16)


def weights_kernel(ids_ref, cells_ref, w_ref, out_ref):
    half = out_ref.shape[1]
    chosen = one_hot(cells_ref, ids_ref[1] * half, half)
    out_ref[...] = sum(
        lax.dot_general(
            part, chosen, (((1,), (1,)), ((), ())), preferred_element_type=F32
        )
        for part in split3(w_ref[...])
    )


def modes_kernel(cells_ref, table_ref, sens_ref, out_ref):
    devices = sens_ref.shape[0] // 2
    pieces = sens_ref.shape[1]
    half = pieces * 128
    total = []
    for side in range(2):
        modes = jnp.concatenate(
            [
                jnp.dot(
                    table_ref[side],
                    sens_ref[:, c, :],
                    precision=lax.Precision.HIGHEST,
                    preferred_element_type=F32,
                )
                for c in range(pieces)
            ],
            axis=1,
        )
        chosen = one_hot(cells_ref, side * half, half)
        for part in split3(modes):
            total.append(jnp.dot(part, chosen, preferred_element_type=F32))
    out_ref[...] = functools.reduce(lambda x, y: x + y, total)


def mode_table(devices):
    per = devices // PASSAGES
    m = jnp.arange(PASSAGES, dtype=jnp.int32)[:, None]
    d = jnp.arange(devices, dtype=jnp.int32)[None, :]
    angle = 2.0 * jnp.pi * (m * (d // per) % PASSAGES).astype(F32) / PASSAGES
    base = jnp.concatenate([jnp.cos(angle), -jnp.sin(angle)]) / PASSAGES**0.5
    sides = [jnp.where(d % per == s, base, 0.0) for s in range(per)]
    return jnp.repeat(jnp.stack(sides), 2, axis=2)


def body(start, source, jac, sigma, damping, cells, weights):
    nt, nv, ni, nj, nk = start.shape
    ring = lax.axis_size("passage")
    cell = lax.axis_index("cell")
    ids = jnp.stack([cell % 2, lax.axis_index("passage") % 2]).astype(jnp.int32)
    n_cell = lax.axis_size("cell")
    even = [(c, c ^ 1) for c in range(n_cell)]
    odd = [(c, c + 1) for c in range(1, n_cell - 1, 2)]
    odd += [(b, a) for a, b in odd]
    up = [(d, (d + 1) % ring) for d in range(ring)]
    down = [(d, (d - 1) % ring) for d in range(ring)]
    swap = [(0, 1), (1, 0)]

    field_like = jax.ShapeDtypeStruct(start.shape, F32)
    layer_like = jax.ShapeDtypeStruct((nt, nv, nj, nk), BF16)
    rows_like = jax.ShapeDtypeStruct((nt * nv * ni, nk), F32)
    sends = [layer_like, layer_like, rows_like, rows_like]

    def exchange(a, b, low, high):
        with jax.named_scope("halos"):
            return (
                lax.ppermute(high, "passage", up),
                lax.ppermute(low, "passage", down),
                lax.ppermute(a, "cell", even),
                lax.ppermute(b, "cell", odd),
            )

    a, b, low, high = call(
        prepare_kernel, sends, (ids, start), [SMEM, VMEM], 8, 10**6, "prepare"
    )
    before, after, ha, hb = exchange(a, b, low, high)
    pa = lax.ppermute(a, "tm", swap)
    pb = lax.ppermute(b, "tm", swap)
    ordered = call(
        weights_kernel,
        [jax.ShapeDtypeStruct((nt * nv, ni * nk), F32)],
        (ids, cells, weights.reshape(nt * nv, -1)),
        [SMEM, VMEM, VMEM],
        16,
        10**6,
        "weights",
    )[0]
    rhs = call(
        rhs_kernel,
        [field_like],
        (ids, start, source, pa, pb),
        [SMEM] + [VMEM] * 4,
        16,
        10**7,
        "rhs",
    )[0]
    field, a, b, low, high = call(
        first_kernel,
        [field_like] + sends,
        (ids, start, rhs, jac, sigma, damping, before, after, ha, hb),
        [SMEM] + [VMEM] * 9,
        24,
        2 * 10**7,
        "first_sweep",
    )
    before, after, ha, hb = exchange(a, b, low, high)
    group = ("passage", "tm")
    members = 2 * ring
    field, sens = call(
        second_kernel,
        [field_like, jax.ShapeDtypeStruct((members, ni * nk // 128, 128), F32)],
        (ids, field, rhs, jac, sigma, damping, before, after, ha, hb, ordered),
        [SMEM] + [VMEM] * 10,
        24,
        2 * 10**7,
        "second_sweep",
    )
    with jax.named_scope("share_sensitivities"):
        gathered = lax.all_to_all(sens, group, 0, 0, tiled=True)
    modes = call(
        modes_kernel,
        [jax.ShapeDtypeStruct((2 * PASSAGES, cells.shape[1]), F32)],
        (cells, mode_table(ring), gathered),
        [VMEM] * 3,
        16,
        10**7,
        "modes",
    )[0]
    return field, modes.reshape(2, PASSAGES, -1)


def solution(mesh):
    in_specs = (
        P("tm", None, "cell", "passage", None),
        P("tm", None, "cell", "passage", None),
        P(None, None, None, "cell", "passage", None),
        P("cell", "passage", None),
        P("cell", "passage", None),
        P("cell", None),
        P("tm", None, "cell"),
    )
    out_specs = (P("tm", None, "cell", "passage", None), P(None, None, "cell"))
    return jax.shard_map(
        body, mesh=mesh, in_specs=in_specs, out_specs=out_specs, check_vma=False
    )
```

time: 323 us -> 64.3 us (0.20)
  waiting for transfers between devices: 194 us -> 10.8 us
  local copies, waits for them, and re-layouts: 49 us -> 6.88 us
  other arithmetic: 33.8 us -> 1.52 us
  between operations: 15.6 us -> 0.91 us
  Pallas kernels: 0 us -> 13.1 us
  starting transfers between devices: 18.4 us -> 30 us
  matrix products: 9.57 us -> 0 us
    psum x1 -> x0, waiting for transfers between devices: 170 us -> none  [body(): diameter_modes = lax.psum(mode_terms, ('passage', 'tm'))]
    ppermute x8 -> x10, waiting for transfers between devices: 23.5 us -> 0.03 us  [the longest x2 0.01 us: exchange(): lax.ppermute(low, 'passage', down)]
    gather x2 -> x0, local copies, waits for them, and re-layouts: 22.3 us -> none  [the longest x1 20.8 us: body(): picked = jnp.take(rows, surface_cells[0], axis=3)]
    unnamed x9 -> x0, other arithmetic: 15.6 us -> none
    pallas_call x0 -> x6, Pallas kernels: none -> 13.1 us  [call(): pl.pallas_call(kernel, out_shape=outs, in_specs=specs, out_specs=[VMEM] *...]
    all_to_all x0 -> x1, waiting for transfers between devices: none -> 10.8 us  [body(): gathered = lax.all_to_all(sens, group, 0, 0, tiled=True)]
    dot_general x2 -> x0, matrix products: 9.57 us -> none  [the longest x1 8.3 us: body(): jnp.einsum('ab,avipk->bvipk', own_columns, lax.all_gather(start_rounded,...]
    unnamed x240 -> x29, local copies, waits for them, and re-layouts: 14.4 us -> 5.87 us
  transfers between devices with their start and end apart: 10 -> 11, of which waited for: 5 -> 1; matrix products, arithmetic and copies ran while one was open for 8% -> 5% of each run, Pallas kernels for 0% -> 4%
where the time goes in v1:
time: 64.3 us; the launch traced here: 63.2 us
  starting transfers between devices  30 us (47%)
  Pallas kernels  13.1 us (20%)
  waiting for transfers between devices  10.8 us (17%)
  local copies, waits for them, and re-layouts  6.88 us (11%)
  other arithmetic  1.52 us (2%)
  between operations  0.91 us (1%)
    ppermute x2, starting transfers between devices, exchange(): lax.ppermute(low, 'passage', down)  13.2 us
    pallas_call x6, Pallas kernels, call(): pl.pallas_call(kernel, out_shape=outs, in_specs=specs, out_specs=[VMEM] *...  13.1 us
    all_to_all x1, waiting for transfers between devices, body(): gathered = lax.all_to_all(sens, group, 0, 0, tiled=True)  10.8 us
    all_to_all x1, starting transfers between devices, body(): gathered = lax.all_to_all(sens, group, 0, 0, tiled=True)  7.9 us
    unnamed x29, local copies, waits for them, and re-layouts  5.87 us
    ppermute x2, starting transfers between devices, exchange(): lax.ppermute(b, 'cell', odd)  4.48 us
    ppermute x2, starting transfers between devices, exchange(): lax.ppermute(a, 'cell', even)  2.19 us
    ppermute x2, starting transfers between devices, exchange(): lax.ppermute(high, 'passage', up)  1.58 us
  transfers between devices with their start and end apart: 11, of which 1 were waited for; matrix products, arithmetic and copies ran while one was open for 5% of the time, Pallas kernels for 4%

profile of v1, /device:TPU:8, one launch (start us, length us, event | category | flops | bytes accessed | tf_op | source)
XLA Modules:
  0.0 63.2 jit_solution(17279194046590210333)
XLA Ops:
  0.6 0.1 pad_add_fusion.ids_ref
  0.7 0.0 copy-start
  0.7 1.3 %copy-done = f32[4,5,2,32,256]{4,3,2,1,0:T(8,128)S(1)} copy-done((f32[4,5,2,32,256]{4,3,2,1,0:T(8,128)S(1)}, f32[4,5,2,32,256]{4,3,2,1,0:T(8,128)}, u32[]{:S(2)}) %copy-start) | copy-done | bytes 1310744
  2.0 0.0 copy-start.1
  2.0 0.6 %prepare.1 = (bf16[4,5,32,256]{3,2,1,0:T(8,128)(2,1)S(1)}, bf16[4,5,32,256]{3,2,1,0:T(8,128)(2,1)S(1)}, f32[40,256]{1,0:T(8,128)S(1)}, f32[40,256]{1,0:T(8,128)S(1)}) custom-call(s32[2]{0:T(128)S(1)} %pad_add_fusion.ids_ref, f32[4,5,2,32,256]{4,3,2,1,0:T(8,128)S(1)} %copy-done), custom_call_target="tpu_custom_call" | custom-call | flops 1000000 | bytes 2048008 | tf_op jit(solution)/shard_map/prepare/pallas_call | solution.py:32
  2.7 0.1 collective-permute-start
  2.8 0.5 collective-permute-start.1
  3.3 2.2 %collective-permute-start.4 = (bf16[4,5,32,256]{3,2,1,0:T(8,128)(2,1)S(1)}, bf16[4,5,32,256]{3,2,1,0:T(8,128)(2,1)S(1)}, u32[]{:S(2)}, u32[]{:S(2)}) collective-permute-start(bf16[4,5,32,256]{3,2,1,0:T(8,128)(2,1)S(1)} %get-tuple-element.13), channel_id=1, source_target_pairs={{0,2},{2,0},{4,6},{6,4},{1,3},{3,1},{5,7},{7,5},{8,10},{10,8},{12,... | collective-permute-start | bytes 983048 | tf_op jit(solution)/shard_map/halos/ppermute | solution.py:291
  5.5 2.6 %collective-permute-start.5 = (bf16[4,5,32,256]{3,2,1,0:T(8,128)(2,1)S(1)}, bf16[4,5,32,256]{3,2,1,0:T(8,128)(2,1)S(1)}, u32[]{:S(2)}, u32[]{:S(2)}) collective-permute-start(bf16[4,5,32,256]{3,2,1,0:T(8,128)(2,1)S(1)} %get-tuple-element.14), channel_id=1, source_target_pairs={{2,4},{4,2},{3,5},{5,3},{10,12},{12,10},{11,13},{13,11},{18,20},{2... | collective-permute-start | bytes 983048 | tf_op jit(solution)/shard_map/halos/ppermute | solution.py:292
  8.1 1.6 %collective-permute-start.2 = (f32[40,256]{1,0:T(8,128)S(1)}, f32[40,256]{1,0:T(8,128)S(1)}, u32[]{:S(2)}, u32[]{:S(2)}) collective-permute-start(f32[40,256]{1,0:T(8,128)S(1)} %get-tuple-element.15), channel_id=1, source_target_pairs={{0,8},{8,16},{16,24},{24,32},{32,40},{40,48},{48,56},{56,64},{64,7... | collective-permute-start | bytes 122888 | tf_op jit(solution)/shard_map/halos/ppermute | solution.py:289
  9.6 0.0 collective-permute-done.pa_ref
  9.6 6.7 %collective-permute-start.3 = (f32[40,256]{1,0:T(8,128)S(1)}, f32[40,256]{1,0:T(8,128)S(1)}, u32[]{:S(2)}, u32[]{:S(2)}) collective-permute-start(f32[40,256]{1,0:T(8,128)S(1)} %get-tuple-element.16), channel_id=1, source_target_pairs={{0,248},{8,0},{16,8},{24,16},{32,24},{40,32},{48,40},{56,48},{64,5... | collective-permute-start | bytes 122888 | tf_op jit(solution)/shard_map/halos/ppermute | solution.py:290
  16.3 0.0 copy-start.2
  16.3 0.0 collective-permute-done.1.pb_ref
  16.3 0.0 copy-done.1
  16.3 0.0 copy-start.3
  16.3 1.4 %copy-done.3 = f32[4,5,2,32,256]{4,3,2,1,0:T(8,128)S(1)} copy-done((f32[4,5,2,32,256]{4,3,2,1,0:T(8,128)S(1)}, f32[4,5,2,32,256]{4,3,2,1,0:T(8,128)}, u32[]{:S(2)}) %copy-start.3) | copy-done | bytes 1310744
  17.7 0.0 copy-start.6
  17.7 0.0 copy-start.7
  17.7 1.1 %rhs.1.refs_1_ = f32[4,5,2,32,256]{4,3,2,1,0:T(8,128)S(1)} custom-call(s32[2]{0:T(128)S(1)} %pad_add_fusion.ids_ref, f32[4,5,2,32,256]{4,3,2,1,0:T(8,128)S(1)} %copy-done.1, f32[4,5,2,32,256]{4,3,2,1,0:T(8,128)S(1)} %copy-done.3, bf16[4,5,32,256]{3,2,1,0:T(8,128)(2,1)S(1)} %collective-permute-done.pa_ref, ...), custom_call_target="tpu_custom_call" | custom-call | flops 10000000 | bytes 4587528 | tf_op jit(solution)/shard_map/rhs/pallas_call | solution.py:32
  18.9 0.0 copy-start.9
  18.9 0.0 copy-start.8
  18.9 0.0 collective-permute-done.2.refs_5_
  18.9 0.0 collective-permute-done.3.refs_6_
  18.9 0.0 collective-permute-done.4.refs_7_
  18.9 0.0 collective-permute-done.5.refs_8_
  18.9 0.0 copy-done.2
  18.9 0.0 copy-done.6
  18.9 0.0 copy-done.7
  18.9 3.5 %first_sweep.1 = (f32[4,5,2,32,256]{4,3,2,1,0:T(8,128)S(1)}, bf16[4,5,32,256]{3,2,1,0:T(8,128)(2,1)}, bf16[4,5,32,256]{3,2,1,0:T(8,128)(2,1)}, f32[40,256]{1,0:T(8,128)}, f32[40,256]{1,0:T(8,128)}) custom-call(s32[2]{0:T(128)S(1)} %pad_add_fusion.ids_ref, f32[4,5,2,32,256]{4,3,2,1,0:T(8,128)S(1)} %copy-done.1, f32[4,5,2,32,256]{4,3,2,1,0:T(8,128)S(1)} %rhs.1.refs_1_, ...), custom_call_target="tpu_custom_call" | custom-call | flops 20000000 | bytes 7176200 | tf_op jit(solution)/shard_map/first_sweep/pallas_call | solution.py:32
  22.4 0.0 copy-start.4
  22.4 1.1 %copy-done.4 = f32[4,5,2,32,256]{4,3,2,1,0:T(8,128)} copy-done((f32[4,5,2,32,256]{4,3,2,1,0:T(8,128)}, f32[4,5,2,32,256]{4,3,2,1,0:T(8,128)S(1)}, u32[]{:S(2)}) %copy-start.4) | copy-done | bytes 1310744
  23.5 0.0 collective-permute-start.8
  23.5 1.9 %collective-permute-start.9 = (bf16[4,5,32,256]{3,2,1,0:T(8,128)(2,1)}, bf16[4,5,32,256]{3,2,1,0:T(8,128)(2,1)}, u32[]{:S(2)}, u32[]{:S(2)}) collective-permute-start(bf16[4,5,32,256]{3,2,1,0:T(8,128)(2,1)} %get-tuple-element.21), channel_id=1, source_target_pairs={{2,4},{4,2},{3,5},{5,3},{10,12},{12,10},{11,13},{13,11},{18,20},{2... | collective-permute-start | bytes 983048 | tf_op jit(solution)/shard_map/halos/ppermute | solution.py:292
  25.4 0.8 %cosine_bitcast_fusion = (f32[1,16,32]{1,2,0:T(8,128)}, f32[1,16,32]{1,2,0:T(8,128)}) fusion(s32[32]{0:T(128)S(1)} %and_select_fusion), kind=kLoop, calls=%fused_computation.9 | loop fusion | flops 7680 | bytes 4224 | tf_op jit(solution)/shard_map/concatenate | solution.py:263
  26.2 0.0 collective-permute-start.6
  26.2 6.6 %collective-permute-start.7 = (f32[40,256]{1,0:T(8,128)}, f32[40,256]{1,0:T(8,128)}, u32[]{:S(2)}, u32[]{:S(2)}) collective-permute-start(f32[40,256]{1,0:T(8,128)} %get-tuple-element.19), channel_id=1, source_target_pairs={{0,248},{8,0},{16,8},{24,16},{32,24},{40,32},{48,40},{56,48},{64,5... | collective-permute-start | bytes 122888 | tf_op jit(solution)/shard_map/halos/ppermute | solution.py:290
  32.7 0.6 broadcast_compare_fusion
  33.3 0.0 copy-done.9
  33.3 0.7 %copy.10 = f32[4,5,1024]{2,1,0:T(8,128)} copy(f32[4,5,1024]{2,0,1:T(4,128)S(1)} %copy-done.9) | data formatting | bytes 163840 | tf_op args[6]
  34.0 0.9 %reshape.197.w_ref = f32[20,1024]{1,0:T(8,128)S(1)} reshape(f32[4,5,1024]{2,1,0:T(8,128)} %copy.10) | data formatting | bytes 163840 | tf_op jit(solution)/shard_map/reshape | solution.py:304
  34.9 0.0 copy-done.8
  35.0 1.6 %weights.1.refs_9_ = f32[20,512]{1,0:T(8,128)S(1)} custom-call(s32[2]{0:T(128)S(1)} %pad_add_fusion.ids_ref, s32[1,1024]{1,0:T(1,128)S(1)} %copy-done.8, f32[20,1024]{1,0:T(8,128)S(1)} %reshape.197.w_ref), custom_call_target="tpu_custom_call" | custom-call | flops 1000000 | bytes 126984 | tf_op jit(solution)/shard_map/weights/pallas_call | solution.py:32
  36.5 0.0 collective-permute-done.6.refs_5_
  36.5 0.0 collective-permute-done.7.refs_6_
  36.5 0.0 collective-permute-done.8.refs_7_
  36.5 0.0 collective-permute-done.9.refs_8_
  36.6 0.0 copy-start.5
  36.6 1.3 %copy-done.5 = f32[4,5,2,32,256]{4,3,2,1,0:T(8,128)S(1)} copy-done((f32[4,5,2,32,256]{4,3,2,1,0:T(8,128)S(1)}, f32[4,5,2,32,256]{4,3,2,1,0:T(8,128)}, u32[]{:S(2)}) %copy-start.5) | copy-done | bytes 1310744
  37.9 0.0 copy-start.10
  37.9 0.0 copy-start.11
  37.9 0.0 copy-start.12
  37.9 0.0 copy-start.13
  37.9 4.1 %second_sweep.1 = (f32[4,5,2,32,256]{4,3,2,1,0:T(8,128)}, f32[64,4,128]{2,1,0:T(4,128)}) custom-call(s32[2]{0:T(128)S(1)} %pad_add_fusion.ids_ref, f32[4,5,2,32,256]{4,3,2,1,0:T(8,128)S(1)} %copy-done.5, f32[4,5,2,32,256]{4,3,2,1,0:T(8,128)S(1)} %rhs.1.refs_1_, bf16[2,5,5,2,32,256]{5,4,3,2,1,0:T(8,128)(2,1)S(1)} %copy-done.2, f32[2,32,256]{2,1,0:T(8,128)S(1)} %copy-done.6, ...), custom_call_target="tpu_custom_call" | custom-call | flops 20000000 | bytes 6610952 | tf_op jit(solution)/shard_map/second_sweep/pallas_call | solution.py:32
  42.0 7.9 %all-to-all-start = ((f32[64,4,128]{2,1,0:T(4,128)}), f32[64,4,128]{2,1,0:T(4,128)S(1)}, u32[]{:S(2)}, u32[]{:S(2)}) async-start(f32[64,4,128]{2,1,0:T(4,128)} %get-tuple-element.23), calls=%async_computation | async-start | bytes 262144 | tf_op jit(solution)/shard_map/share_sensitivities/all_to_all | solution.py:341
  49.9 0.0 copy-done.10
  49.9 0.0 copy-done.11
  49.9 0.0 copy-done.12
  50.0 0.0 copy-done.13
  50.0 0.1 broadcast_select_fusion.1
  50.1 0.1 copy.11.table_ref
  50.2 10.8 %all-to-all-done.sens_ref = f32[64,4,128]{2,1,0:T(4,128)S(1)} async-done(((f32[64,4,128]{2,1,0:T(4,128)}), f32[64,4,128]{2,1,0:T(4,128)S(1)}, u32[]{:S(2)}, u32[]{:S(2)}) %all-to-all-start) | async-done | bytes 131104 | tf_op jit(solution)/shard_map/share_sensitivities/all_to_all | solution.py:341
  61.0 2.2 %modes.1 = f32[32,1024]{1,0:T(8,128)} custom-call(s32[1,1024]{1,0:T(1,128)S(1)} %copy-done.8, f32[2,32,64]{2,1,0:T(8,128)S(1)} %copy.11.table_ref, f32[64,4,128]{2,1,0:T(4,128)S(1)} %all-to-all-done.sens_ref), custom_call_target="tpu_custom_call" | custom-call | flops 10000000 | bytes 282624 | tf_op jit(solution)/shard_map/modes/pallas_call | solution.py:32
  (3 shorter events, 0.0 us)
Async XLA Ops:
  0.7 1.3 %copy-start = (f32[4,5,2,32,256]{4,3,2,1,0:T(8,128)S(1)}, f32[4,5,2,32,256]{4,3,2,1,0:T(8,128)}, u32[]{:S(2)}) copy-start(f32[4,5,2,32,256]{4,3,2,1,0:T(8,128)} %refs_0_.1) | copy-start | bytes 3932164
  2.0 14.3 %copy-start.1 = (f32[4,5,2,32,256]{4,3,2,1,0:T(8,128)S(1)}, f32[4,5,2,32,256]{4,3,2,1,0:T(8,128)}, u32[]{:S(2)}) copy-start(f32[4,5,2,32,256]{4,3,2,1,0:T(8,128)} %refs_0_.1) | copy-start | bytes 3932164
  2.7 6.9 %collective-permute-start = (bf16[4,5,32,256]{3,2,1,0:T(8,128)(2,1)S(1)}, bf16[4,5,32,256]{3,2,1,0:T(8,128)(2,1)S(1)}, u32[]{:S(2)}, u32[]{:S(2)}) collective-permute-start(bf16[4,5,32,256]{3,2,1,0:T(8,128)(2,1)S(1)} %get-tuple-element.13), channel_id=1, source_target_pairs={{0,1},{1,0},{2,3},{3,2},{4,5},{5,4},{6,7},{7,6},{8,9},{9,8},{10,11... | collective-permute-start | bytes 983048 | tf_op jit(solution)/shard_map/ppermute | solution.py:299
  2.8 13.5 %collective-permute-start.1 = (bf16[4,5,32,256]{3,2,1,0:T(8,128)(2,1)S(1)}, bf16[4,5,32,256]{3,2,1,0:T(8,128)(2,1)S(1)}, u32[]{:S(2)}, u32[]{:S(2)}) collective-permute-start(bf16[4,5,32,256]{3,2,1,0:T(8,128)(2,1)S(1)} %get-tuple-element.14), channel_id=1, source_target_pairs={{0,1},{1,0},{2,3},{3,2},{4,5},{5,4},{6,7},{7,6},{8,9},{9,8},{10,11... | collective-permute-start | bytes 983048 | tf_op jit(solution)/shard_map/ppermute | solution.py:300
  3.3 15.6 %collective-permute-start.4 = (bf16[4,5,32,256]{3,2,1,0:T(8,128)(2,1)S(1)}, bf16[4,5,32,256]{3,2,1,0:T(8,128)(2,1)S(1)}, u32[]{:S(2)}, u32[]{:S(2)}) collective-permute-start(bf16[4,5,32,256]{3,2,1,0:T(8,128)(2,1)S(1)} %get-tuple-element.13), channel_id=1, source_target_pairs={{0,2},{2,0},{4,6},{6,4},{1,3},{3,1},{5,7},{7,5},{8,10},{10,8},{12,... | collective-permute-start | bytes 983048 | tf_op jit(solution)/shard_map/halos/ppermute | solution.py:291
  5.5 13.4 %collective-permute-start.5 = (bf16[4,5,32,256]{3,2,1,0:T(8,128)(2,1)S(1)}, bf16[4,5,32,256]{3,2,1,0:T(8,128)(2,1)S(1)}, u32[]{:S(2)}, u32[]{:S(2)}) collective-permute-start(bf16[4,5,32,256]{3,2,1,0:T(8,128)(2,1)S(1)} %get-tuple-element.14), channel_id=1, source_target_pairs={{2,4},{4,2},{3,5},{5,3},{10,12},{12,10},{11,13},{13,11},{18,20},{2... | collective-permute-start | bytes 983048 | tf_op jit(solution)/shard_map/halos/ppermute | solution.py:292
  8.1 10.8 %collective-permute-start.2 = (f32[40,256]{1,0:T(8,128)S(1)}, f32[40,256]{1,0:T(8,128)S(1)}, u32[]{:S(2)}, u32[]{:S(2)}) collective-permute-start(f32[40,256]{1,0:T(8,128)S(1)} %get-tuple-element.15), channel_id=1, source_target_pairs={{0,8},{8,16},{16,24},{24,32},{32,40},{40,48},{48,56},{56,64},{64,7... | collective-permute-start | bytes 122888 | tf_op jit(solution)/shard_map/halos/ppermute | solution.py:289
  9.6 9.3 %collective-permute-start.3 = (f32[40,256]{1,0:T(8,128)S(1)}, f32[40,256]{1,0:T(8,128)S(1)}, u32[]{:S(2)}, u32[]{:S(2)}) collective-permute-start(f32[40,256]{1,0:T(8,128)S(1)} %get-tuple-element.16), channel_id=1, source_target_pairs={{0,248},{8,0},{16,8},{24,16},{32,24},{40,32},{48,40},{56,48},{64,5... | collective-permute-start | bytes 122888 | tf_op jit(solution)/shard_map/halos/ppermute | solution.py:290
  16.3 2.6 %copy-start.2 = (bf16[2,5,5,2,32,256]{5,4,3,2,1,0:T(8,128)(2,1)S(1)}, bf16[2,5,5,2,32,256]{5,4,3,2,1,0:T(8,128)(2,1)}, u32[]{:S(2)}) copy-start(bf16[2,5,5,2,32,256]{5,4,3,2,1,0:T(8,128)(2,1)} %refs_2_.3) | copy-start | bytes 4915204
  16.3 1.4 %copy-start.3 = (f32[4,5,2,32,256]{4,3,2,1,0:T(8,128)S(1)}, f32[4,5,2,32,256]{4,3,2,1,0:T(8,128)}, u32[]{:S(2)}) copy-start(f32[4,5,2,32,256]{4,3,2,1,0:T(8,128)} %src_ref.1) | copy-start | bytes 3932164
  17.7 1.2 %copy-start.6 = (f32[2,32,256]{2,1,0:T(8,128)S(1)}, f32[2,32,256]{2,1,0:T(8,128)}, u32[]{:S(2)}) copy-start(f32[2,32,256]{2,1,0:T(8,128)} %refs_3_.3) | copy-start | bytes 196612
  17.7 1.2 %copy-start.7 = (f32[2,32,256]{2,1,0:T(8,128)S(1)}, f32[2,32,256]{2,1,0:T(8,128)}, u32[]{:S(2)}) copy-start(f32[2,32,256]{2,1,0:T(8,128)} %refs_4_.3) | copy-start | bytes 196612
  18.9 14.5 %copy-start.9 = (f32[4,5,1024]{2,0,1:T(4,128)S(1)}, f32[4,5,1024]{2,0,1:T(4,128)}, u32[]{:S(2)}) copy-start(f32[4,5,1024]{2,0,1:T(4,128)} %param.13) | copy-start | bytes 245764
  18.9 16.1 %copy-start.8 = (s32[1,1024]{1,0:T(1,128)S(1)}, s32[1,1024]{1,0:T(1,128)}, u32[]{:S(2)}) copy-start(s32[1,1024]{1,0:T(1,128)} %cells_ref.3) | copy-start | bytes 12292
  22.4 1.1 %copy-start.4 = (f32[4,5,2,32,256]{4,3,2,1,0:T(8,128)}, f32[4,5,2,32,256]{4,3,2,1,0:T(8,128)S(1)}, u32[]{:S(2)}) copy-start(f32[4,5,2,32,256]{4,3,2,1,0:T(8,128)S(1)} %get-tuple-element.17.refs_0_) | copy-start | bytes 3932164
  23.5 13.1 %collective-permute-start.8 = (bf16[4,5,32,256]{3,2,1,0:T(8,128)(2,1)}, bf16[4,5,32,256]{3,2,1,0:T(8,128)(2,1)S(1)}, u32[]{:S(2)}, u32[]{:S(2)}) collective-permute-start(bf16[4,5,32,256]{3,2,1,0:T(8,128)(2,1)} %get-tuple-element.20), channel_id=1, source_target_pairs={{0,2},{2,0},{4,6},{6,4},{1,3},{3,1},{5,7},{7,5},{8,10},{10,8},{12,... | collective-permute-start | bytes 983048 | tf_op jit(solution)/shard_map/halos/ppermute | solution.py:291
  23.5 13.1 %collective-permute-start.9 = (bf16[4,5,32,256]{3,2,1,0:T(8,128)(2,1)}, bf16[4,5,32,256]{3,2,1,0:T(8,128)(2,1)}, u32[]{:S(2)}, u32[]{:S(2)}) collective-permute-start(bf16[4,5,32,256]{3,2,1,0:T(8,128)(2,1)} %get-tuple-element.21), channel_id=1, source_target_pairs={{2,4},{4,2},{3,5},{5,3},{10,12},{12,10},{11,13},{13,11},{18,20},{2... | collective-permute-start | bytes 983048 | tf_op jit(solution)/shard_map/halos/ppermute | solution.py:292
  26.2 10.4 %collective-permute-start.6 = (f32[40,256]{1,0:T(8,128)}, f32[40,256]{1,0:T(8,128)S(1)}, u32[]{:S(2)}, u32[]{:S(2)}) collective-permute-start(f32[40,256]{1,0:T(8,128)} %get-tuple-element.18), channel_id=1, source_target_pairs={{0,8},{8,16},{16,24},{24,32},{32,40},{40,48},{48,56},{56,64},{64,7... | collective-permute-start | bytes 122888 | tf_op jit(solution)/shard_map/halos/ppermute | solution.py:289
  26.2 10.4 %collective-permute-start.7 = (f32[40,256]{1,0:T(8,128)}, f32[40,256]{1,0:T(8,128)}, u32[]{:S(2)}, u32[]{:S(2)}) collective-permute-start(f32[40,256]{1,0:T(8,128)} %get-tuple-element.19), channel_id=1, source_target_pairs={{0,248},{8,0},{16,8},{24,16},{32,24},{40,32},{48,40},{56,48},{64,5... | collective-permute-start | bytes 122888 | tf_op jit(solution)/shard_map/halos/ppermute | solution.py:290
  36.6 1.3 %copy-start.5 = (f32[4,5,2,32,256]{4,3,2,1,0:T(8,128)S(1)}, f32[4,5,2,32,256]{4,3,2,1,0:T(8,128)}, u32[]{:S(2)}) copy-start(f32[4,5,2,32,256]{4,3,2,1,0:T(8,128)} %copy-done.4) | copy-start | bytes 3932164
  37.9 12.0 %copy-start.10 = (f32[1,16,32]{1,2,0:T(8,128)S(1)}, f32[1,16,32]{1,2,0:T(8,128)}, u32[]{:S(2)}) copy-start(f32[1,16,32]{1,2,0:T(8,128)} %get-tuple-element.26) | copy-start | bytes 6148
  37.9 12.1 %copy-start.11 = (f32[1,16,32]{1,2,0:T(8,128)S(1)}, f32[1,16,32]{1,2,0:T(8,128)}, u32[]{:S(2)}) copy-start(f32[1,16,32]{1,2,0:T(8,128)} %get-tuple-element.27) | copy-start | bytes 6148
  37.9 12.1 %copy-start.12 = (pred[32]{0:T(512)(128)(4,1)S(1)}, pred[32]{0:T(512)(128)(4,1)}, u32[]{:S(2)}) copy-start(pred[32]{0:T(512)(128)(4,1)} %get-tuple-element.28) | copy-start | bytes 100
  37.9 12.1 %copy-start.13 = (pred[32]{0:T(512)(128)(4,1)S(1)}, pred[32]{0:T(512)(128)(4,1)}, u32[]{:S(2)}) copy-start(pred[32]{0:T(512)(128)(4,1)} %get-tuple-element.29) | copy-start | bytes 100
  42.0 19.0 %all-to-all-start = ((f32[64,4,128]{2,1,0:T(4,128)}), f32[64,4,128]{2,1,0:T(4,128)S(1)}, u32[]{:S(2)}, u32[]{:S(2)}) async-start(f32[64,4,128]{2,1,0:T(4,128)} %get-tuple-element.23), calls=%async_computation | async-start | bytes 262144 | tf_op jit(solution)/shard_map/share_sensitivities/all_to_all | solution.py:341

commit v2 on v1

v2 whole, which is shorter than its diff:
```python
import functools
import math

import jax
import jax.numpy as jnp
import numpy as np
from jax import lax
from jax.experimental import pallas as pl
from jax.experimental.pallas import tpu as pltpu
from jax.sharding import PartitionSpec as P

PASSAGES = 16
SWEEPS = 2
NT = 8
F32 = jnp.float32
BF16 = jnp.bfloat16
VMEM = pl.BlockSpec(memory_space=pltpu.VMEM)
SMEM = pl.BlockSpec(memory_space=pltpu.SMEM)


def derivative(offset):
    offset = offset % NT
    if offset in (0, NT // 2):
        return 0.0
    angle = math.pi * offset / NT
    return 0.5 * (-1) ** offset * math.cos(angle) / math.sin(angle)


def call(kernel, outs, args, specs, mib, flops, name):
    nbytes = sum(a.size * a.dtype.itemsize for a in args) + sum(
        math.prod(o.shape) * o.dtype.itemsize for o in outs
    )
    return pl.pallas_call(
        kernel,
        out_shape=outs,
        in_specs=specs,
        out_specs=[VMEM] * len(outs),
        compiler_params=pltpu.CompilerParams(vmem_limit_bytes=mib << 20),
        cost_estimate=pl.CostEstimate(
            flops=flops, bytes_accessed=nbytes, transcendentals=0
        ),
        name=name,
    )(*args)


def by_parity(ids_ref, run):
    @pl.when(ids_ref[0] == 0)
    def _():
        run(1, 0)

    @pl.when(ids_ref[0] != 0)
    def _():
        run(0, 1)


def edge_row(ids_ref, f_ref, t, v, i, outer):
    nj = f_ref.shape[3]
    low, high = f_ref[t, v, i, 0:1, :], f_ref[t, v, i, nj - 1 : nj, :]
    first = ids_ref[1] == (0 if outer else 1)
    return jnp.where(first, low, high)


def pack_layers(f_ref, a_ref, b_ref, layer_a, layer_b):
    nt, nv = f_ref.shape[:2]
    for t in range(nt):
        for v in range(nv):
            a_ref[t, v] = f_ref[t, v, layer_a].astype(BF16)
            b_ref[t, v] = f_ref[t, v, layer_b].astype(BF16)


def pack_rows(ids_ref, f_ref, outer_ref, inner_ref, ra_ref=None, rb_ref=None, layer_a=0):
    nt, nv, ni = f_ref.shape[:3]
    for t in range(nt):
        for v in range(nv):
            at = t * nv + v
            for i in range(ni):
                row = at * ni + i
                outer = edge_row(ids_ref, f_ref, t, v, i, True)
                outer_ref[row : row + 1, :] = outer
                inner_ref[row : row + 1, :] = edge_row(ids_ref, f_ref, t, v, i, False)
                if ra_ref is not None:
                    to = ra_ref if i == layer_a else rb_ref
                    to[at : at + 1, :] = outer


def prepare_kernel(ids_ref, f_ref, a_ref, b_ref, outer_ref, inner_ref):
    pack_rows(ids_ref, f_ref, outer_ref, inner_ref)
    by_parity(ids_ref, functools.partial(pack_layers, f_ref, a_ref, b_ref))


def rhs_kernel(ids_ref, f_ref, src_ref, pa_ref, pb_ref, out_ref):
    nt, nv, ni, nj, nk = f_ref.shape

    def run(layer_a, layer_b):
        for layer, other in ((layer_a, pa_ref), (layer_b, pb_ref)):

            def one(v, carry):
                for j in range(0, nj, 16):
                    rows = slice(j, j + 16)
                    own = [
                        f_ref[t, v, layer, rows, :].astype(BF16).astype(F32)
                        for t in range(nt)
                    ]
                    far = [other[t, v, rows, :].astype(F32) for t in range(nt)]
                    times = own + far
                    for b in range(nt):
                        total = src_ref[b, v, layer, rows, :]
                        for n in range(1, NT // 2):
                            diff = times[(b + n) % NT] - times[(b - n) % NT]
                            total = total - derivative(n) * diff
                        out_ref[b, v, layer, rows, :] = total
                return carry

            lax.fori_loop(0, nv, one, 0)

    by_parity(ids_ref, run)


def shifted(f_ref, t, u, i, j, lanes, edges, rows_id):
    nj = f_ref.shape[3]
    here = f_ref[t, u, i, j : j + 8, lanes]
    if j + 8 < nj:
        after = pltpu.roll(f_ref[t, u, i, j + 8 : j + 16, lanes], 7, 0)
    else:
        after = edges(t, u, i, True)
    if j > 0:
        before = pltpu.roll(f_ref[t, u, i, j - 8 : j, lanes], 1, 0)
    else:
        before = edges(t, u, i, False)
    plus = jnp.where(rows_id == 7, after, pltpu.roll(here, 7, 0))
    minus = jnp.where(rows_id == 0, before, pltpu.roll(here, 1, 0))
    return here, plus, minus


def sweep_tile(refs, halo, edges, i, j, lanes):
    f_ref, rhs_ref, jac_ref, sig_ref, dmp_ref = refs
    nt, nv, ni = f_ref.shape[:3]
    pair = slice(j // 16 * 16, j // 16 * 16 + 16)
    half = slice(j % 16, j % 16 + 8)
    sigma = sig_ref[i, j : j + 8, lanes]
    damping = dmp_ref[i, j : j + 8, lanes]
    scaling = 1.0 / (sigma + 4.0 * damping)
    rows_id = lax.broadcasted_iota(jnp.int32, sigma.shape, 0)
    acc = [[None] * nv for _ in range(nt)]
    for u in range(nv):
        jac = [
            [jac_ref[d, u, v, i, pair, lanes].astype(F32)[half] for v in range(nv)]
            for d in range(2)
        ]
        for t in range(nt):
            here, plus_j, minus_j = shifted(f_ref, t, u, i, j, lanes, edges, rows_id)
            outer = halo(t, u)
            inner = f_ref[t, u, 1 - i, j : j + 8, lanes]
            plus_i, minus_i = (outer, inner) if i else (inner, outer)
            diff_i, diff_j = here - plus_i, here - plus_j
            both = diff_i + diff_j + ((here - minus_i) + (here - minus_j))
            own = sigma * here + damping * both
            for v in range(nv):
                term = jac[0][v] * diff_i + jac[1][v] * diff_j
                if v == u:
                    term = term + own
                acc[t][v] = term if acc[t][v] is None else acc[t][v] + term
    return [
        [
            f_ref[t, v, i, j : j + 8, lanes]
            + (rhs_ref[t, v, i, j : j + 8, lanes] - acc[t][v]) * scaling
            for v in range(nv)
        ]
        for t in range(nt)
    ]


def lanes_at(k):
    return pl.ds(pl.multiple_of(k * 128, 128), 128)


def sweep_all(ids_ref, refs, outer_ref, inner_ref, out_ref, layers):
    nt, nv, ni, nj, nk = out_ref.shape
    upper = ids_ref[1] == 1

    def one(k, carry):
        lanes = lanes_at(k)

        def edges(t, u, i, high):
            row = (t * nv + u) * ni + i
            outer = outer_ref[row : row + 1, lanes]
            inner = inner_ref[row : row + 1, lanes]
            edge = jnp.where(upper, outer, inner) if high else jnp.where(upper, inner, outer)
            return jnp.broadcast_to(edge, (8, 128))

        for i in range(ni):
            for j in range(0, nj, 8):
                pair = slice(j // 16 * 16, j // 16 * 16 + 16)
                half = slice(j % 16, j % 16 + 8)
                new = sweep_tile(
                    refs,
                    lambda t, u: layers[i][t, u, pair, lanes].astype(F32)[half],
                    edges,
                    i,
                    j,
                    lanes,
                )
                for t in range(nt):
                    for v in range(nv):
                        out_ref[t, v, i, j : j + 8, lanes] = new[t][v]
        return carry

    lax.fori_loop(0, nk // 128, one, 0)


def first_kernel(ids_ref, *refs):
    ins, outer_ref, inner_ref, ha_ref, hb_ref = refs[:5], *refs[5:9]
    out_ref, no_ref, ni_ref, ra_ref, rb_ref = refs[9:]

    def run(layer_a, layer_b):
        layers = {layer_a: ha_ref, layer_b: hb_ref}
        sweep_all(ids_ref, ins, outer_ref, inner_ref, out_ref, layers)
        pack_rows(ids_ref, out_ref, no_ref, ni_ref, ra_ref, rb_ref, layer_a)

    by_parity(ids_ref, run)


def surface_kernel(ids_ref, *refs):
    ins, outer_ref, ra_ref, rb_ref, w_ref = refs[:5], *refs[5:9]
    sens_ref, a_ref, b_ref = refs[9:]
    f_ref = ins[0]
    nt, nv, ni, nj, nk = f_ref.shape

    def row_of(side, layers):
        j = side * (nj - 8)
        mask = lax.broadcasted_iota(jnp.int32, (8, 128), 0) == side * 7

        def one(k, carry):
            lanes = lanes_at(k)

            def edges(t, u, i, high):
                row = (t * nv + u) * ni + i
                return jnp.broadcast_to(outer_ref[row : row + 1, lanes], (8, 128))

            def halo(i, t, u):
                at = t * nv + u
                return jnp.broadcast_to(layers[i][at : at + 1, lanes], (8, 128))

            for i in range(ni):
                new = sweep_tile(ins, functools.partial(halo, i), edges, i, j, lanes)
                total = jnp.zeros((8, 128), F32)
                for t in range(nt):
                    for v in range(nv):
                        at = t * nv + v
                        start = pl.multiple_of(i * nk + k * 128, 128)
                        weight = w_ref[at : at + 1, pl.ds(start, 128)]
                        total = total + new[t][v] * weight
                value = jnp.sum(jnp.where(mask, total, 0.0), axis=0, keepdims=True)
                sens_ref[:, pl.ds(i * (nk // 128) + k, 1), :] = jnp.broadcast_to(
                    value[None], (sens_ref.shape[0], 1, 128)
                )
            return carry

        lax.fori_loop(0, nk // 128, one, 0)

    def run(layer_a, layer_b):
        layers = {layer_a: ra_ref, layer_b: rb_ref}
        for side in range(2):
            pl.when(ids_ref[1] == side)(functools.partial(row_of, side, layers))
        pack_layers(f_ref, a_ref, b_ref, layer_a, layer_b)

    by_parity(ids_ref, run)


def second_kernel(ids_ref, *refs):
    ins, outer_ref, inner_ref, ha_ref, hb_ref = refs[:5], *refs[5:9]
    out_ref, done_ref = refs[9:]
    done_ref[...] = jnp.zeros(done_ref.shape, F32)

    def run(layer_a, layer_b):
        layers = {layer_a: ha_ref, layer_b: hb_ref}
        sweep_all(ids_ref, ins, outer_ref, inner_ref, out_ref, layers)

    by_parity(ids_ref, run)


def split3(x):
    one = x.astype(BF16)
    rest = x - one.astype(F32)
    two = rest.astype(BF16)
    three = (rest - two.astype(F32)).astype(BF16)
    return one, two, three


def one_hot(cells_ref, first, rows):
    cells = cells_ref.shape[1]
    index = lax.broadcasted_iota(jnp.int32, (rows, cells), 0) + first
    return jnp.where(cells_ref[0:1, :] == index, 1.0, 0.0).astype(BF16)


def order_kernel(ids_ref, cells_ref, w_ref, out_ref, chosen_ref):
    half = out_ref.shape[1]
    nv, nt, _ = w_ref.shape
    chosen_ref[...] = one_hot(cells_ref, 0, chosen_ref.shape[0])
    own = chosen_ref[pl.ds(pl.multiple_of(ids_ref[1] * half, 512), half), :]
    for v in range(nv):
        parts = [
            lax.dot_general(
                part, own, (((1,), (1,)), ((), ())), preferred_element_type=F32
            )
            for part in split3(w_ref[v])
        ]
        total = parts[0] + (parts[1] + parts[2])
        for t in range(nt):
            out_ref[t * nv + v : t * nv + v + 1, :] = total[t : t + 1]


def modes_kernel(table_ref, chosen_ref, sens_ref, done_ref, out_ref):
    pieces = sens_ref.shape[1]
    half = pieces * 128
    rows = out_ref.shape[0]
    seen = jnp.concatenate([sens_ref[:, c, :] for c in range(pieces)], axis=1)
    both = jnp.dot(
        table_ref[...],
        seen,
        precision=lax.Precision.HIGHEST,
        preferred_element_type=F32,
    )
    total = None
    for side in range(2):
        modes = both[side * rows : (side + 1) * rows]
        parts = jnp.concatenate(split3(modes), axis=0)
        chosen = chosen_ref[side * half : (side + 1) * half, :]
        found = jnp.dot(parts, chosen, preferred_element_type=F32)
        found = found[:rows] + (found[rows : 2 * rows] + found[2 * rows :])
        total = found if total is None else total + found
    out_ref[...] = total


def mode_table(devices):
    per = devices // PASSAGES
    m = np.arange(PASSAGES)[:, None]
    d = np.arange(devices)[None, :]
    angle = 2.0 * np.pi * (m * (d // per) % PASSAGES) / PASSAGES
    base = np.concatenate([np.cos(angle), -np.sin(angle)]) / PASSAGES**0.5
    sides = [np.where(d % per == s, base, 0.0) for s in range(per)]
    return np.repeat(np.concatenate(sides), 2, axis=1).astype(np.float32)


def body(start, source, jac, sigma, damping, cells, weights):
    nt, nv, ni, nj, nk = start.shape
    ring = lax.axis_size("passage")
    n_cell = lax.axis_size("cell")
    ids = jnp.stack([lax.axis_index("cell") & 1, lax.axis_index("passage") & 1])
    even = [(c, c ^ 1) for c in range(n_cell)]
    odd = [(c, c + 1) for c in range(1, n_cell - 1, 2)]
    odd += [(b, a) for a, b in odd]
    within = [(d, d ^ 1) for d in range(ring)]
    across = [(d, (d + 1) % ring) for d in range(1, ring, 2)]
    across += [(b, a) for a, b in across]
    swap = [(0, 1), (1, 0)]

    field_like = jax.ShapeDtypeStruct(start.shape, F32)
    layer_like = jax.ShapeDtypeStruct((nt, nv, nj, nk), BF16)
    rows_like = jax.ShapeDtypeStruct((nt * nv * ni, nk), F32)
    row_like = jax.ShapeDtypeStruct((nt * nv, nk), F32)

    a, b, outer, inner = call(
        prepare_kernel,
        [layer_like, layer_like, rows_like, rows_like],
        (ids, start),
        [SMEM, VMEM],
        4,
        10**6,
        "prepare",
    )
    with jax.named_scope("halos"):
        outer = lax.ppermute(outer, "passage", across)
        inner = lax.ppermute(inner, "passage", within)
        ha = lax.ppermute(a, "cell", even)
        hb = lax.ppermute(b, "cell", odd)
        pa = lax.ppermute(a, "tm", swap)
        pb = lax.ppermute(b, "tm", swap)
    rhs = call(
        rhs_kernel,
        [field_like],
        (ids, start, source, pa, pb),
        [SMEM] + [VMEM] * 4,
        4,
        10**7,
        "rhs",
    )[0]
    ordered, chosen = call(
        order_kernel,
        [
            jax.ShapeDtypeStruct((nt * nv, ni * nk), F32),
            jax.ShapeDtypeStruct((cells.shape[1], cells.shape[1]), BF16),
        ],
        (ids, cells, weights.transpose(1, 0, 2)),
        [SMEM, VMEM, VMEM],
        8,
        10**6,
        "order",
    )
    fixed = (jac, sigma, damping)
    field, outer, inner, ra, rb = call(
        first_kernel,
        [field_like, rows_like, rows_like, row_like, row_like],
        (ids, start, rhs, *fixed, outer, inner, ha, hb),
        [SMEM] + [VMEM] * 9,
        8,
        2 * 10**7,
        "first_sweep",
    )
    with jax.named_scope("surface_halos"):
        outer = lax.ppermute(outer, "passage", across)
        ra = lax.ppermute(ra, "cell", even)
        rb = lax.ppermute(rb, "cell", odd)
        inner = lax.ppermute(inner, "passage", within)
    sens, a, b = call(
        surface_kernel,
        [
            jax.ShapeDtypeStruct((2 * ring, ni * nk // 128, 128), F32),
            layer_like,
            layer_like,
        ],
        (ids, field, rhs, *fixed, outer, ra, rb, ordered),
        [SMEM] + [VMEM] * 9,
        8,
        5 * 10**6,
        "surface",
    )
    with jax.named_scope("halos"):
        ha = lax.ppermute(a, "cell", even)
        hb = lax.ppermute(b, "cell", odd)
    with jax.named_scope("share_sensitivities"):
        gathered = lax.all_to_all(sens, ("passage", "tm"), 0, 0, tiled=True)
    field, done = call(
        second_kernel,
        [field_like, jax.ShapeDtypeStruct((8, 128), F32)],
        (ids, field, rhs, *fixed, outer, inner, ha, hb),
        [SMEM] + [VMEM] * 9,
        8,
        2 * 10**7,
        "second_sweep",
    )
    modes = call(
        modes_kernel,
        [jax.ShapeDtypeStruct((2 * PASSAGES, cells.shape[1]), F32)],
        (mode_table(ring), chosen, gathered, done),
        [VMEM] * 4,
        8,
        10**7,
        "modes",
    )[0]
    return field, modes.reshape(2, PASSAGES, -1)


def solution(mesh):
    in_specs = (
        P("tm", None, "cell", "passage", None),
        P("tm", None, "cell", "passage", None),
        P(None, None, None, "cell", "passage", None),
        P("cell", "passage", None),
        P("cell", "passage", None),
        P("cell", None),
        P("tm", None, "cell"),
    )
    out_specs = (P("tm", None, "cell", "passage", None), P(None, None, "cell"))
    return jax.shard_map(
        body, mesh=mesh, in_specs=in_specs, out_specs=out_specs, check_vma=False
    )
```

time: 64.3 us -> 63.3 us (0.984)
  the two profiles are of different devices: /device:TPU:8 before, /device:TPU:1 now
where the time goes in v2:
time: 63.3 us; the launch traced here: 62.8 us
  starting transfers between devices  32 us (51%)
  Pallas kernels  17.4 us (27%)
  local copies, waits for them, and re-layouts  7.07 us (11%)
  waiting for transfers between devices  5.3 us (8%)
  between operations  0.85 us (1%)
    pallas_call x7, Pallas kernels, call(): pl.pallas_call(kernel, out_shape=outs, in_specs=specs, out_specs=[VMEM] *...  17.4 us
    ppermute x2, starting transfers between devices, body(): outer = lax.ppermute(outer, 'passage', across)  11.3 us
    unnamed x34, local copies, waits for them, and re-layouts  7.07 us
    all_to_all x1, starting transfers between devices, body(): gathered = lax.all_to_all(sens, ('passage', 'tm'), 0, 0, tiled=True)  6.7 us
    ppermute x1, starting transfers between devices, body(): ra = lax.ppermute(ra, 'cell', even)  4.01 us
    ppermute x2, waiting for transfers between devices, body(): inner = lax.ppermute(inner, 'passage', within)  3.64 us
    ppermute x1, starting transfers between devices, body(): pa = lax.ppermute(a, 'tm', swap)  3.33 us
    ppermute x2, starting transfers between devices, body(): ha = lax.ppermute(a, 'cell', even)  2.38 us
  transfers between devices with their start and end apart: 13, of which 4 were waited for; matrix products, arithmetic and copies ran while one was open for 0% of the time, Pallas kernels for 17%

profile of v2, /device:TPU:1, one launch (start us, length us, event | category | flops | bytes accessed | tf_op | source)
XLA Modules:
  0.0 62.8 jit_solution(5847611899695333458)
XLA Ops:
  0.6 0.1 pad_add_fusion.ids_ref
  0.7 0.0 copy-start.1
  0.7 1.3 %copy-done.1 = f32[4,5,2,32,256]{4,3,2,1,0:T(8,128)S(1)} copy-done((f32[4,5,2,32,256]{4,3,2,1,0:T(8,128)S(1)}, f32[4,5,2,32,256]{4,3,2,1,0:T(8,128)}, u32[]{:S(2)}) %copy-start.1) | copy-done | bytes 1310744
  2.0 0.0 copy-start.7
  2.0 0.7 %prepare.1 = (bf16[4,5,32,256]{3,2,1,0:T(8,128)(2,1)S(1)}, bf16[4,5,32,256]{3,2,1,0:T(8,128)(2,1)S(1)}, f32[40,256]{1,0:T(8,128)S(1)}, f32[40,256]{1,0:T(8,128)S(1)}) custom-call(s32[2]{0:T(128)S(1)} %pad_add_fusion.ids_ref, f32[4,5,2,32,256]{4,3,2,1,0:T(8,128)S(1)} %copy-done.1), custom_call_target="tpu_custom_call" | custom-call | flops 1000000 | bytes 2048008 | tf_op jit(solution)/shard_map/prepare/pallas_call | solution.py:33
  2.7 3.3 %collective-permute-start = (bf16[4,5,32,256]{3,2,1,0:T(8,128)(2,1)S(1)}, bf16[4,5,32,256]{3,2,1,0:T(8,128)(2,1)S(1)}, u32[]{:S(2)}, u32[]{:S(2)}) collective-permute-start(bf16[4,5,32,256]{3,2,1,0:T(8,128)(2,1)S(1)} %get-tuple-element.18), channel_id=1, source_target_pairs={{0,1},{1,0},{2,3},{3,2},{4,5},{5,4},{6,7},{7,6},{8,9},{9,8},{10,11... | collective-permute-start | bytes 983048 | tf_op jit(solution)/shard_map/halos/ppermute | solution.py:377
  6.0 0.1 collective-permute-start.1
  6.1 0.0 collective-permute-start.4
  6.1 0.7 %collective-permute-start.5 = (bf16[4,5,32,256]{3,2,1,0:T(8,128)(2,1)S(1)}, bf16[4,5,32,256]{3,2,1,0:T(8,128)(2,1)S(1)}, u32[]{:S(2)}, u32[]{:S(2)}) collective-permute-start(bf16[4,5,32,256]{3,2,1,0:T(8,128)(2,1)S(1)} %get-tuple-element.19), channel_id=1, source_target_pairs={{2,4},{4,2},{3,5},{5,3},{10,12},{12,10},{11,13},{13,11},{18,20},{2... | collective-permute-start | bytes 983048 | tf_op jit(solution)/shard_map/halos/ppermute | solution.py:376
  6.8 7.4 %collective-permute-start.2 = (f32[40,256]{1,0:T(8,128)S(1)}, f32[40,256]{1,0:T(8,128)S(1)}, u32[]{:S(2)}, u32[]{:S(2)}) collective-permute-start(f32[40,256]{1,0:T(8,128)S(1)} %get-tuple-element.20), channel_id=1, source_target_pairs={{8,16},{24,32},{40,48},{56,64},{72,80},{88,96},{104,112},{120,128}... | collective-permute-start | bytes 122888 | tf_op jit(solution)/shard_map/halos/ppermute | solution.py:373
  14.2 0.0 collective-permute-done.pa_ref
  14.2 0.0 copy-start
  14.2 0.0 copy-start.2
  14.2 0.0 copy-start.8
  14.2 0.0 copy-start.9
  14.2 0.1 collective-permute-start.3
  14.3 0.0 collective-permute-done.1.pb_ref
  14.4 0.0 copy-done.7
  14.4 1.1 %rhs.1.refs_1_ = f32[4,5,2,32,256]{4,3,2,1,0:T(8,128)S(1)} custom-call(s32[2]{0:T(128)S(1)} %pad_add_fusion.ids_ref, f32[4,5,2,32,256]{4,3,2,1,0:T(8,128)S(1)} %copy-done.1, f32[4,5,2,32,256]{4,3,2,1,0:T(8,128)S(1)} %copy-done.7, bf16[4,5,32,256]{3,2,1,0:T(8,128)(2,1)S(1)} %collective-permute-done.pa_ref, ...), custom_call_target="tpu_custom_call" | custom-call | flops 10000000 | bytes 4587528 | tf_op jit(solution)/shard_map/rhs/pallas_call | solution.py:33
  15.5 0.0 copy-start.13
  15.5 0.0 copy-start.15
  15.5 0.1 collective-permute-done.2.refs_5_
  15.6 1.6 %collective-permute-done.3.refs_6_ = f32[40,256]{1,0:T(8,128)S(1)} collective-permute-done((f32[40,256]{1,0:T(8,128)S(1)}, f32[40,256]{1,0:T(8,128)S(1)}, u32[]{:S(2)}, u32[]{:S(2)}) %collective-permute-start.3) | collective-permute-done | bytes 40992 | tf_op jit(solution)/shard_map/halos/ppermute | solution.py:374
  17.2 0.0 collective-permute-done.4.refs_7_
  17.2 0.0 collective-permute-done.5.refs_8_
  17.2 0.0 copy-done
  17.2 0.0 copy-done.2
  17.2 0.0 copy-done.8
  17.2 0.0 copy-done.9
  17.2 2.6 %first_sweep.1 = (f32[4,5,2,32,256]{4,3,2,1,0:T(8,128)S(1)}, f32[40,256]{1,0:T(8,128)S(1)}, f32[40,256]{1,0:T(8,128)S(1)}, f32[20,256]{1,0:T(8,128)S(1)}, f32[20,256]{1,0:T(8,128)S(1)}) custom-call(s32[2]{0:T(128)S(1)} %pad_add_fusion.ids_ref, f32[4,5,2,32,256]{4,3,2,1,0:T(8,128)S(1)} %copy-done.2, f32[4,5,2,32,256]{4,3,2,1,0:T(8,128)S(1)} %rhs.1.refs_1_, ...), custom_call_target="tpu_custom_call" | custom-call | flops 20000000 | bytes 6561800 | tf_op jit(solution)/shard_map/first_sweep/pallas_call | solution.py:33
  19.8 0.0 copy-start.16
  19.8 0.6 copy-done.16
  20.4 0.0 copy-start.3
  20.4 3.8 %collective-permute-start.6 = (f32[40,256]{1,0:T(8,128)S(1)}, f32[40,256]{1,0:T(8,128)S(1)}, u32[]{:S(2)}, u32[]{:S(2)}) collective-permute-start(f32[40,256]{1,0:T(8,128)S(1)} %get-tuple-element.23), channel_id=1, source_target_pairs={{8,16},{24,32},{40,48},{56,64},{72,80},{88,96},{104,112},{120,128}... | collective-permute-start | bytes 122888 | tf_op jit(solution)/shard_map/surface_halos/ppermute | solution.py:411
  24.3 4.0 %collective-permute-start.8 = (f32[20,256]{1,0:T(8,128)S(1)}, f32[20,256]{1,0:T(8,128)S(1)}, u32[]{:S(2)}, u32[]{:S(2)}) collective-permute-start(f32[20,256]{1,0:T(8,128)S(1)} %get-tuple-element.25), channel_id=1, source_target_pairs={{0,2},{2,0},{4,6},{6,4},{1,3},{3,1},{5,7},{7,5},{8,10},{10,8},{12,... | collective-permute-start | bytes 61448 | tf_op jit(solution)/shard_map/surface_halos/ppermute | solution.py:412
  28.3 0.7 %collective-permute-start.9 = (f32[20,256]{1,0:T(8,128)S(1)}, f32[20,256]{1,0:T(8,128)S(1)}, u32[]{:S(2)}, u32[]{:S(2)}) collective-permute-start(f32[20,256]{1,0:T(8,128)S(1)} %get-tuple-element.26), channel_id=1, source_target_pairs={{2,4},{4,2},{3,5},{5,3},{10,12},{12,10},{11,13},{13,11},{18,20},{2... | collective-permute-start | bytes 61448 | tf_op jit(solution)/shard_map/surface_halos/ppermute | solution.py:413
  28.9 0.0 copy-done.13
  28.9 0.0 copy-done.15
  29.0 5.6 %order.1 = (f32[20,512]{1,0:T(8,128)S(1)}, bf16[1024,1024]{1,0:T(8,128)(2,1)S(1)}) custom-call(s32[2]{0:T(128)S(1)} %pad_add_fusion.ids_ref, s32[1,1024]{1,0:T(1,128)S(1)} %copy-done.15, f32[5,4,1024]{2,1,0:T(4,128)S(1)} %bitcast.4), custom_call_target="tpu_custom_call" | custom-call | flops 1000000 | bytes 2224136 | tf_op jit(solution)/shard_map/order/pallas_call | solution.py:33
  34.5 0.0 copy-start.5
  34.5 0.0 collective-permute-done.8.refs_6_
  34.6 0.0 collective-permute-done.9.refs_7_
  34.6 0.0 collective-permute-done.6.refs_5_
  34.6 0.0 copy-start.10
  34.6 2.1 %surface.1 = (f32[64,4,128]{2,1,0:T(4,128)S(1)}, bf16[4,5,32,256]{3,2,1,0:T(8,128)(2,1)}, bf16[4,5,32,256]{3,2,1,0:T(8,128)(2,1)}) custom-call(s32[2]{0:T(128)S(1)} %pad_add_fusion.ids_ref, f32[4,5,2,32,256]{4,3,2,1,0:T(8,128)S(1)} %get-tuple-element.22.refs_0_, f32[4,5,2,32,256]{4,3,2,1,0:T(8,128)S(1)} %rhs.1.refs_1_, ...), custom_call_target="tpu_custom_call" | custom-call | flops 5000000 | bytes 5300232 | tf_op jit(solution)/shard_map/surface/pallas_call | solution.py:33
  36.7 0.0 copy-done.3
  36.7 0.0 copy-done.5
  36.7 0.0 copy-done.10
  36.7 0.0 copy-start.12
  36.7 0.6 %copy-done.12 = f32[64,4,128]{2,1,0:T(4,128)} copy-done((f32[64,4,128]{2,1,0:T(4,128)}, f32[64,4,128]{2,1,0:T(4,128)S(1)}, u32[]{:S(2)}) %copy-start.12) | copy-done | bytes 131096
  37.3 2.4 %collective-permute-start.10 = (bf16[4,5,32,256]{3,2,1,0:T(8,128)(2,1)}, bf16[4,5,32,256]{3,2,1,0:T(8,128)(2,1)S(1)}, u32[]{:S(2)}, u32[]{:S(2)}) collective-permute-start(bf16[4,5,32,256]{3,2,1,0:T(8,128)(2,1)} %get-tuple-element.28), channel_id=1, source_target_pairs={{0,2},{2,0},{4,6},{6,4},{1,3},{3,1},{5,7},{7,5},{8,10},{10,8},{12,... | collective-permute-start | bytes 983048 | tf_op jit(solution)/shard_map/halos/ppermute | solution.py:429
  39.7 1.4 %collective-permute-start.11 = (bf16[4,5,32,256]{3,2,1,0:T(8,128)(2,1)}, bf16[4,5,32,256]{3,2,1,0:T(8,128)(2,1)}, u32[]{:S(2)}, u32[]{:S(2)}) collective-permute-start(bf16[4,5,32,256]{3,2,1,0:T(8,128)(2,1)} %get-tuple-element.29), channel_id=1, source_target_pairs={{2,4},{4,2},{3,5},{5,3},{10,12},{12,10},{11,13},{13,11},{18,20},{2... | collective-permute-start | bytes 983048 | tf_op jit(solution)/shard_map/halos/ppermute | solution.py:430
  41.1 6.7 %all-to-all-start = ((f32[64,4,128]{2,1,0:T(4,128)}), f32[64,4,128]{2,1,0:T(4,128)S(1)}, u32[]{:S(2)}, u32[]{:S(2)}) async-start(f32[64,4,128]{2,1,0:T(4,128)} %copy-done.12), calls=%async_computation | async-start | bytes 262144 | tf_op jit(solution)/shard_map/share_sensitivities/all_to_all | solution.py:432
  47.8 1.5 %collective-permute-start.7 = (f32[40,256]{1,0:T(8,128)}, f32[40,256]{1,0:T(8,128)S(1)}, u32[]{:S(2)}, u32[]{:S(2)}) collective-permute-start(f32[40,256]{1,0:T(8,128)} %copy-done.16), channel_id=1, source_target_pairs={{0,8},{8,0},{16,24},{24,16},{32,40},{40,32},{48,56},{56,48},{64,72... | collective-permute-start | bytes 122888 | tf_op jit(solution)/shard_map/surface_halos/ppermute | solution.py:414
  49.3 2.1 %collective-permute-done.7.refs_6_ = f32[40,256]{1,0:T(8,128)S(1)} collective-permute-done((f32[40,256]{1,0:T(8,128)}, f32[40,256]{1,0:T(8,128)S(1)}, u32[]{:S(2)}, u32[]{:S(2)}) %collective-permute-start.7) | collective-permute-done | bytes 40992 | tf_op jit(solution)/shard_map/surface_halos/ppermute | solution.py:414
  51.3 0.0 collective-permute-done.10.refs_7_
  51.3 0.0 collective-permute-done.11.refs_8_
  51.4 1.3 %copy-done.4 = f32[4,5,2,32,256]{4,3,2,1,0:T(8,128)S(1)} copy-done((f32[4,5,2,32,256]{4,3,2,1,0:T(8,128)S(1)}, f32[4,5,2,32,256]{4,3,2,1,0:T(8,128)}, u32[]{:S(2)}) %copy-start.4) | copy-done | bytes 1310744
  52.7 0.8 %copy-done.11 = f32[40,256]{1,0:T(8,128)S(1)} copy-done((f32[40,256]{1,0:T(8,128)S(1)}, f32[40,256]{1,0:T(8,128)}, u32[]{:S(2)}) %copy-start.11) | copy-done | bytes 40984
  53.4 4.1 %second_sweep.1 = (f32[4,5,2,32,256]{4,3,2,1,0:T(8,128)}, f32[8,128]{1,0:T(8,128)S(1)}) custom-call(s32[2]{0:T(128)S(1)} %pad_add_fusion.ids_ref, f32[4,5,2,32,256]{4,3,2,1,0:T(8,128)S(1)} %copy-done.4, f32[4,5,2,32,256]{4,3,2,1,0:T(8,128)S(1)} %rhs.1.refs_1_, bf16[2,5,5,2,32,256]{5,4,3,2,1,0:T(8,128)(2,1)S(1)} %copy-done, f32[2,32,256]{2,1,0:T(8,128)S(1)} %copy-done.8, ...), custom_call_target="tpu_custom_call" | custom-call | flops 20000000 | bytes 6443016 | tf_op jit(solution)/shard_map/second_sweep/pallas_call | solution.py:33
  57.5 1.5 %all-to-all-done.sens_ref = f32[64,4,128]{2,1,0:T(4,128)S(1)} async-done(((f32[64,4,128]{2,1,0:T(4,128)}), f32[64,4,128]{2,1,0:T(4,128)S(1)}, u32[]{:S(2)}, u32[]{:S(2)}) %all-to-all-start) | async-done | bytes 131104 | tf_op jit(solution)/shard_map/share_sensitivities/all_to_all | solution.py:432
  59.0 1.6 %copy-done.6 = bf16[1024,1024]{1,0:T(8,128)(2,1)S(1)} copy-done((bf16[1024,1024]{1,0:T(8,128)(2,1)S(1)}, bf16[1024,1024]{1,0:T(8,128)(2,1)}, u32[]{:S(2)}) %copy-start.6) | copy-done | bytes 2097176
  60.6 0.8 %copy-done.14 = f32[64,64]{1,0:T(8,128)S(1)} copy-done((f32[64,64]{1,0:T(8,128)S(1)}, f32[64,64]{1,0:T(8,128)}, u32[]{:S(2)}) %copy-start.14) | copy-done | bytes 16408
  61.4 1.4 %modes.1 = f32[32,1024]{1,0:T(8,128)} custom-call(f32[64,64]{1,0:T(8,128)S(1)} %copy-done.14, bf16[1024,1024]{1,0:T(8,128)(2,1)S(1)} %copy-done.6, f32[64,4,128]{2,1,0:T(4,128)S(1)} %all-to-all-done.sens_ref, f32[8,128]{1,0:T(8,128)S(1)} %get-tuple-element.33.done_ref), custom_call_target="tpu_custom_call" | custom-call | flops 10000000 | bytes 2379776 | tf_op jit(solution)/shard_map/modes/pallas_call | solution.py:33
  (4 shorter events, 0.0 us)
Async XLA Ops:
  0.7 1.3 %copy-start.1 = (f32[4,5,2,32,256]{4,3,2,1,0:T(8,128)S(1)}, f32[4,5,2,32,256]{4,3,2,1,0:T(8,128)}, u32[]{:S(2)}) copy-start(f32[4,5,2,32,256]{4,3,2,1,0:T(8,128)} %refs_0_.1) | copy-start | bytes 3932164
  2.0 12.3 %copy-start.7 = (f32[4,5,2,32,256]{4,3,2,1,0:T(8,128)S(1)}, f32[4,5,2,32,256]{4,3,2,1,0:T(8,128)}, u32[]{:S(2)}) copy-start(f32[4,5,2,32,256]{4,3,2,1,0:T(8,128)} %src_ref.1) | copy-start | bytes 3932164
  2.7 11.5 %collective-permute-start = (bf16[4,5,32,256]{3,2,1,0:T(8,128)(2,1)S(1)}, bf16[4,5,32,256]{3,2,1,0:T(8,128)(2,1)S(1)}, u32[]{:S(2)}, u32[]{:S(2)}) collective-permute-start(bf16[4,5,32,256]{3,2,1,0:T(8,128)(2,1)S(1)} %get-tuple-element.18), channel_id=1, source_target_pairs={{0,1},{1,0},{2,3},{3,2},{4,5},{5,4},{6,7},{7,6},{8,9},{9,8},{10,11... | collective-permute-start | bytes 983048 | tf_op jit(solution)/shard_map/halos/ppermute | solution.py:377
  6.0 8.3 %collective-permute-start.1 = (bf16[4,5,32,256]{3,2,1,0:T(8,128)(2,1)S(1)}, bf16[4,5,32,256]{3,2,1,0:T(8,128)(2,1)S(1)}, u32[]{:S(2)}, u32[]{:S(2)}) collective-permute-start(bf16[4,5,32,256]{3,2,1,0:T(8,128)(2,1)S(1)} %get-tuple-element.19), channel_id=1, source_target_pairs={{0,1},{1,0},{2,3},{3,2},{4,5},{5,4},{6,7},{7,6},{8,9},{9,8},{10,11... | collective-permute-start | bytes 983048 | tf_op jit(solution)/shard_map/halos/ppermute | solution.py:378
  6.1 11.1 %collective-permute-start.4 = (bf16[4,5,32,256]{3,2,1,0:T(8,128)(2,1)S(1)}, bf16[4,5,32,256]{3,2,1,0:T(8,128)(2,1)S(1)}, u32[]{:S(2)}, u32[]{:S(2)}) collective-permute-start(bf16[4,5,32,256]{3,2,1,0:T(8,128)(2,1)S(1)} %get-tuple-element.18), channel_id=1, source_target_pairs={{0,2},{2,0},{4,6},{6,4},{1,3},{3,1},{5,7},{7,5},{8,10},{10,8},{12,... | collective-permute-start | bytes 983048 | tf_op jit(solution)/shard_map/halos/ppermute | solution.py:375
  6.1 11.1 %collective-permute-start.5 = (bf16[4,5,32,256]{3,2,1,0:T(8,128)(2,1)S(1)}, bf16[4,5,32,256]{3,2,1,0:T(8,128)(2,1)S(1)}, u32[]{:S(2)}, u32[]{:S(2)}) collective-permute-start(bf16[4,5,32,256]{3,2,1,0:T(8,128)(2,1)S(1)} %get-tuple-element.19), channel_id=1, source_target_pairs={{2,4},{4,2},{3,5},{5,3},{10,12},{12,10},{11,13},{13,11},{18,20},{2... | collective-permute-start | bytes 983048 | tf_op jit(solution)/shard_map/halos/ppermute | solution.py:376
  6.8 8.8 %collective-permute-start.2 = (f32[40,256]{1,0:T(8,128)S(1)}, f32[40,256]{1,0:T(8,128)S(1)}, u32[]{:S(2)}, u32[]{:S(2)}) collective-permute-start(f32[40,256]{1,0:T(8,128)S(1)} %get-tuple-element.20), channel_id=1, source_target_pairs={{8,16},{24,32},{40,48},{56,64},{72,80},{88,96},{104,112},{120,128}... | collective-permute-start | bytes 122888 | tf_op jit(solution)/shard_map/halos/ppermute | solution.py:373
  14.2 3.0 %copy-start = (bf16[2,5,5,2,32,256]{5,4,3,2,1,0:T(8,128)(2,1)S(1)}, bf16[2,5,5,2,32,256]{5,4,3,2,1,0:T(8,128)(2,1)}, u32[]{:S(2)}) copy-start(bf16[2,5,5,2,32,256]{5,4,3,2,1,0:T(8,128)(2,1)} %refs_2_.5) | copy-start | bytes 4915204
  14.2 3.0 %copy-start.2 = (f32[4,5,2,32,256]{4,3,2,1,0:T(8,128)S(1)}, f32[4,5,2,32,256]{4,3,2,1,0:T(8,128)}, u32[]{:S(2)}) copy-start(f32[4,5,2,32,256]{4,3,2,1,0:T(8,128)} %refs_0_.1) | copy-start | bytes 3932164
  14.2 3.0 %copy-start.8 = (f32[2,32,256]{2,1,0:T(8,128)S(1)}, f32[2,32,256]{2,1,0:T(8,128)}, u32[]{:S(2)}) copy-start(f32[2,32,256]{2,1,0:T(8,128)} %refs_3_.5) | copy-start | bytes 196612
  14.2 3.0 %copy-start.9 = (f32[2,32,256]{2,1,0:T(8,128)S(1)}, f32[2,32,256]{2,1,0:T(8,128)}, u32[]{:S(2)}) copy-start(f32[2,32,256]{2,1,0:T(8,128)} %refs_4_.5) | copy-start | bytes 196612
  14.2 2.9 %collective-permute-start.3 = (f32[40,256]{1,0:T(8,128)S(1)}, f32[40,256]{1,0:T(8,128)S(1)}, u32[]{:S(2)}, u32[]{:S(2)}) collective-permute-start(f32[40,256]{1,0:T(8,128)S(1)} %get-tuple-element.21), channel_id=1, source_target_pairs={{0,8},{8,0},{16,24},{24,16},{32,40},{40,32},{48,56},{56,48},{64,72... | collective-permute-start | bytes 122888 | tf_op jit(solution)/shard_map/halos/ppermute | solution.py:374
  15.5 13.5 %copy-start.13 = (f32[4,5,1024]{2,0,1:T(4,128)S(1)}, f32[4,5,1024]{2,0,1:T(4,128)}, u32[]{:S(2)}) copy-start(f32[4,5,1024]{2,0,1:T(4,128)} %param.14) | copy-start | bytes 245764
  15.5 13.5 %copy-start.15 = (s32[1,1024]{1,0:T(1,128)S(1)}, s32[1,1024]{1,0:T(1,128)}, u32[]{:S(2)}) copy-start(s32[1,1024]{1,0:T(1,128)} %cells_ref.1) | copy-start | bytes 12292
  19.8 0.6 copy-start.16
  20.4 16.2 %copy-start.3 = (f32[4,5,2,32,256]{4,3,2,1,0:T(8,128)}, f32[4,5,2,32,256]{4,3,2,1,0:T(8,128)S(1)}, u32[]{:S(2)}) copy-start(f32[4,5,2,32,256]{4,3,2,1,0:T(8,128)S(1)} %get-tuple-element.22.refs_0_) | copy-start | bytes 3932164
  20.4 14.2 %collective-permute-start.6 = (f32[40,256]{1,0:T(8,128)S(1)}, f32[40,256]{1,0:T(8,128)S(1)}, u32[]{:S(2)}, u32[]{:S(2)}) collective-permute-start(f32[40,256]{1,0:T(8,128)S(1)} %get-tuple-element.23), channel_id=1, source_target_pairs={{8,16},{24,32},{40,48},{56,64},{72,80},{88,96},{104,112},{120,128}... | collective-permute-start | bytes 122888 | tf_op jit(solution)/shard_map/surface_halos/ppermute | solution.py:411
  24.3 10.3 %collective-permute-start.8 = (f32[20,256]{1,0:T(8,128)S(1)}, f32[20,256]{1,0:T(8,128)S(1)}, u32[]{:S(2)}, u32[]{:S(2)}) collective-permute-start(f32[20,256]{1,0:T(8,128)S(1)} %get-tuple-element.25), channel_id=1, source_target_pairs={{0,2},{2,0},{4,6},{6,4},{1,3},{3,1},{5,7},{7,5},{8,10},{10,8},{12,... | collective-permute-start | bytes 61448 | tf_op jit(solution)/shard_map/surface_halos/ppermute | solution.py:412
  28.3 6.3 %collective-permute-start.9 = (f32[20,256]{1,0:T(8,128)S(1)}, f32[20,256]{1,0:T(8,128)S(1)}, u32[]{:S(2)}, u32[]{:S(2)}) collective-permute-start(f32[20,256]{1,0:T(8,128)S(1)} %get-tuple-element.26), channel_id=1, source_target_pairs={{2,4},{4,2},{3,5},{5,3},{10,12},{12,10},{11,13},{13,11},{18,20},{2... | collective-permute-start | bytes 61448 | tf_op jit(solution)/shard_map/surface_halos/ppermute | solution.py:413
  34.5 2.1 %copy-start.5 = (bf16[1024,1024]{1,0:T(8,128)(2,1)}, bf16[1024,1024]{1,0:T(8,128)(2,1)S(1)}, u32[]{:S(2)}) copy-start(bf16[1024,1024]{1,0:T(8,128)(2,1)S(1)} %get-tuple-element.31.chosen_ref) | copy-start | bytes 6291460
  34.6 2.1 %copy-start.10 = (f32[40,256]{1,0:T(8,128)}, f32[40,256]{1,0:T(8,128)S(1)}, u32[]{:S(2)}) copy-start(f32[40,256]{1,0:T(8,128)S(1)} %collective-permute-done.6.refs_5_) | copy-start | bytes 122884
  36.7 0.7 %copy-start.12 = (f32[64,4,128]{2,1,0:T(4,128)}, f32[64,4,128]{2,1,0:T(4,128)S(1)}, u32[]{:S(2)}) copy-start(f32[64,4,128]{2,1,0:T(4,128)S(1)} %get-tuple-element.32) | copy-start | bytes 393220
  37.3 14.0 %collective-permute-start.10 = (bf16[4,5,32,256]{3,2,1,0:T(8,128)(2,1)}, bf16[4,5,32,256]{3,2,1,0:T(8,128)(2,1)S(1)}, u32[]{:S(2)}, u32[]{:S(2)}) collective-permute-start(bf16[4,5,32,256]{3,2,1,0:T(8,128)(2,1)} %get-tuple-element.28), channel_id=1, source_target_pairs={{0,2},{2,0},{4,6},{6,4},{1,3},{3,1},{5,7},{7,5},{8,10},{10,8},{12,... | collective-permute-start | bytes 983048 | tf_op jit(solution)/shard_map/halos/ppermute | solution.py:429
  39.7 11.6 %collective-permute-start.11 = (bf16[4,5,32,256]{3,2,1,0:T(8,128)(2,1)}, bf16[4,5,32,256]{3,2,1,0:T(8,128)(2,1)}, u32[]{:S(2)}, u32[]{:S(2)}) collective-permute-start(bf16[4,5,32,256]{3,2,1,0:T(8,128)(2,1)} %get-tuple-element.29), channel_id=1, source_target_pairs={{2,4},{4,2},{3,5},{5,3},{10,12},{12,10},{11,13},{13,11},{18,20},{2... | collective-permute-start | bytes 983048 | tf_op jit(solution)/shard_map/halos/ppermute | solution.py:430
  41.1 17.9 %all-to-all-start = ((f32[64,4,128]{2,1,0:T(4,128)}), f32[64,4,128]{2,1,0:T(4,128)S(1)}, u32[]{:S(2)}, u32[]{:S(2)}) async-start(f32[64,4,128]{2,1,0:T(4,128)} %copy-done.12), calls=%async_computation | async-start | bytes 262144 | tf_op jit(solution)/shard_map/share_sensitivities/all_to_all | solution.py:432
  47.8 3.5 %collective-permute-start.7 = (f32[40,256]{1,0:T(8,128)}, f32[40,256]{1,0:T(8,128)S(1)}, u32[]{:S(2)}, u32[]{:S(2)}) collective-permute-start(f32[40,256]{1,0:T(8,128)} %copy-done.16), channel_id=1, source_target_pairs={{0,8},{8,0},{16,24},{24,16},{32,40},{40,32},{48,56},{56,48},{64,72... | collective-permute-start | bytes 122888 | tf_op jit(solution)/shard_map/surface_halos/ppermute | solution.py:414
  51.3 1.3 %copy-start.4 = (f32[4,5,2,32,256]{4,3,2,1,0:T(8,128)S(1)}, f32[4,5,2,32,256]{4,3,2,1,0:T(8,128)}, u32[]{:S(2)}) copy-start(f32[4,5,2,32,256]{4,3,2,1,0:T(8,128)} %copy-done.3) | copy-start | bytes 3932164
  52.7 0.8 %copy-start.11 = (f32[40,256]{1,0:T(8,128)S(1)}, f32[40,256]{1,0:T(8,128)}, u32[]{:S(2)}) copy-start(f32[40,256]{1,0:T(8,128)} %copy-done.10) | copy-start | bytes 122884
  59.0 1.6 %copy-start.6 = (bf16[1024,1024]{1,0:T(8,128)(2,1)S(1)}, bf16[1024,1024]{1,0:T(8,128)(2,1)}, u32[]{:S(2)}) copy-start(bf16[1024,1024]{1,0:T(8,128)(2,1)} %copy-done.5) | copy-start | bytes 6291460
  60.6 0.8 %copy-start.14 = (f32[64,64]{1,0:T(8,128)S(1)}, f32[64,64]{1,0:T(8,128)}, u32[]{:S(2)}) copy-start(f32[64,64]{1,0:T(8,128)} %constant.15.clone.table_ref) | copy-start | bytes 49156

commit v3 on v2

--- a/solution.py
+++ b/solution.py
@@ -3,7 +3,6 @@
 
 import jax
 import jax.numpy as jnp
-import numpy as np
 from jax import lax
 from jax.experimental import pallas as pl
 from jax.experimental.pallas import tpu as pltpu
@@ -210,7 +209,7 @@
 
 def first_kernel(ids_ref, *refs):
     ins, outer_ref, inner_ref, ha_ref, hb_ref = refs[:5], *refs[5:9]
-    out_ref, no_ref, ni_ref, ra_ref, rb_ref = refs[9:]
+    out_ref, no_ref, ni_ref, ra_ref, rb_ref = refs[10:]
 
     def run(layer_a, layer_b):
         layers = {layer_a: ha_ref, layer_b: hb_ref}
@@ -222,7 +221,8 @@
 
 def surface_kernel(ids_ref, *refs):
     ins, outer_ref, ra_ref, rb_ref, w_ref = refs[:5], *refs[5:9]
-    sens_ref, a_ref, b_ref = refs[9:]
+    sens_ref, done_ref = refs[10:]
+    done_ref[...] = jnp.zeros(done_ref.shape, F32)
     f_ref = ins[0]
     nt, nv, ni, nj, nk = f_ref.shape
 
@@ -262,9 +262,12 @@
         layers = {layer_a: ra_ref, layer_b: rb_ref}
         for side in range(2):
             pl.when(ids_ref[1] == side)(functools.partial(row_of, side, layers))
-        pack_layers(f_ref, a_ref, b_ref, layer_a, layer_b)
 
     by_parity(ids_ref, run)
+
+
+def pack_kernel(ids_ref, f_ref, done_ref, a_ref, b_ref):
+    by_parity(ids_ref, functools.partial(pack_layers, f_ref, a_ref, b_ref))
 
 
 def second_kernel(ids_ref, *refs):
@@ -293,30 +296,42 @@
     return jnp.where(cells_ref[0:1, :] == index, 1.0, 0.0).astype(BF16)
 
 
-def order_kernel(ids_ref, cells_ref, w_ref, out_ref, chosen_ref):
-    half = out_ref.shape[1]
+def order_kernel(ids_ref, cells_ref, w_ref, out_ref):
+    rows, half = out_ref.shape
     nv, nt, _ = w_ref.shape
-    chosen_ref[...] = one_hot(cells_ref, 0, chosen_ref.shape[0])
-    own = chosen_ref[pl.ds(pl.multiple_of(ids_ref[1] * half, 512), half), :]
-    for v in range(nv):
-        parts = [
-            lax.dot_general(
-                part, own, (((1,), (1,)), ((), ())), preferred_element_type=F32
-            )
-            for part in split3(w_ref[v])
-        ]
-        total = parts[0] + (parts[1] + parts[2])
-        for t in range(nt):
-            out_ref[t * nv + v : t * nv + v + 1, :] = total[t : t + 1]
-
-
-def modes_kernel(table_ref, chosen_ref, sens_ref, done_ref, out_ref):
-    pieces = sens_ref.shape[1]
+    own = one_hot(cells_ref, ids_ref[1] * half, half)
+    parts = [part for v in range(nv) for part in split3(w_ref[v])]
+    found = lax.dot_general(
+        jnp.concatenate(parts, axis=0),
+        own,
+        (((1,), (1,)), ((), ())),
+        preferred_element_type=F32,
+    )
+    for t in range(nt):
+        for v in range(nv):
+            one, two, three = (found[(v * 3 + p) * nt + t][None] for p in range(3))
+            out_ref[t * nv + v : t * nv + v + 1, :] = one + (two + three)
+
+
+def mode_table(side, modes, senders):
+    row = lax.broadcasted_iota(jnp.int32, (2 * modes, senders), 0)
+    sender = lax.broadcasted_iota(jnp.int32, (2 * modes, senders), 1)
+    turns = ((row % modes) * (sender // 4)) % PASSAGES
+    angle = turns.astype(F32) * (2.0 * math.pi / PASSAGES)
+    value = jnp.where(row < modes, jnp.cos(angle), -jnp.sin(angle)) / PASSAGES**0.5
+    return jnp.where((sender // 2) % 2 == side, value, 0.0)
+
+
+def modes_kernel(cells_ref, sens_ref, done_ref, out_ref):
+    senders, pieces = sens_ref.shape[:2]
     half = pieces * 128
     rows = out_ref.shape[0]
+    table = jnp.concatenate(
+        [mode_table(side, rows // 2, senders) for side in range(2)], axis=0
+    )
     seen = jnp.concatenate([sens_ref[:, c, :] for c in range(pieces)], axis=1)
     both = jnp.dot(
-        table_ref[...],
+        table,
         seen,
         precision=lax.Precision.HIGHEST,
         preferred_element_type=F32,
@@ -325,21 +340,11 @@
     for side in range(2):
         modes = both[side * rows : (side + 1) * rows]
         parts = jnp.concatenate(split3(modes), axis=0)
-        chosen = chosen_ref[side * half : (side + 1) * half, :]
+        chosen = one_hot(cells_ref, side * half, half)
         found = jnp.dot(parts, chosen, preferred_element_type=F32)
         found = found[:rows] + (found[rows : 2 * rows] + found[2 * rows :])
         total = found if total is None else total + found
     out_ref[...] = total
-
-
-def mode_table(devices):
-    per = devices // PASSAGES
-    m = np.arange(PASSAGES)[:, None]
-    d = np.arange(devices)[None, :]
-    angle = 2.0 * np.pi * (m * (d // per) % PASSAGES) / PASSAGES
-    base = np.concatenate([np.cos(angle), -np.sin(angle)]) / PASSAGES**0.5
-    sides = [np.where(d % per == s, base, 0.0) for s in range(per)]
-    return np.repeat(np.concatenate(sides), 2, axis=1).astype(np.float32)
 
 
 def body(start, source, jac, sigma, damping, cells, weights):
@@ -385,24 +390,21 @@
         10**7,
         "rhs",
     )[0]
-    ordered, chosen = call(
+    ordered = call(
         order_kernel,
-        [
-            jax.ShapeDtypeStruct((nt * nv, ni * nk), F32),
-            jax.ShapeDtypeStruct((cells.shape[1], cells.shape[1]), BF16),
-        ],
+        [jax.ShapeDtypeStruct((nt * nv, ni * nk), F32)],
         (ids, cells, weights.transpose(1, 0, 2)),
         [SMEM, VMEM, VMEM],
         8,
         10**6,
         "order",
-    )
+    )[0]
     fixed = (jac, sigma, damping)
     field, outer, inner, ra, rb = call(
         first_kernel,
         [field_like, rows_like, rows_like, row_like, row_like],
-        (ids, start, rhs, *fixed, outer, inner, ha, hb),
-        [SMEM] + [VMEM] * 9,
+        (ids, start, rhs, *fixed, outer, inner, ha, hb, ordered),
+        [SMEM] + [VMEM] * 10,
         8,
         2 * 10**7,
         "first_sweep",
@@ -412,18 +414,24 @@
         ra = lax.ppermute(ra, "cell", even)
         rb = lax.ppermute(rb, "cell", odd)
         inner = lax.ppermute(inner, "passage", within)
-    sens, a, b = call(
+    token_like = jax.ShapeDtypeStruct((8, 128), F32)
+    sens, done = call(
         surface_kernel,
-        [
-            jax.ShapeDtypeStruct((2 * ring, ni * nk // 128, 128), F32),
-            layer_like,
-            layer_like,
-        ],
-        (ids, field, rhs, *fixed, outer, ra, rb, ordered),
-        [SMEM] + [VMEM] * 9,
+        [jax.ShapeDtypeStruct((2 * ring, ni * nk // 128, 128), F32), token_like],
+        (ids, field, rhs, *fixed, outer, ra, rb, ordered, inner),
+        [SMEM] + [VMEM] * 10,
         8,
         5 * 10**6,
         "surface",
+    )
+    a, b = call(
+        pack_kernel,
+        [layer_like, layer_like],
+        (ids, field, done),
+        [SMEM, VMEM, VMEM],
+        4,
+        10**6,
+        "pack",
     )
     with jax.named_scope("halos"):
         ha = lax.ppermute(a, "cell", even)
@@ -432,7 +440,7 @@
         gathered = lax.all_to_all(sens, ("passage", "tm"), 0, 0, tiled=True)
     field, done = call(
         second_kernel,
-        [field_like, jax.ShapeDtypeStruct((8, 128), F32)],
+        [field_like, token_like],
         (ids, field, rhs, *fixed, outer, inner, ha, hb),
         [SMEM] + [VMEM] * 9,
         8,
@@ -442,8 +450,8 @@
     modes = call(
         modes_kernel,
         [jax.ShapeDtypeStruct((2 * PASSAGES, cells.shape[1]), F32)],
-        (mode_table(ring), chosen, gathered, done),
-        [VMEM] * 4,
+        (cells, gathered, done),
+        [VMEM] * 3,
         8,
         10**7,
         "modes",

time: 63.3 us -> 58.2 us (0.919)
  the two profiles are of different devices: /device:TPU:1 before, /device:TPU:8 now
where the time goes in v3:
time: 58.2 us; the launch traced here: 57.1 us
  starting transfers between devices  29.9 us (51%)
  Pallas kernels  13.4 us (23%)
  local copies, waits for them, and re-layouts  6.54 us (11%)
  waiting for transfers between devices  6.27 us (11%)
  between operations  0.9 us (2%)
    pallas_call x8, Pallas kernels, call(): pl.pallas_call(kernel, out_shape=outs, in_specs=specs, out_specs=[VMEM] *...  13.4 us
    ppermute x2, starting transfers between devices, body(): outer = lax.ppermute(outer, 'passage', across)  11.3 us
    unnamed x30, local copies, waits for them, and re-layouts  6.54 us
    ppermute x2, starting transfers between devices, body(): hb = lax.ppermute(b, 'cell', odd)  6.2 us
    all_to_all x1, starting transfers between devices, body(): gathered = lax.all_to_all(sens, ('passage', 'tm'), 0, 0, tiled=True)  6.03 us
    all_to_all x1, waiting for transfers between devices, body(): gathered = lax.all_to_all(sens, ('passage', 'tm'), 0, 0, tiled=True)  3.93 us
    ppermute x1, starting transfers between devices, body(): rb = lax.ppermute(rb, 'cell', odd)  3.63 us
    ppermute x2, starting transfers between devices, body(): ha = lax.ppermute(a, 'cell', even)  2.19 us
  transfers between devices with their start and end apart: 13, of which 4 were waited for; matrix products, arithmetic and copies ran while one was open for 0% of the time, Pallas kernels for 11%

profile of v3, /device:TPU:8, one launch (start us, length us, event | category | flops | bytes accessed | tf_op | source)
XLA Modules:
  0.0 57.1 jit_solution(2566171966846219550)
XLA Ops:
  0.6 0.0 copy-start.14
  0.6 0.1 pad_add_fusion.ids_ref
  0.7 0.0 copy-start.1
  0.7 1.3 %copy-done.1 = f32[4,5,2,32,256]{4,3,2,1,0:T(8,128)S(1)} copy-done((f32[4,5,2,32,256]{4,3,2,1,0:T(8,128)S(1)}, f32[4,5,2,32,256]{4,3,2,1,0:T(8,128)}, u32[]{:S(2)}) %copy-start.1) | copy-done | bytes 1310744
  2.0 0.0 copy-start.2
  2.0 0.7 %prepare.1 = (bf16[4,5,32,256]{3,2,1,0:T(8,128)(2,1)S(1)}, bf16[4,5,32,256]{3,2,1,0:T(8,128)(2,1)S(1)}, f32[40,256]{1,0:T(8,128)S(1)}, f32[40,256]{1,0:T(8,128)S(1)}) custom-call(s32[2]{0:T(128)S(1)} %pad_add_fusion.ids_ref, f32[4,5,2,32,256]{4,3,2,1,0:T(8,128)S(1)} %copy-done.1), custom_call_target="tpu_custom_call" | custom-call | flops 1000000 | bytes 2048008 | tf_op jit(solution)/shard_map/prepare/pallas_call | solution.py:32
  2.7 0.1 collective-permute-start
  2.8 0.5 collective-permute-start.1
  3.3 2.2 %collective-permute-start.4 = (bf16[4,5,32,256]{3,2,1,0:T(8,128)(2,1)S(1)}, bf16[4,5,32,256]{3,2,1,0:T(8,128)(2,1)S(1)}, u32[]{:S(2)}, u32[]{:S(2)}) collective-permute-start(bf16[4,5,32,256]{3,2,1,0:T(8,128)(2,1)S(1)} %get-tuple-element.17), channel_id=1, source_target_pairs={{0,2},{2,0},{4,6},{6,4},{1,3},{3,1},{5,7},{7,5},{8,10},{10,8},{12,... | collective-permute-start | bytes 983048 | tf_op jit(solution)/shard_map/halos/ppermute | solution.py:380
  5.5 2.6 %collective-permute-start.5 = (bf16[4,5,32,256]{3,2,1,0:T(8,128)(2,1)S(1)}, bf16[4,5,32,256]{3,2,1,0:T(8,128)(2,1)S(1)}, u32[]{:S(2)}, u32[]{:S(2)}) collective-permute-start(bf16[4,5,32,256]{3,2,1,0:T(8,128)(2,1)S(1)} %get-tuple-element.18), channel_id=1, source_target_pairs={{2,4},{4,2},{3,5},{5,3},{10,12},{12,10},{11,13},{13,11},{18,20},{2... | collective-permute-start | bytes 983048 | tf_op jit(solution)/shard_map/halos/ppermute | solution.py:381
  8.1 8.1 %collective-permute-start.2 = (f32[40,256]{1,0:T(8,128)S(1)}, f32[40,256]{1,0:T(8,128)S(1)}, u32[]{:S(2)}, u32[]{:S(2)}) collective-permute-start(f32[40,256]{1,0:T(8,128)S(1)} %get-tuple-element.19), channel_id=1, source_target_pairs={{8,16},{24,32},{40,48},{56,64},{72,80},{88,96},{104,112},{120,128}... | collective-permute-start | bytes 122888 | tf_op jit(solution)/shard_map/halos/ppermute | solution.py:378
  16.2 0.0 collective-permute-done.pa_ref
  16.2 0.0 collective-permute-start.3
  16.2 0.0 copy-done.14
  16.2 0.0 copy-start.13
  16.2 0.9 %copy-done.13 = f32[4,5,1024]{2,0,1:T(4,128)S(1)} copy-done((f32[4,5,1024]{2,0,1:T(4,128)S(1)}, f32[4,5,1024]{2,0,1:T(4,128)}, u32[]{:S(2)}) %copy-start.13) | copy-done | bytes 81944
  17.1 1.0 %order.1.refs_9_.refs_8_ = f32[20,512]{1,0:T(8,128)S(1)} custom-call(s32[2]{0:T(128)S(1)} %pad_add_fusion.ids_ref, s32[1,1024]{1,0:T(1,128)S(1)} %copy-done.14, f32[5,4,1024]{2,1,0:T(4,128)S(1)} %bitcast.4), custom_call_target="tpu_custom_call" | custom-call | flops 1000000 | bytes 126984 | tf_op jit(solution)/shard_map/order/pallas_call | solution.py:32
  18.1 0.0 copy-start
  18.1 0.0 collective-permute-done.1.pb_ref
  18.1 0.0 copy-done.2
  18.1 0.0 copy-start.5
  18.2 1.4 %copy-done.5 = f32[4,5,2,32,256]{4,3,2,1,0:T(8,128)S(1)} copy-done((f32[4,5,2,32,256]{4,3,2,1,0:T(8,128)S(1)}, f32[4,5,2,32,256]{4,3,2,1,0:T(8,128)}, u32[]{:S(2)}) %copy-start.5) | copy-done | bytes 1310744
  19.6 0.0 copy-start.6
  19.6 0.0 copy-start.7
  19.6 1.1 %rhs.1.refs_1_ = f32[4,5,2,32,256]{4,3,2,1,0:T(8,128)S(1)} custom-call(s32[2]{0:T(128)S(1)} %pad_add_fusion.ids_ref, f32[4,5,2,32,256]{4,3,2,1,0:T(8,128)S(1)} %copy-done.2, f32[4,5,2,32,256]{4,3,2,1,0:T(8,128)S(1)} %copy-done.5, bf16[4,5,32,256]{3,2,1,0:T(8,128)(2,1)S(1)} %collective-permute-done.pa_ref, ...), custom_call_target="tpu_custom_call" | custom-call | flops 10000000 | bytes 4587528 | tf_op jit(solution)/shard_map/rhs/pallas_call | solution.py:32
  20.7 0.0 collective-permute-done.2.refs_5_
  20.7 0.0 collective-permute-done.3.refs_6_
  20.7 0.0 collective-permute-done.4.refs_7_
  20.7 0.0 collective-permute-done.5.refs_8_
  20.7 0.0 copy-done
  20.7 0.0 copy-done.6
  20.8 0.0 copy-done.7
  20.8 2.5 %first_sweep.1 = (f32[4,5,2,32,256]{4,3,2,1,0:T(8,128)S(1)}, f32[40,256]{1,0:T(8,128)S(1)}, f32[40,256]{1,0:T(8,128)S(1)}, f32[20,256]{1,0:T(8,128)S(1)}, f32[20,256]{1,0:T(8,128)S(1)}) custom-call(s32[2]{0:T(128)S(1)} %pad_add_fusion.ids_ref, f32[4,5,2,32,256]{4,3,2,1,0:T(8,128)S(1)} %copy-done.2, f32[4,5,2,32,256]{4,3,2,1,0:T(8,128)S(1)} %rhs.1.refs_1_, ...), custom_call_target="tpu_custom_call" | custom-call | flops 20000000 | bytes 6602760 | tf_op jit(solution)/shard_map/first_sweep/pallas_call | solution.py:32
  23.3 0.0 copy-start.3
  23.3 3.1 %collective-permute-start.6 = (f32[40,256]{1,0:T(8,128)S(1)}, f32[40,256]{1,0:T(8,128)S(1)}, u32[]{:S(2)}, u32[]{:S(2)}) collective-permute-start(f32[40,256]{1,0:T(8,128)S(1)} %get-tuple-element.22), channel_id=1, source_target_pairs={{8,16},{24,32},{40,48},{56,64},{72,80},{88,96},{104,112},{120,128}... | collective-permute-start | bytes 122888 | tf_op jit(solution)/shard_map/surface_halos/ppermute | solution.py:413
  26.4 0.0 collective-permute-start.7
  26.4 0.0 collective-permute-start.8
  26.4 3.6 %collective-permute-start.9 = (f32[20,256]{1,0:T(8,128)S(1)}, f32[20,256]{1,0:T(8,128)S(1)}, u32[]{:S(2)}, u32[]{:S(2)}) collective-permute-start(f32[20,256]{1,0:T(8,128)S(1)} %get-tuple-element.25), channel_id=1, source_target_pairs={{2,4},{4,2},{3,5},{5,3},{10,12},{12,10},{11,13},{13,11},{18,20},{2... | collective-permute-start | bytes 61448 | tf_op jit(solution)/shard_map/surface_halos/ppermute | solution.py:415
  30.1 0.2 collective-permute-done.8.refs_6_
  30.3 1.9 %collective-permute-done.9.refs_7_ = f32[20,256]{1,0:T(8,128)S(1)} collective-permute-done((f32[20,256]{1,0:T(8,128)S(1)}, f32[20,256]{1,0:T(8,128)S(1)}, u32[]{:S(2)}, u32[]{:S(2)}) %collective-permute-start.9) | collective-permute-done | bytes 20512 | tf_op jit(solution)/shard_map/surface_halos/ppermute | solution.py:415
  32.2 0.0 collective-permute-done.6.refs_5_
  32.2 0.0 copy-start.8
  32.2 0.0 collective-permute-done.7.refs_9_.refs_6_
  32.2 0.0 copy-start.10
  32.2 1.1 %surface.1 = (f32[64,4,128]{2,1,0:T(4,128)S(1)}, f32[8,128]{1,0:T(8,128)S(1)}) custom-call(s32[2]{0:T(128)S(1)} %pad_add_fusion.ids_ref, f32[4,5,2,32,256]{4,3,2,1,0:T(8,128)S(1)} %get-tuple-element.21.refs_0_.f_ref, f32[4,5,2,32,256]{4,3,2,1,0:T(8,128)S(1)} %rhs.1.refs_1_, bf16[2,5,5,2,32,256]{5,4,3,2,1,0:T(8,128)(2,1)S(1)} %copy-done, ...), custom_call_target="tpu_custom_call" | custom-call | flops 5000000 | bytes 4689928 | tf_op jit(solution)/shard_map/surface/pallas_call | solution.py:32
  33.3 0.0 copy-done.8
  33.3 0.0 copy-done.10
  33.4 0.0 copy-start.12
  33.4 0.0 copy-done.3
  33.4 1.5 %pack.1 = (bf16[4,5,32,256]{3,2,1,0:T(8,128)(2,1)}, bf16[4,5,32,256]{3,2,1,0:T(8,128)(2,1)}) custom-call(s32[2]{0:T(128)S(1)} %pad_add_fusion.ids_ref, f32[4,5,2,32,256]{4,3,2,1,0:T(8,128)S(1)} %get-tuple-element.21.refs_0_.f_ref, f32[8,128]{1,0:T(8,128)S(1)} %get-tuple-element.26.done_ref), custom_call_target="tpu_custom_call" | custom-call | flops 1000000 | bytes 1970184 | tf_op jit(solution)/shard_map/pack/pallas_call | solution.py:32
  34.9 0.0 collective-permute-start.10
  34.9 3.6 %collective-permute-start.11 = (bf16[4,5,32,256]{3,2,1,0:T(8,128)(2,1)}, bf16[4,5,32,256]{3,2,1,0:T(8,128)(2,1)}, u32[]{:S(2)}, u32[]{:S(2)}) collective-permute-start(bf16[4,5,32,256]{3,2,1,0:T(8,128)(2,1)} %get-tuple-element.28), channel_id=1, source_target_pairs={{2,4},{4,2},{3,5},{5,3},{10,12},{12,10},{11,13},{13,11},{18,20},{2... | collective-permute-start | bytes 983048 | tf_op jit(solution)/shard_map/halos/ppermute | solution.py:438
  38.5 0.0 copy-done.12
  38.5 6.0 %all-to-all-start = ((f32[64,4,128]{2,1,0:T(4,128)}), f32[64,4,128]{2,1,0:T(4,128)S(1)}, u32[]{:S(2)}, u32[]{:S(2)}) async-start(f32[64,4,128]{2,1,0:T(4,128)} %copy-done.12), calls=%async_computation | async-start | bytes 262144 | tf_op jit(solution)/shard_map/share_sensitivities/all_to_all | solution.py:440
  44.5 0.0 collective-permute-done.10.refs_7_
  44.5 0.3 collective-permute-done.11.refs_8_
  44.8 0.0 copy-start.4
  44.8 1.3 %copy-done.4 = f32[4,5,2,32,256]{4,3,2,1,0:T(8,128)S(1)} copy-done((f32[4,5,2,32,256]{4,3,2,1,0:T(8,128)S(1)}, f32[4,5,2,32,256]{4,3,2,1,0:T(8,128)}, u32[]{:S(2)}) %copy-start.4) | copy-done | bytes 1310744
  46.1 0.0 copy-start.9
  46.1 0.8 %copy-done.9 = f32[40,256]{1,0:T(8,128)S(1)} copy-done((f32[40,256]{1,0:T(8,128)S(1)}, f32[40,256]{1,0:T(8,128)}, u32[]{:S(2)}) %copy-start.9) | copy-done | bytes 40984
  46.9 0.8 %copy-done.11 = f32[40,256]{1,0:T(8,128)S(1)} copy-done((f32[40,256]{1,0:T(8,128)S(1)}, f32[40,256]{1,0:T(8,128)}, u32[]{:S(2)}) %copy-start.11) | copy-done | bytes 40984
  47.7 4.0 %second_sweep.1 = (f32[4,5,2,32,256]{4,3,2,1,0:T(8,128)}, f32[8,128]{1,0:T(8,128)S(1)}) custom-call(s32[2]{0:T(128)S(1)} %pad_add_fusion.ids_ref, f32[4,5,2,32,256]{4,3,2,1,0:T(8,128)S(1)} %copy-done.4, f32[4,5,2,32,256]{4,3,2,1,0:T(8,128)S(1)} %rhs.1.refs_1_, bf16[2,5,5,2,32,256]{5,4,3,2,1,0:T(8,128)(2,1)S(1)} %copy-done, f32[2,32,256]{2,1,0:T(8,128)S(1)} %copy-done.6, ...), custom_call_target="tpu_custom_call" | custom-call | flops 20000000 | bytes 6443016 | tf_op jit(solution)/shard_map/second_sweep/pallas_call | solution.py:32
  51.7 3.9 %all-to-all-done.sens_ref = f32[64,4,128]{2,1,0:T(4,128)S(1)} async-done(((f32[64,4,128]{2,1,0:T(4,128)}), f32[64,4,128]{2,1,0:T(4,128)S(1)}, u32[]{:S(2)}, u32[]{:S(2)}) %all-to-all-start) | async-done | bytes 131104 | tf_op jit(solution)/shard_map/share_sensitivities/all_to_all | solution.py:440
  55.6 1.5 %modes.1 = f32[32,1024]{1,0:T(8,128)} custom-call(s32[1,1024]{1,0:T(1,128)S(1)} %copy-done.14, f32[64,4,128]{2,1,0:T(4,128)S(1)} %all-to-all-done.sens_ref, f32[8,128]{1,0:T(8,128)S(1)} %get-tuple-element.31.done_ref), custom_call_target="tpu_custom_call" | custom-call | flops 10000000 | bytes 270336 | tf_op jit(solution)/shard_map/modes/pallas_call | solution.py:32
  (1 shorter events, 0.0 us)
Async XLA Ops:
  0.6 15.6 %copy-start.14 = (s32[1,1024]{1,0:T(1,128)S(1)}, s32[1,1024]{1,0:T(1,128)}, u32[]{:S(2)}) copy-start(s32[1,1024]{1,0:T(1,128)} %cells_ref.3) | copy-start | bytes 12292
  0.7 1.3 %copy-start.1 = (f32[4,5,2,32,256]{4,3,2,1,0:T(8,128)S(1)}, f32[4,5,2,32,256]{4,3,2,1,0:T(8,128)}, u32[]{:S(2)}) copy-start(f32[4,5,2,32,256]{4,3,2,1,0:T(8,128)} %refs_0_.1) | copy-start | bytes 3932164
  2.0 16.1 %copy-start.2 = (f32[4,5,2,32,256]{4,3,2,1,0:T(8,128)S(1)}, f32[4,5,2,32,256]{4,3,2,1,0:T(8,128)}, u32[]{:S(2)}) copy-start(f32[4,5,2,32,256]{4,3,2,1,0:T(8,128)} %refs_0_.1) | copy-start | bytes 3932164
  2.7 13.5 %collective-permute-start = (bf16[4,5,32,256]{3,2,1,0:T(8,128)(2,1)S(1)}, bf16[4,5,32,256]{3,2,1,0:T(8,128)(2,1)S(1)}, u32[]{:S(2)}, u32[]{:S(2)}) collective-permute-start(bf16[4,5,32,256]{3,2,1,0:T(8,128)(2,1)S(1)} %get-tuple-element.17), channel_id=1, source_target_pairs={{0,1},{1,0},{2,3},{3,2},{4,5},{5,4},{6,7},{7,6},{8,9},{9,8},{10,11... | collective-permute-start | bytes 983048 | tf_op jit(solution)/shard_map/halos/ppermute | solution.py:382
  2.8 15.3 %collective-permute-start.1 = (bf16[4,5,32,256]{3,2,1,0:T(8,128)(2,1)S(1)}, bf16[4,5,32,256]{3,2,1,0:T(8,128)(2,1)S(1)}, u32[]{:S(2)}, u32[]{:S(2)}) collective-permute-start(bf16[4,5,32,256]{3,2,1,0:T(8,128)(2,1)S(1)} %get-tuple-element.18), channel_id=1, source_target_pairs={{0,1},{1,0},{2,3},{3,2},{4,5},{5,4},{6,7},{7,6},{8,9},{9,8},{10,11... | collective-permute-start | bytes 983048 | tf_op jit(solution)/shard_map/halos/ppermute | solution.py:383
  3.3 17.4 %collective-permute-start.4 = (bf16[4,5,32,256]{3,2,1,0:T(8,128)(2,1)S(1)}, bf16[4,5,32,256]{3,2,1,0:T(8,128)(2,1)S(1)}, u32[]{:S(2)}, u32[]{:S(2)}) collective-permute-start(bf16[4,5,32,256]{3,2,1,0:T(8,128)(2,1)S(1)} %get-tuple-element.17), channel_id=1, source_target_pairs={{0,2},{2,0},{4,6},{6,4},{1,3},{3,1},{5,7},{7,5},{8,10},{10,8},{12,... | collective-permute-start | bytes 983048 | tf_op jit(solution)/shard_map/halos/ppermute | solution.py:380
  5.5 15.2 %collective-permute-start.5 = (bf16[4,5,32,256]{3,2,1,0:T(8,128)(2,1)S(1)}, bf16[4,5,32,256]{3,2,1,0:T(8,128)(2,1)S(1)}, u32[]{:S(2)}, u32[]{:S(2)}) collective-permute-start(bf16[4,5,32,256]{3,2,1,0:T(8,128)(2,1)S(1)} %get-tuple-element.18), channel_id=1, source_target_pairs={{2,4},{4,2},{3,5},{5,3},{10,12},{12,10},{11,13},{13,11},{18,20},{2... | collective-permute-start | bytes 983048 | tf_op jit(solution)/shard_map/halos/ppermute | solution.py:381
  8.1 12.6 %collective-permute-start.2 = (f32[40,256]{1,0:T(8,128)S(1)}, f32[40,256]{1,0:T(8,128)S(1)}, u32[]{:S(2)}, u32[]{:S(2)}) collective-permute-start(f32[40,256]{1,0:T(8,128)S(1)} %get-tuple-element.19), channel_id=1, source_target_pairs={{8,16},{24,32},{40,48},{56,64},{72,80},{88,96},{104,112},{120,128}... | collective-permute-start | bytes 122888 | tf_op jit(solution)/shard_map/halos/ppermute | solution.py:378
  16.2 4.5 %collective-permute-start.3 = (f32[40,256]{1,0:T(8,128)S(1)}, f32[40,256]{1,0:T(8,128)S(1)}, u32[]{:S(2)}, u32[]{:S(2)}) collective-permute-start(f32[40,256]{1,0:T(8,128)S(1)} %get-tuple-element.20), channel_id=1, source_target_pairs={{0,8},{8,0},{16,24},{24,16},{32,40},{40,32},{48,56},{56,48},{64,72... | collective-permute-start | bytes 122888 | tf_op jit(solution)/shard_map/halos/ppermute | solution.py:379
  16.2 0.9 %copy-start.13 = (f32[4,5,1024]{2,0,1:T(4,128)S(1)}, f32[4,5,1024]{2,0,1:T(4,128)}, u32[]{:S(2)}) copy-start(f32[4,5,1024]{2,0,1:T(4,128)} %param.13) | copy-start | bytes 245764
  18.1 2.6 %copy-start = (bf16[2,5,5,2,32,256]{5,4,3,2,1,0:T(8,128)(2,1)S(1)}, bf16[2,5,5,2,32,256]{5,4,3,2,1,0:T(8,128)(2,1)}, u32[]{:S(2)}) copy-start(bf16[2,5,5,2,32,256]{5,4,3,2,1,0:T(8,128)(2,1)} %refs_2_.5) | copy-start | bytes 4915204
  18.1 1.4 %copy-start.5 = (f32[4,5,2,32,256]{4,3,2,1,0:T(8,128)S(1)}, f32[4,5,2,32,256]{4,3,2,1,0:T(8,128)}, u32[]{:S(2)}) copy-start(f32[4,5,2,32,256]{4,3,2,1,0:T(8,128)} %src_ref.1) | copy-start | bytes 3932164
  19.6 1.2 %copy-start.6 = (f32[2,32,256]{2,1,0:T(8,128)S(1)}, f32[2,32,256]{2,1,0:T(8,128)}, u32[]{:S(2)}) copy-start(f32[2,32,256]{2,1,0:T(8,128)} %refs_3_.5) | copy-start | bytes 196612
  19.6 1.2 %copy-start.7 = (f32[2,32,256]{2,1,0:T(8,128)S(1)}, f32[2,32,256]{2,1,0:T(8,128)}, u32[]{:S(2)}) copy-start(f32[2,32,256]{2,1,0:T(8,128)} %refs_4_.5) | copy-start | bytes 196612
  23.3 10.1 %copy-start.3 = (f32[4,5,2,32,256]{4,3,2,1,0:T(8,128)}, f32[4,5,2,32,256]{4,3,2,1,0:T(8,128)S(1)}, u32[]{:S(2)}) copy-start(f32[4,5,2,32,256]{4,3,2,1,0:T(8,128)S(1)} %get-tuple-element.21.refs_0_.f_ref) | copy-start | bytes 3932164
  23.3 8.9 %collective-permute-start.6 = (f32[40,256]{1,0:T(8,128)S(1)}, f32[40,256]{1,0:T(8,128)S(1)}, u32[]{:S(2)}, u32[]{:S(2)}) collective-permute-start(f32[40,256]{1,0:T(8,128)S(1)} %get-tuple-element.22), channel_id=1, source_target_pairs={{8,16},{24,32},{40,48},{56,64},{72,80},{88,96},{104,112},{120,128}... | collective-permute-start | bytes 122888 | tf_op jit(solution)/shard_map/surface_halos/ppermute | solution.py:413
  26.4 5.7 %collective-permute-start.7 = (f32[40,256]{1,0:T(8,128)S(1)}, f32[40,256]{1,0:T(8,128)S(1)}, u32[]{:S(2)}, u32[]{:S(2)}) collective-permute-start(f32[40,256]{1,0:T(8,128)S(1)} %get-tuple-element.23), channel_id=1, source_target_pairs={{0,8},{8,0},{16,24},{24,16},{32,40},{40,32},{48,56},{56,48},{64,72... | collective-permute-start | bytes 122888 | tf_op jit(solution)/shard_map/surface_halos/ppermute | solution.py:416
  26.4 3.8 %collective-permute-start.8 = (f32[20,256]{1,0:T(8,128)S(1)}, f32[20,256]{1,0:T(8,128)S(1)}, u32[]{:S(2)}, u32[]{:S(2)}) collective-permute-start(f32[20,256]{1,0:T(8,128)S(1)} %get-tuple-element.24), channel_id=1, source_target_pairs={{0,2},{2,0},{4,6},{6,4},{1,3},{3,1},{5,7},{7,5},{8,10},{10,8},{12,... | collective-permute-start | bytes 61448 | tf_op jit(solution)/shard_map/surface_halos/ppermute | solution.py:414
  26.4 5.7 %collective-permute-start.9 = (f32[20,256]{1,0:T(8,128)S(1)}, f32[20,256]{1,0:T(8,128)S(1)}, u32[]{:S(2)}, u32[]{:S(2)}) collective-permute-start(f32[20,256]{1,0:T(8,128)S(1)} %get-tuple-element.25), channel_id=1, source_target_pairs={{2,4},{4,2},{3,5},{5,3},{10,12},{12,10},{11,13},{13,11},{18,20},{2... | collective-permute-start | bytes 61448 | tf_op jit(solution)/shard_map/surface_halos/ppermute | solution.py:415
  32.2 1.2 %copy-start.8 = (f32[40,256]{1,0:T(8,128)}, f32[40,256]{1,0:T(8,128)S(1)}, u32[]{:S(2)}) copy-start(f32[40,256]{1,0:T(8,128)S(1)} %collective-permute-done.6.refs_5_) | copy-start | bytes 122884
  32.2 1.2 %copy-start.10 = (f32[40,256]{1,0:T(8,128)}, f32[40,256]{1,0:T(8,128)S(1)}, u32[]{:S(2)}) copy-start(f32[40,256]{1,0:T(8,128)S(1)} %collective-permute-done.7.refs_9_.refs_6_) | copy-start | bytes 122884
  33.4 5.1 %copy-start.12 = (f32[64,4,128]{2,1,0:T(4,128)}, f32[64,4,128]{2,1,0:T(4,128)S(1)}, u32[]{:S(2)}) copy-start(f32[64,4,128]{2,1,0:T(4,128)S(1)} %get-tuple-element.30) | copy-start | bytes 393220
  34.9 9.7 %collective-permute-start.10 = (bf16[4,5,32,256]{3,2,1,0:T(8,128)(2,1)}, bf16[4,5,32,256]{3,2,1,0:T(8,128)(2,1)S(1)}, u32[]{:S(2)}, u32[]{:S(2)}) collective-permute-start(bf16[4,5,32,256]{3,2,1,0:T(8,128)(2,1)} %get-tuple-element.27), channel_id=1, source_target_pairs={{0,2},{2,0},{4,6},{6,4},{1,3},{3,1},{5,7},{7,5},{8,10},{10,8},{12,... | collective-permute-start | bytes 983048 | tf_op jit(solution)/shard_map/halos/ppermute | solution.py:437
  34.9 9.9 %collective-permute-start.11 = (bf16[4,5,32,256]{3,2,1,0:T(8,128)(2,1)}, bf16[4,5,32,256]{3,2,1,0:T(8,128)(2,1)}, u32[]{:S(2)}, u32[]{:S(2)}) collective-permute-start(bf16[4,5,32,256]{3,2,1,0:T(8,128)(2,1)} %get-tuple-element.28), channel_id=1, source_target_pairs={{2,4},{4,2},{3,5},{5,3},{10,12},{12,10},{11,13},{13,11},{18,20},{2... | collective-permute-start | bytes 983048 | tf_op jit(solution)/shard_map/halos/ppermute | solution.py:438
  38.5 17.1 %all-to-all-start = ((f32[64,4,128]{2,1,0:T(4,128)}), f32[64,4,128]{2,1,0:T(4,128)S(1)}, u32[]{:S(2)}, u32[]{:S(2)}) async-start(f32[64,4,128]{2,1,0:T(4,128)} %copy-done.12), calls=%async_computation | async-start | bytes 262144 | tf_op jit(solution)/shard_map/share_sensitivities/all_to_all | solution.py:440
  44.8 1.3 %copy-start.4 = (f32[4,5,2,32,256]{4,3,2,1,0:T(8,128)S(1)}, f32[4,5,2,32,256]{4,3,2,1,0:T(8,128)}, u32[]{:S(2)}) copy-start(f32[4,5,2,32,256]{4,3,2,1,0:T(8,128)} %copy-done.3) | copy-start | bytes 3932164
  46.1 0.8 %copy-start.9 = (f32[40,256]{1,0:T(8,128)S(1)}, f32[40,256]{1,0:T(8,128)}, u32[]{:S(2)}) copy-start(f32[40,256]{1,0:T(8,128)} %copy-done.8) | copy-start | bytes 122884
  46.9 0.8 %copy-start.11 = (f32[40,256]{1,0:T(8,128)S(1)}, f32[40,256]{1,0:T(8,128)}, u32[]{:S(2)}) copy-start(f32[40,256]{1,0:T(8,128)} %copy-done.10) | copy-start | bytes 122884

commit v4 on v3

--- a/solution.py
+++ b/solution.py
@@ -9,7 +9,6 @@
 from jax.sharding import PartitionSpec as P
 
 PASSAGES = 16
-SWEEPS = 2
 NT = 8
 F32 = jnp.float32
 BF16 = jnp.bfloat16
@@ -67,19 +66,15 @@
             b_ref[t, v] = f_ref[t, v, layer_b].astype(BF16)
 
 
-def pack_rows(ids_ref, f_ref, outer_ref, inner_ref, ra_ref=None, rb_ref=None, layer_a=0):
+def pack_rows(ids_ref, f_ref, outer_ref, inner_ref):
     nt, nv, ni = f_ref.shape[:3]
     for t in range(nt):
         for v in range(nv):
-            at = t * nv + v
             for i in range(ni):
-                row = at * ni + i
-                outer = edge_row(ids_ref, f_ref, t, v, i, True)
-                outer_ref[row : row + 1, :] = outer
-                inner_ref[row : row + 1, :] = edge_row(ids_ref, f_ref, t, v, i, False)
-                if ra_ref is not None:
-                    to = ra_ref if i == layer_a else rb_ref
-                    to[at : at + 1, :] = outer
+                row = (t * nv + v) * ni + i
+                here = slice(row, row + 1)
+                outer_ref[here, :] = edge_row(ids_ref, f_ref, t, v, i, True)
+                inner_ref[here, :] = edge_row(ids_ref, f_ref, t, v, i, False)
 
 
 def prepare_kernel(ids_ref, f_ref, a_ref, b_ref, outer_ref, inner_ref):
@@ -131,7 +126,7 @@
     return here, plus, minus
 
 
-def sweep_tile(refs, halo, edges, i, j, lanes):
+def local_tile(refs, edges, i, j, lanes):
     f_ref, rhs_ref, jac_ref, sig_ref, dmp_ref = refs
     nt, nv, ni = f_ref.shape[:3]
     pair = slice(j // 16 * 16, j // 16 * 16 + 16)
@@ -148,11 +143,10 @@
         ]
         for t in range(nt):
             here, plus_j, minus_j = shifted(f_ref, t, u, i, j, lanes, edges, rows_id)
-            outer = halo(t, u)
             inner = f_ref[t, u, 1 - i, j : j + 8, lanes]
-            plus_i, minus_i = (outer, inner) if i else (inner, outer)
-            diff_i, diff_j = here - plus_i, here - plus_j
-            both = diff_i + diff_j + ((here - minus_i) + (here - minus_j))
+            diff_i = here if i else here - inner
+            diff_j = here - plus_j
+            both = (here + (here - inner)) + (diff_j + (here - minus_j))
             own = sigma * here + damping * both
             for v in range(nv):
                 term = jac[0][v] * diff_i + jac[1][v] * diff_j
@@ -169,11 +163,44 @@
     ]
 
 
+def finish_tile(refs, layer_ref, i, j, lanes):
+    part_ref, jac_ref, sig_ref, dmp_ref = refs
+    nt, nv = part_ref.shape[:2]
+    pair = slice(j // 16 * 16, j // 16 * 16 + 16)
+    half = slice(j % 16, j % 16 + 8)
+    sigma = sig_ref[i, j : j + 8, lanes]
+    damping = dmp_ref[i, j : j + 8, lanes]
+    scaling = 1.0 / (sigma + 4.0 * damping)
+    damping = damping * scaling
+    acc = [[None] * nv for _ in range(nt)]
+    for u in range(nv):
+        jac = (
+            [
+                jac_ref[0, u, v, i, pair, lanes].astype(F32)[half] * scaling
+                for v in range(nv)
+            ]
+            if i
+            else None
+        )
+        for t in range(nt):
+            layer = layer_ref[t, u, pair, lanes].astype(F32)[half]
+            for v in range(nv) if i else (u,):
+                term = jac[v] * layer if i else damping * layer
+                if i and v == u:
+                    term = term + damping * layer
+                acc[t][v] = term if acc[t][v] is None else acc[t][v] + term
+    return [
+        [part_ref[t, v, i, j : j + 8, lanes] + acc[t][v] for v in range(nv)]
+        for t in range(nt)
+    ]
+
+
 def lanes_at(k):
     return pl.ds(pl.multiple_of(k * 128, 128), 128)
 
 
-def sweep_all(ids_ref, refs, outer_ref, inner_ref, out_ref, layers):
+def local_kernel(ids_ref, *refs):
+    ins, outer_ref, inner_ref, out_ref = refs[:5], *refs[5:8]
     nt, nv, ni, nj, nk = out_ref.shape
     upper = ids_ref[1] == 1
 
@@ -184,21 +211,12 @@
             row = (t * nv + u) * ni + i
             outer = outer_ref[row : row + 1, lanes]
             inner = inner_ref[row : row + 1, lanes]
-            edge = jnp.where(upper, outer, inner) if high else jnp.where(upper, inner, outer)
+            edge = jnp.where(upper == high, outer, inner)
             return jnp.broadcast_to(edge, (8, 128))
 
         for i in range(ni):
             for j in range(0, nj, 8):
-                pair = slice(j // 16 * 16, j // 16 * 16 + 16)
-                half = slice(j % 16, j % 16 + 8)
-                new = sweep_tile(
-                    refs,
-                    lambda t, u: layers[i][t, u, pair, lanes].astype(F32)[half],
-                    edges,
-                    i,
-                    j,
-                    lanes,
-                )
+                new = local_tile(ins, edges, i, j, lanes)
                 for t in range(nt):
                     for v in range(nv):
                         out_ref[t, v, i, j : j + 8, lanes] = new[t][v]
@@ -207,24 +225,37 @@
     lax.fori_loop(0, nk // 128, one, 0)
 
 
+def finish_all(ins, out_ref, layers):
+    nt, nv, ni, nj, nk = out_ref.shape
+
+    def one(k, carry):
+        lanes = lanes_at(k)
+        for i in range(ni):
+            for j in range(0, nj, 8):
+                new = finish_tile(ins, layers[i], i, j, lanes)
+                for t in range(nt):
+                    for v in range(nv):
+                        out_ref[t, v, i, j : j + 8, lanes] = new[t][v]
+        return carry
+
+    lax.fori_loop(0, nk // 128, one, 0)
+
+
 def first_kernel(ids_ref, *refs):
-    ins, outer_ref, inner_ref, ha_ref, hb_ref = refs[:5], *refs[5:9]
-    out_ref, no_ref, ni_ref, ra_ref, rb_ref = refs[10:]
+    ins, ha_ref, hb_ref = refs[:4], refs[4], refs[5]
+    out_ref, a_ref, b_ref, no_ref, ni_ref = refs[6:]
 
     def run(layer_a, layer_b):
-        layers = {layer_a: ha_ref, layer_b: hb_ref}
-        sweep_all(ids_ref, ins, outer_ref, inner_ref, out_ref, layers)
-        pack_rows(ids_ref, out_ref, no_ref, ni_ref, ra_ref, rb_ref, layer_a)
+        finish_all(ins, out_ref, {layer_a: ha_ref, layer_b: hb_ref})
+        pack_layers(out_ref, a_ref, b_ref, layer_a, layer_b)
 
     by_parity(ids_ref, run)
+    pack_rows(ids_ref, out_ref, no_ref, ni_ref)
 
 
 def surface_kernel(ids_ref, *refs):
-    ins, outer_ref, ra_ref, rb_ref, w_ref = refs[:5], *refs[5:9]
-    sens_ref, done_ref = refs[10:]
-    done_ref[...] = jnp.zeros(done_ref.shape, F32)
-    f_ref = ins[0]
-    nt, nv, ni, nj, nk = f_ref.shape
+    ins, ha_ref, hb_ref, w_ref, sens_ref = refs[:4], *refs[4:8]
+    nt, nv, ni, nj, nk = ins[0].shape
 
     def row_of(side, layers):
         j = side * (nj - 8)
@@ -232,17 +263,8 @@
 
         def one(k, carry):
             lanes = lanes_at(k)
-
-            def edges(t, u, i, high):
-                row = (t * nv + u) * ni + i
-                return jnp.broadcast_to(outer_ref[row : row + 1, lanes], (8, 128))
-
-            def halo(i, t, u):
-                at = t * nv + u
-                return jnp.broadcast_to(layers[i][at : at + 1, lanes], (8, 128))
-
             for i in range(ni):
-                new = sweep_tile(ins, functools.partial(halo, i), edges, i, j, lanes)
+                new = finish_tile(ins, layers[i], i, j, lanes)
                 total = jnp.zeros((8, 128), F32)
                 for t in range(nt):
                     for v in range(nv):
@@ -259,25 +281,19 @@
         lax.fori_loop(0, nk // 128, one, 0)
 
     def run(layer_a, layer_b):
-        layers = {layer_a: ra_ref, layer_b: rb_ref}
+        layers = {layer_a: ha_ref, layer_b: hb_ref}
         for side in range(2):
             pl.when(ids_ref[1] == side)(functools.partial(row_of, side, layers))
 
     by_parity(ids_ref, run)
 
 
-def pack_kernel(ids_ref, f_ref, done_ref, a_ref, b_ref):
-    by_parity(ids_ref, functools.partial(pack_layers, f_ref, a_ref, b_ref))
-
-
 def second_kernel(ids_ref, *refs):
-    ins, outer_ref, inner_ref, ha_ref, hb_ref = refs[:5], *refs[5:9]
-    out_ref, done_ref = refs[9:]
+    ins, ha_ref, hb_ref, out_ref, done_ref = refs[:4], *refs[4:8]
     done_ref[...] = jnp.zeros(done_ref.shape, F32)
 
     def run(layer_a, layer_b):
-        layers = {layer_a: ha_ref, layer_b: hb_ref}
-        sweep_all(ids_ref, ins, outer_ref, inner_ref, out_ref, layers)
+        finish_all(ins, out_ref, {layer_a: ha_ref, layer_b: hb_ref})
 
     by_parity(ids_ref, run)
 
@@ -363,24 +379,25 @@
     field_like = jax.ShapeDtypeStruct(start.shape, F32)
     layer_like = jax.ShapeDtypeStruct((nt, nv, nj, nk), BF16)
     rows_like = jax.ShapeDtypeStruct((nt * nv * ni, nk), F32)
-    row_like = jax.ShapeDtypeStruct((nt * nv, nk), F32)
-
-    a, b, outer, inner = call(
-        prepare_kernel,
-        [layer_like, layer_like, rows_like, rows_like],
-        (ids, start),
-        [SMEM, VMEM],
-        4,
-        10**6,
-        "prepare",
-    )
-    with jax.named_scope("halos"):
-        outer = lax.ppermute(outer, "passage", across)
-        inner = lax.ppermute(inner, "passage", within)
-        ha = lax.ppermute(a, "cell", even)
-        hb = lax.ppermute(b, "cell", odd)
-        pa = lax.ppermute(a, "tm", swap)
-        pb = lax.ppermute(b, "tm", swap)
+
+    sends = [layer_like, layer_like, rows_like, rows_like]
+
+    def exchange(a, b, outer, inner):
+        with jax.named_scope("halos"):
+            return (
+                lax.ppermute(outer, "passage", across),
+                lax.ppermute(inner, "passage", within),
+                lax.ppermute(a, "cell", even),
+                lax.ppermute(b, "cell", odd),
+            )
+
+    packed = call(
+        prepare_kernel, sends, (ids, start), [SMEM, VMEM], 4, 10**6, "prepare"
+    )
+    with jax.named_scope("other_times"):
+        pa = lax.ppermute(packed[0], "tm", swap)
+        pb = lax.ppermute(packed[1], "tm", swap)
+    outer, inner, ha, hb = exchange(*packed)
     rhs = call(
         rhs_kernel,
         [field_like],
@@ -400,52 +417,44 @@
         "order",
     )[0]
     fixed = (jac, sigma, damping)
-    field, outer, inner, ra, rb = call(
+
+    def local(field, outer, inner, name):
+        args = (ids, field, rhs, *fixed, outer, inner)
+        specs = [SMEM] + [VMEM] * 7
+        return call(local_kernel, [field_like], args, specs, 4, 2 * 10**7, name)[0]
+
+    part = local(start, outer, inner, "first_local")
+    field, *packed = call(
         first_kernel,
-        [field_like, rows_like, rows_like, row_like, row_like],
-        (ids, start, rhs, *fixed, outer, inner, ha, hb, ordered),
-        [SMEM] + [VMEM] * 10,
-        8,
-        2 * 10**7,
-        "first_sweep",
-    )
-    with jax.named_scope("surface_halos"):
-        outer = lax.ppermute(outer, "passage", across)
-        ra = lax.ppermute(ra, "cell", even)
-        rb = lax.ppermute(rb, "cell", odd)
-        inner = lax.ppermute(inner, "passage", within)
-    token_like = jax.ShapeDtypeStruct((8, 128), F32)
-    sens, done = call(
+        [field_like] + sends,
+        (ids, part, *fixed, ha, hb),
+        [SMEM] + [VMEM] * 6,
+        4,
+        10**7,
+        "first_finish",
+    )
+    outer, inner, ha, hb = exchange(*packed)
+    part = local(field, outer, inner, "second_local")
+    sens = call(
         surface_kernel,
-        [jax.ShapeDtypeStruct((2 * ring, ni * nk // 128, 128), F32), token_like],
-        (ids, field, rhs, *fixed, outer, ra, rb, ordered, inner),
-        [SMEM] + [VMEM] * 10,
-        8,
+        [jax.ShapeDtypeStruct((2 * ring, ni * nk // 128, 128), F32)],
+        (ids, part, *fixed, ha, hb, ordered),
+        [SMEM] + [VMEM] * 7,
+        4,
         5 * 10**6,
         "surface",
-    )
-    a, b = call(
-        pack_kernel,
-        [layer_like, layer_like],
-        (ids, field, done),
-        [SMEM, VMEM, VMEM],
-        4,
-        10**6,
-        "pack",
-    )
-    with jax.named_scope("halos"):
-        ha = lax.ppermute(a, "cell", even)
-        hb = lax.ppermute(b, "cell", odd)
+    )[0]
+    token_like = jax.ShapeDtypeStruct((8, 128), F32)
     with jax.named_scope("share_sensitivities"):
         gathered = lax.all_to_all(sens, ("passage", "tm"), 0, 0, tiled=True)
     field, done = call(
         second_kernel,
         [field_like, token_like],
-        (ids, field, rhs, *fixed, outer, inner, ha, hb),
-        [SMEM] + [VMEM] * 9,
-        8,
-        2 * 10**7,
-        "second_sweep",
+        (ids, part, *fixed, ha, hb),
+        [SMEM] + [VMEM] * 6,
+        4,
+        10**7,
+        "second_finish",
     )
     modes = call(
         modes_kernel,

time: 58.2 us -> 57.8 us (level)
  the two profiles are of different devices: /device:TPU:8 before, /device:TPU:1 now
where the time goes in v4:
time: 57.8 us; the launch traced here: 57.5 us
  starting transfers between devices  27.9 us (48%)
  Pallas kernels  13.9 us (24%)
  waiting for transfers between devices  11.9 us (21%)
  local copies, waits for them, and re-layouts  3.03 us (5%)
  between operations  0.8 us (1%)
    pallas_call x9, Pallas kernels, call(): pl.pallas_call(kernel, out_shape=outs, in_specs=specs, out_specs=[VMEM] *...  13.9 us
    ppermute x2, starting transfers between devices, exchange(): lax.ppermute(outer, 'passage', across)  10.7 us
    all_to_all x1, starting transfers between devices, body(): gathered = lax.all_to_all(sens, ('passage', 'tm'), 0, 0, tiled=True)  8.67 us
    all_to_all x1, waiting for transfers between devices, body(): gathered = lax.all_to_all(sens, ('passage', 'tm'), 0, 0, tiled=True)  8.02 us
    ppermute x2, starting transfers between devices, exchange(): lax.ppermute(a, 'cell', even)  3.62 us
    ppermute x1, starting transfers between devices, body(): pa = lax.ppermute(packed[0], 'tm', swap)  3.33 us
    unnamed x18, local copies, waits for them, and re-layouts  3.03 us
    ppermute x2, waiting for transfers between devices, exchange(): lax.ppermute(outer, 'passage', across)  2.08 us
  transfers between devices with their start and end apart: 11, of which 5 were waited for; matrix products, arithmetic and copies ran while one was open for 0% of the time, Pallas kernels for 16%

profile of v4, /device:TPU:1, one launch (start us, length us, event | category | flops | bytes accessed | tf_op | source)
XLA Modules:
  0.0 57.5 jit_solution(10981526155607822688)
XLA Ops:
  0.6 0.1 pad_add_fusion.ids_ref
  0.7 0.0 copy-start.1
  0.7 1.3 %copy-done.1 = f32[4,5,2,32,256]{4,3,2,1,0:T(8,128)S(1)} copy-done((f32[4,5,2,32,256]{4,3,2,1,0:T(8,128)S(1)}, f32[4,5,2,32,256]{4,3,2,1,0:T(8,128)}, u32[]{:S(2)}) %copy-start.1) | copy-done | bytes 1310744
  2.0 0.0 copy-start.4
  2.0 0.7 %prepare.1 = (bf16[4,5,32,256]{3,2,1,0:T(8,128)(2,1)S(1)}, bf16[4,5,32,256]{3,2,1,0:T(8,128)(2,1)S(1)}, f32[40,256]{1,0:T(8,128)S(1)}, f32[40,256]{1,0:T(8,128)S(1)}) custom-call(s32[2]{0:T(128)S(1)} %pad_add_fusion.ids_ref, f32[4,5,2,32,256]{4,3,2,1,0:T(8,128)S(1)} %copy-done.1), custom_call_target="tpu_custom_call" | custom-call | flops 1000000 | bytes 2048008 | tf_op jit(solution)/shard_map/prepare/pallas_call | solution.py:31
  2.7 3.3 %collective-permute-start = (bf16[4,5,32,256]{3,2,1,0:T(8,128)(2,1)S(1)}, bf16[4,5,32,256]{3,2,1,0:T(8,128)(2,1)S(1)}, u32[]{:S(2)}, u32[]{:S(2)}) collective-permute-start(bf16[4,5,32,256]{3,2,1,0:T(8,128)(2,1)S(1)} %get-tuple-element.13), channel_id=1, source_target_pairs={{0,1},{1,0},{2,3},{3,2},{4,5},{5,4},{6,7},{7,6},{8,9},{9,8},{10,11... | collective-permute-start | bytes 983048 | tf_op jit(solution)/shard_map/other_times/ppermute | solution.py:398
  6.0 0.1 collective-permute-start.1
  6.1 0.0 collective-permute-start.4
  6.1 0.7 %collective-permute-start.5 = (bf16[4,5,32,256]{3,2,1,0:T(8,128)(2,1)S(1)}, bf16[4,5,32,256]{3,2,1,0:T(8,128)(2,1)S(1)}, u32[]{:S(2)}, u32[]{:S(2)}) collective-permute-start(bf16[4,5,32,256]{3,2,1,0:T(8,128)(2,1)S(1)} %get-tuple-element.14), channel_id=1, source_target_pairs={{2,4},{4,2},{3,5},{5,3},{10,12},{12,10},{11,13},{13,11},{18,20},{2... | collective-permute-start | bytes 983048 | tf_op jit(solution)/shard_map/halos/ppermute | solution.py:391
  6.8 7.4 %collective-permute-start.2 = (f32[40,256]{1,0:T(8,128)S(1)}, f32[40,256]{1,0:T(8,128)S(1)}, u32[]{:S(2)}, u32[]{:S(2)}) collective-permute-start(f32[40,256]{1,0:T(8,128)S(1)} %get-tuple-element.15), channel_id=1, source_target_pairs={{8,16},{24,32},{40,48},{56,64},{72,80},{88,96},{104,112},{120,128}... | collective-permute-start | bytes 122888 | tf_op jit(solution)/shard_map/halos/ppermute | solution.py:388
  14.2 0.0 collective-permute-done.pa_ref
  14.2 0.0 copy-start
  14.2 0.0 copy-start.2
  14.2 0.0 copy-start.3
  14.2 0.1 collective-permute-start.3
  14.3 0.0 collective-permute-done.1.pb_ref
  14.3 0.0 copy-done.4
  14.4 1.1 %rhs.1.refs_1_ = f32[4,5,2,32,256]{4,3,2,1,0:T(8,128)S(1)} custom-call(s32[2]{0:T(128)S(1)} %pad_add_fusion.ids_ref, f32[4,5,2,32,256]{4,3,2,1,0:T(8,128)S(1)} %copy-done.1, f32[4,5,2,32,256]{4,3,2,1,0:T(8,128)S(1)} %copy-done.4, bf16[4,5,32,256]{3,2,1,0:T(8,128)(2,1)S(1)} %collective-permute-done.pa_ref, ...), custom_call_target="tpu_custom_call" | custom-call | flops 10000000 | bytes 4587528 | tf_op jit(solution)/shard_map/rhs/pallas_call | solution.py:31
  15.5 0.1 collective-permute-done.2.refs_5_
  15.6 1.6 %collective-permute-done.3.refs_6_ = f32[40,256]{1,0:T(8,128)S(1)} collective-permute-done((f32[40,256]{1,0:T(8,128)S(1)}, f32[40,256]{1,0:T(8,128)S(1)}, u32[]{:S(2)}, u32[]{:S(2)}) %collective-permute-start.3) | collective-permute-done | bytes 40992 | tf_op jit(solution)/shard_map/halos/ppermute | solution.py:389
  17.2 0.0 copy-done
  17.2 0.0 copy-done.2
  17.2 0.0 copy-done.3
  17.2 2.4 %first_local.1.refs_0_ = f32[4,5,2,32,256]{4,3,2,1,0:T(8,128)S(1)} custom-call(s32[2]{0:T(128)S(1)} %pad_add_fusion.ids_ref, f32[4,5,2,32,256]{4,3,2,1,0:T(8,128)S(1)} %copy-done.1, f32[4,5,2,32,256]{4,3,2,1,0:T(8,128)S(1)} %rhs.1.refs_1_, bf16[2,5,5,2,32,256]{5,4,3,2,1,0:T(8,128)(2,1)S(1)} %copy-done, f32[2,32,256]{2,1,0:T(8,128)S(1)} %copy-done.2, ...), custom_call_target="tpu_custom_call" | custom-call | flops 20000000 | bytes 5783560 | tf_op jit(solution)/shard_map/first_local/pallas_call | solution.py:31
  19.6 0.0 copy-start.7
  19.6 0.0 copy-start.8
  19.6 0.0 collective-permute-done.4.refs_4_
  19.6 0.0 collective-permute-done.5.refs_5_
  19.6 1.2 %first_finish.1 = (f32[4,5,2,32,256]{4,3,2,1,0:T(8,128)S(1)}, bf16[4,5,32,256]{3,2,1,0:T(8,128)(2,1)S(1)}, bf16[4,5,32,256]{3,2,1,0:T(8,128)(2,1)S(1)}, f32[40,256]{1,0:T(8,128)S(1)}, f32[40,256]{1,0:T(8,128)S(1)}) custom-call(s32[2]{0:T(128)S(1)} %pad_add_fusion.ids_ref, f32[4,5,2,32,256]{4,3,2,1,0:T(8,128)S(1)} %first_local.1.refs_0_, ...), custom_call_target="tpu_custom_call" | custom-call | flops 10000000 | bytes 5783560 | tf_op jit(solution)/shard_map/first_finish/pallas_call | solution.py:31
  20.8 3.6 %collective-permute-start.8 = (bf16[4,5,32,256]{3,2,1,0:T(8,128)(2,1)S(1)}, bf16[4,5,32,256]{3,2,1,0:T(8,128)(2,1)S(1)}, u32[]{:S(2)}, u32[]{:S(2)}) collective-permute-start(bf16[4,5,32,256]{3,2,1,0:T(8,128)(2,1)S(1)} %get-tuple-element.20), channel_id=1, source_target_pairs={{0,2},{2,0},{4,6},{6,4},{1,3},{3,1},{5,7},{7,5},{8,10},{10,8},{12,... | collective-permute-start | bytes 983048 | tf_op jit(solution)/shard_map/halos/ppermute | solution.py:390
  24.4 0.7 %collective-permute-start.9 = (bf16[4,5,32,256]{3,2,1,0:T(8,128)(2,1)S(1)}, bf16[4,5,32,256]{3,2,1,0:T(8,128)(2,1)S(1)}, u32[]{:S(2)}, u32[]{:S(2)}) collective-permute-start(bf16[4,5,32,256]{3,2,1,0:T(8,128)(2,1)S(1)} %get-tuple-element.21), channel_id=1, source_target_pairs={{2,4},{4,2},{3,5},{5,3},{10,12},{12,10},{11,13},{13,11},{18,20},{2... | collective-permute-start | bytes 983048 | tf_op jit(solution)/shard_map/halos/ppermute | solution.py:391
  25.1 3.3 %collective-permute-start.6 = (f32[40,256]{1,0:T(8,128)S(1)}, f32[40,256]{1,0:T(8,128)S(1)}, u32[]{:S(2)}, u32[]{:S(2)}) collective-permute-start(f32[40,256]{1,0:T(8,128)S(1)} %get-tuple-element.18), channel_id=1, source_target_pairs={{8,16},{24,32},{40,48},{56,64},{72,80},{88,96},{104,112},{120,128}... | collective-permute-start | bytes 122888 | tf_op jit(solution)/shard_map/halos/ppermute | solution.py:388
  28.4 0.0 collective-permute-start.7
  28.4 0.0 copy-done.7
  28.4 0.0 copy-done.8
  28.4 1.0 %order.1.refs_6_ = f32[20,512]{1,0:T(8,128)S(1)} custom-call(s32[2]{0:T(128)S(1)} %pad_add_fusion.ids_ref, s32[1,1024]{1,0:T(1,128)S(1)} %copy-done.8, f32[5,4,1024]{2,1,0:T(4,128)S(1)} %bitcast.4), custom_call_target="tpu_custom_call" | custom-call | flops 1000000 | bytes 126984 | tf_op jit(solution)/shard_map/order/pallas_call | solution.py:31
  29.4 1.9 %collective-permute-done.6.refs_5_ = f32[40,256]{1,0:T(8,128)S(1)} collective-permute-done((f32[40,256]{1,0:T(8,128)S(1)}, f32[40,256]{1,0:T(8,128)S(1)}, u32[]{:S(2)}, u32[]{:S(2)}) %collective-permute-start.6) | collective-permute-done | bytes 40992 | tf_op jit(solution)/shard_map/halos/ppermute | solution.py:388
  31.4 0.2 collective-permute-done.7.refs_6_
  31.6 2.4 %second_local.1.refs_0_ = f32[4,5,2,32,256]{4,3,2,1,0:T(8,128)S(1)} custom-call(s32[2]{0:T(128)S(1)} %pad_add_fusion.ids_ref, f32[4,5,2,32,256]{4,3,2,1,0:T(8,128)S(1)} %get-tuple-element.17.refs_0_, f32[4,5,2,32,256]{4,3,2,1,0:T(8,128)S(1)} %rhs.1.refs_1_, bf16[2,5,5,2,32,256]{5,4,3,2,1,0:T(8,128)(2,1)S(1)} %copy-done, f32[2,32,256]{2,1,0:T(8,128)S(1)} %copy-done.2, ...), custom_call_target="tpu_custom_call" | custom-call | flops 20000000 | bytes 5783560 | tf_op jit(solution)/shard_map/second_local/pallas_call | solution.py:31
  34.0 0.0 collective-permute-done.8.refs_4_
  34.0 0.0 collective-permute-done.9.refs_5_
  34.0 1.5 %surface.1 = f32[64,4,128]{2,1,0:T(4,128)} custom-call(s32[2]{0:T(128)S(1)} %pad_add_fusion.ids_ref, f32[4,5,2,32,256]{4,3,2,1,0:T(8,128)S(1)} %second_local.1.refs_0_, bf16[2,5,5,2,32,256]{5,4,3,2,1,0:T(8,128)(2,1)S(1)} %copy-done, f32[2,32,256]{2,1,0:T(8,128)S(1)} %copy-done.2, f32[2,32,256]{2,1,0:T(8,128)S(1)} %copy-done.3, ...), custom_call_target="tpu_custom_call" | custom-call | flops 5000000 | bytes 3907592 | tf_op jit(solution)/shard_map/surface/pallas_call | solution.py:31
  35.5 0.0 copy-start.5
  35.5 0.7 %copy-done.5 = bf16[4,5,32,256]{3,2,1,0:T(8,128)(2,1)} copy-done((bf16[4,5,32,256]{3,2,1,0:T(8,128)(2,1)}, bf16[4,5,32,256]{3,2,1,0:T(8,128)(2,1)S(1)}, u32[]{:S(2)}) %copy-start.5) | copy-done | bytes 327704
  36.2 8.7 %all-to-all-start = ((f32[64,4,128]{2,1,0:T(4,128)}), f32[64,4,128]{2,1,0:T(4,128)S(1)}, u32[]{:S(2)}, u32[]{:S(2)}) async-start(f32[64,4,128]{2,1,0:T(4,128)} %surface.1), calls=%async_computation | async-start | bytes 262144 | tf_op jit(solution)/shard_map/share_sensitivities/all_to_all | solution.py:449
  44.9 0.0 copy-start.6
  44.9 1.0 %copy-done.6 = bf16[4,5,32,256]{3,2,1,0:T(8,128)(2,1)S(1)} copy-done((bf16[4,5,32,256]{3,2,1,0:T(8,128)(2,1)S(1)}, bf16[4,5,32,256]{3,2,1,0:T(8,128)(2,1)}, u32[]{:S(2)}) %copy-start.6) | copy-done | bytes 327704
  45.9 2.1 %second_finish.1 = (f32[4,5,2,32,256]{4,3,2,1,0:T(8,128)}, f32[8,128]{1,0:T(8,128)S(1)}) custom-call(s32[2]{0:T(128)S(1)} %pad_add_fusion.ids_ref, f32[4,5,2,32,256]{4,3,2,1,0:T(8,128)S(1)} %second_local.1.refs_0_, bf16[2,5,5,2,32,256]{5,4,3,2,1,0:T(8,128)(2,1)S(1)} %copy-done, f32[2,32,256]{2,1,0:T(8,128)S(1)} %copy-done.2, f32[2,32,256]{2,1,0:T(8,128)S(1)} %copy-done.3, ...), custom_call_target="tpu_custom_call" | custom-call | flops 10000000 | bytes 5050376 | tf_op jit(solution)/shard_map/second_finish/pallas_call | solution.py:31
  48.0 8.0 %all-to-all-done.sens_ref = f32[64,4,128]{2,1,0:T(4,128)S(1)} async-done(((f32[64,4,128]{2,1,0:T(4,128)}), f32[64,4,128]{2,1,0:T(4,128)S(1)}, u32[]{:S(2)}, u32[]{:S(2)}) %all-to-all-start) | async-done | bytes 131104 | tf_op jit(solution)/shard_map/share_sensitivities/all_to_all | solution.py:449
  56.0 1.5 %modes.1 = f32[32,1024]{1,0:T(8,128)} custom-call(s32[1,1024]{1,0:T(1,128)S(1)} %copy-done.8, f32[64,4,128]{2,1,0:T(4,128)S(1)} %all-to-all-done.sens_ref, f32[8,128]{1,0:T(8,128)S(1)} %get-tuple-element.23.done_ref), custom_call_target="tpu_custom_call" | custom-call | flops 10000000 | bytes 270336 | tf_op jit(solution)/shard_map/modes/pallas_call | solution.py:31
Async XLA Ops:
  0.7 1.3 %copy-start.1 = (f32[4,5,2,32,256]{4,3,2,1,0:T(8,128)S(1)}, f32[4,5,2,32,256]{4,3,2,1,0:T(8,128)}, u32[]{:S(2)}) copy-start(f32[4,5,2,32,256]{4,3,2,1,0:T(8,128)} %refs_0_.1) | copy-start | bytes 3932164
  2.0 12.3 %copy-start.4 = (f32[4,5,2,32,256]{4,3,2,1,0:T(8,128)S(1)}, f32[4,5,2,32,256]{4,3,2,1,0:T(8,128)}, u32[]{:S(2)}) copy-start(f32[4,5,2,32,256]{4,3,2,1,0:T(8,128)} %src_ref.1) | copy-start | bytes 3932164
  2.7 11.5 %collective-permute-start = (bf16[4,5,32,256]{3,2,1,0:T(8,128)(2,1)S(1)}, bf16[4,5,32,256]{3,2,1,0:T(8,128)(2,1)S(1)}, u32[]{:S(2)}, u32[]{:S(2)}) collective-permute-start(bf16[4,5,32,256]{3,2,1,0:T(8,128)(2,1)S(1)} %get-tuple-element.13), channel_id=1, source_target_pairs={{0,1},{1,0},{2,3},{3,2},{4,5},{5,4},{6,7},{7,6},{8,9},{9,8},{10,11... | collective-permute-start | bytes 983048 | tf_op jit(solution)/shard_map/other_times/ppermute | solution.py:398
  6.0 8.3 %collective-permute-start.1 = (bf16[4,5,32,256]{3,2,1,0:T(8,128)(2,1)S(1)}, bf16[4,5,32,256]{3,2,1,0:T(8,128)(2,1)S(1)}, u32[]{:S(2)}, u32[]{:S(2)}) collective-permute-start(bf16[4,5,32,256]{3,2,1,0:T(8,128)(2,1)S(1)} %get-tuple-element.14), channel_id=1, source_target_pairs={{0,1},{1,0},{2,3},{3,2},{4,5},{5,4},{6,7},{7,6},{8,9},{9,8},{10,11... | collective-permute-start | bytes 983048 | tf_op jit(solution)/shard_map/other_times/ppermute | solution.py:399
  6.1 13.5 %collective-permute-start.4 = (bf16[4,5,32,256]{3,2,1,0:T(8,128)(2,1)S(1)}, bf16[4,5,32,256]{3,2,1,0:T(8,128)(2,1)S(1)}, u32[]{:S(2)}, u32[]{:S(2)}) collective-permute-start(bf16[4,5,32,256]{3,2,1,0:T(8,128)(2,1)S(1)} %get-tuple-element.13), channel_id=1, source_target_pairs={{0,2},{2,0},{4,6},{6,4},{1,3},{3,1},{5,7},{7,5},{8,10},{10,8},{12,... | collective-permute-start | bytes 983048 | tf_op jit(solution)/shard_map/halos/ppermute | solution.py:390
  6.1 13.5 %collective-permute-start.5 = (bf16[4,5,32,256]{3,2,1,0:T(8,128)(2,1)S(1)}, bf16[4,5,32,256]{3,2,1,0:T(8,128)(2,1)S(1)}, u32[]{:S(2)}, u32[]{:S(2)}) collective-permute-start(bf16[4,5,32,256]{3,2,1,0:T(8,128)(2,1)S(1)} %get-tuple-element.14), channel_id=1, source_target_pairs={{2,4},{4,2},{3,5},{5,3},{10,12},{12,10},{11,13},{13,11},{18,20},{2... | collective-permute-start | bytes 983048 | tf_op jit(solution)/shard_map/halos/ppermute | solution.py:391
  6.8 8.8 %collective-permute-start.2 = (f32[40,256]{1,0:T(8,128)S(1)}, f32[40,256]{1,0:T(8,128)S(1)}, u32[]{:S(2)}, u32[]{:S(2)}) collective-permute-start(f32[40,256]{1,0:T(8,128)S(1)} %get-tuple-element.15), channel_id=1, source_target_pairs={{8,16},{24,32},{40,48},{56,64},{72,80},{88,96},{104,112},{120,128}... | collective-permute-start | bytes 122888 | tf_op jit(solution)/shard_map/halos/ppermute | solution.py:388
  14.2 3.0 %copy-start = (bf16[2,5,5,2,32,256]{5,4,3,2,1,0:T(8,128)(2,1)S(1)}, bf16[2,5,5,2,32,256]{5,4,3,2,1,0:T(8,128)(2,1)}, u32[]{:S(2)}) copy-start(bf16[2,5,5,2,32,256]{5,4,3,2,1,0:T(8,128)(2,1)} %refs_1_.5) | copy-start | bytes 4915204
  14.2 3.0 %copy-start.2 = (f32[2,32,256]{2,1,0:T(8,128)S(1)}, f32[2,32,256]{2,1,0:T(8,128)}, u32[]{:S(2)}) copy-start(f32[2,32,256]{2,1,0:T(8,128)} %refs_2_.9) | copy-start | bytes 196612
  14.2 3.0 %copy-start.3 = (f32[2,32,256]{2,1,0:T(8,128)S(1)}, f32[2,32,256]{2,1,0:T(8,128)}, u32[]{:S(2)}) copy-start(f32[2,32,256]{2,1,0:T(8,128)} %refs_3_.9) | copy-start | bytes 196612
  14.2 2.9 %collective-permute-start.3 = (f32[40,256]{1,0:T(8,128)S(1)}, f32[40,256]{1,0:T(8,128)S(1)}, u32[]{:S(2)}, u32[]{:S(2)}) collective-permute-start(f32[40,256]{1,0:T(8,128)S(1)} %get-tuple-element.16), channel_id=1, source_target_pairs={{0,8},{8,0},{16,24},{24,16},{32,40},{40,32},{48,56},{56,48},{64,72... | collective-permute-start | bytes 122888 | tf_op jit(solution)/shard_map/halos/ppermute | solution.py:389
  19.6 8.8 %copy-start.7 = (f32[4,5,1024]{2,0,1:T(4,128)S(1)}, f32[4,5,1024]{2,0,1:T(4,128)}, u32[]{:S(2)}) copy-start(f32[4,5,1024]{2,0,1:T(4,128)} %param.13) | copy-start | bytes 245764
  19.6 8.8 %copy-start.8 = (s32[1,1024]{1,0:T(1,128)S(1)}, s32[1,1024]{1,0:T(1,128)}, u32[]{:S(2)}) copy-start(s32[1,1024]{1,0:T(1,128)} %cells_ref.3) | copy-start | bytes 12292
  20.8 13.1 %collective-permute-start.8 = (bf16[4,5,32,256]{3,2,1,0:T(8,128)(2,1)S(1)}, bf16[4,5,32,256]{3,2,1,0:T(8,128)(2,1)S(1)}, u32[]{:S(2)}, u32[]{:S(2)}) collective-permute-start(bf16[4,5,32,256]{3,2,1,0:T(8,128)(2,1)S(1)} %get-tuple-element.20), channel_id=1, source_target_pairs={{0,2},{2,0},{4,6},{6,4},{1,3},{3,1},{5,7},{7,5},{8,10},{10,8},{12,... | collective-permute-start | bytes 983048 | tf_op jit(solution)/shard_map/halos/ppermute | solution.py:390
  24.4 9.5 %collective-permute-start.9 = (bf16[4,5,32,256]{3,2,1,0:T(8,128)(2,1)S(1)}, bf16[4,5,32,256]{3,2,1,0:T(8,128)(2,1)S(1)}, u32[]{:S(2)}, u32[]{:S(2)}) collective-permute-start(bf16[4,5,32,256]{3,2,1,0:T(8,128)(2,1)S(1)} %get-tuple-element.21), channel_id=1, source_target_pairs={{2,4},{4,2},{3,5},{5,3},{10,12},{12,10},{11,13},{13,11},{18,20},{2... | collective-permute-start | bytes 983048 | tf_op jit(solution)/shard_map/halos/ppermute | solution.py:391
  25.1 6.3 %collective-permute-start.6 = (f32[40,256]{1,0:T(8,128)S(1)}, f32[40,256]{1,0:T(8,128)S(1)}, u32[]{:S(2)}, u32[]{:S(2)}) collective-permute-start(f32[40,256]{1,0:T(8,128)S(1)} %get-tuple-element.18), channel_id=1, source_target_pairs={{8,16},{24,32},{40,48},{56,64},{72,80},{88,96},{104,112},{120,128}... | collective-permute-start | bytes 122888 | tf_op jit(solution)/shard_map/halos/ppermute | solution.py:388
  28.4 3.1 %collective-permute-start.7 = (f32[40,256]{1,0:T(8,128)S(1)}, f32[40,256]{1,0:T(8,128)S(1)}, u32[]{:S(2)}, u32[]{:S(2)}) collective-permute-start(f32[40,256]{1,0:T(8,128)S(1)} %get-tuple-element.19), channel_id=1, source_target_pairs={{0,8},{8,0},{16,24},{24,16},{32,40},{40,32},{48,56},{56,48},{64,72... | collective-permute-start | bytes 122888 | tf_op jit(solution)/shard_map/halos/ppermute | solution.py:389
  35.5 0.7 %copy-start.5 = (bf16[4,5,32,256]{3,2,1,0:T(8,128)(2,1)}, bf16[4,5,32,256]{3,2,1,0:T(8,128)(2,1)S(1)}, u32[]{:S(2)}) copy-start(bf16[4,5,32,256]{3,2,1,0:T(8,128)(2,1)S(1)} %collective-permute-done.9.refs_5_) | copy-start | bytes 983044
  36.2 19.8 %all-to-all-start = ((f32[64,4,128]{2,1,0:T(4,128)}), f32[64,4,128]{2,1,0:T(4,128)S(1)}, u32[]{:S(2)}, u32[]{:S(2)}) async-start(f32[64,4,128]{2,1,0:T(4,128)} %surface.1), calls=%async_computation | async-start | bytes 262144 | tf_op jit(solution)/shard_map/share_sensitivities/all_to_all | solution.py:449
  44.9 1.0 %copy-start.6 = (bf16[4,5,32,256]{3,2,1,0:T(8,128)(2,1)S(1)}, bf16[4,5,32,256]{3,2,1,0:T(8,128)(2,1)}, u32[]{:S(2)}) copy-start(bf16[4,5,32,256]{3,2,1,0:T(8,128)(2,1)} %copy-done.5) | copy-start | bytes 983044

commit v5 on v4

--- a/solution.py
+++ b/solution.py
@@ -110,23 +110,20 @@
     by_parity(ids_ref, run)
 
 
-def shifted(f_ref, t, u, i, j, lanes, edges, rows_id):
+def shifted(f_ref, t, u, i, j, lanes, rows_id):
     nj = f_ref.shape[3]
     here = f_ref[t, u, i, j : j + 8, lanes]
+    after = before = jnp.zeros_like(here)
     if j + 8 < nj:
         after = pltpu.roll(f_ref[t, u, i, j + 8 : j + 16, lanes], 7, 0)
-    else:
-        after = edges(t, u, i, True)
     if j > 0:
         before = pltpu.roll(f_ref[t, u, i, j - 8 : j, lanes], 1, 0)
-    else:
-        before = edges(t, u, i, False)
     plus = jnp.where(rows_id == 7, after, pltpu.roll(here, 7, 0))
     minus = jnp.where(rows_id == 0, before, pltpu.roll(here, 1, 0))
     return here, plus, minus
 
 
-def local_tile(refs, edges, i, j, lanes):
+def local_tile(refs, i, j, lanes):
     f_ref, rhs_ref, jac_ref, sig_ref, dmp_ref = refs
     nt, nv, ni = f_ref.shape[:3]
     pair = slice(j // 16 * 16, j // 16 * 16 + 16)
@@ -142,7 +139,7 @@
             for d in range(2)
         ]
         for t in range(nt):
-            here, plus_j, minus_j = shifted(f_ref, t, u, i, j, lanes, edges, rows_id)
+            here, plus_j, minus_j = shifted(f_ref, t, u, i, j, lanes, rows_id)
             inner = f_ref[t, u, 1 - i, j : j + 8, lanes]
             diff_i = here if i else here - inner
             diff_j = here - plus_j
@@ -163,32 +160,53 @@
     ]
 
 
-def finish_tile(refs, layer_ref, i, j, lanes):
-    part_ref, jac_ref, sig_ref, dmp_ref = refs
-    nt, nv = part_ref.shape[:2]
+def finish_tile(upper, refs, layer_ref, i, j, lanes):
+    part_ref, jac_i_ref, jac_j_ref, sig_ref, dmp_ref, outer_ref, inner_ref = refs
+    nt, nv, ni, nj, nk = part_ref.shape
     pair = slice(j // 16 * 16, j // 16 * 16 + 16)
     half = slice(j % 16, j % 16 + 8)
     sigma = sig_ref[i, j : j + 8, lanes]
     damping = dmp_ref[i, j : j + 8, lanes]
     scaling = 1.0 / (sigma + 4.0 * damping)
     damping = damping * scaling
-    acc = [[None] * nv for _ in range(nt)]
+    first, last = j == 0, j == nj - 8
+    rows_id = lax.broadcasted_iota(jnp.int32, sigma.shape, 0)
+    acc = [[0.0] * nv for _ in range(nt)]
+
+    def edge(t, u, high):
+        row = (t * nv + u) * ni + i
+        outer = outer_ref[row : row + 1, lanes]
+        inner = inner_ref[row : row + 1, lanes]
+        value = jnp.where(upper == high, outer, inner)
+        mask = rows_id == (7 if high else 0)
+        return jnp.where(mask, jnp.broadcast_to(value, sigma.shape), 0.0)
+
     for u in range(nv):
-        jac = (
-            [
-                jac_ref[0, u, v, i, pair, lanes].astype(F32)[half] * scaling
+        jac_i = jac_j = None
+        if i > 0:
+            jac_i = [
+                jac_i_ref[u, v, pair, lanes].astype(F32)[half] * scaling
                 for v in range(nv)
             ]
-            if i
-            else None
-        )
+        if last:
+            jac_j = [
+                jac_j_ref[u, v, i, :, lanes].astype(F32)[8:] * scaling
+                for v in range(nv)
+            ]
         for t in range(nt):
             layer = layer_ref[t, u, pair, lanes].astype(F32)[half]
-            for v in range(nv) if i else (u,):
-                term = jac[v] * layer if i else damping * layer
-                if i and v == u:
-                    term = term + damping * layer
-                acc[t][v] = term if acc[t][v] is None else acc[t][v] + term
+            near = layer
+            if first:
+                near = near + edge(t, u, False)
+            if last:
+                high = edge(t, u, True)
+                near = near + high
+            acc[t][u] = acc[t][u] + damping * near
+            for v in range(nv):
+                if jac_i is not None:
+                    acc[t][v] = acc[t][v] + jac_i[v] * layer
+                if jac_j is not None:
+                    acc[t][v] = acc[t][v] + jac_j[v] * high
     return [
         [part_ref[t, v, i, j : j + 8, lanes] + acc[t][v] for v in range(nv)]
         for t in range(nt)
@@ -199,24 +217,15 @@
     return pl.ds(pl.multiple_of(k * 128, 128), 128)
 
 
-def local_kernel(ids_ref, *refs):
-    ins, outer_ref, inner_ref, out_ref = refs[:5], *refs[5:8]
+def local_kernel(*refs):
+    ins, out_ref = refs[:5], refs[5]
     nt, nv, ni, nj, nk = out_ref.shape
-    upper = ids_ref[1] == 1
 
     def one(k, carry):
         lanes = lanes_at(k)
-
-        def edges(t, u, i, high):
-            row = (t * nv + u) * ni + i
-            outer = outer_ref[row : row + 1, lanes]
-            inner = inner_ref[row : row + 1, lanes]
-            edge = jnp.where(upper == high, outer, inner)
-            return jnp.broadcast_to(edge, (8, 128))
-
         for i in range(ni):
             for j in range(0, nj, 8):
-                new = local_tile(ins, edges, i, j, lanes)
+                new = local_tile(ins, i, j, lanes)
                 for t in range(nt):
                     for v in range(nv):
                         out_ref[t, v, i, j : j + 8, lanes] = new[t][v]
@@ -225,14 +234,15 @@
     lax.fori_loop(0, nk // 128, one, 0)
 
 
-def finish_all(ins, out_ref, layers):
+def finish_all(ids_ref, ins, out_ref, layers):
     nt, nv, ni, nj, nk = out_ref.shape
+    upper = ids_ref[1] == 1
 
     def one(k, carry):
         lanes = lanes_at(k)
         for i in range(ni):
             for j in range(0, nj, 8):
-                new = finish_tile(ins, layers[i], i, j, lanes)
+                new = finish_tile(upper, ins, layers[i], i, j, lanes)
                 for t in range(nt):
                     for v in range(nv):
                         out_ref[t, v, i, j : j + 8, lanes] = new[t][v]
@@ -242,11 +252,11 @@
 
 
 def first_kernel(ids_ref, *refs):
-    ins, ha_ref, hb_ref = refs[:4], refs[4], refs[5]
-    out_ref, a_ref, b_ref, no_ref, ni_ref = refs[6:]
+    ins, ha_ref, hb_ref = refs[:7], refs[7], refs[8]
+    out_ref, a_ref, b_ref, no_ref, ni_ref = refs[9:]
 
     def run(layer_a, layer_b):
-        finish_all(ins, out_ref, {layer_a: ha_ref, layer_b: hb_ref})
+        finish_all(ids_ref, ins, out_ref, {layer_a: ha_ref, layer_b: hb_ref})
         pack_layers(out_ref, a_ref, b_ref, layer_a, layer_b)
 
     by_parity(ids_ref, run)
@@ -254,31 +264,28 @@
 
 
 def surface_kernel(ids_ref, *refs):
-    ins, ha_ref, hb_ref, w_ref, sens_ref = refs[:4], *refs[4:8]
+    ins, ha_ref, hb_ref, w_ref, sens_ref = refs[:7], *refs[7:11]
     nt, nv, ni, nj, nk = ins[0].shape
 
     def row_of(side, layers):
         j = side * (nj - 8)
         mask = lax.broadcasted_iota(jnp.int32, (8, 128), 0) == side * 7
-
-        def one(k, carry):
-            lanes = lanes_at(k)
-            for i in range(ni):
-                new = finish_tile(ins, layers[i], i, j, lanes)
+        values = []
+        for i in range(ni):
+            for k in range(0, nk, 128):
+                new = finish_tile(side == 1, ins, layers[i], i, j, slice(k, k + 128))
                 total = jnp.zeros((8, 128), F32)
                 for t in range(nt):
                     for v in range(nv):
                         at = t * nv + v
-                        start = pl.multiple_of(i * nk + k * 128, 128)
-                        weight = w_ref[at : at + 1, pl.ds(start, 128)]
+                        weight = w_ref[at : at + 1, i * nk + k : i * nk + k + 128]
                         total = total + new[t][v] * weight
-                value = jnp.sum(jnp.where(mask, total, 0.0), axis=0, keepdims=True)
-                sens_ref[:, pl.ds(i * (nk // 128) + k, 1), :] = jnp.broadcast_to(
-                    value[None], (sens_ref.shape[0], 1, 128)
+                values.append(
+                    jnp.sum(jnp.where(mask, total, 0.0), axis=0, keepdims=True)
                 )
-            return carry
-
-        lax.fori_loop(0, nk // 128, one, 0)
+        value = jnp.concatenate(values, axis=0)
+        for member in range(sens_ref.shape[0]):
+            sens_ref[member] = value
 
     def run(layer_a, layer_b):
         layers = {layer_a: ha_ref, layer_b: hb_ref}
@@ -289,11 +296,11 @@
 
 
 def second_kernel(ids_ref, *refs):
-    ins, ha_ref, hb_ref, out_ref, done_ref = refs[:4], *refs[4:8]
+    ins, ha_ref, hb_ref, out_ref, done_ref = refs[:7], *refs[7:11]
     done_ref[...] = jnp.zeros(done_ref.shape, F32)
 
     def run(layer_a, layer_b):
-        finish_all(ins, out_ref, {layer_a: ha_ref, layer_b: hb_ref})
+        finish_all(ids_ref, ins, out_ref, {layer_a: ha_ref, layer_b: hb_ref})
 
     by_parity(ids_ref, run)
 
@@ -338,29 +345,32 @@
     return jnp.where((sender // 2) % 2 == side, value, 0.0)
 
 
-def modes_kernel(cells_ref, sens_ref, done_ref, out_ref):
+def tables_kernel(cells_ref, done_ref, chosen_ref, table_ref):
+    chosen_ref[...] = one_hot(cells_ref, 0, chosen_ref.shape[0])
+    rows, senders = table_ref.shape
+    for side in range(2):
+        here = slice(side * rows // 2, (side + 1) * rows // 2)
+        table_ref[here, :] = mode_table(side, rows // 4, senders)
+
+
+def modes_kernel(chosen_ref, table_ref, sens_ref, out_ref):
     senders, pieces = sens_ref.shape[:2]
     half = pieces * 128
     rows = out_ref.shape[0]
-    table = jnp.concatenate(
-        [mode_table(side, rows // 2, senders) for side in range(2)], axis=0
-    )
     seen = jnp.concatenate([sens_ref[:, c, :] for c in range(pieces)], axis=1)
     both = jnp.dot(
-        table,
+        table_ref[...],
         seen,
         precision=lax.Precision.HIGHEST,
         preferred_element_type=F32,
     )
-    total = None
-    for side in range(2):
-        modes = both[side * rows : (side + 1) * rows]
-        parts = jnp.concatenate(split3(modes), axis=0)
-        chosen = one_hot(cells_ref, side * half, half)
-        found = jnp.dot(parts, chosen, preferred_element_type=F32)
-        found = found[:rows] + (found[rows : 2 * rows] + found[2 * rows :])
-        total = found if total is None else total + found
-    out_ref[...] = total
+    modes = jnp.concatenate([both[:rows], both[rows:]], axis=1)
+    found = jnp.dot(
+        jnp.concatenate(split3(modes), axis=0),
+        chosen_ref[...],
+        preferred_element_type=F32,
+    )
+    out_ref[...] = found[:rows] + (found[rows : 2 * rows] + found[2 * rows :])
 
 
 def body(start, source, jac, sigma, damping, cells, weights):
@@ -397,7 +407,7 @@
     with jax.named_scope("other_times"):
         pa = lax.ppermute(packed[0], "tm", swap)
         pb = lax.ppermute(packed[1], "tm", swap)
-    outer, inner, ha, hb = exchange(*packed)
+    halos = exchange(*packed)
     rhs = call(
         rhs_kernel,
         [field_like],
@@ -416,50 +426,53 @@
         10**6,
         "order",
     )[0]
-    fixed = (jac, sigma, damping)
-
-    def local(field, outer, inner, name):
-        args = (ids, field, rhs, *fixed, outer, inner)
-        specs = [SMEM] + [VMEM] * 7
-        return call(local_kernel, [field_like], args, specs, 4, 2 * 10**7, name)[0]
-
-    part = local(start, outer, inner, "first_local")
-    field, *packed = call(
+    def local(field, name):
+        args = (field, rhs, jac, sigma, damping)
+        return call(local_kernel, [field_like], args, [VMEM] * 5, 4, 2 * 10**7, name)[0]
+
+    jac_i = jac[0, :, :, ni - 1]
+    jac_j = jac[1, :, :, :, nj - 16 :]
+
+    def finish(kernel, outs, part, halos, more, name):
+        outer, inner, ha, hb = halos
+        args = (ids, part, jac_i, jac_j, sigma, damping, outer, inner, ha, hb, *more)
+        specs = [SMEM] + [VMEM] * (len(args) - 1)
+        return call(kernel, outs, args, specs, 4, 10**7, name)
+
+    field, *packed = finish(
         first_kernel,
         [field_like] + sends,
-        (ids, part, *fixed, ha, hb),
-        [SMEM] + [VMEM] * 6,
-        4,
-        10**7,
+        local(start, "first_local"),
+        halos,
+        (),
         "first_finish",
     )
-    outer, inner, ha, hb = exchange(*packed)
-    part = local(field, outer, inner, "second_local")
-    sens = call(
-        surface_kernel,
-        [jax.ShapeDtypeStruct((2 * ring, ni * nk // 128, 128), F32)],
-        (ids, part, *fixed, ha, hb, ordered),
-        [SMEM] + [VMEM] * 7,
-        4,
-        5 * 10**6,
-        "surface",
-    )[0]
-    token_like = jax.ShapeDtypeStruct((8, 128), F32)
+    halos = exchange(*packed)
+    part = local(field, "second_local")
+    share_like = jax.ShapeDtypeStruct((2 * ring, ni * nk // 128, 128), F32)
+    sens = finish(surface_kernel, [share_like], part, halos, (ordered,), "surface")[0]
     with jax.named_scope("share_sensitivities"):
         gathered = lax.all_to_all(sens, ("passage", "tm"), 0, 0, tiled=True)
-    field, done = call(
-        second_kernel,
-        [field_like, token_like],
-        (ids, part, *fixed, ha, hb),
-        [SMEM] + [VMEM] * 6,
-        4,
-        10**7,
-        "second_finish",
+    token_like = jax.ShapeDtypeStruct((8, 128), F32)
+    field, done = finish(
+        second_kernel, [field_like, token_like], part, halos, (), "second_finish"
+    )
+    chosen, table = call(
+        tables_kernel,
+        [
+            jax.ShapeDtypeStruct((cells.shape[1], cells.shape[1]), BF16),
+            jax.ShapeDtypeStruct((4 * PASSAGES, 2 * ring), F32),
+        ],
+        (cells, done),
+        [VMEM] * 2,
+        8,
+        10**6,
+        "tables",
     )
     modes = call(
         modes_kernel,
         [jax.ShapeDtypeStruct((2 * PASSAGES, cells.shape[1]), F32)],
-        (cells, gathered, done),
+        (chosen, table, gathered),
         [VMEM] * 3,
         8,
         10**7,

time: 57.8 us -> 55.2 us (0.955)
  the two profiles are of different devices: /device:TPU:1 before, /device:TPU:8 now
where the time goes in v5:
time: 55.2 us; the launch traced here: 54.6 us
  starting transfers between devices  26.3 us (48%)
  Pallas kernels  13.2 us (24%)
  waiting for transfers between devices  10.5 us (19%)
  local copies, waits for them, and re-layouts  3.69 us (7%)
  between operations  0.84 us (2%)
    pallas_call x10, Pallas kernels, call(): pl.pallas_call(kernel, out_shape=outs, in_specs=specs, out_specs=[VMEM] *...  13.2 us
    ppermute x2, starting transfers between devices, exchange(): lax.ppermute(outer, 'passage', across)  12.6 us
    all_to_all x1, waiting for transfers between devices, body(): gathered = lax.all_to_all(sens, ('passage', 'tm'), 0, 0, tiled=True)  8.29 us
    all_to_all x1, starting transfers between devices, body(): gathered = lax.all_to_all(sens, ('passage', 'tm'), 0, 0, tiled=True)  6.52 us
    ppermute x2, starting transfers between devices, exchange(): lax.ppermute(b, 'cell', odd)  4.5 us
    ppermute x2, starting transfers between devices, exchange(): lax.ppermute(a, 'cell', even)  2.37 us
    unnamed x16, local copies, waits for them, and re-layouts  1.61 us
  transfers between devices with their start and end apart: 11, of which 4 were waited for; matrix products, arithmetic and copies ran while one was open for 4% of the time, Pallas kernels for 15%

profile of v5, /device:TPU:8, one launch (start us, length us, event | category | flops | bytes accessed | tf_op | source)
XLA Modules:
  0.0 54.6 jit_solution(15125925314538732197)
XLA Ops:
  0.6 0.1 pad_add_fusion.ids_ref
  0.7 0.0 copy-start
  0.7 1.3 %copy-done = f32[4,5,2,32,256]{4,3,2,1,0:T(8,128)S(1)} copy-done((f32[4,5,2,32,256]{4,3,2,1,0:T(8,128)S(1)}, f32[4,5,2,32,256]{4,3,2,1,0:T(8,128)}, u32[]{:S(2)}) %copy-start) | copy-done | bytes 1310744
  2.0 0.0 copy-start.1
  2.0 0.0 copy-start.5
  2.0 0.7 %prepare.1 = (bf16[4,5,32,256]{3,2,1,0:T(8,128)(2,1)S(1)}, bf16[4,5,32,256]{3,2,1,0:T(8,128)(2,1)S(1)}, f32[40,256]{1,0:T(8,128)S(1)}, f32[40,256]{1,0:T(8,128)S(1)}) custom-call(s32[2]{0:T(128)S(1)} %pad_add_fusion.ids_ref, f32[4,5,2,32,256]{4,3,2,1,0:T(8,128)S(1)} %copy-done), custom_call_target="tpu_custom_call" | custom-call | flops 1000000 | bytes 2048008 | tf_op jit(solution)/shard_map/prepare/pallas_call | solution.py:31
  2.7 0.1 collective-permute-start
  2.8 2.3 %collective-permute-start.4 = (bf16[4,5,32,256]{3,2,1,0:T(8,128)(2,1)S(1)}, bf16[4,5,32,256]{3,2,1,0:T(8,128)(2,1)S(1)}, u32[]{:S(2)}, u32[]{:S(2)}) collective-permute-start(bf16[4,5,32,256]{3,2,1,0:T(8,128)(2,1)S(1)} %get-tuple-element.15), channel_id=1, source_target_pairs={{0,2},{2,0},{4,6},{6,4},{1,3},{3,1},{5,7},{7,5},{8,10},{10,8},{12,... | collective-permute-start | bytes 983048 | tf_op jit(solution)/shard_map/halos/ppermute | solution.py:400
  5.1 0.1 collective-permute-start.1
  5.2 2.6 %collective-permute-start.5 = (bf16[4,5,32,256]{3,2,1,0:T(8,128)(2,1)S(1)}, bf16[4,5,32,256]{3,2,1,0:T(8,128)(2,1)S(1)}, u32[]{:S(2)}, u32[]{:S(2)}) collective-permute-start(bf16[4,5,32,256]{3,2,1,0:T(8,128)(2,1)S(1)} %get-tuple-element.16), channel_id=1, source_target_pairs={{2,4},{4,2},{3,5},{5,3},{10,12},{12,10},{11,13},{13,11},{18,20},{2... | collective-permute-start | bytes 983048 | tf_op jit(solution)/shard_map/halos/ppermute | solution.py:401
  7.8 8.1 %collective-permute-start.2 = (f32[40,256]{1,0:T(8,128)S(1)}, f32[40,256]{1,0:T(8,128)S(1)}, u32[]{:S(2)}, u32[]{:S(2)}) collective-permute-start(f32[40,256]{1,0:T(8,128)S(1)} %get-tuple-element.17), channel_id=1, source_target_pairs={{8,16},{24,32},{40,48},{56,64},{72,80},{88,96},{104,112},{120,128}... | collective-permute-start | bytes 122888 | tf_op jit(solution)/shard_map/halos/ppermute | solution.py:398
  15.9 1.0 %slice_bitcast_fusion.refs_2_ = bf16[5,5,2,16,256]{4,3,2,1,0:T(8,128)(2,1)S(1)} fusion(bf16[2,5,5,2,32,256]{5,4,3,2,1,0:T(8,128)(2,1)} %refs_2_.3), kind=kLoop, calls=%fused_computation | loop fusion | bytes 819200 | tf_op jit(solution)/shard_map/squeeze | solution.py:434
  17.0 0.0 collective-permute-done.pa_ref
  17.0 0.1 collective-permute-start.3
  17.1 1.0 %slice_bitcast_fusion.1.refs_1_ = bf16[5,5,32,256]{3,2,1,0:T(8,128)(2,1)S(1)} fusion(bf16[2,5,5,2,32,256]{5,4,3,2,1,0:T(8,128)(2,1)} %refs_2_.3), kind=kLoop, calls=%fused_computation.1 | loop fusion | bytes 819200 | tf_op jit(solution)/shard_map/squeeze | solution.py:433
  18.1 0.0 copy-start.2
  18.2 0.0 copy-start.3
  18.2 0.0 copy-start.4
  18.2 0.0 collective-permute-done.1.pb_ref
  18.2 0.0 copy-done.1
  18.2 0.0 copy-done.5
  18.2 1.1 %rhs.1.refs_1_ = f32[4,5,2,32,256]{4,3,2,1,0:T(8,128)S(1)} custom-call(s32[2]{0:T(128)S(1)} %pad_add_fusion.ids_ref, f32[4,5,2,32,256]{4,3,2,1,0:T(8,128)S(1)} %copy-done.1, f32[4,5,2,32,256]{4,3,2,1,0:T(8,128)S(1)} %copy-done.5, bf16[4,5,32,256]{3,2,1,0:T(8,128)(2,1)S(1)} %collective-permute-done.pa_ref, ...), custom_call_target="tpu_custom_call" | custom-call | flops 10000000 | bytes 4587528 | tf_op jit(solution)/shard_map/rhs/pallas_call | solution.py:31
  19.3 0.3 copy-done.2
  19.6 0.0 copy-done.3
  19.6 0.0 copy-done.4
  19.6 1.8 %first_local.1.refs_0_ = f32[4,5,2,32,256]{4,3,2,1,0:T(8,128)S(1)} custom-call(f32[4,5,2,32,256]{4,3,2,1,0:T(8,128)S(1)} %copy-done.1, f32[4,5,2,32,256]{4,3,2,1,0:T(8,128)S(1)} %rhs.1.refs_1_, bf16[2,5,5,2,32,256]{5,4,3,2,1,0:T(8,128)(2,1)S(1)} %copy-done.2, f32[2,32,256]{2,1,0:T(8,128)S(1)} %copy-done.3, f32[2,32,256]{2,1,0:T(8,128)S(1)} %copy-done.4), custom_call_target="tpu_custom_call" | custom-call | flops 20000000 | bytes 5701632 | tf_op jit(solution)/shard_map/first_local/pallas_call | solution.py:31
  21.4 0.0 copy-start.6
  21.4 0.0 copy-start.7
  21.4 0.0 collective-permute-done.2.refs_5_
  21.4 0.0 collective-permute-done.3.refs_6_
  21.4 0.0 collective-permute-done.4.refs_7_
  21.4 0.0 collective-permute-done.5.refs_8_
  21.4 1.4 %first_finish.1 = (f32[4,5,2,32,256]{4,3,2,1,0:T(8,128)S(1)}, bf16[4,5,32,256]{3,2,1,0:T(8,128)(2,1)S(1)}, bf16[4,5,32,256]{3,2,1,0:T(8,128)(2,1)S(1)}, f32[40,256]{1,0:T(8,128)S(1)}, f32[40,256]{1,0:T(8,128)S(1)}) custom-call(s32[2]{0:T(128)S(1)} %pad_add_fusion.ids_ref, f32[4,5,2,32,256]{4,3,2,1,0:T(8,128)S(1)} %first_local.1.refs_0_, ...), custom_call_target="tpu_custom_call" | custom-call | flops 10000000 | bytes 5046280 | tf_op jit(solution)/shard_map/first_finish/pallas_call | solution.py:31
  22.8 0.1 collective-permute-start.8
  22.9 1.9 %collective-permute-start.9 = (bf16[4,5,32,256]{3,2,1,0:T(8,128)(2,1)S(1)}, bf16[4,5,32,256]{3,2,1,0:T(8,128)(2,1)S(1)}, u32[]{:S(2)}, u32[]{:S(2)}) collective-permute-start(bf16[4,5,32,256]{3,2,1,0:T(8,128)(2,1)S(1)} %get-tuple-element.23), channel_id=1, source_target_pairs={{2,4},{4,2},{3,5},{5,3},{10,12},{12,10},{11,13},{13,11},{18,20},{2... | collective-permute-start | bytes 983048 | tf_op jit(solution)/shard_map/halos/ppermute | solution.py:401
  24.8 4.4 %collective-permute-start.6 = (f32[40,256]{1,0:T(8,128)S(1)}, f32[40,256]{1,0:T(8,128)S(1)}, u32[]{:S(2)}, u32[]{:S(2)}) collective-permute-start(f32[40,256]{1,0:T(8,128)S(1)} %get-tuple-element.20), channel_id=1, source_target_pairs={{8,16},{24,32},{40,48},{56,64},{72,80},{88,96},{104,112},{120,128}... | collective-permute-start | bytes 122888 | tf_op jit(solution)/shard_map/halos/ppermute | solution.py:398
  29.3 0.0 collective-permute-start.7
  29.3 0.0 copy-done.6
  29.3 0.0 copy-done.7
  29.3 1.0 %order.1.refs_9_ = f32[20,512]{1,0:T(8,128)S(1)} custom-call(s32[2]{0:T(128)S(1)} %pad_add_fusion.ids_ref, s32[1,1024]{1,0:T(1,128)S(1)} %copy-done.7, f32[5,4,1024]{2,1,0:T(4,128)S(1)} %bitcast.10), custom_call_target="tpu_custom_call" | custom-call | flops 1000000 | bytes 126984 | tf_op jit(solution)/shard_map/order/pallas_call | solution.py:31
  30.3 1.8 %second_local.1.refs_0_ = f32[4,5,2,32,256]{4,3,2,1,0:T(8,128)S(1)} custom-call(f32[4,5,2,32,256]{4,3,2,1,0:T(8,128)S(1)} %get-tuple-element.19.refs_0_, f32[4,5,2,32,256]{4,3,2,1,0:T(8,128)S(1)} %rhs.1.refs_1_, bf16[2,5,5,2,32,256]{5,4,3,2,1,0:T(8,128)(2,1)S(1)} %copy-done.2, f32[2,32,256]{2,1,0:T(8,128)S(1)} %copy-done.3, f32[2,32,256]{2,1,0:T(8,128)S(1)} %copy-done.4), custom_call_target="tpu_custom_call" | custom-call | flops 20000000 | bytes 5701632 | tf_op jit(solution)/shard_map/second_local/pallas_call | solution.py:31
  32.1 0.2 collective-permute-done.6.refs_5_
  32.3 1.0 %collective-permute-done.7.refs_6_ = f32[40,256]{1,0:T(8,128)S(1)} collective-permute-done((f32[40,256]{1,0:T(8,128)S(1)}, f32[40,256]{1,0:T(8,128)S(1)}, u32[]{:S(2)}, u32[]{:S(2)}) %collective-permute-start.7) | collective-permute-done | bytes 40992 | tf_op jit(solution)/shard_map/halos/ppermute | solution.py:399
  33.3 0.0 collective-permute-done.8.refs_7_
  33.3 0.9 %collective-permute-done.9.refs_8_ = bf16[4,5,32,256]{3,2,1,0:T(8,128)(2,1)S(1)} collective-permute-done((bf16[4,5,32,256]{3,2,1,0:T(8,128)(2,1)S(1)}, bf16[4,5,32,256]{3,2,1,0:T(8,128)(2,1)S(1)}, u32[]{:S(2)}, u32[]{:S(2)}) %collective-permute-start.9) | collective-permute-done | bytes 327712 | tf_op jit(solution)/shard_map/halos/ppermute | solution.py:401
  34.2 1.4 %surface.1 = f32[64,4,128]{2,1,0:T(4,128)} custom-call(s32[2]{0:T(128)S(1)} %pad_add_fusion.ids_ref, f32[4,5,2,32,256]{4,3,2,1,0:T(8,128)S(1)} %second_local.1.refs_0_, bf16[5,5,32,256]{3,2,1,0:T(8,128)(2,1)S(1)} %slice_bitcast_fusion.1.refs_1_, bf16[5,5,2,16,256]{4,3,2,1,0:T(8,128)(2,1)S(1)} %slice_bitcast_fusion.refs_2_, f32[2,32,256]{2,1,0:T(8,128)S(1)} %copy-done.3, ...), custom_call_target="tpu_custom_call" | custom-call | flops 10000000 | bytes 3170312 | tf_op jit(solution)/shard_map/surface/pallas_call | solution.py:31
  35.6 6.5 %all-to-all-start = ((f32[64,4,128]{2,1,0:T(4,128)}), f32[64,4,128]{2,1,0:T(4,128)S(1)}, u32[]{:S(2)}, u32[]{:S(2)}) async-start(f32[64,4,128]{2,1,0:T(4,128)} %surface.1), calls=%async_computation | async-start | bytes 262144 | tf_op jit(solution)/shard_map/share_sensitivities/all_to_all | solution.py:455
  42.1 2.3 %second_finish.1 = (f32[4,5,2,32,256]{4,3,2,1,0:T(8,128)}, f32[8,128]{1,0:T(8,128)S(1)}) custom-call(s32[2]{0:T(128)S(1)} %pad_add_fusion.ids_ref, f32[4,5,2,32,256]{4,3,2,1,0:T(8,128)S(1)} %second_local.1.refs_0_, bf16[5,5,32,256]{3,2,1,0:T(8,128)(2,1)S(1)} %slice_bitcast_fusion.1.refs_1_, bf16[5,5,2,16,256]{4,3,2,1,0:T(8,128)(2,1)S(1)} %slice_bitcast_fusion.refs_2_, ...), custom_call_target="tpu_custom_call" | custom-call | flops 10000000 | bytes 4313096 | tf_op jit(solution)/shard_map/second_finish/pallas_call | solution.py:31
  44.5 0.4 tables.1
  44.9 8.3 %all-to-all-done.sens_ref = f32[64,4,128]{2,1,0:T(4,128)S(1)} async-done(((f32[64,4,128]{2,1,0:T(4,128)}), f32[64,4,128]{2,1,0:T(4,128)S(1)}, u32[]{:S(2)}, u32[]{:S(2)}) %all-to-all-start) | async-done | bytes 131104 | tf_op jit(solution)/shard_map/share_sensitivities/all_to_all | solution.py:455
  53.2 1.4 %modes.1 = f32[32,1024]{1,0:T(8,128)} custom-call(bf16[1024,1024]{1,0:T(8,128)(2,1)S(1)} %get-tuple-element.26.chosen_ref, f32[64,64]{1,0:T(8,128)S(1)} %get-tuple-element.27.table_ref, f32[64,4,128]{2,1,0:T(4,128)S(1)} %all-to-all-done.sens_ref), custom_call_target="tpu_custom_call" | custom-call | flops 10000000 | bytes 2375680 | tf_op jit(solution)/shard_map/modes/pallas_call | solution.py:31
Async XLA Ops:
  0.7 1.3 %copy-start = (f32[4,5,2,32,256]{4,3,2,1,0:T(8,128)S(1)}, f32[4,5,2,32,256]{4,3,2,1,0:T(8,128)}, u32[]{:S(2)}) copy-start(f32[4,5,2,32,256]{4,3,2,1,0:T(8,128)} %refs_0_.1) | copy-start | bytes 3932164
  2.0 16.2 %copy-start.1 = (f32[4,5,2,32,256]{4,3,2,1,0:T(8,128)S(1)}, f32[4,5,2,32,256]{4,3,2,1,0:T(8,128)}, u32[]{:S(2)}) copy-start(f32[4,5,2,32,256]{4,3,2,1,0:T(8,128)} %refs_0_.1) | copy-start | bytes 3932164
  2.0 16.2 %copy-start.5 = (f32[4,5,2,32,256]{4,3,2,1,0:T(8,128)S(1)}, f32[4,5,2,32,256]{4,3,2,1,0:T(8,128)}, u32[]{:S(2)}) copy-start(f32[4,5,2,32,256]{4,3,2,1,0:T(8,128)} %src_ref.1) | copy-start | bytes 3932164
  2.7 14.3 %collective-permute-start = (bf16[4,5,32,256]{3,2,1,0:T(8,128)(2,1)S(1)}, bf16[4,5,32,256]{3,2,1,0:T(8,128)(2,1)S(1)}, u32[]{:S(2)}, u32[]{:S(2)}) collective-permute-start(bf16[4,5,32,256]{3,2,1,0:T(8,128)(2,1)S(1)} %get-tuple-element.15), channel_id=1, source_target_pairs={{0,1},{1,0},{2,3},{3,2},{4,5},{5,4},{6,7},{7,6},{8,9},{9,8},{10,11... | collective-permute-start | bytes 983048 | tf_op jit(solution)/shard_map/other_times/ppermute | solution.py:408
  2.8 18.6 %collective-permute-start.4 = (bf16[4,5,32,256]{3,2,1,0:T(8,128)(2,1)S(1)}, bf16[4,5,32,256]{3,2,1,0:T(8,128)(2,1)S(1)}, u32[]{:S(2)}, u32[]{:S(2)}) collective-permute-start(bf16[4,5,32,256]{3,2,1,0:T(8,128)(2,1)S(1)} %get-tuple-element.15), channel_id=1, source_target_pairs={{0,2},{2,0},{4,6},{6,4},{1,3},{3,1},{5,7},{7,5},{8,10},{10,8},{12,... | collective-permute-start | bytes 983048 | tf_op jit(solution)/shard_map/halos/ppermute | solution.py:400
  5.1 13.1 %collective-permute-start.1 = (bf16[4,5,32,256]{3,2,1,0:T(8,128)(2,1)S(1)}, bf16[4,5,32,256]{3,2,1,0:T(8,128)(2,1)S(1)}, u32[]{:S(2)}, u32[]{:S(2)}) collective-permute-start(bf16[4,5,32,256]{3,2,1,0:T(8,128)(2,1)S(1)} %get-tuple-element.16), channel_id=1, source_target_pairs={{0,1},{1,0},{2,3},{3,2},{4,5},{5,4},{6,7},{7,6},{8,9},{9,8},{10,11... | collective-permute-start | bytes 983048 | tf_op jit(solution)/shard_map/other_times/ppermute | solution.py:409
  5.2 16.2 %collective-permute-start.5 = (bf16[4,5,32,256]{3,2,1,0:T(8,128)(2,1)S(1)}, bf16[4,5,32,256]{3,2,1,0:T(8,128)(2,1)S(1)}, u32[]{:S(2)}, u32[]{:S(2)}) collective-permute-start(bf16[4,5,32,256]{3,2,1,0:T(8,128)(2,1)S(1)} %get-tuple-element.16), channel_id=1, source_target_pairs={{2,4},{4,2},{3,5},{5,3},{10,12},{12,10},{11,13},{13,11},{18,20},{2... | collective-permute-start | bytes 983048 | tf_op jit(solution)/shard_map/halos/ppermute | solution.py:401
  7.8 13.6 %collective-permute-start.2 = (f32[40,256]{1,0:T(8,128)S(1)}, f32[40,256]{1,0:T(8,128)S(1)}, u32[]{:S(2)}, u32[]{:S(2)}) collective-permute-start(f32[40,256]{1,0:T(8,128)S(1)} %get-tuple-element.17), channel_id=1, source_target_pairs={{8,16},{24,32},{40,48},{56,64},{72,80},{88,96},{104,112},{120,128}... | collective-permute-start | bytes 122888 | tf_op jit(solution)/shard_map/halos/ppermute | solution.py:398
  17.0 4.4 %collective-permute-start.3 = (f32[40,256]{1,0:T(8,128)S(1)}, f32[40,256]{1,0:T(8,128)S(1)}, u32[]{:S(2)}, u32[]{:S(2)}) collective-permute-start(f32[40,256]{1,0:T(8,128)S(1)} %get-tuple-element.18), channel_id=1, source_target_pairs={{0,8},{8,0},{16,24},{24,16},{32,40},{40,32},{48,56},{56,48},{64,72... | collective-permute-start | bytes 122888 | tf_op jit(solution)/shard_map/halos/ppermute | solution.py:399
  18.1 1.4 %copy-start.2 = (bf16[2,5,5,2,32,256]{5,4,3,2,1,0:T(8,128)(2,1)S(1)}, bf16[2,5,5,2,32,256]{5,4,3,2,1,0:T(8,128)(2,1)}, u32[]{:S(2)}) copy-start(bf16[2,5,5,2,32,256]{5,4,3,2,1,0:T(8,128)(2,1)} %refs_2_.3) | copy-start | bytes 4915204
  18.2 1.4 %copy-start.3 = (f32[2,32,256]{2,1,0:T(8,128)S(1)}, f32[2,32,256]{2,1,0:T(8,128)}, u32[]{:S(2)}) copy-start(f32[2,32,256]{2,1,0:T(8,128)} %refs_3_.9) | copy-start | bytes 196612
  18.2 1.4 %copy-start.4 = (f32[2,32,256]{2,1,0:T(8,128)S(1)}, f32[2,32,256]{2,1,0:T(8,128)}, u32[]{:S(2)}) copy-start(f32[2,32,256]{2,1,0:T(8,128)} %refs_4_.9) | copy-start | bytes 196612
  21.4 7.9 %copy-start.6 = (f32[4,5,1024]{2,0,1:T(4,128)S(1)}, f32[4,5,1024]{2,0,1:T(4,128)}, u32[]{:S(2)}) copy-start(f32[4,5,1024]{2,0,1:T(4,128)} %param.13) | copy-start | bytes 245764
  21.4 7.9 %copy-start.7 = (s32[1,1024]{1,0:T(1,128)S(1)}, s32[1,1024]{1,0:T(1,128)}, u32[]{:S(2)}) copy-start(s32[1,1024]{1,0:T(1,128)} %cells_ref.3) | copy-start | bytes 12292
  22.8 10.5 %collective-permute-start.8 = (bf16[4,5,32,256]{3,2,1,0:T(8,128)(2,1)S(1)}, bf16[4,5,32,256]{3,2,1,0:T(8,128)(2,1)S(1)}, u32[]{:S(2)}, u32[]{:S(2)}) collective-permute-start(bf16[4,5,32,256]{3,2,1,0:T(8,128)(2,1)S(1)} %get-tuple-element.22), channel_id=1, source_target_pairs={{0,2},{2,0},{4,6},{6,4},{1,3},{3,1},{5,7},{7,5},{8,10},{10,8},{12,... | collective-permute-start | bytes 983048 | tf_op jit(solution)/shard_map/halos/ppermute | solution.py:400
  22.9 11.3 %collective-permute-start.9 = (bf16[4,5,32,256]{3,2,1,0:T(8,128)(2,1)S(1)}, bf16[4,5,32,256]{3,2,1,0:T(8,128)(2,1)S(1)}, u32[]{:S(2)}, u32[]{:S(2)}) collective-permute-start(bf16[4,5,32,256]{3,2,1,0:T(8,128)(2,1)S(1)} %get-tuple-element.23), channel_id=1, source_target_pairs={{2,4},{4,2},{3,5},{5,3},{10,12},{12,10},{11,13},{13,11},{18,20},{2... | collective-permute-start | bytes 983048 | tf_op jit(solution)/shard_map/halos/ppermute | solution.py:401
  24.8 7.4 %collective-permute-start.6 = (f32[40,256]{1,0:T(8,128)S(1)}, f32[40,256]{1,0:T(8,128)S(1)}, u32[]{:S(2)}, u32[]{:S(2)}) collective-permute-start(f32[40,256]{1,0:T(8,128)S(1)} %get-tuple-element.20), channel_id=1, source_target_pairs={{8,16},{24,32},{40,48},{56,64},{72,80},{88,96},{104,112},{120,128}... | collective-permute-start | bytes 122888 | tf_op jit(solution)/shard_map/halos/ppermute | solution.py:398
  29.3 4.0 %collective-permute-start.7 = (f32[40,256]{1,0:T(8,128)S(1)}, f32[40,256]{1,0:T(8,128)S(1)}, u32[]{:S(2)}, u32[]{:S(2)}) collective-permute-start(f32[40,256]{1,0:T(8,128)S(1)} %get-tuple-element.21), channel_id=1, source_target_pairs={{0,8},{8,0},{16,24},{24,16},{32,40},{40,32},{48,56},{56,48},{64,72... | collective-permute-start | bytes 122888 | tf_op jit(solution)/shard_map/halos/ppermute | solution.py:399
  35.6 17.6 %all-to-all-start = ((f32[64,4,128]{2,1,0:T(4,128)}), f32[64,4,128]{2,1,0:T(4,128)S(1)}, u32[]{:S(2)}, u32[]{:S(2)}) async-start(f32[64,4,128]{2,1,0:T(4,128)} %surface.1), calls=%async_computation | async-start | bytes 262144 | tf_op jit(solution)/shard_map/share_sensitivities/all_to_all | solution.py:455

commit v6 on v5

--- a/solution.py
+++ b/solution.py
@@ -86,7 +86,7 @@
     nt, nv, ni, nj, nk = f_ref.shape
 
     def run(layer_a, layer_b):
-        for layer, other in ((layer_a, pa_ref), (layer_b, pb_ref)):
+        for layer, other in ((layer_a, pb_ref), (layer_b, pa_ref)):
 
             def one(v, carry):
                 for j in range(0, nj, 16):
@@ -377,10 +377,15 @@
     nt, nv, ni, nj, nk = start.shape
     ring = lax.axis_size("passage")
     n_cell = lax.axis_size("cell")
-    ids = jnp.stack([lax.axis_index("cell") & 1, lax.axis_index("passage") & 1])
+    parity = (lax.axis_index("cell") ^ lax.axis_index("tm")) & 1
+    ids = jnp.stack([parity, lax.axis_index("passage") & 1])
     even = [(c, c ^ 1) for c in range(n_cell)]
     odd = [(c, c + 1) for c in range(1, n_cell - 1, 2)]
     odd += [(b, a) for a, b in odd]
+    turns = [
+        [(2 * c + core, 2 * d + core) for core in range(2) for c, d in pairs[core]]
+        for pairs in ((even, odd), (odd, even))
+    ]
     within = [(d, d ^ 1) for d in range(ring)]
     across = [(d, (d + 1) % ring) for d in range(1, ring, 2)]
     across += [(b, a) for a, b in across]
@@ -397,8 +402,8 @@
             return (
                 lax.ppermute(outer, "passage", across),
                 lax.ppermute(inner, "passage", within),
-                lax.ppermute(a, "cell", even),
-                lax.ppermute(b, "cell", odd),
+                lax.ppermute(a, ("cell", "tm"), turns[0]),
+                lax.ppermute(b, ("cell", "tm"), turns[1]),
             )
 
     packed = call(

time: 55.2 us -> 57.6 us (1.043)
  starting transfers between devices: 26.3 us -> 27.9 us
    ppermute x4, starting transfers between devices: 6.87 us -> 11.4 us  [the longest x2 6.15 us: exchange(): lax.ppermute(a, ('cell', 'tm'), turns[0])]
    ppermute x2, starting transfers between devices: 12.6 us -> 10.1 us  [exchange(): lax.ppermute(outer, 'passage', across)]
    ppermute x2, waiting for transfers between devices: 0.19 us -> 2.44 us  [exchange(): lax.ppermute(outer, 'passage', across)]
    ppermute x2, waiting for transfers between devices: 1.03 us -> 0.01 us  [exchange(): lax.ppermute(inner, 'passage', within)]
    ppermute x4, waiting for transfers between devices: 0.93 us -> 0.01 us  [the longest x2 0.01 us: exchange(): lax.ppermute(a, ('cell', 'tm'), turns[0])]
    all_to_all x1, starting transfers between devices: 6.52 us -> 5.84 us  [body(): gathered = lax.all_to_all(sens, ('passage', 'tm'), 0, 0, tiled=True)]
  transfers between devices with their start and end apart: 11 -> 11, of which waited for: 4 -> 2; matrix products, arithmetic and copies ran while one was open for 4% -> 4% of each run, Pallas kernels for 15% -> 15%
where the time goes in v6:
time: 57.6 us; the launch traced here: 56.5 us
  starting transfers between devices  27.9 us (48%)
  Pallas kernels  13.2 us (23%)
  waiting for transfers between devices  10.8 us (19%)
  local copies, waits for them, and re-layouts  3.69 us (6%)
  between operations  0.86 us (1%)
    pallas_call x10, Pallas kernels, call(): pl.pallas_call(kernel, out_shape=outs, in_specs=specs, out_specs=[VMEM] *...  13.2 us
    ppermute x2, starting transfers between devices, exchange(): lax.ppermute(outer, 'passage', across)  10.1 us
    all_to_all x1, waiting for transfers between devices, body(): gathered = lax.all_to_all(sens, ('passage', 'tm'), 0, 0, tiled=True)  8.29 us
    ppermute x2, starting transfers between devices, exchange(): lax.ppermute(a, ('cell', 'tm'), turns[0])  6.15 us
    all_to_all x1, starting transfers between devices, body(): gathered = lax.all_to_all(sens, ('passage', 'tm'), 0, 0, tiled=True)  5.84 us
    ppermute x2, starting transfers between devices, exchange(): lax.ppermute(b, ('cell', 'tm'), turns[1])  5.28 us
    ppermute x2, waiting for transfers between devices, exchange(): lax.ppermute(outer, 'passage', across)  2.44 us
    unnamed x16, local copies, waits for them, and re-layouts  1.61 us
  transfers between devices with their start and end apart: 11, of which 2 were waited for; matrix products, arithmetic and copies ran while one was open for 4% of the time, Pallas kernels for 15%

profile of v6, /device:TPU:8, one launch (start us, length us, event | category | flops | bytes accessed | tf_op | source)
XLA Modules:
  0.0 56.5 jit_solution(3329253062056407483)
XLA Ops:
  0.6 0.1 pad_add_fusion.ids_ref
  0.7 0.0 copy-start
  0.7 1.3 %copy-done = f32[4,5,2,32,256]{4,3,2,1,0:T(8,128)S(1)} copy-done((f32[4,5,2,32,256]{4,3,2,1,0:T(8,128)S(1)}, f32[4,5,2,32,256]{4,3,2,1,0:T(8,128)}, u32[]{:S(2)}) %copy-start) | copy-done | bytes 1310744
  2.0 0.0 copy-start.1
  2.0 0.0 copy-start.5
  2.0 0.7 %prepare.1 = (bf16[4,5,32,256]{3,2,1,0:T(8,128)(2,1)S(1)}, bf16[4,5,32,256]{3,2,1,0:T(8,128)(2,1)S(1)}, f32[40,256]{1,0:T(8,128)S(1)}, f32[40,256]{1,0:T(8,128)S(1)}) custom-call(s32[2]{0:T(128)S(1)} %pad_add_fusion.ids_ref, f32[4,5,2,32,256]{4,3,2,1,0:T(8,128)S(1)} %copy-done), custom_call_target="tpu_custom_call" | custom-call | flops 1000000 | bytes 2048008 | tf_op jit(solution)/shard_map/prepare/pallas_call | solution.py:31
  2.7 0.1 collective-permute-start
  2.8 4.2 %collective-permute-start.4 = (bf16[4,5,32,256]{3,2,1,0:T(8,128)(2,1)S(1)}, bf16[4,5,32,256]{3,2,1,0:T(8,128)(2,1)S(1)}, u32[]{:S(2)}, u32[]{:S(2)}) collective-permute-start(bf16[4,5,32,256]{3,2,1,0:T(8,128)(2,1)S(1)} %get-tuple-element.15), channel_id=1, source_target_pairs={{0,2},{2,0},{4,6},{6,4},{3,5},{5,3},{8,10},{10,8},{12,14},{14,12},... | collective-permute-start | bytes 983048 | tf_op jit(solution)/shard_map/halos/ppermute | solution.py:405
  7.0 0.1 collective-permute-start.1
  7.1 2.6 %collective-permute-start.5 = (bf16[4,5,32,256]{3,2,1,0:T(8,128)(2,1)S(1)}, bf16[4,5,32,256]{3,2,1,0:T(8,128)(2,1)S(1)}, u32[]{:S(2)}, u32[]{:S(2)}) collective-permute-start(bf16[4,5,32,256]{3,2,1,0:T(8,128)(2,1)S(1)} %get-tuple-element.16), channel_id=1, source_target_pairs={{2,4},{4,2},{1,3},{3,1},{5,7},{7,5},{10,12},{12,10},{9,11},{11,9},... | collective-permute-start | bytes 983048 | tf_op jit(solution)/shard_map/halos/ppermute | solution.py:406
  9.7 8.1 %collective-permute-start.2 = (f32[40,256]{1,0:T(8,128)S(1)}, f32[40,256]{1,0:T(8,128)S(1)}, u32[]{:S(2)}, u32[]{:S(2)}) collective-permute-start(f32[40,256]{1,0:T(8,128)S(1)} %get-tuple-element.17), channel_id=1, source_target_pairs={{8,16},{24,32},{40,48},{56,64},{72,80},{88,96},{104,112},{120,128}... | collective-permute-start | bytes 122888 | tf_op jit(solution)/shard_map/halos/ppermute | solution.py:403
  17.9 1.0 %slice_bitcast_fusion.refs_2_ = bf16[5,5,2,16,256]{4,3,2,1,0:T(8,128)(2,1)S(1)} fusion(bf16[2,5,5,2,32,256]{5,4,3,2,1,0:T(8,128)(2,1)} %refs_2_.3), kind=kLoop, calls=%fused_computation | loop fusion | bytes 819200 | tf_op jit(solution)/shard_map/squeeze | solution.py:439
  18.9 0.0 collective-permute-done.pa_ref
  18.9 0.1 collective-permute-start.3
  19.0 1.0 %slice_bitcast_fusion.1.refs_1_ = bf16[5,5,32,256]{3,2,1,0:T(8,128)(2,1)S(1)} fusion(bf16[2,5,5,2,32,256]{5,4,3,2,1,0:T(8,128)(2,1)} %refs_2_.3), kind=kLoop, calls=%fused_computation.1 | loop fusion | bytes 819200 | tf_op jit(solution)/shard_map/squeeze | solution.py:438
  20.0 0.0 copy-start.2
  20.1 0.0 copy-start.3
  20.1 0.0 copy-start.4
  20.1 0.0 collective-permute-done.1.pb_ref
  20.1 0.0 copy-done.1
  20.1 0.0 copy-done.5
  20.1 1.1 %rhs.1.refs_1_ = f32[4,5,2,32,256]{4,3,2,1,0:T(8,128)S(1)} custom-call(s32[2]{0:T(128)S(1)} %pad_add_fusion.ids_ref, f32[4,5,2,32,256]{4,3,2,1,0:T(8,128)S(1)} %copy-done.1, f32[4,5,2,32,256]{4,3,2,1,0:T(8,128)S(1)} %copy-done.5, bf16[4,5,32,256]{3,2,1,0:T(8,128)(2,1)S(1)} %collective-permute-done.pa_ref, ...), custom_call_target="tpu_custom_call" | custom-call | flops 10000000 | bytes 4587528 | tf_op jit(solution)/shard_map/rhs/pallas_call | solution.py:31
  21.2 0.3 copy-done.2
  21.5 0.0 copy-done.3
  21.5 0.0 copy-done.4
  21.5 1.8 %first_local.1.refs_0_ = f32[4,5,2,32,256]{4,3,2,1,0:T(8,128)S(1)} custom-call(f32[4,5,2,32,256]{4,3,2,1,0:T(8,128)S(1)} %copy-done.1, f32[4,5,2,32,256]{4,3,2,1,0:T(8,128)S(1)} %rhs.1.refs_1_, bf16[2,5,5,2,32,256]{5,4,3,2,1,0:T(8,128)(2,1)S(1)} %copy-done.2, f32[2,32,256]{2,1,0:T(8,128)S(1)} %copy-done.3, f32[2,32,256]{2,1,0:T(8,128)S(1)} %copy-done.4), custom_call_target="tpu_custom_call" | custom-call | flops 20000000 | bytes 5701632 | tf_op jit(solution)/shard_map/first_local/pallas_call | solution.py:31
  23.3 0.0 copy-start.6
  23.3 0.0 copy-start.7
  23.3 0.0 collective-permute-done.2.refs_5_
  23.3 0.0 collective-permute-done.3.refs_6_
  23.3 0.0 collective-permute-done.4.refs_7_
  23.3 0.0 collective-permute-done.5.refs_8_
  23.3 1.4 %first_finish.1 = (f32[4,5,2,32,256]{4,3,2,1,0:T(8,128)S(1)}, bf16[4,5,32,256]{3,2,1,0:T(8,128)(2,1)S(1)}, bf16[4,5,32,256]{3,2,1,0:T(8,128)(2,1)S(1)}, f32[40,256]{1,0:T(8,128)S(1)}, f32[40,256]{1,0:T(8,128)S(1)}) custom-call(s32[2]{0:T(128)S(1)} %pad_add_fusion.ids_ref, f32[4,5,2,32,256]{4,3,2,1,0:T(8,128)S(1)} %first_local.1.refs_0_, ...), custom_call_target="tpu_custom_call" | custom-call | flops 10000000 | bytes 5046280 | tf_op jit(solution)/shard_map/first_finish/pallas_call | solution.py:31
  24.7 1.9 %collective-permute-start.8 = (bf16[4,5,32,256]{3,2,1,0:T(8,128)(2,1)S(1)}, bf16[4,5,32,256]{3,2,1,0:T(8,128)(2,1)S(1)}, u32[]{:S(2)}, u32[]{:S(2)}) collective-permute-start(bf16[4,5,32,256]{3,2,1,0:T(8,128)(2,1)S(1)} %get-tuple-element.22), channel_id=1, source_target_pairs={{0,2},{2,0},{4,6},{6,4},{3,5},{5,3},{8,10},{10,8},{12,14},{14,12},... | collective-permute-start | bytes 983048 | tf_op jit(solution)/shard_map/halos/ppermute | solution.py:405
  26.7 2.7 %collective-permute-start.9 = (bf16[4,5,32,256]{3,2,1,0:T(8,128)(2,1)S(1)}, bf16[4,5,32,256]{3,2,1,0:T(8,128)(2,1)S(1)}, u32[]{:S(2)}, u32[]{:S(2)}) collective-permute-start(bf16[4,5,32,256]{3,2,1,0:T(8,128)(2,1)S(1)} %get-tuple-element.23), channel_id=1, source_target_pairs={{2,4},{4,2},{1,3},{3,1},{5,7},{7,5},{10,12},{12,10},{9,11},{11,9},... | collective-permute-start | bytes 983048 | tf_op jit(solution)/shard_map/halos/ppermute | solution.py:406
  29.4 1.9 %collective-permute-start.6 = (f32[40,256]{1,0:T(8,128)S(1)}, f32[40,256]{1,0:T(8,128)S(1)}, u32[]{:S(2)}, u32[]{:S(2)}) collective-permute-start(f32[40,256]{1,0:T(8,128)S(1)} %get-tuple-element.20), channel_id=1, source_target_pairs={{8,16},{24,32},{40,48},{56,64},{72,80},{88,96},{104,112},{120,128}... | collective-permute-start | bytes 122888 | tf_op jit(solution)/shard_map/halos/ppermute | solution.py:403
  31.3 0.3 collective-permute-start.7
  31.6 0.0 copy-done.6
  31.6 0.0 copy-done.7
  31.6 1.0 %order.1.refs_9_ = f32[20,512]{1,0:T(8,128)S(1)} custom-call(s32[2]{0:T(128)S(1)} %pad_add_fusion.ids_ref, s32[1,1024]{1,0:T(1,128)S(1)} %copy-done.7, f32[5,4,1024]{2,1,0:T(4,128)S(1)} %bitcast.10), custom_call_target="tpu_custom_call" | custom-call | flops 1000000 | bytes 126984 | tf_op jit(solution)/shard_map/order/pallas_call | solution.py:31
  32.6 1.8 %second_local.1.refs_0_ = f32[4,5,2,32,256]{4,3,2,1,0:T(8,128)S(1)} custom-call(f32[4,5,2,32,256]{4,3,2,1,0:T(8,128)S(1)} %get-tuple-element.19.refs_0_, f32[4,5,2,32,256]{4,3,2,1,0:T(8,128)S(1)} %rhs.1.refs_1_, bf16[2,5,5,2,32,256]{5,4,3,2,1,0:T(8,128)(2,1)S(1)} %copy-done.2, f32[2,32,256]{2,1,0:T(8,128)S(1)} %copy-done.3, f32[2,32,256]{2,1,0:T(8,128)S(1)} %copy-done.4), custom_call_target="tpu_custom_call" | custom-call | flops 20000000 | bytes 5701632 | tf_op jit(solution)/shard_map/second_local/pallas_call | solution.py:31
  34.3 2.4 %collective-permute-done.6.refs_5_ = f32[40,256]{1,0:T(8,128)S(1)} collective-permute-done((f32[40,256]{1,0:T(8,128)S(1)}, f32[40,256]{1,0:T(8,128)S(1)}, u32[]{:S(2)}, u32[]{:S(2)}) %collective-permute-start.6) | collective-permute-done | bytes 40992 | tf_op jit(solution)/shard_map/halos/ppermute | solution.py:403
  36.8 0.0 collective-permute-done.7.refs_6_
  36.8 0.0 collective-permute-done.8.refs_7_
  36.8 0.0 collective-permute-done.9.refs_8_
  36.8 1.4 %surface.1 = f32[64,4,128]{2,1,0:T(4,128)} custom-call(s32[2]{0:T(128)S(1)} %pad_add_fusion.ids_ref, f32[4,5,2,32,256]{4,3,2,1,0:T(8,128)S(1)} %second_local.1.refs_0_, bf16[5,5,32,256]{3,2,1,0:T(8,128)(2,1)S(1)} %slice_bitcast_fusion.1.refs_1_, bf16[5,5,2,16,256]{4,3,2,1,0:T(8,128)(2,1)S(1)} %slice_bitcast_fusion.refs_2_, f32[2,32,256]{2,1,0:T(8,128)S(1)} %copy-done.3, ...), custom_call_target="tpu_custom_call" | custom-call | flops 10000000 | bytes 3170312 | tf_op jit(solution)/shard_map/surface/pallas_call | solution.py:31
  38.2 5.8 %all-to-all-start = ((f32[64,4,128]{2,1,0:T(4,128)}), f32[64,4,128]{2,1,0:T(4,128)S(1)}, u32[]{:S(2)}, u32[]{:S(2)}) async-start(f32[64,4,128]{2,1,0:T(4,128)} %surface.1), calls=%async_computation | async-start | bytes 262144 | tf_op jit(solution)/shard_map/share_sensitivities/all_to_all | solution.py:460
  44.0 2.3 %second_finish.1 = (f32[4,5,2,32,256]{4,3,2,1,0:T(8,128)}, f32[8,128]{1,0:T(8,128)S(1)}) custom-call(s32[2]{0:T(128)S(1)} %pad_add_fusion.ids_ref, f32[4,5,2,32,256]{4,3,2,1,0:T(8,128)S(1)} %second_local.1.refs_0_, bf16[5,5,32,256]{3,2,1,0:T(8,128)(2,1)S(1)} %slice_bitcast_fusion.1.refs_1_, bf16[5,5,2,16,256]{4,3,2,1,0:T(8,128)(2,1)S(1)} %slice_bitcast_fusion.refs_2_, ...), custom_call_target="tpu_custom_call" | custom-call | flops 10000000 | bytes 4313096 | tf_op jit(solution)/shard_map/second_finish/pallas_call | solution.py:31
  46.4 0.4 tables.1
  46.8 8.3 %all-to-all-done.sens_ref = f32[64,4,128]{2,1,0:T(4,128)S(1)} async-done(((f32[64,4,128]{2,1,0:T(4,128)}), f32[64,4,128]{2,1,0:T(4,128)S(1)}, u32[]{:S(2)}, u32[]{:S(2)}) %all-to-all-start) | async-done | bytes 131104 | tf_op jit(solution)/shard_map/share_sensitivities/all_to_all | solution.py:460
  55.1 1.4 %modes.1 = f32[32,1024]{1,0:T(8,128)} custom-call(bf16[1024,1024]{1,0:T(8,128)(2,1)S(1)} %get-tuple-element.26.chosen_ref, f32[64,64]{1,0:T(8,128)S(1)} %get-tuple-element.27.table_ref, f32[64,4,128]{2,1,0:T(4,128)S(1)} %all-to-all-done.sens_ref), custom_call_target="tpu_custom_call" | custom-call | flops 10000000 | bytes 2375680 | tf_op jit(solution)/shard_map/modes/pallas_call | solution.py:31
Async XLA Ops:
  0.7 1.3 %copy-start = (f32[4,5,2,32,256]{4,3,2,1,0:T(8,128)S(1)}, f32[4,5,2,32,256]{4,3,2,1,0:T(8,128)}, u32[]{:S(2)}) copy-start(f32[4,5,2,32,256]{4,3,2,1,0:T(8,128)} %refs_0_.1) | copy-start | bytes 3932164
  2.0 18.1 %copy-start.1 = (f32[4,5,2,32,256]{4,3,2,1,0:T(8,128)S(1)}, f32[4,5,2,32,256]{4,3,2,1,0:T(8,128)}, u32[]{:S(2)}) copy-start(f32[4,5,2,32,256]{4,3,2,1,0:T(8,128)} %refs_0_.1) | copy-start | bytes 3932164
  2.0 18.1 %copy-start.5 = (f32[4,5,2,32,256]{4,3,2,1,0:T(8,128)S(1)}, f32[4,5,2,32,256]{4,3,2,1,0:T(8,128)}, u32[]{:S(2)}) copy-start(f32[4,5,2,32,256]{4,3,2,1,0:T(8,128)} %src_ref.1) | copy-start | bytes 3932164
  2.7 16.2 %collective-permute-start = (bf16[4,5,32,256]{3,2,1,0:T(8,128)(2,1)S(1)}, bf16[4,5,32,256]{3,2,1,0:T(8,128)(2,1)S(1)}, u32[]{:S(2)}, u32[]{:S(2)}) collective-permute-start(bf16[4,5,32,256]{3,2,1,0:T(8,128)(2,1)S(1)} %get-tuple-element.15), channel_id=1, source_target_pairs={{0,1},{1,0},{2,3},{3,2},{4,5},{5,4},{6,7},{7,6},{8,9},{9,8},{10,11... | collective-permute-start | bytes 983048 | tf_op jit(solution)/shard_map/other_times/ppermute | solution.py:413
  2.8 20.5 %collective-permute-start.4 = (bf16[4,5,32,256]{3,2,1,0:T(8,128)(2,1)S(1)}, bf16[4,5,32,256]{3,2,1,0:T(8,128)(2,1)S(1)}, u32[]{:S(2)}, u32[]{:S(2)}) collective-permute-start(bf16[4,5,32,256]{3,2,1,0:T(8,128)(2,1)S(1)} %get-tuple-element.15), channel_id=1, source_target_pairs={{0,2},{2,0},{4,6},{6,4},{3,5},{5,3},{8,10},{10,8},{12,14},{14,12},... | collective-permute-start | bytes 983048 | tf_op jit(solution)/shard_map/halos/ppermute | solution.py:405
  7.0 13.1 %collective-permute-start.1 = (bf16[4,5,32,256]{3,2,1,0:T(8,128)(2,1)S(1)}, bf16[4,5,32,256]{3,2,1,0:T(8,128)(2,1)S(1)}, u32[]{:S(2)}, u32[]{:S(2)}) collective-permute-start(bf16[4,5,32,256]{3,2,1,0:T(8,128)(2,1)S(1)} %get-tuple-element.16), channel_id=1, source_target_pairs={{0,1},{1,0},{2,3},{3,2},{4,5},{5,4},{6,7},{7,6},{8,9},{9,8},{10,11... | collective-permute-start | bytes 983048 | tf_op jit(solution)/shard_map/other_times/ppermute | solution.py:414
  7.1 16.2 %collective-permute-start.5 = (bf16[4,5,32,256]{3,2,1,0:T(8,128)(2,1)S(1)}, bf16[4,5,32,256]{3,2,1,0:T(8,128)(2,1)S(1)}, u32[]{:S(2)}, u32[]{:S(2)}) collective-permute-start(bf16[4,5,32,256]{3,2,1,0:T(8,128)(2,1)S(1)} %get-tuple-element.16), channel_id=1, source_target_pairs={{2,4},{4,2},{1,3},{3,1},{5,7},{7,5},{10,12},{12,10},{9,11},{11,9},... | collective-permute-start | bytes 983048 | tf_op jit(solution)/shard_map/halos/ppermute | solution.py:406
  9.7 13.6 %collective-permute-start.2 = (f32[40,256]{1,0:T(8,128)S(1)}, f32[40,256]{1,0:T(8,128)S(1)}, u32[]{:S(2)}, u32[]{:S(2)}) collective-permute-start(f32[40,256]{1,0:T(8,128)S(1)} %get-tuple-element.17), channel_id=1, source_target_pairs={{8,16},{24,32},{40,48},{56,64},{72,80},{88,96},{104,112},{120,128}... | collective-permute-start | bytes 122888 | tf_op jit(solution)/shard_map/halos/ppermute | solution.py:403
  18.9 4.4 %collective-permute-start.3 = (f32[40,256]{1,0:T(8,128)S(1)}, f32[40,256]{1,0:T(8,128)S(1)}, u32[]{:S(2)}, u32[]{:S(2)}) collective-permute-start(f32[40,256]{1,0:T(8,128)S(1)} %get-tuple-element.18), channel_id=1, source_target_pairs={{0,8},{8,0},{16,24},{24,16},{32,40},{40,32},{48,56},{56,48},{64,72... | collective-permute-start | bytes 122888 | tf_op jit(solution)/shard_map/halos/ppermute | solution.py:404
  20.0 1.4 %copy-start.2 = (bf16[2,5,5,2,32,256]{5,4,3,2,1,0:T(8,128)(2,1)S(1)}, bf16[2,5,5,2,32,256]{5,4,3,2,1,0:T(8,128)(2,1)}, u32[]{:S(2)}) copy-start(bf16[2,5,5,2,32,256]{5,4,3,2,1,0:T(8,128)(2,1)} %refs_2_.3) | copy-start | bytes 4915204
  20.1 1.4 %copy-start.3 = (f32[2,32,256]{2,1,0:T(8,128)S(1)}, f32[2,32,256]{2,1,0:T(8,128)}, u32[]{:S(2)}) copy-start(f32[2,32,256]{2,1,0:T(8,128)} %refs_3_.9) | copy-start | bytes 196612
  20.1 1.4 %copy-start.4 = (f32[2,32,256]{2,1,0:T(8,128)S(1)}, f32[2,32,256]{2,1,0:T(8,128)}, u32[]{:S(2)}) copy-start(f32[2,32,256]{2,1,0:T(8,128)} %refs_4_.9) | copy-start | bytes 196612
  23.3 8.3 %copy-start.6 = (f32[4,5,1024]{2,0,1:T(4,128)S(1)}, f32[4,5,1024]{2,0,1:T(4,128)}, u32[]{:S(2)}) copy-start(f32[4,5,1024]{2,0,1:T(4,128)} %param.13) | copy-start | bytes 245764
  23.3 8.3 %copy-start.7 = (s32[1,1024]{1,0:T(1,128)S(1)}, s32[1,1024]{1,0:T(1,128)}, u32[]{:S(2)}) copy-start(s32[1,1024]{1,0:T(1,128)} %cells_ref.3) | copy-start | bytes 12292
  24.7 12.1 %collective-permute-start.8 = (bf16[4,5,32,256]{3,2,1,0:T(8,128)(2,1)S(1)}, bf16[4,5,32,256]{3,2,1,0:T(8,128)(2,1)S(1)}, u32[]{:S(2)}, u32[]{:S(2)}) collective-permute-start(bf16[4,5,32,256]{3,2,1,0:T(8,128)(2,1)S(1)} %get-tuple-element.22), channel_id=1, source_target_pairs={{0,2},{2,0},{4,6},{6,4},{3,5},{5,3},{8,10},{10,8},{12,14},{14,12},... | collective-permute-start | bytes 983048 | tf_op jit(solution)/shard_map/halos/ppermute | solution.py:405
  26.7 10.1 %collective-permute-start.9 = (bf16[4,5,32,256]{3,2,1,0:T(8,128)(2,1)S(1)}, bf16[4,5,32,256]{3,2,1,0:T(8,128)(2,1)S(1)}, u32[]{:S(2)}, u32[]{:S(2)}) collective-permute-start(bf16[4,5,32,256]{3,2,1,0:T(8,128)(2,1)S(1)} %get-tuple-element.23), channel_id=1, source_target_pairs={{2,4},{4,2},{1,3},{3,1},{5,7},{7,5},{10,12},{12,10},{9,11},{11,9},... | collective-permute-start | bytes 983048 | tf_op jit(solution)/shard_map/halos/ppermute | solution.py:406
  29.4 7.4 %collective-permute-start.6 = (f32[40,256]{1,0:T(8,128)S(1)}, f32[40,256]{1,0:T(8,128)S(1)}, u32[]{:S(2)}, u32[]{:S(2)}) collective-permute-start(f32[40,256]{1,0:T(8,128)S(1)} %get-tuple-element.20), channel_id=1, source_target_pairs={{8,16},{24,32},{40,48},{56,64},{72,80},{88,96},{104,112},{120,128}... | collective-permute-start | bytes 122888 | tf_op jit(solution)/shard_map/halos/ppermute | solution.py:403
  31.3 5.5 %collective-permute-start.7 = (f32[40,256]{1,0:T(8,128)S(1)}, f32[40,256]{1,0:T(8,128)S(1)}, u32[]{:S(2)}, u32[]{:S(2)}) collective-permute-start(f32[40,256]{1,0:T(8,128)S(1)} %get-tuple-element.21), channel_id=1, source_target_pairs={{0,8},{8,0},{16,24},{24,16},{32,40},{40,32},{48,56},{56,48},{64,72... | collective-permute-start | bytes 122888 | tf_op jit(solution)/shard_map/halos/ppermute | solution.py:404
  38.2 16.9 %all-to-all-start = ((f32[64,4,128]{2,1,0:T(4,128)}), f32[64,4,128]{2,1,0:T(4,128)S(1)}, u32[]{:S(2)}, u32[]{:S(2)}) async-start(f32[64,4,128]{2,1,0:T(4,128)} %surface.1), calls=%async_computation | async-start | bytes 262144 | tf_op jit(solution)/shard_map/share_sensitivities/all_to_all | solution.py:460

commit v7 on v5

--- a/solution.py
+++ b/solution.py
@@ -218,8 +218,15 @@
 
 
 def local_kernel(*refs):
-    ins, out_ref = refs[:5], refs[5]
+    ins, out_ref, slices = refs[:5], refs[5], refs[6:]
     nt, nv, ni, nj, nk = out_ref.shape
+    if slices:
+        jac_ref, (jac_i_ref, jac_j_ref) = ins[2], slices
+        for u in range(nv):
+            for v in range(nv):
+                jac_i_ref[u, v] = jac_ref[0, u, v, ni - 1]
+                for i in range(ni):
+                    jac_j_ref[u, v, i] = jac_ref[1, u, v, i, nj - 16 :, :]
 
     def one(k, carry):
         lanes = lanes_at(k)
@@ -283,9 +290,7 @@
                 values.append(
                     jnp.sum(jnp.where(mask, total, 0.0), axis=0, keepdims=True)
                 )
-        value = jnp.concatenate(values, axis=0)
-        for member in range(sens_ref.shape[0]):
-            sens_ref[member] = value
+        sens_ref[...] = jnp.concatenate(values, axis=0)
 
     def run(layer_a, layer_b):
         layers = {layer_a: ha_ref, layer_b: hb_ref}
@@ -295,8 +300,15 @@
     by_parity(ids_ref, run)
 
 
+def share_kernel(own_ref, other_ref, out_ref, done_ref):
+    done_ref[...] = jnp.zeros(done_ref.shape, F32)
+    value = own_ref[...] + other_ref[...]
+    for member in range(out_ref.shape[0]):
+        out_ref[member] = value
+
+
 def second_kernel(ids_ref, *refs):
-    ins, ha_ref, hb_ref, out_ref, done_ref = refs[:7], *refs[7:11]
+    ins, ha_ref, hb_ref, out_ref, done_ref = refs[:7], *refs[7:9], *refs[10:12]
     done_ref[...] = jnp.zeros(done_ref.shape, F32)
 
     def run(layer_a, layer_b):
@@ -339,10 +351,10 @@
 def mode_table(side, modes, senders):
     row = lax.broadcasted_iota(jnp.int32, (2 * modes, senders), 0)
     sender = lax.broadcasted_iota(jnp.int32, (2 * modes, senders), 1)
-    turns = ((row % modes) * (sender // 4)) % PASSAGES
+    turns = ((row % modes) * (sender // 2)) % PASSAGES
     angle = turns.astype(F32) * (2.0 * math.pi / PASSAGES)
     value = jnp.where(row < modes, jnp.cos(angle), -jnp.sin(angle)) / PASSAGES**0.5
-    return jnp.where((sender // 2) % 2 == side, value, 0.0)
+    return jnp.where(sender % 2 == side, value, 0.0)
 
 
 def tables_kernel(cells_ref, done_ref, chosen_ref, table_ref):
@@ -426,12 +438,15 @@
         10**6,
         "order",
     )[0]
-    def local(field, name):
+    def local(field, outs, name):
         args = (field, rhs, jac, sigma, damping)
-        return call(local_kernel, [field_like], args, [VMEM] * 5, 4, 2 * 10**7, name)[0]
-
-    jac_i = jac[0, :, :, ni - 1]
-    jac_j = jac[1, :, :, :, nj - 16 :]
+        return call(local_kernel, outs, args, [VMEM] * 5, 4, 2 * 10**7, name)
+
+    slices = [
+        jax.ShapeDtypeStruct((nv, nv, nj, nk), BF16),
+        jax.ShapeDtypeStruct((nv, nv, ni, 16, nk), BF16),
+    ]
+    part, jac_i, jac_j = local(start, [field_like] + slices, "first_local")
 
     def finish(kernel, outs, part, halos, more, name):
         outer, inner, ha, hb = halos
@@ -442,26 +457,37 @@
     field, *packed = finish(
         first_kernel,
         [field_like] + sends,
-        local(start, "first_local"),
+        part,
         halos,
         (),
         "first_finish",
     )
     halos = exchange(*packed)
-    part = local(field, "second_local")
-    share_like = jax.ShapeDtypeStruct((2 * ring, ni * nk // 128, 128), F32)
-    sens = finish(surface_kernel, [share_like], part, halos, (ordered,), "surface")[0]
+    part = local(field, [field_like], "second_local")[0]
+    token_like = jax.ShapeDtypeStruct((8, 128), F32)
+    pieces = ni * nk // 128
+    sens_like = jax.ShapeDtypeStruct((pieces, 128), F32)
+    sens = finish(surface_kernel, [sens_like], part, halos, (ordered,), "surface")[0]
     with jax.named_scope("share_sensitivities"):
-        gathered = lax.all_to_all(sens, ("passage", "tm"), 0, 0, tiled=True)
-    token_like = jax.ShapeDtypeStruct((8, 128), F32)
+        other = lax.ppermute(sens, "tm", swap)
+        sens, done = call(
+            share_kernel,
+            [jax.ShapeDtypeStruct((ring, pieces, 128), F32), token_like],
+            (sens, other),
+            [VMEM] * 2,
+            4,
+            10**4,
+            "share",
+        )
+        gathered = lax.all_to_all(sens, "passage", 0, 0, tiled=True)
     field, done = finish(
-        second_kernel, [field_like, token_like], part, halos, (), "second_finish"
+        second_kernel, [field_like, token_like], part, halos, (done,), "second_finish"
     )
     chosen, table = call(
         tables_kernel,
         [
             jax.ShapeDtypeStruct((cells.shape[1], cells.shape[1]), BF16),
-            jax.ShapeDtypeStruct((4 * PASSAGES, 2 * ring), F32),
+            jax.ShapeDtypeStruct((4 * PASSAGES, ring), F32),
         ],
         (cells, done),
         [VMEM] * 2,

time: 55.2 us -> 53.5 us (0.969)
  local copies, waits for them, and re-layouts: 3.69 us -> 1.92 us
  starting transfers between devices: 26.3 us -> 27.2 us
    squeeze x2 -> x0, local copies, waits for them, and re-layouts: 2.07 us -> none  [the longest x1 1.04 us: body(): jac_i = jac[0, :, :, ni - 1]]
    ppermute x0 -> x1, waiting for transfers between devices: none -> 1.14 us  [body(): other = lax.ppermute(sens, 'tm', swap)]
    all_to_all x1, waiting for transfers between devices: 8.29 us -> 7.21 us  [body(): gathered = lax.all_to_all(sens, 'passage', 0, 0, tiled=True)]
    ppermute x2, waiting for transfers between devices: 0.93 us -> 0.01 us  [exchange(): lax.ppermute(b, 'cell', odd)]
    ppermute x2, starting transfers between devices: 12.6 us -> 13.4 us  [exchange(): lax.ppermute(outer, 'passage', across)]
    ppermute x2, waiting for transfers between devices: 1.03 us -> 1.62 us  [exchange(): lax.ppermute(inner, 'passage', within)]
    pallas_call x10 -> x11, Pallas kernels: 13.2 us -> 13.2 us  [call(): pl.pallas_call(kernel, out_shape=outs, in_specs=specs, out_specs=[VMEM] *...]
  transfers between devices with their start and end apart: 11 -> 12, of which waited for: 4 -> 4; matrix products, arithmetic and copies ran while one was open for 4% -> 0% of each run, Pallas kernels for 15% -> 16%
where the time goes in v7:
time: 53.5 us; the launch traced here: 53.3 us
  starting transfers between devices  27.2 us (51%)
  Pallas kernels  13.2 us (25%)
  waiting for transfers between devices  9.99 us (19%)
  local copies, waits for them, and re-layouts  1.92 us (4%)
  between operations  0.81 us (2%)
    ppermute x2, starting transfers between devices, exchange(): lax.ppermute(outer, 'passage', across)  13.4 us
    pallas_call x11, Pallas kernels, call(): pl.pallas_call(kernel, out_shape=outs, in_specs=specs, out_specs=[VMEM] *...  13.2 us
    all_to_all x1, waiting for transfers between devices, body(): gathered = lax.all_to_all(sens, 'passage', 0, 0, tiled=True)  7.21 us
    all_to_all x1, starting transfers between devices, body(): gathered = lax.all_to_all(sens, 'passage', 0, 0, tiled=True)  6.29 us
    ppermute x2, starting transfers between devices, exchange(): lax.ppermute(b, 'cell', odd)  4.49 us
    ppermute x2, starting transfers between devices, exchange(): lax.ppermute(a, 'cell', even)  2.28 us
    unnamed x16, local copies, waits for them, and re-layouts  1.92 us
    ppermute x2, waiting for transfers between devices, exchange(): lax.ppermute(inner, 'passage', within)  1.62 us
  transfers between devices with their start and end apart: 12, of which 4 were waited for; matrix products, arithmetic and copies ran while one was open for 0% of the time, Pallas kernels for 16%

profile of v7, /device:TPU:8, one launch (start us, length us, event | category | flops | bytes accessed | tf_op | source)
XLA Modules:
  0.0 53.3 jit_solution(3411823008848908513)
XLA Ops:
  0.6 0.1 pad_add_fusion.ids_ref
  0.7 0.0 copy-start
  0.7 1.3 %copy-done = f32[4,5,2,32,256]{4,3,2,1,0:T(8,128)S(1)} copy-done((f32[4,5,2,32,256]{4,3,2,1,0:T(8,128)S(1)}, f32[4,5,2,32,256]{4,3,2,1,0:T(8,128)}, u32[]{:S(2)}) %copy-start) | copy-done | bytes 1310744
  2.0 0.0 copy-start.5
  2.0 0.7 %prepare.1 = (bf16[4,5,32,256]{3,2,1,0:T(8,128)(2,1)S(1)}, bf16[4,5,32,256]{3,2,1,0:T(8,128)(2,1)S(1)}, f32[40,256]{1,0:T(8,128)S(1)}, f32[40,256]{1,0:T(8,128)S(1)}) custom-call(s32[2]{0:T(128)S(1)} %pad_add_fusion.ids_ref, f32[4,5,2,32,256]{4,3,2,1,0:T(8,128)S(1)} %copy-done), custom_call_target="tpu_custom_call" | custom-call | flops 1000000 | bytes 2048008 | tf_op jit(solution)/shard_map/prepare/pallas_call | solution.py:31
  2.7 0.1 collective-permute-start
  2.8 0.5 collective-permute-start.1
  3.3 2.2 %collective-permute-start.4 = (bf16[4,5,32,256]{3,2,1,0:T(8,128)(2,1)S(1)}, bf16[4,5,32,256]{3,2,1,0:T(8,128)(2,1)S(1)}, u32[]{:S(2)}, u32[]{:S(2)}) collective-permute-start(bf16[4,5,32,256]{3,2,1,0:T(8,128)(2,1)S(1)} %get-tuple-element.20), channel_id=1, source_target_pairs={{0,2},{2,0},{4,6},{6,4},{1,3},{3,1},{5,7},{7,5},{8,10},{10,8},{12,... | collective-permute-start | bytes 983048 | tf_op jit(solution)/shard_map/halos/ppermute | solution.py:412
  5.5 2.6 %collective-permute-start.5 = (bf16[4,5,32,256]{3,2,1,0:T(8,128)(2,1)S(1)}, bf16[4,5,32,256]{3,2,1,0:T(8,128)(2,1)S(1)}, u32[]{:S(2)}, u32[]{:S(2)}) collective-permute-start(bf16[4,5,32,256]{3,2,1,0:T(8,128)(2,1)S(1)} %get-tuple-element.21), channel_id=1, source_target_pairs={{2,4},{4,2},{3,5},{5,3},{10,12},{12,10},{11,13},{13,11},{18,20},{2... | collective-permute-start | bytes 983048 | tf_op jit(solution)/shard_map/halos/ppermute | solution.py:413
  8.1 8.1 %collective-permute-start.2 = (f32[40,256]{1,0:T(8,128)S(1)}, f32[40,256]{1,0:T(8,128)S(1)}, u32[]{:S(2)}, u32[]{:S(2)}) collective-permute-start(f32[40,256]{1,0:T(8,128)S(1)} %get-tuple-element.25), channel_id=1, source_target_pairs={{8,16},{24,32},{40,48},{56,64},{72,80},{88,96},{104,112},{120,128}... | collective-permute-start | bytes 122888 | tf_op jit(solution)/shard_map/halos/ppermute | solution.py:410
  16.2 0.0 collective-permute-done.pa_ref
  16.2 0.0 copy-start.1
  16.2 0.0 copy-start.2
  16.2 0.0 copy-start.3
  16.2 0.0 copy-start.4
  16.2 0.1 collective-permute-start.3
  16.3 0.0 collective-permute-done.1.pb_ref
  16.3 0.0 copy-done.5
  16.3 1.1 %rhs.1.refs_1_ = f32[4,5,2,32,256]{4,3,2,1,0:T(8,128)S(1)} custom-call(s32[2]{0:T(128)S(1)} %pad_add_fusion.ids_ref, f32[4,5,2,32,256]{4,3,2,1,0:T(8,128)S(1)} %copy-done, f32[4,5,2,32,256]{4,3,2,1,0:T(8,128)S(1)} %copy-done.5, bf16[4,5,32,256]{3,2,1,0:T(8,128)(2,1)S(1)} %collective-permute-done.pa_ref, bf16[4,5,32,256]{3,2,1,0:T(8,128)(2,1)S(1)} %collective-permute-done.1.pb_ref), custom_call_target="tpu_custom_call" | custom-call | flops 10000000 | bytes 4587528 | tf_op jit(solution)/shard_map/rhs/pallas_call | solution.py:31
  17.4 0.1 copy-done.1
  17.5 0.5 copy-done.2
  18.0 0.0 copy-done.3
  18.0 0.0 copy-done.4
  18.0 1.8 %first_local.1 = (f32[4,5,2,32,256]{4,3,2,1,0:T(8,128)S(1)}, bf16[5,5,32,256]{3,2,1,0:T(8,128)(2,1)S(1)}, bf16[5,5,2,16,256]{4,3,2,1,0:T(8,128)(2,1)S(1)}) custom-call(f32[4,5,2,32,256]{4,3,2,1,0:T(8,128)S(1)} %copy-done.1, f32[4,5,2,32,256]{4,3,2,1,0:T(8,128)S(1)} %rhs.1.refs_1_, bf16[2,5,5,2,32,256]{5,4,3,2,1,0:T(8,128)(2,1)S(1)} %copy-done.2, ...), custom_call_target="tpu_custom_call" | custom-call | flops 20000000 | bytes 6520832 | tf_op jit(solution)/shard_map/first_local/pallas_call | solution.py:31
  19.9 0.0 collective-permute-done.2.refs_5_
  19.9 0.4 collective-permute-done.3.refs_6_
  20.3 0.0 collective-permute-done.4.refs_7_
  20.3 0.0 collective-permute-done.5.refs_8_
  20.3 0.0 copy-start.6
  20.3 0.0 copy-start.7
  20.3 1.4 %first_finish.1 = (f32[4,5,2,32,256]{4,3,2,1,0:T(8,128)S(1)}, bf16[4,5,32,256]{3,2,1,0:T(8,128)(2,1)S(1)}, bf16[4,5,32,256]{3,2,1,0:T(8,128)(2,1)S(1)}, f32[40,256]{1,0:T(8,128)S(1)}, f32[40,256]{1,0:T(8,128)S(1)}) custom-call(s32[2]{0:T(128)S(1)} %pad_add_fusion.ids_ref, f32[4,5,2,32,256]{4,3,2,1,0:T(8,128)S(1)} %get-tuple-element.22.refs_0_, ...), custom_call_target="tpu_custom_call" | custom-call | flops 10000000 | bytes 5046280 | tf_op jit(solution)/shard_map/first_finish/pallas_call | solution.py:31
  21.7 0.1 collective-permute-start.8
  21.8 1.9 %collective-permute-start.9 = (bf16[4,5,32,256]{3,2,1,0:T(8,128)(2,1)S(1)}, bf16[4,5,32,256]{3,2,1,0:T(8,128)(2,1)S(1)}, u32[]{:S(2)}, u32[]{:S(2)}) collective-permute-start(bf16[4,5,32,256]{3,2,1,0:T(8,128)(2,1)S(1)} %get-tuple-element.31), channel_id=1, source_target_pairs={{2,4},{4,2},{3,5},{5,3},{10,12},{12,10},{11,13},{13,11},{18,20},{2... | collective-permute-start | bytes 983048 | tf_op jit(solution)/shard_map/halos/ppermute | solution.py:413
  23.8 5.3 %collective-permute-start.6 = (f32[40,256]{1,0:T(8,128)S(1)}, f32[40,256]{1,0:T(8,128)S(1)}, u32[]{:S(2)}, u32[]{:S(2)}) collective-permute-start(f32[40,256]{1,0:T(8,128)S(1)} %get-tuple-element.28), channel_id=1, source_target_pairs={{8,16},{24,32},{40,48},{56,64},{72,80},{88,96},{104,112},{120,128}... | collective-permute-start | bytes 122888 | tf_op jit(solution)/shard_map/halos/ppermute | solution.py:410
  29.0 0.0 collective-permute-start.7
  29.0 0.0 copy-done.6
  29.0 0.0 copy-done.7
  29.0 1.0 %order.1.refs_9_ = f32[20,512]{1,0:T(8,128)S(1)} custom-call(s32[2]{0:T(128)S(1)} %pad_add_fusion.ids_ref, s32[1,1024]{1,0:T(1,128)S(1)} %copy-done.7, f32[5,4,1024]{2,1,0:T(4,128)S(1)} %bitcast.4), custom_call_target="tpu_custom_call" | custom-call | flops 1000000 | bytes 126984 | tf_op jit(solution)/shard_map/order/pallas_call | solution.py:31
  30.0 1.8 %second_local.1.refs_0_ = f32[4,5,2,32,256]{4,3,2,1,0:T(8,128)S(1)} custom-call(f32[4,5,2,32,256]{4,3,2,1,0:T(8,128)S(1)} %get-tuple-element.27.refs_0_, f32[4,5,2,32,256]{4,3,2,1,0:T(8,128)S(1)} %rhs.1.refs_1_, bf16[2,5,5,2,32,256]{5,4,3,2,1,0:T(8,128)(2,1)S(1)} %copy-done.2, f32[2,32,256]{2,1,0:T(8,128)S(1)} %copy-done.3, f32[2,32,256]{2,1,0:T(8,128)S(1)} %copy-done.4), custom_call_target="tpu_custom_call" | custom-call | flops 20000000 | bytes 5701632 | tf_op jit(solution)/shard_map/second_local/pallas_call | solution.py:31
  31.8 0.0 collective-permute-done.6.refs_5_
  31.8 1.2 %collective-permute-done.7.refs_6_ = f32[40,256]{1,0:T(8,128)S(1)} collective-permute-done((f32[40,256]{1,0:T(8,128)S(1)}, f32[40,256]{1,0:T(8,128)S(1)}, u32[]{:S(2)}, u32[]{:S(2)}) %collective-permute-start.7) | collective-permute-done | bytes 40992 | tf_op jit(solution)/shard_map/halos/ppermute | solution.py:411
  33.0 0.0 collective-permute-done.8.refs_7_
  33.0 0.0 collective-permute-done.9.refs_8_
  33.0 0.7 %surface.1.own_ref = f32[4,128]{1,0:T(4,128)S(1)} custom-call(s32[2]{0:T(128)S(1)} %pad_add_fusion.ids_ref, f32[4,5,2,32,256]{4,3,2,1,0:T(8,128)S(1)} %second_local.1.refs_0_, bf16[5,5,32,256]{3,2,1,0:T(8,128)(2,1)S(1)} %get-tuple-element.23.refs_1_, bf16[5,5,2,16,256]{4,3,2,1,0:T(8,128)(2,1)S(1)} %get-tuple-element.24.refs_2_, f32[2,32,256]{2,1,0:T(8,128)S(1)} %copy-done.3, ...), custom_call_target="tpu_custom_call" | custom-call | flops 10000000 | bytes 3041288 | tf_op jit(solution)/shard_map/surface/pallas_call | solution.py:31
  33.8 0.1 collective-permute-start.10
  33.9 1.1 %collective-permute-done.10.other_ref = f32[4,128]{1,0:T(4,128)S(1)} collective-permute-done((f32[4,128]{1,0:T(4,128)S(1)}, f32[4,128]{1,0:T(4,128)S(1)}, u32[]{:S(2)}, u32[]{:S(2)}) %collective-permute-start.10) | collective-permute-done | bytes 2080 | tf_op jit(solution)/shard_map/share_sensitivities/ppermute | solution.py:472
  35.0 0.6 %share.1 = (f32[32,4,128]{2,1,0:T(4,128)}, f32[8,128]{1,0:T(8,128)S(1)}) custom-call(f32[4,128]{1,0:T(4,128)S(1)} %surface.1.own_ref, f32[4,128]{1,0:T(4,128)S(1)} %collective-permute-done.10.other_ref), custom_call_target="tpu_custom_call" | custom-call | flops 10000 | bytes 73728 | tf_op jit(solution)/shard_map/share_sensitivities/share/pallas_call | solution.py:31
  35.6 6.3 %all-to-all-start = ((f32[32,4,128]{2,1,0:T(4,128)}), f32[32,4,128]{2,1,0:T(4,128)S(1)}, u32[]{:S(2)}, u32[]{:S(2)}) async-start(f32[32,4,128]{2,1,0:T(4,128)} %get-tuple-element.37), calls=%async_computation | async-start | bytes 131072 | tf_op jit(solution)/shard_map/share_sensitivities/all_to_all | solution.py:482
  41.9 2.3 %second_finish.1 = (f32[4,5,2,32,256]{4,3,2,1,0:T(8,128)}, f32[8,128]{1,0:T(8,128)S(1)}) custom-call(s32[2]{0:T(128)S(1)} %pad_add_fusion.ids_ref, f32[4,5,2,32,256]{4,3,2,1,0:T(8,128)S(1)} %second_local.1.refs_0_, bf16[5,5,32,256]{3,2,1,0:T(8,128)(2,1)S(1)} %get-tuple-element.23.refs_1_, bf16[5,5,2,16,256]{4,3,2,1,0:T(8,128)(2,1)S(1)} %get-tuple-element.24.refs_2_, ...), custom_call_target="tpu_custom_call" | custom-call | flops 10000000 | bytes 4317192 | tf_op jit(solution)/shard_map/second_finish/pallas_call | solution.py:31
  44.3 0.4 tables.1
  44.7 7.2 %all-to-all-done.sens_ref = f32[32,4,128]{2,1,0:T(4,128)S(1)} async-done(((f32[32,4,128]{2,1,0:T(4,128)}), f32[32,4,128]{2,1,0:T(4,128)S(1)}, u32[]{:S(2)}, u32[]{:S(2)}) %all-to-all-start) | async-done | bytes 65568 | tf_op jit(solution)/shard_map/share_sensitivities/all_to_all | solution.py:482
  51.9 1.4 %modes.1 = f32[32,1024]{1,0:T(8,128)} custom-call(bf16[1024,1024]{1,0:T(8,128)(2,1)S(1)} %get-tuple-element.35.chosen_ref, f32[64,32]{1,0:T(8,128)S(1)} %get-tuple-element.36.table_ref, f32[32,4,128]{2,1,0:T(4,128)S(1)} %all-to-all-done.sens_ref), custom_call_target="tpu_custom_call" | custom-call | flops 10000000 | bytes 2301952 | tf_op jit(solution)/shard_map/modes/pallas_call | solution.py:31
Async XLA Ops:
  0.7 1.3 %copy-start = (f32[4,5,2,32,256]{4,3,2,1,0:T(8,128)S(1)}, f32[4,5,2,32,256]{4,3,2,1,0:T(8,128)}, u32[]{:S(2)}) copy-start(f32[4,5,2,32,256]{4,3,2,1,0:T(8,128)} %refs_0_.1) | copy-start | bytes 3932164
  2.0 14.3 %copy-start.5 = (f32[4,5,2,32,256]{4,3,2,1,0:T(8,128)S(1)}, f32[4,5,2,32,256]{4,3,2,1,0:T(8,128)}, u32[]{:S(2)}) copy-start(f32[4,5,2,32,256]{4,3,2,1,0:T(8,128)} %src_ref.1) | copy-start | bytes 3932164
  2.7 13.5 %collective-permute-start = (bf16[4,5,32,256]{3,2,1,0:T(8,128)(2,1)S(1)}, bf16[4,5,32,256]{3,2,1,0:T(8,128)(2,1)S(1)}, u32[]{:S(2)}, u32[]{:S(2)}) collective-permute-start(bf16[4,5,32,256]{3,2,1,0:T(8,128)(2,1)S(1)} %get-tuple-element.20), channel_id=1, source_target_pairs={{0,1},{1,0},{2,3},{3,2},{4,5},{5,4},{6,7},{7,6},{8,9},{9,8},{10,11... | collective-permute-start | bytes 983048 | tf_op jit(solution)/shard_map/other_times/ppermute | solution.py:420
  2.8 13.5 %collective-permute-start.1 = (bf16[4,5,32,256]{3,2,1,0:T(8,128)(2,1)S(1)}, bf16[4,5,32,256]{3,2,1,0:T(8,128)(2,1)S(1)}, u32[]{:S(2)}, u32[]{:S(2)}) collective-permute-start(bf16[4,5,32,256]{3,2,1,0:T(8,128)(2,1)S(1)} %get-tuple-element.21), channel_id=1, source_target_pairs={{0,1},{1,0},{2,3},{3,2},{4,5},{5,4},{6,7},{7,6},{8,9},{9,8},{10,11... | collective-permute-start | bytes 983048 | tf_op jit(solution)/shard_map/other_times/ppermute | solution.py:421
  3.3 17.0 %collective-permute-start.4 = (bf16[4,5,32,256]{3,2,1,0:T(8,128)(2,1)S(1)}, bf16[4,5,32,256]{3,2,1,0:T(8,128)(2,1)S(1)}, u32[]{:S(2)}, u32[]{:S(2)}) collective-permute-start(bf16[4,5,32,256]{3,2,1,0:T(8,128)(2,1)S(1)} %get-tuple-element.20), channel_id=1, source_target_pairs={{0,2},{2,0},{4,6},{6,4},{1,3},{3,1},{5,7},{7,5},{8,10},{10,8},{12,... | collective-permute-start | bytes 983048 | tf_op jit(solution)/shard_map/halos/ppermute | solution.py:412
  5.5 14.8 %collective-permute-start.5 = (bf16[4,5,32,256]{3,2,1,0:T(8,128)(2,1)S(1)}, bf16[4,5,32,256]{3,2,1,0:T(8,128)(2,1)S(1)}, u32[]{:S(2)}, u32[]{:S(2)}) collective-permute-start(bf16[4,5,32,256]{3,2,1,0:T(8,128)(2,1)S(1)} %get-tuple-element.21), channel_id=1, source_target_pairs={{2,4},{4,2},{3,5},{5,3},{10,12},{12,10},{11,13},{13,11},{18,20},{2... | collective-permute-start | bytes 983048 | tf_op jit(solution)/shard_map/halos/ppermute | solution.py:413
  8.1 11.8 %collective-permute-start.2 = (f32[40,256]{1,0:T(8,128)S(1)}, f32[40,256]{1,0:T(8,128)S(1)}, u32[]{:S(2)}, u32[]{:S(2)}) collective-permute-start(f32[40,256]{1,0:T(8,128)S(1)} %get-tuple-element.25), channel_id=1, source_target_pairs={{8,16},{24,32},{40,48},{56,64},{72,80},{88,96},{104,112},{120,128}... | collective-permute-start | bytes 122888 | tf_op jit(solution)/shard_map/halos/ppermute | solution.py:410
  16.2 1.3 %copy-start.1 = (f32[4,5,2,32,256]{4,3,2,1,0:T(8,128)S(1)}, f32[4,5,2,32,256]{4,3,2,1,0:T(8,128)}, u32[]{:S(2)}) copy-start(f32[4,5,2,32,256]{4,3,2,1,0:T(8,128)} %refs_0_.1) | copy-start | bytes 3932164
  16.2 1.8 %copy-start.2 = (bf16[2,5,5,2,32,256]{5,4,3,2,1,0:T(8,128)(2,1)S(1)}, bf16[2,5,5,2,32,256]{5,4,3,2,1,0:T(8,128)(2,1)}, u32[]{:S(2)}) copy-start(bf16[2,5,5,2,32,256]{5,4,3,2,1,0:T(8,128)(2,1)} %refs_2_.3) | copy-start | bytes 4915204
  16.2 1.8 %copy-start.3 = (f32[2,32,256]{2,1,0:T(8,128)S(1)}, f32[2,32,256]{2,1,0:T(8,128)}, u32[]{:S(2)}) copy-start(f32[2,32,256]{2,1,0:T(8,128)} %refs_3_.9) | copy-start | bytes 196612
  16.2 1.8 %copy-start.4 = (f32[2,32,256]{2,1,0:T(8,128)S(1)}, f32[2,32,256]{2,1,0:T(8,128)}, u32[]{:S(2)}) copy-start(f32[2,32,256]{2,1,0:T(8,128)} %refs_4_.9) | copy-start | bytes 196612
  16.2 4.1 %collective-permute-start.3 = (f32[40,256]{1,0:T(8,128)S(1)}, f32[40,256]{1,0:T(8,128)S(1)}, u32[]{:S(2)}, u32[]{:S(2)}) collective-permute-start(f32[40,256]{1,0:T(8,128)S(1)} %get-tuple-element.26), channel_id=1, source_target_pairs={{0,8},{8,0},{16,24},{24,16},{32,40},{40,32},{48,56},{56,48},{64,72... | collective-permute-start | bytes 122888 | tf_op jit(solution)/shard_map/halos/ppermute | solution.py:411
  20.3 8.7 %copy-start.6 = (f32[4,5,1024]{2,0,1:T(4,128)S(1)}, f32[4,5,1024]{2,0,1:T(4,128)}, u32[]{:S(2)}) copy-start(f32[4,5,1024]{2,0,1:T(4,128)} %param.13) | copy-start | bytes 245764
  20.3 8.7 %copy-start.7 = (s32[1,1024]{1,0:T(1,128)S(1)}, s32[1,1024]{1,0:T(1,128)}, u32[]{:S(2)}) copy-start(s32[1,1024]{1,0:T(1,128)} %cells_ref.3) | copy-start | bytes 12292
  21.7 11.3 %collective-permute-start.8 = (bf16[4,5,32,256]{3,2,1,0:T(8,128)(2,1)S(1)}, bf16[4,5,32,256]{3,2,1,0:T(8,128)(2,1)S(1)}, u32[]{:S(2)}, u32[]{:S(2)}) collective-permute-start(bf16[4,5,32,256]{3,2,1,0:T(8,128)(2,1)S(1)} %get-tuple-element.30), channel_id=1, source_target_pairs={{0,2},{2,0},{4,6},{6,4},{1,3},{3,1},{5,7},{7,5},{8,10},{10,8},{12,... | collective-permute-start | bytes 983048 | tf_op jit(solution)/shard_map/halos/ppermute | solution.py:412
  21.8 11.2 %collective-permute-start.9 = (bf16[4,5,32,256]{3,2,1,0:T(8,128)(2,1)S(1)}, bf16[4,5,32,256]{3,2,1,0:T(8,128)(2,1)S(1)}, u32[]{:S(2)}, u32[]{:S(2)}) collective-permute-start(bf16[4,5,32,256]{3,2,1,0:T(8,128)(2,1)S(1)} %get-tuple-element.31), channel_id=1, source_target_pairs={{2,4},{4,2},{3,5},{5,3},{10,12},{12,10},{11,13},{13,11},{18,20},{2... | collective-permute-start | bytes 983048 | tf_op jit(solution)/shard_map/halos/ppermute | solution.py:413
  23.8 8.1 %collective-permute-start.6 = (f32[40,256]{1,0:T(8,128)S(1)}, f32[40,256]{1,0:T(8,128)S(1)}, u32[]{:S(2)}, u32[]{:S(2)}) collective-permute-start(f32[40,256]{1,0:T(8,128)S(1)} %get-tuple-element.28), channel_id=1, source_target_pairs={{8,16},{24,32},{40,48},{56,64},{72,80},{88,96},{104,112},{120,128}... | collective-permute-start | bytes 122888 | tf_op jit(solution)/shard_map/halos/ppermute | solution.py:410
  29.0 4.0 %collective-permute-start.7 = (f32[40,256]{1,0:T(8,128)S(1)}, f32[40,256]{1,0:T(8,128)S(1)}, u32[]{:S(2)}, u32[]{:S(2)}) collective-permute-start(f32[40,256]{1,0:T(8,128)S(1)} %get-tuple-element.29), channel_id=1, source_target_pairs={{0,8},{8,0},{16,24},{24,16},{32,40},{40,32},{48,56},{56,48},{64,72... | collective-permute-start | bytes 122888 | tf_op jit(solution)/shard_map/halos/ppermute | solution.py:411
  33.8 1.2 %collective-permute-start.10 = (f32[4,128]{1,0:T(4,128)S(1)}, f32[4,128]{1,0:T(4,128)S(1)}, u32[]{:S(2)}, u32[]{:S(2)}) collective-permute-start(f32[4,128]{1,0:T(4,128)S(1)} %surface.1.own_ref), channel_id=1, source_target_pairs={{0,1},{1,0},{2,3},{3,2},{4,5},{5,4},{6,7},{7,6},{8,9},{9,8},{10,11... | collective-permute-start | bytes 6152 | tf_op jit(solution)/shard_map/share_sensitivities/ppermute | solution.py:472
  35.6 16.3 %all-to-all-start = ((f32[32,4,128]{2,1,0:T(4,128)}), f32[32,4,128]{2,1,0:T(4,128)S(1)}, u32[]{:S(2)}, u32[]{:S(2)}) async-start(f32[32,4,128]{2,1,0:T(4,128)} %get-tuple-element.37), calls=%async_computation | async-start | bytes 131072 | tf_op jit(solution)/shard_map/share_sensitivities/all_to_all | solution.py:482

commit v8 on v7

--- a/solution.py
+++ b/solution.py
@@ -13,6 +13,7 @@
 F32 = jnp.float32
 BF16 = jnp.bfloat16
 VMEM = pl.BlockSpec(memory_space=pltpu.VMEM)
+ANY = pl.BlockSpec(memory_space=pl.ANY)
 SMEM = pl.BlockSpec(memory_space=pltpu.SMEM)
 
 
@@ -24,7 +25,7 @@
     return 0.5 * (-1) ** offset * math.cos(angle) / math.sin(angle)
 
 
-def call(kernel, outs, args, specs, mib, flops, name):
+def call(kernel, outs, args, specs, mib, flops, name, scratch=()):
     nbytes = sum(a.size * a.dtype.itemsize for a in args) + sum(
         math.prod(o.shape) * o.dtype.itemsize for o in outs
     )
@@ -33,6 +34,7 @@
         out_shape=outs,
         in_specs=specs,
         out_specs=[VMEM] * len(outs),
+        scratch_shapes=scratch,
         compiler_params=pltpu.CompilerParams(vmem_limit_bytes=mib << 20),
         cost_estimate=pl.CostEstimate(
             flops=flops, bytes_accessed=nbytes, transcendentals=0
@@ -77,37 +79,61 @@
                 inner_ref[here, :] = edge_row(ids_ref, f_ref, t, v, i, False)
 
 
-def prepare_kernel(ids_ref, f_ref, a_ref, b_ref, outer_ref, inner_ref):
+def prepare_kernel(ids_ref, from_ref, a_ref, b_ref, outer_ref, inner_ref, f_ref, loads):
+    nt, nv = f_ref.shape[:2]
+    load = [
+        pltpu.make_async_copy(from_ref.at[t], f_ref.at[t], loads.at[t])
+        for t in range(nt)
+    ]
+    for copy in load:
+        copy.start()
+    for t in range(nt):
+        load[t].wait()
+
+        def run(layer_a, layer_b):
+            for v in range(nv):
+                a_ref[t, v] = f_ref[t, v, layer_a].astype(BF16)
+                b_ref[t, v] = f_ref[t, v, layer_b].astype(BF16)
+
+        by_parity(ids_ref, run)
     pack_rows(ids_ref, f_ref, outer_ref, inner_ref)
-    by_parity(ids_ref, functools.partial(pack_layers, f_ref, a_ref, b_ref))
-
-
-def rhs_kernel(ids_ref, f_ref, src_ref, pa_ref, pb_ref, out_ref):
+
+
+def rhs_kernel(f_ref, from_src_ref, from_far_ref, out_ref, src_ref, far_ref, loads):
     nt, nv, ni, nj, nk = f_ref.shape
-
-    def run(layer_a, layer_b):
-        for layer, other in ((layer_a, pa_ref), (layer_b, pb_ref)):
-
-            def one(v, carry):
-                for j in range(0, nj, 16):
-                    rows = slice(j, j + 16)
-                    own = [
-                        f_ref[t, v, layer, rows, :].astype(BF16).astype(F32)
-                        for t in range(nt)
-                    ]
-                    far = [other[t, v, rows, :].astype(F32) for t in range(nt)]
-                    times = own + far
-                    for b in range(nt):
-                        total = src_ref[b, v, layer, rows, :]
-                        for n in range(1, NT // 2):
-                            diff = times[(b + n) % NT] - times[(b - n) % NT]
-                            total = total - derivative(n) * diff
-                        out_ref[b, v, layer, rows, :] = total
-                return carry
-
-            lax.fori_loop(0, nv, one, 0)
-
-    by_parity(ids_ref, run)
+    load = [
+        [
+            pltpu.make_async_copy(come.at[:, v], ref.at[:, v], loads.at[2 * v + at])
+            for at, (come, ref) in enumerate(
+                ((from_src_ref, src_ref), (from_far_ref, far_ref))
+            )
+        ]
+        for v in range(nv)
+    ]
+    for pair in load:
+        for copy in pair:
+            copy.start()
+    for v in range(nv):
+        for copy in load[v]:
+            copy.wait()
+
+        def one(i, carry):
+            for j in range(0, nj, 16):
+                rows = slice(j, j + 16)
+                times = [
+                    ref[t, v, i, rows, :].astype(BF16).astype(F32)
+                    for ref in (f_ref, far_ref)
+                    for t in range(nt)
+                ]
+                for b in range(nt):
+                    total = src_ref[b, v, i, rows, :]
+                    for n in range(1, NT // 2):
+                        diff = times[(b + n) % NT] - times[(b - n) % NT]
+                        total = total - derivative(n) * diff
+                    out_ref[b, v, i, rows, :] = total
+            return carry
+
+        lax.fori_loop(0, ni, one, 0)
 
 
 def shifted(f_ref, t, u, i, j, lanes, rows_id):
@@ -413,21 +439,35 @@
                 lax.ppermute(b, "cell", odd),
             )
 
+    in_hbm = functools.partial(
+        pltpu.with_memory_space_constraint, memory_space=pltpu.HBM
+    )
+    with jax.named_scope("other_times"):
+        far = lax.ppermute(start, "tm", swap)
     packed = call(
-        prepare_kernel, sends, (ids, start), [SMEM, VMEM], 4, 10**6, "prepare"
-    )
-    with jax.named_scope("other_times"):
-        pa = lax.ppermute(packed[0], "tm", swap)
-        pb = lax.ppermute(packed[1], "tm", swap)
+        prepare_kernel,
+        sends,
+        (ids, in_hbm(start)),
+        [SMEM, ANY],
+        8,
+        10**6,
+        "prepare",
+        scratch=[pltpu.VMEM(start.shape, F32), pltpu.SemaphoreType.DMA((nt,))],
+    )
     halos = exchange(*packed)
     rhs = call(
         rhs_kernel,
         [field_like],
-        (ids, start, source, pa, pb),
-        [SMEM] + [VMEM] * 4,
-        4,
+        (start, in_hbm(source), in_hbm(far)),
+        [VMEM, ANY, ANY],
+        8,
         10**7,
         "rhs",
+        scratch=[
+            pltpu.VMEM(start.shape, F32),
+            pltpu.VMEM(start.shape, F32),
+            pltpu.SemaphoreType.DMA((2 * nv,)),
+        ],
     )[0]
     ordered = call(
         order_kernel,

time: 53.5 us -> 53.9 us (level)
  Pallas kernels: 13.2 us -> 15.4 us
  local copies, waits for them, and re-layouts: 1.92 us -> 0.22 us
    pallas_call x11, Pallas kernels: 13.2 us -> 15.4 us  [call(): pl.pallas_call(kernel, out_shape=outs, in_specs=specs, out_specs=[VMEM] *...]
    unnamed x16 -> x12, local copies, waits for them, and re-layouts: 1.92 us -> 0.22 us
  transfers between devices with their start and end apart: 12 -> 11, of which waited for: 4 -> 3; matrix products, arithmetic and copies ran while one was open for 0% -> 0% of each run, Pallas kernels for 16% -> 21%
where the time goes in v8:
time: 53.9 us; the launch traced here: 53.6 us
  starting transfers between devices  27.6 us (51%)
  Pallas kernels  15.4 us (29%)
  waiting for transfers between devices  9.57 us (18%)
  between operations  0.83 us (2%)
    pallas_call x11, Pallas kernels, call(): pl.pallas_call(kernel, out_shape=outs, in_specs=specs, out_specs=[VMEM] *...  15.4 us
    ppermute x2, starting transfers between devices, exchange(): lax.ppermute(outer, 'passage', across)  13.8 us
    all_to_all x1, waiting for transfers between devices, body(): gathered = lax.all_to_all(sens, 'passage', 0, 0, tiled=True)  7.21 us
    all_to_all x1, starting transfers between devices, body(): gathered = lax.all_to_all(sens, 'passage', 0, 0, tiled=True)  6.73 us
    ppermute x2, starting transfers between devices, exchange(): lax.ppermute(b, 'cell', odd)  4.49 us
    ppermute x2, starting transfers between devices, exchange(): lax.ppermute(a, 'cell', even)  2.37 us
    ppermute x2, waiting for transfers between devices, exchange(): lax.ppermute(inner, 'passage', within)  1.21 us
    ppermute x1, waiting for transfers between devices, body(): other = lax.ppermute(sens, 'tm', swap)  1.14 us
  transfers between devices with their start and end apart: 11, of which 3 were waited for; matrix products, arithmetic and copies ran while one was open for 0% of the time, Pallas kernels for 21%

profile of v8, /device:TPU:8, one launch (start us, length us, event | category | flops | bytes accessed | tf_op | source)
XLA Modules:
  0.0 53.6 jit_solution(16936611561180972755)
XLA Ops:
  0.6 0.0 copy-start
  0.6 0.1 collective-permute-start
  0.8 0.1 pad_add_fusion.ids_ref
  0.8 1.9 %prepare.1 = (bf16[4,5,32,256]{3,2,1,0:T(8,128)(2,1)S(1)}, bf16[4,5,32,256]{3,2,1,0:T(8,128)(2,1)S(1)}, f32[40,256]{1,0:T(8,128)S(1)}, f32[40,256]{1,0:T(8,128)S(1)}) custom-call(s32[2]{0:T(128)S(1)} %pad_add_fusion.ids_ref, f32[4,5,2,32,256]{4,3,2,1,0:T(8,128)} %from_ref.1), custom_call_target="tpu_custom_call" | custom-call | flops 1000000 | bytes 2048008 | tf_op jit(solution)/shard_map/prepare/pallas_call | solution.py:32
  2.7 2.3 %collective-permute-start.3 = (bf16[4,5,32,256]{3,2,1,0:T(8,128)(2,1)S(1)}, bf16[4,5,32,256]{3,2,1,0:T(8,128)(2,1)S(1)}, u32[]{:S(2)}, u32[]{:S(2)}) collective-permute-start(bf16[4,5,32,256]{3,2,1,0:T(8,128)(2,1)S(1)} %get-tuple-element.25), channel_id=1, source_target_pairs={{0,2},{2,0},{4,6},{6,4},{1,3},{3,1},{5,7},{7,5},{8,10},{10,8},{12,... | collective-permute-start | bytes 983048 | tf_op jit(solution)/shard_map/halos/ppermute | solution.py:438
  5.0 2.6 %collective-permute-start.4 = (bf16[4,5,32,256]{3,2,1,0:T(8,128)(2,1)S(1)}, bf16[4,5,32,256]{3,2,1,0:T(8,128)(2,1)S(1)}, u32[]{:S(2)}, u32[]{:S(2)}) collective-permute-start(bf16[4,5,32,256]{3,2,1,0:T(8,128)(2,1)S(1)} %get-tuple-element.26), channel_id=1, source_target_pairs={{2,4},{4,2},{3,5},{5,3},{10,12},{12,10},{11,13},{13,11},{18,20},{2... | collective-permute-start | bytes 983048 | tf_op jit(solution)/shard_map/halos/ppermute | solution.py:439
  7.6 8.1 %collective-permute-start.1 = (f32[40,256]{1,0:T(8,128)S(1)}, f32[40,256]{1,0:T(8,128)S(1)}, u32[]{:S(2)}, u32[]{:S(2)}) collective-permute-start(f32[40,256]{1,0:T(8,128)S(1)} %get-tuple-element.23), channel_id=1, source_target_pairs={{8,16},{24,32},{40,48},{56,64},{72,80},{88,96},{104,112},{120,128}... | collective-permute-start | bytes 122888 | tf_op jit(solution)/shard_map/halos/ppermute | solution.py:436
  15.7 0.0 copy-start.1
  15.7 0.0 copy-start.2
  15.7 0.0 copy-start.3
  15.7 0.0 collective-permute-start.2
  15.7 0.0 collective-permute-done.from_far_ref
  15.8 0.0 copy-done
  15.8 2.0 %rhs.1.refs_1_ = f32[4,5,2,32,256]{4,3,2,1,0:T(8,128)S(1)} custom-call(f32[4,5,2,32,256]{4,3,2,1,0:T(8,128)S(1)} %copy-done, f32[4,5,2,32,256]{4,3,2,1,0:T(8,128)} %from_src_ref.1, f32[4,5,2,32,256]{4,3,2,1,0:T(8,128)} %collective-permute-done.from_far_ref), custom_call_target="tpu_custom_call" | custom-call | flops 10000000 | bytes 5242880 | tf_op jit(solution)/shard_map/rhs/pallas_call | solution.py:32
  17.8 0.2 copy-done.1
  17.9 0.0 copy-done.2
  17.9 0.0 copy-done.3
  17.9 1.8 %first_local.1 = (f32[4,5,2,32,256]{4,3,2,1,0:T(8,128)S(1)}, bf16[5,5,32,256]{3,2,1,0:T(8,128)(2,1)S(1)}, bf16[5,5,2,16,256]{4,3,2,1,0:T(8,128)(2,1)S(1)}) custom-call(f32[4,5,2,32,256]{4,3,2,1,0:T(8,128)S(1)} %copy-done, f32[4,5,2,32,256]{4,3,2,1,0:T(8,128)S(1)} %rhs.1.refs_1_, bf16[2,5,5,2,32,256]{5,4,3,2,1,0:T(8,128)(2,1)S(1)} %copy-done.1, ...), custom_call_target="tpu_custom_call" | custom-call | flops 20000000 | bytes 6520832 | tf_op jit(solution)/shard_map/first_local/pallas_call | solution.py:32
  19.8 0.0 collective-permute-done.1.refs_5_
  19.8 0.0 collective-permute-done.2.refs_6_
  19.8 0.0 collective-permute-done.3.refs_7_
  19.8 0.0 collective-permute-done.4.refs_8_
  19.8 0.0 copy-start.4
  19.8 0.0 copy-start.5
  19.8 1.4 %first_finish.1 = (f32[4,5,2,32,256]{4,3,2,1,0:T(8,128)S(1)}, bf16[4,5,32,256]{3,2,1,0:T(8,128)(2,1)S(1)}, bf16[4,5,32,256]{3,2,1,0:T(8,128)(2,1)S(1)}, f32[40,256]{1,0:T(8,128)S(1)}, f32[40,256]{1,0:T(8,128)S(1)}) custom-call(s32[2]{0:T(128)S(1)} %pad_add_fusion.ids_ref, f32[4,5,2,32,256]{4,3,2,1,0:T(8,128)S(1)} %get-tuple-element.20.refs_0_, ...), custom_call_target="tpu_custom_call" | custom-call | flops 10000000 | bytes 5046280 | tf_op jit(solution)/shard_map/first_finish/pallas_call | solution.py:32
  21.2 0.1 collective-permute-start.7
  21.3 1.9 %collective-permute-start.8 = (bf16[4,5,32,256]{3,2,1,0:T(8,128)(2,1)S(1)}, bf16[4,5,32,256]{3,2,1,0:T(8,128)(2,1)S(1)}, u32[]{:S(2)}, u32[]{:S(2)}) collective-permute-start(bf16[4,5,32,256]{3,2,1,0:T(8,128)(2,1)S(1)} %get-tuple-element.31), channel_id=1, source_target_pairs={{2,4},{4,2},{3,5},{5,3},{10,12},{12,10},{11,13},{13,11},{18,20},{2... | collective-permute-start | bytes 983048 | tf_op jit(solution)/shard_map/halos/ppermute | solution.py:439
  23.3 5.7 %collective-permute-start.5 = (f32[40,256]{1,0:T(8,128)S(1)}, f32[40,256]{1,0:T(8,128)S(1)}, u32[]{:S(2)}, u32[]{:S(2)}) collective-permute-start(f32[40,256]{1,0:T(8,128)S(1)} %get-tuple-element.28), channel_id=1, source_target_pairs={{8,16},{24,32},{40,48},{56,64},{72,80},{88,96},{104,112},{120,128}... | collective-permute-start | bytes 122888 | tf_op jit(solution)/shard_map/halos/ppermute | solution.py:436
  28.9 0.0 collective-permute-start.6
  28.9 0.0 copy-done.4
  28.9 0.0 copy-done.5
  28.9 1.0 %order.1.refs_9_ = f32[20,512]{1,0:T(8,128)S(1)} custom-call(s32[2]{0:T(128)S(1)} %pad_add_fusion.ids_ref, s32[1,1024]{1,0:T(1,128)S(1)} %copy-done.5, f32[5,4,1024]{2,1,0:T(4,128)S(1)} %bitcast.4), custom_call_target="tpu_custom_call" | custom-call | flops 1000000 | bytes 126984 | tf_op jit(solution)/shard_map/order/pallas_call | solution.py:32
  29.9 1.8 %second_local.1.refs_0_ = f32[4,5,2,32,256]{4,3,2,1,0:T(8,128)S(1)} custom-call(f32[4,5,2,32,256]{4,3,2,1,0:T(8,128)S(1)} %get-tuple-element.27.refs_0_, f32[4,5,2,32,256]{4,3,2,1,0:T(8,128)S(1)} %rhs.1.refs_1_, bf16[2,5,5,2,32,256]{5,4,3,2,1,0:T(8,128)(2,1)S(1)} %copy-done.1, f32[2,32,256]{2,1,0:T(8,128)S(1)} %copy-done.2, f32[2,32,256]{2,1,0:T(8,128)S(1)} %copy-done.3), custom_call_target="tpu_custom_call" | custom-call | flops 20000000 | bytes 5701632 | tf_op jit(solution)/shard_map/second_local/pallas_call | solution.py:32
  31.7 0.0 collective-permute-done.5.refs_5_
  31.7 1.2 %collective-permute-done.6.refs_6_ = f32[40,256]{1,0:T(8,128)S(1)} collective-permute-done((f32[40,256]{1,0:T(8,128)S(1)}, f32[40,256]{1,0:T(8,128)S(1)}, u32[]{:S(2)}, u32[]{:S(2)}) %collective-permute-start.6) | collective-permute-done | bytes 40992 | tf_op jit(solution)/shard_map/halos/ppermute | solution.py:437
  32.9 0.0 collective-permute-done.7.refs_7_
  32.9 0.0 collective-permute-done.8.refs_8_
  32.9 0.7 %surface.1.own_ref = f32[4,128]{1,0:T(4,128)S(1)} custom-call(s32[2]{0:T(128)S(1)} %pad_add_fusion.ids_ref, f32[4,5,2,32,256]{4,3,2,1,0:T(8,128)S(1)} %second_local.1.refs_0_, bf16[5,5,32,256]{3,2,1,0:T(8,128)(2,1)S(1)} %get-tuple-element.21.refs_1_, bf16[5,5,2,16,256]{4,3,2,1,0:T(8,128)(2,1)S(1)} %get-tuple-element.22.refs_2_, f32[2,32,256]{2,1,0:T(8,128)S(1)} %copy-done.2, ...), custom_call_target="tpu_custom_call" | custom-call | flops 10000000 | bytes 3041288 | tf_op jit(solution)/shard_map/surface/pallas_call | solution.py:32
  33.7 0.1 collective-permute-start.9
  33.8 1.1 %collective-permute-done.9.other_ref = f32[4,128]{1,0:T(4,128)S(1)} collective-permute-done((f32[4,128]{1,0:T(4,128)S(1)}, f32[4,128]{1,0:T(4,128)S(1)}, u32[]{:S(2)}, u32[]{:S(2)}) %collective-permute-start.9) | collective-permute-done | bytes 2080 | tf_op jit(solution)/shard_map/share_sensitivities/ppermute | solution.py:512
  34.9 0.6 %share.1 = (f32[32,4,128]{2,1,0:T(4,128)}, f32[8,128]{1,0:T(8,128)S(1)}) custom-call(f32[4,128]{1,0:T(4,128)S(1)} %surface.1.own_ref, f32[4,128]{1,0:T(4,128)S(1)} %collective-permute-done.9.other_ref), custom_call_target="tpu_custom_call" | custom-call | flops 10000 | bytes 73728 | tf_op jit(solution)/shard_map/share_sensitivities/share/pallas_call | solution.py:32
  35.6 6.7 %all-to-all-start = ((f32[32,4,128]{2,1,0:T(4,128)}), f32[32,4,128]{2,1,0:T(4,128)S(1)}, u32[]{:S(2)}, u32[]{:S(2)}) async-start(f32[32,4,128]{2,1,0:T(4,128)} %get-tuple-element.37), calls=%async_computation | async-start | bytes 131072 | tf_op jit(solution)/shard_map/share_sensitivities/all_to_all | solution.py:522
  42.3 2.3 %second_finish.1 = (f32[4,5,2,32,256]{4,3,2,1,0:T(8,128)}, f32[8,128]{1,0:T(8,128)S(1)}) custom-call(s32[2]{0:T(128)S(1)} %pad_add_fusion.ids_ref, f32[4,5,2,32,256]{4,3,2,1,0:T(8,128)S(1)} %second_local.1.refs_0_, bf16[5,5,32,256]{3,2,1,0:T(8,128)(2,1)S(1)} %get-tuple-element.21.refs_1_, bf16[5,5,2,16,256]{4,3,2,1,0:T(8,128)(2,1)S(1)} %get-tuple-element.22.refs_2_, ...), custom_call_target="tpu_custom_call" | custom-call | flops 10000000 | bytes 4317192 | tf_op jit(solution)/shard_map/second_finish/pallas_call | solution.py:32
  44.6 0.4 tables.1
  45.1 7.2 %all-to-all-done.sens_ref = f32[32,4,128]{2,1,0:T(4,128)S(1)} async-done(((f32[32,4,128]{2,1,0:T(4,128)}), f32[32,4,128]{2,1,0:T(4,128)S(1)}, u32[]{:S(2)}, u32[]{:S(2)}) %all-to-all-start) | async-done | bytes 65568 | tf_op jit(solution)/shard_map/share_sensitivities/all_to_all | solution.py:522
  52.3 1.4 %modes.1 = f32[32,1024]{1,0:T(8,128)} custom-call(bf16[1024,1024]{1,0:T(8,128)(2,1)S(1)} %get-tuple-element.35.chosen_ref, f32[64,32]{1,0:T(8,128)S(1)} %get-tuple-element.36.table_ref, f32[32,4,128]{2,1,0:T(4,128)S(1)} %all-to-all-done.sens_ref), custom_call_target="tpu_custom_call" | custom-call | flops 10000000 | bytes 2301952 | tf_op jit(solution)/shard_map/modes/pallas_call | solution.py:32
Async XLA Ops:
  0.6 15.1 %copy-start = (f32[4,5,2,32,256]{4,3,2,1,0:T(8,128)S(1)}, f32[4,5,2,32,256]{4,3,2,1,0:T(8,128)}, u32[]{:S(2)}) copy-start(f32[4,5,2,32,256]{4,3,2,1,0:T(8,128)} %from_ref.1) | copy-start | bytes 3932164
  0.6 15.1 %collective-permute-start = (f32[4,5,2,32,256]{4,3,2,1,0:T(8,128)}, f32[4,5,2,32,256]{4,3,2,1,0:T(8,128)}, u32[]{:S(2)}, u32[]{:S(2)}) collective-permute-start(f32[4,5,2,32,256]{4,3,2,1,0:T(8,128)} %from_ref.1), channel_id=1, source_target_pairs={{0,1},{1,0},{2,3},{3,2},{4,5},{5,4},{6,7},{7,6},{8,9},{9,8},{10,11... | collective-permute-start | bytes 3932168 | tf_op jit(solution)/shard_map/other_times/ppermute | solution.py:446
  2.7 17.1 %collective-permute-start.3 = (bf16[4,5,32,256]{3,2,1,0:T(8,128)(2,1)S(1)}, bf16[4,5,32,256]{3,2,1,0:T(8,128)(2,1)S(1)}, u32[]{:S(2)}, u32[]{:S(2)}) collective-permute-start(bf16[4,5,32,256]{3,2,1,0:T(8,128)(2,1)S(1)} %get-tuple-element.25), channel_id=1, source_target_pairs={{0,2},{2,0},{4,6},{6,4},{1,3},{3,1},{5,7},{7,5},{8,10},{10,8},{12,... | collective-permute-start | bytes 983048 | tf_op jit(solution)/shard_map/halos/ppermute | solution.py:438
  5.0 14.8 %collective-permute-start.4 = (bf16[4,5,32,256]{3,2,1,0:T(8,128)(2,1)S(1)}, bf16[4,5,32,256]{3,2,1,0:T(8,128)(2,1)S(1)}, u32[]{:S(2)}, u32[]{:S(2)}) collective-permute-start(bf16[4,5,32,256]{3,2,1,0:T(8,128)(2,1)S(1)} %get-tuple-element.26), channel_id=1, source_target_pairs={{2,4},{4,2},{3,5},{5,3},{10,12},{12,10},{11,13},{13,11},{18,20},{2... | collective-permute-start | bytes 983048 | tf_op jit(solution)/shard_map/halos/ppermute | solution.py:439
  7.6 12.2 %collective-permute-start.1 = (f32[40,256]{1,0:T(8,128)S(1)}, f32[40,256]{1,0:T(8,128)S(1)}, u32[]{:S(2)}, u32[]{:S(2)}) collective-permute-start(f32[40,256]{1,0:T(8,128)S(1)} %get-tuple-element.23), channel_id=1, source_target_pairs={{8,16},{24,32},{40,48},{56,64},{72,80},{88,96},{104,112},{120,128}... | collective-permute-start | bytes 122888 | tf_op jit(solution)/shard_map/halos/ppermute | solution.py:436
  15.7 2.2 %copy-start.1 = (bf16[2,5,5,2,32,256]{5,4,3,2,1,0:T(8,128)(2,1)S(1)}, bf16[2,5,5,2,32,256]{5,4,3,2,1,0:T(8,128)(2,1)}, u32[]{:S(2)}) copy-start(bf16[2,5,5,2,32,256]{5,4,3,2,1,0:T(8,128)(2,1)} %refs_2_.3) | copy-start | bytes 4915204
  15.7 2.2 %copy-start.2 = (f32[2,32,256]{2,1,0:T(8,128)S(1)}, f32[2,32,256]{2,1,0:T(8,128)}, u32[]{:S(2)}) copy-start(f32[2,32,256]{2,1,0:T(8,128)} %refs_3_.9) | copy-start | bytes 196612
  15.7 2.2 %copy-start.3 = (f32[2,32,256]{2,1,0:T(8,128)S(1)}, f32[2,32,256]{2,1,0:T(8,128)}, u32[]{:S(2)}) copy-start(f32[2,32,256]{2,1,0:T(8,128)} %refs_4_.9) | copy-start | bytes 196612
  15.7 4.1 %collective-permute-start.2 = (f32[40,256]{1,0:T(8,128)S(1)}, f32[40,256]{1,0:T(8,128)S(1)}, u32[]{:S(2)}, u32[]{:S(2)}) collective-permute-start(f32[40,256]{1,0:T(8,128)S(1)} %get-tuple-element.24), channel_id=1, source_target_pairs={{0,8},{8,0},{16,24},{24,16},{32,40},{40,32},{48,56},{56,48},{64,72... | collective-permute-start | bytes 122888 | tf_op jit(solution)/shard_map/halos/ppermute | solution.py:437
  19.8 9.1 %copy-start.4 = (f32[4,5,1024]{2,0,1:T(4,128)S(1)}, f32[4,5,1024]{2,0,1:T(4,128)}, u32[]{:S(2)}) copy-start(f32[4,5,1024]{2,0,1:T(4,128)} %param.13) | copy-start | bytes 245764
  19.8 9.1 %copy-start.5 = (s32[1,1024]{1,0:T(1,128)S(1)}, s32[1,1024]{1,0:T(1,128)}, u32[]{:S(2)}) copy-start(s32[1,1024]{1,0:T(1,128)} %cells_ref.3) | copy-start | bytes 12292
  21.2 11.7 %collective-permute-start.7 = (bf16[4,5,32,256]{3,2,1,0:T(8,128)(2,1)S(1)}, bf16[4,5,32,256]{3,2,1,0:T(8,128)(2,1)S(1)}, u32[]{:S(2)}, u32[]{:S(2)}) collective-permute-start(bf16[4,5,32,256]{3,2,1,0:T(8,128)(2,1)S(1)} %get-tuple-element.30), channel_id=1, source_target_pairs={{0,2},{2,0},{4,6},{6,4},{1,3},{3,1},{5,7},{7,5},{8,10},{10,8},{12,... | collective-permute-start | bytes 983048 | tf_op jit(solution)/shard_map/halos/ppermute | solution.py:438
  21.3 11.6 %collective-permute-start.8 = (bf16[4,5,32,256]{3,2,1,0:T(8,128)(2,1)S(1)}, bf16[4,5,32,256]{3,2,1,0:T(8,128)(2,1)S(1)}, u32[]{:S(2)}, u32[]{:S(2)}) collective-permute-start(bf16[4,5,32,256]{3,2,1,0:T(8,128)(2,1)S(1)} %get-tuple-element.31), channel_id=1, source_target_pairs={{2,4},{4,2},{3,5},{5,3},{10,12},{12,10},{11,13},{13,11},{18,20},{2... | collective-permute-start | bytes 983048 | tf_op jit(solution)/shard_map/halos/ppermute | solution.py:439
  23.3 8.5 %collective-permute-start.5 = (f32[40,256]{1,0:T(8,128)S(1)}, f32[40,256]{1,0:T(8,128)S(1)}, u32[]{:S(2)}, u32[]{:S(2)}) collective-permute-start(f32[40,256]{1,0:T(8,128)S(1)} %get-tuple-element.28), channel_id=1, source_target_pairs={{8,16},{24,32},{40,48},{56,64},{72,80},{88,96},{104,112},{120,128}... | collective-permute-start | bytes 122888 | tf_op jit(solution)/shard_map/halos/ppermute | solution.py:436
  28.9 4.0 %collective-permute-start.6 = (f32[40,256]{1,0:T(8,128)S(1)}, f32[40,256]{1,0:T(8,128)S(1)}, u32[]{:S(2)}, u32[]{:S(2)}) collective-permute-start(f32[40,256]{1,0:T(8,128)S(1)} %get-tuple-element.29), channel_id=1, source_target_pairs={{0,8},{8,0},{16,24},{24,16},{32,40},{40,32},{48,56},{56,48},{64,72... | collective-permute-start | bytes 122888 | tf_op jit(solution)/shard_map/halos/ppermute | solution.py:437
  33.7 1.2 %collective-permute-start.9 = (f32[4,128]{1,0:T(4,128)S(1)}, f32[4,128]{1,0:T(4,128)S(1)}, u32[]{:S(2)}, u32[]{:S(2)}) collective-permute-start(f32[4,128]{1,0:T(4,128)S(1)} %surface.1.own_ref), channel_id=1, source_target_pairs={{0,1},{1,0},{2,3},{3,2},{4,5},{5,4},{6,7},{7,6},{8,9},{9,8},{10,11... | collective-permute-start | bytes 6152 | tf_op jit(solution)/shard_map/share_sensitivities/ppermute | solution.py:512
  35.6 16.7 %all-to-all-start = ((f32[32,4,128]{2,1,0:T(4,128)}), f32[32,4,128]{2,1,0:T(4,128)S(1)}, u32[]{:S(2)}, u32[]{:S(2)}) async-start(f32[32,4,128]{2,1,0:T(4,128)} %get-tuple-element.37), calls=%async_computation | async-start | bytes 131072 | tf_op jit(solution)/shard_map/share_sensitivities/all_to_all | solution.py:522

commit v9 on v7

--- a/solution.py
+++ b/solution.py
@@ -389,7 +389,8 @@
     nt, nv, ni, nj, nk = start.shape
     ring = lax.axis_size("passage")
     n_cell = lax.axis_size("cell")
-    ids = jnp.stack([lax.axis_index("cell") & 1, lax.axis_index("passage") & 1])
+    parity = 1 - (lax.axis_index("cell") & 1)
+    ids = jnp.stack([parity, lax.axis_index("passage") & 1])
     even = [(c, c ^ 1) for c in range(n_cell)]
     odd = [(c, c + 1) for c in range(1, n_cell - 1, 2)]
     odd += [(b, a) for a, b in odd]
@@ -409,8 +410,8 @@
             return (
                 lax.ppermute(outer, "passage", across),
                 lax.ppermute(inner, "passage", within),
-                lax.ppermute(a, "cell", even),
-                lax.ppermute(b, "cell", odd),
+                lax.ppermute(a, "cell", odd),
+                lax.ppermute(b, "cell", even),
             )
 
     packed = call(

time: 53.5 us -> 54 us (level)
    all_to_all x1, starting transfers between devices: 6.29 us -> 7.48 us  [body(): gathered = lax.all_to_all(sens, 'passage', 0, 0, tiled=True)]
where the time goes in v9:
time: 54 us; the launch traced here: 53.7 us
  starting transfers between devices  27.7 us (51%)
  Pallas kernels  13.2 us (24%)
  waiting for transfers between devices  10 us (19%)
  local copies, waits for them, and re-layouts  1.92 us (4%)
  between operations  0.81 us (2%)
    pallas_call x11, Pallas kernels, call(): pl.pallas_call(kernel, out_shape=outs, in_specs=specs, out_specs=[VMEM] *...  13.2 us
    ppermute x2, starting transfers between devices, exchange(): lax.ppermute(outer, 'passage', across)  13.2 us
    all_to_all x1, starting transfers between devices, body(): gathered = lax.all_to_all(sens, 'passage', 0, 0, tiled=True)  7.48 us
    all_to_all x1, waiting for transfers between devices, body(): gathered = lax.all_to_all(sens, 'passage', 0, 0, tiled=True)  7.21 us
    ppermute x2, starting transfers between devices, exchange(): lax.ppermute(a, 'cell', odd)  5.83 us
    unnamed x16, local copies, waits for them, and re-layouts  1.92 us
    ppermute x2, waiting for transfers between devices, exchange(): lax.ppermute(inner, 'passage', within)  1.62 us
    ppermute x1, waiting for transfers between devices, body(): other = lax.ppermute(sens, 'tm', swap)  1.14 us
  transfers between devices with their start and end apart: 12, of which 4 were waited for; matrix products, arithmetic and copies ran while one was open for 0% of the time, Pallas kernels for 16%

profile of v9, /device:TPU:8, one launch (start us, length us, event | category | flops | bytes accessed | tf_op | source)
XLA Modules:
  0.0 53.7 jit_solution(3145461180930576967)
XLA Ops:
  0.6 0.1 pad_add_fusion.ids_ref
  0.7 0.0 copy-start
  0.7 1.3 %copy-done = f32[4,5,2,32,256]{4,3,2,1,0:T(8,128)S(1)} copy-done((f32[4,5,2,32,256]{4,3,2,1,0:T(8,128)S(1)}, f32[4,5,2,32,256]{4,3,2,1,0:T(8,128)}, u32[]{:S(2)}) %copy-start) | copy-done | bytes 1310744
  2.0 0.0 copy-start.5
  2.0 0.7 %prepare.1 = (bf16[4,5,32,256]{3,2,1,0:T(8,128)(2,1)S(1)}, bf16[4,5,32,256]{3,2,1,0:T(8,128)(2,1)S(1)}, f32[40,256]{1,0:T(8,128)S(1)}, f32[40,256]{1,0:T(8,128)S(1)}) custom-call(s32[2]{0:T(128)S(1)} %pad_add_fusion.ids_ref, f32[4,5,2,32,256]{4,3,2,1,0:T(8,128)S(1)} %copy-done), custom_call_target="tpu_custom_call" | custom-call | flops 1000000 | bytes 2048008 | tf_op jit(solution)/shard_map/prepare/pallas_call | solution.py:31
  2.7 0.1 collective-permute-start
  2.8 0.5 collective-permute-start.1
  3.3 3.5 %collective-permute-start.4 = (bf16[4,5,32,256]{3,2,1,0:T(8,128)(2,1)S(1)}, bf16[4,5,32,256]{3,2,1,0:T(8,128)(2,1)S(1)}, u32[]{:S(2)}, u32[]{:S(2)}) collective-permute-start(bf16[4,5,32,256]{3,2,1,0:T(8,128)(2,1)S(1)} %get-tuple-element.20), channel_id=1, source_target_pairs={{2,4},{4,2},{3,5},{5,3},{10,12},{12,10},{11,13},{13,11},{18,20},{2... | collective-permute-start | bytes 983048 | tf_op jit(solution)/shard_map/halos/ppermute | solution.py:413
  6.8 0.1 collective-permute-start.5
  6.9 8.1 %collective-permute-start.2 = (f32[40,256]{1,0:T(8,128)S(1)}, f32[40,256]{1,0:T(8,128)S(1)}, u32[]{:S(2)}, u32[]{:S(2)}) collective-permute-start(f32[40,256]{1,0:T(8,128)S(1)} %get-tuple-element.25), channel_id=1, source_target_pairs={{8,16},{24,32},{40,48},{56,64},{72,80},{88,96},{104,112},{120,128}... | collective-permute-start | bytes 122888 | tf_op jit(solution)/shard_map/halos/ppermute | solution.py:411
  15.0 0.0 collective-permute-done.pa_ref
  15.0 0.0 copy-start.1
  15.0 0.0 copy-start.2
  15.0 0.0 copy-start.3
  15.0 0.0 copy-start.4
  15.0 0.1 collective-permute-start.3
  15.1 0.0 collective-permute-done.1.pb_ref
  15.1 0.0 copy-done.5
  15.2 1.1 %rhs.1.refs_1_ = f32[4,5,2,32,256]{4,3,2,1,0:T(8,128)S(1)} custom-call(s32[2]{0:T(128)S(1)} %pad_add_fusion.ids_ref, f32[4,5,2,32,256]{4,3,2,1,0:T(8,128)S(1)} %copy-done, f32[4,5,2,32,256]{4,3,2,1,0:T(8,128)S(1)} %copy-done.5, bf16[4,5,32,256]{3,2,1,0:T(8,128)(2,1)S(1)} %collective-permute-done.pa_ref, bf16[4,5,32,256]{3,2,1,0:T(8,128)(2,1)S(1)} %collective-permute-done.1.pb_ref), custom_call_target="tpu_custom_call" | custom-call | flops 10000000 | bytes 4587528 | tf_op jit(solution)/shard_map/rhs/pallas_call | solution.py:31
  16.3 0.1 copy-done.1
  16.3 0.5 copy-done.2
  16.8 0.0 copy-done.3
  16.8 0.0 copy-done.4
  16.8 1.8 %first_local.1 = (f32[4,5,2,32,256]{4,3,2,1,0:T(8,128)S(1)}, bf16[5,5,32,256]{3,2,1,0:T(8,128)(2,1)S(1)}, bf16[5,5,2,16,256]{4,3,2,1,0:T(8,128)(2,1)S(1)}) custom-call(f32[4,5,2,32,256]{4,3,2,1,0:T(8,128)S(1)} %copy-done.1, f32[4,5,2,32,256]{4,3,2,1,0:T(8,128)S(1)} %rhs.1.refs_1_, bf16[2,5,5,2,32,256]{5,4,3,2,1,0:T(8,128)(2,1)S(1)} %copy-done.2, ...), custom_call_target="tpu_custom_call" | custom-call | flops 20000000 | bytes 6520832 | tf_op jit(solution)/shard_map/first_local/pallas_call | solution.py:31
  18.7 0.0 collective-permute-done.2.refs_5_
  18.7 0.4 collective-permute-done.3.refs_6_
  19.1 0.0 collective-permute-done.4.refs_7_
  19.1 0.0 collective-permute-done.5.refs_8_
  19.1 0.0 copy-start.6
  19.1 0.0 copy-start.7
  19.1 1.4 %first_finish.1 = (f32[4,5,2,32,256]{4,3,2,1,0:T(8,128)S(1)}, bf16[4,5,32,256]{3,2,1,0:T(8,128)(2,1)S(1)}, bf16[4,5,32,256]{3,2,1,0:T(8,128)(2,1)S(1)}, f32[40,256]{1,0:T(8,128)S(1)}, f32[40,256]{1,0:T(8,128)S(1)}) custom-call(s32[2]{0:T(128)S(1)} %pad_add_fusion.ids_ref, f32[4,5,2,32,256]{4,3,2,1,0:T(8,128)S(1)} %get-tuple-element.22.refs_0_, ...), custom_call_target="tpu_custom_call" | custom-call | flops 10000000 | bytes 5046280 | tf_op jit(solution)/shard_map/first_finish/pallas_call | solution.py:31
  20.5 2.4 %collective-permute-start.8 = (bf16[4,5,32,256]{3,2,1,0:T(8,128)(2,1)S(1)}, bf16[4,5,32,256]{3,2,1,0:T(8,128)(2,1)S(1)}, u32[]{:S(2)}, u32[]{:S(2)}) collective-permute-start(bf16[4,5,32,256]{3,2,1,0:T(8,128)(2,1)S(1)} %get-tuple-element.30), channel_id=1, source_target_pairs={{2,4},{4,2},{3,5},{5,3},{10,12},{12,10},{11,13},{13,11},{18,20},{2... | collective-permute-start | bytes 983048 | tf_op jit(solution)/shard_map/halos/ppermute | solution.py:413
  22.9 0.3 collective-permute-start.9
  23.2 5.0 %collective-permute-start.6 = (f32[40,256]{1,0:T(8,128)S(1)}, f32[40,256]{1,0:T(8,128)S(1)}, u32[]{:S(2)}, u32[]{:S(2)}) collective-permute-start(f32[40,256]{1,0:T(8,128)S(1)} %get-tuple-element.28), channel_id=1, source_target_pairs={{8,16},{24,32},{40,48},{56,64},{72,80},{88,96},{104,112},{120,128}... | collective-permute-start | bytes 122888 | tf_op jit(solution)/shard_map/halos/ppermute | solution.py:411
  28.3 0.0 collective-permute-start.7
  28.3 0.0 copy-done.6
  28.3 0.0 copy-done.7
  28.3 1.0 %order.1.refs_9_ = f32[20,512]{1,0:T(8,128)S(1)} custom-call(s32[2]{0:T(128)S(1)} %pad_add_fusion.ids_ref, s32[1,1024]{1,0:T(1,128)S(1)} %copy-done.7, f32[5,4,1024]{2,1,0:T(4,128)S(1)} %bitcast.4), custom_call_target="tpu_custom_call" | custom-call | flops 1000000 | bytes 126984 | tf_op jit(solution)/shard_map/order/pallas_call | solution.py:31
  29.3 1.8 %second_local.1.refs_0_ = f32[4,5,2,32,256]{4,3,2,1,0:T(8,128)S(1)} custom-call(f32[4,5,2,32,256]{4,3,2,1,0:T(8,128)S(1)} %get-tuple-element.27.refs_0_, f32[4,5,2,32,256]{4,3,2,1,0:T(8,128)S(1)} %rhs.1.refs_1_, bf16[2,5,5,2,32,256]{5,4,3,2,1,0:T(8,128)(2,1)S(1)} %copy-done.2, f32[2,32,256]{2,1,0:T(8,128)S(1)} %copy-done.3, f32[2,32,256]{2,1,0:T(8,128)S(1)} %copy-done.4), custom_call_target="tpu_custom_call" | custom-call | flops 20000000 | bytes 5701632 | tf_op jit(solution)/shard_map/second_local/pallas_call | solution.py:31
  31.1 0.0 collective-permute-done.6.refs_5_
  31.1 1.2 %collective-permute-done.7.refs_6_ = f32[40,256]{1,0:T(8,128)S(1)} collective-permute-done((f32[40,256]{1,0:T(8,128)S(1)}, f32[40,256]{1,0:T(8,128)S(1)}, u32[]{:S(2)}, u32[]{:S(2)}) %collective-permute-start.7) | collective-permute-done | bytes 40992 | tf_op jit(solution)/shard_map/halos/ppermute | solution.py:412
  32.3 0.0 collective-permute-done.8.refs_7_
  32.3 0.0 collective-permute-done.9.refs_8_
  32.3 0.7 %surface.1.own_ref = f32[4,128]{1,0:T(4,128)S(1)} custom-call(s32[2]{0:T(128)S(1)} %pad_add_fusion.ids_ref, f32[4,5,2,32,256]{4,3,2,1,0:T(8,128)S(1)} %second_local.1.refs_0_, bf16[5,5,32,256]{3,2,1,0:T(8,128)(2,1)S(1)} %get-tuple-element.23.refs_1_, bf16[5,5,2,16,256]{4,3,2,1,0:T(8,128)(2,1)S(1)} %get-tuple-element.24.refs_2_, f32[2,32,256]{2,1,0:T(8,128)S(1)} %copy-done.3, ...), custom_call_target="tpu_custom_call" | custom-call | flops 10000000 | bytes 3041288 | tf_op jit(solution)/shard_map/surface/pallas_call | solution.py:31
  33.0 0.1 collective-permute-start.10
  33.1 1.1 %collective-permute-done.10.other_ref = f32[4,128]{1,0:T(4,128)S(1)} collective-permute-done((f32[4,128]{1,0:T(4,128)S(1)}, f32[4,128]{1,0:T(4,128)S(1)}, u32[]{:S(2)}, u32[]{:S(2)}) %collective-permute-start.10) | collective-permute-done | bytes 2080 | tf_op jit(solution)/shard_map/share_sensitivities/ppermute | solution.py:473
  34.3 0.6 %share.1 = (f32[32,4,128]{2,1,0:T(4,128)}, f32[8,128]{1,0:T(8,128)S(1)}) custom-call(f32[4,128]{1,0:T(4,128)S(1)} %surface.1.own_ref, f32[4,128]{1,0:T(4,128)S(1)} %collective-permute-done.10.other_ref), custom_call_target="tpu_custom_call" | custom-call | flops 10000 | bytes 73728 | tf_op jit(solution)/shard_map/share_sensitivities/share/pallas_call | solution.py:31
  34.9 7.5 %all-to-all-start = ((f32[32,4,128]{2,1,0:T(4,128)}), f32[32,4,128]{2,1,0:T(4,128)S(1)}, u32[]{:S(2)}, u32[]{:S(2)}) async-start(f32[32,4,128]{2,1,0:T(4,128)} %get-tuple-element.37), calls=%async_computation | async-start | bytes 131072 | tf_op jit(solution)/shard_map/share_sensitivities/all_to_all | solution.py:483
  42.4 2.3 %second_finish.1 = (f32[4,5,2,32,256]{4,3,2,1,0:T(8,128)}, f32[8,128]{1,0:T(8,128)S(1)}) custom-call(s32[2]{0:T(128)S(1)} %pad_add_fusion.ids_ref, f32[4,5,2,32,256]{4,3,2,1,0:T(8,128)S(1)} %second_local.1.refs_0_, bf16[5,5,32,256]{3,2,1,0:T(8,128)(2,1)S(1)} %get-tuple-element.23.refs_1_, bf16[5,5,2,16,256]{4,3,2,1,0:T(8,128)(2,1)S(1)} %get-tuple-element.24.refs_2_, ...), custom_call_target="tpu_custom_call" | custom-call | flops 10000000 | bytes 4317192 | tf_op jit(solution)/shard_map/second_finish/pallas_call | solution.py:31
  44.7 0.4 tables.1
  45.2 7.2 %all-to-all-done.sens_ref = f32[32,4,128]{2,1,0:T(4,128)S(1)} async-done(((f32[32,4,128]{2,1,0:T(4,128)}), f32[32,4,128]{2,1,0:T(4,128)S(1)}, u32[]{:S(2)}, u32[]{:S(2)}) %all-to-all-start) | async-done | bytes 65568 | tf_op jit(solution)/shard_map/share_sensitivities/all_to_all | solution.py:483
  52.4 1.4 %modes.1 = f32[32,1024]{1,0:T(8,128)} custom-call(bf16[1024,1024]{1,0:T(8,128)(2,1)S(1)} %get-tuple-element.35.chosen_ref, f32[64,32]{1,0:T(8,128)S(1)} %get-tuple-element.36.table_ref, f32[32,4,128]{2,1,0:T(4,128)S(1)} %all-to-all-done.sens_ref), custom_call_target="tpu_custom_call" | custom-call | flops 10000000 | bytes 2301952 | tf_op jit(solution)/shard_map/modes/pallas_call | solution.py:31
Async XLA Ops:
  0.7 1.3 %copy-start = (f32[4,5,2,32,256]{4,3,2,1,0:T(8,128)S(1)}, f32[4,5,2,32,256]{4,3,2,1,0:T(8,128)}, u32[]{:S(2)}) copy-start(f32[4,5,2,32,256]{4,3,2,1,0:T(8,128)} %refs_0_.1) | copy-start | bytes 3932164
  2.0 13.1 %copy-start.5 = (f32[4,5,2,32,256]{4,3,2,1,0:T(8,128)S(1)}, f32[4,5,2,32,256]{4,3,2,1,0:T(8,128)}, u32[]{:S(2)}) copy-start(f32[4,5,2,32,256]{4,3,2,1,0:T(8,128)} %src_ref.1) | copy-start | bytes 3932164
  2.7 12.3 %collective-permute-start = (bf16[4,5,32,256]{3,2,1,0:T(8,128)(2,1)S(1)}, bf16[4,5,32,256]{3,2,1,0:T(8,128)(2,1)S(1)}, u32[]{:S(2)}, u32[]{:S(2)}) collective-permute-start(bf16[4,5,32,256]{3,2,1,0:T(8,128)(2,1)S(1)} %get-tuple-element.20), channel_id=1, source_target_pairs={{0,1},{1,0},{2,3},{3,2},{4,5},{5,4},{6,7},{7,6},{8,9},{9,8},{10,11... | collective-permute-start | bytes 983048 | tf_op jit(solution)/shard_map/other_times/ppermute | solution.py:421
  2.8 12.3 %collective-permute-start.1 = (bf16[4,5,32,256]{3,2,1,0:T(8,128)(2,1)S(1)}, bf16[4,5,32,256]{3,2,1,0:T(8,128)(2,1)S(1)}, u32[]{:S(2)}, u32[]{:S(2)}) collective-permute-start(bf16[4,5,32,256]{3,2,1,0:T(8,128)(2,1)S(1)} %get-tuple-element.21), channel_id=1, source_target_pairs={{0,1},{1,0},{2,3},{3,2},{4,5},{5,4},{6,7},{7,6},{8,9},{9,8},{10,11... | collective-permute-start | bytes 983048 | tf_op jit(solution)/shard_map/other_times/ppermute | solution.py:422
  3.3 15.8 %collective-permute-start.4 = (bf16[4,5,32,256]{3,2,1,0:T(8,128)(2,1)S(1)}, bf16[4,5,32,256]{3,2,1,0:T(8,128)(2,1)S(1)}, u32[]{:S(2)}, u32[]{:S(2)}) collective-permute-start(bf16[4,5,32,256]{3,2,1,0:T(8,128)(2,1)S(1)} %get-tuple-element.20), channel_id=1, source_target_pairs={{2,4},{4,2},{3,5},{5,3},{10,12},{12,10},{11,13},{13,11},{18,20},{2... | collective-permute-start | bytes 983048 | tf_op jit(solution)/shard_map/halos/ppermute | solution.py:413
  6.8 12.4 %collective-permute-start.5 = (bf16[4,5,32,256]{3,2,1,0:T(8,128)(2,1)S(1)}, bf16[4,5,32,256]{3,2,1,0:T(8,128)(2,1)S(1)}, u32[]{:S(2)}, u32[]{:S(2)}) collective-permute-start(bf16[4,5,32,256]{3,2,1,0:T(8,128)(2,1)S(1)} %get-tuple-element.21), channel_id=1, source_target_pairs={{0,2},{2,0},{4,6},{6,4},{1,3},{3,1},{5,7},{7,5},{8,10},{10,8},{12,... | collective-permute-start | bytes 983048 | tf_op jit(solution)/shard_map/halos/ppermute | solution.py:414
  6.9 11.8 %collective-permute-start.2 = (f32[40,256]{1,0:T(8,128)S(1)}, f32[40,256]{1,0:T(8,128)S(1)}, u32[]{:S(2)}, u32[]{:S(2)}) collective-permute-start(f32[40,256]{1,0:T(8,128)S(1)} %get-tuple-element.25), channel_id=1, source_target_pairs={{8,16},{24,32},{40,48},{56,64},{72,80},{88,96},{104,112},{120,128}... | collective-permute-start | bytes 122888 | tf_op jit(solution)/shard_map/halos/ppermute | solution.py:411
  15.0 1.3 %copy-start.1 = (f32[4,5,2,32,256]{4,3,2,1,0:T(8,128)S(1)}, f32[4,5,2,32,256]{4,3,2,1,0:T(8,128)}, u32[]{:S(2)}) copy-start(f32[4,5,2,32,256]{4,3,2,1,0:T(8,128)} %refs_0_.1) | copy-start | bytes 3932164
  15.0 1.8 %copy-start.2 = (bf16[2,5,5,2,32,256]{5,4,3,2,1,0:T(8,128)(2,1)S(1)}, bf16[2,5,5,2,32,256]{5,4,3,2,1,0:T(8,128)(2,1)}, u32[]{:S(2)}) copy-start(bf16[2,5,5,2,32,256]{5,4,3,2,1,0:T(8,128)(2,1)} %refs_2_.3) | copy-start | bytes 4915204
  15.0 1.8 %copy-start.3 = (f32[2,32,256]{2,1,0:T(8,128)S(1)}, f32[2,32,256]{2,1,0:T(8,128)}, u32[]{:S(2)}) copy-start(f32[2,32,256]{2,1,0:T(8,128)} %refs_3_.9) | copy-start | bytes 196612
  15.0 1.8 %copy-start.4 = (f32[2,32,256]{2,1,0:T(8,128)S(1)}, f32[2,32,256]{2,1,0:T(8,128)}, u32[]{:S(2)}) copy-start(f32[2,32,256]{2,1,0:T(8,128)} %refs_4_.9) | copy-start | bytes 196612
  15.0 4.1 %collective-permute-start.3 = (f32[40,256]{1,0:T(8,128)S(1)}, f32[40,256]{1,0:T(8,128)S(1)}, u32[]{:S(2)}, u32[]{:S(2)}) collective-permute-start(f32[40,256]{1,0:T(8,128)S(1)} %get-tuple-element.26), channel_id=1, source_target_pairs={{0,8},{8,0},{16,24},{24,16},{32,40},{40,32},{48,56},{56,48},{64,72... | collective-permute-start | bytes 122888 | tf_op jit(solution)/shard_map/halos/ppermute | solution.py:412
  19.1 9.2 %copy-start.6 = (f32[4,5,1024]{2,0,1:T(4,128)S(1)}, f32[4,5,1024]{2,0,1:T(4,128)}, u32[]{:S(2)}) copy-start(f32[4,5,1024]{2,0,1:T(4,128)} %param.13) | copy-start | bytes 245764
  19.1 9.2 %copy-start.7 = (s32[1,1024]{1,0:T(1,128)S(1)}, s32[1,1024]{1,0:T(1,128)}, u32[]{:S(2)}) copy-start(s32[1,1024]{1,0:T(1,128)} %cells_ref.3) | copy-start | bytes 12292
  20.5 11.8 %collective-permute-start.8 = (bf16[4,5,32,256]{3,2,1,0:T(8,128)(2,1)S(1)}, bf16[4,5,32,256]{3,2,1,0:T(8,128)(2,1)S(1)}, u32[]{:S(2)}, u32[]{:S(2)}) collective-permute-start(bf16[4,5,32,256]{3,2,1,0:T(8,128)(2,1)S(1)} %get-tuple-element.30), channel_id=1, source_target_pairs={{2,4},{4,2},{3,5},{5,3},{10,12},{12,10},{11,13},{13,11},{18,20},{2... | collective-permute-start | bytes 983048 | tf_op jit(solution)/shard_map/halos/ppermute | solution.py:413
  22.9 9.4 %collective-permute-start.9 = (bf16[4,5,32,256]{3,2,1,0:T(8,128)(2,1)S(1)}, bf16[4,5,32,256]{3,2,1,0:T(8,128)(2,1)S(1)}, u32[]{:S(2)}, u32[]{:S(2)}) collective-permute-start(bf16[4,5,32,256]{3,2,1,0:T(8,128)(2,1)S(1)} %get-tuple-element.31), channel_id=1, source_target_pairs={{0,2},{2,0},{4,6},{6,4},{1,3},{3,1},{5,7},{7,5},{8,10},{10,8},{12,... | collective-permute-start | bytes 983048 | tf_op jit(solution)/shard_map/halos/ppermute | solution.py:414
  23.2 7.9 %collective-permute-start.6 = (f32[40,256]{1,0:T(8,128)S(1)}, f32[40,256]{1,0:T(8,128)S(1)}, u32[]{:S(2)}, u32[]{:S(2)}) collective-permute-start(f32[40,256]{1,0:T(8,128)S(1)} %get-tuple-element.28), channel_id=1, source_target_pairs={{8,16},{24,32},{40,48},{56,64},{72,80},{88,96},{104,112},{120,128}... | collective-permute-start | bytes 122888 | tf_op jit(solution)/shard_map/halos/ppermute | solution.py:411
  28.3 4.0 %collective-permute-start.7 = (f32[40,256]{1,0:T(8,128)S(1)}, f32[40,256]{1,0:T(8,128)S(1)}, u32[]{:S(2)}, u32[]{:S(2)}) collective-permute-start(f32[40,256]{1,0:T(8,128)S(1)} %get-tuple-element.29), channel_id=1, source_target_pairs={{0,8},{8,0},{16,24},{24,16},{32,40},{40,32},{48,56},{56,48},{64,72... | collective-permute-start | bytes 122888 | tf_op jit(solution)/shard_map/halos/ppermute | solution.py:412
  33.0 1.2 %collective-permute-start.10 = (f32[4,128]{1,0:T(4,128)S(1)}, f32[4,128]{1,0:T(4,128)S(1)}, u32[]{:S(2)}, u32[]{:S(2)}) collective-permute-start(f32[4,128]{1,0:T(4,128)S(1)} %surface.1.own_ref), channel_id=1, source_target_pairs={{0,1},{1,0},{2,3},{3,2},{4,5},{5,4},{6,7},{7,6},{8,9},{9,8},{10,11... | collective-permute-start | bytes 6152 | tf_op jit(solution)/shard_map/share_sensitivities/ppermute | solution.py:473
  34.9 17.5 %all-to-all-start = ((f32[32,4,128]{2,1,0:T(4,128)}), f32[32,4,128]{2,1,0:T(4,128)S(1)}, u32[]{:S(2)}, u32[]{:S(2)}) async-start(f32[32,4,128]{2,1,0:T(4,128)} %get-tuple-element.37), calls=%async_computation | async-start | bytes 131072 | tf_op jit(solution)/shard_map/share_sensitivities/all_to_all | solution.py:483

commit v10 on v7

--- a/solution.py
+++ b/solution.py
@@ -24,7 +24,7 @@
     return 0.5 * (-1) ** offset * math.cos(angle) / math.sin(angle)
 
 
-def call(kernel, outs, args, specs, mib, flops, name):
+def call(kernel, outs, args, specs, mib, flops, name, scratch=()):
     nbytes = sum(a.size * a.dtype.itemsize for a in args) + sum(
         math.prod(o.shape) * o.dtype.itemsize for o in outs
     )
@@ -33,6 +33,7 @@
         out_shape=outs,
         in_specs=specs,
         out_specs=[VMEM] * len(outs),
+        scratch_shapes=scratch,
         compiler_params=pltpu.CompilerParams(vmem_limit_bytes=mib << 20),
         cost_estimate=pl.CostEstimate(
             flops=flops, bytes_accessed=nbytes, transcendentals=0
@@ -77,9 +78,25 @@
                 inner_ref[here, :] = edge_row(ids_ref, f_ref, t, v, i, False)
 
 
-def prepare_kernel(ids_ref, f_ref, a_ref, b_ref, outer_ref, inner_ref):
+def prepare_kernel(ids_ref, from_ref, f_ref, a_ref, b_ref, outer_ref, inner_ref, loads):
+    nt, nv = f_ref.shape[:2]
+    pieces = [(t, slice(*v)) for t in range(nt) for v in ((0, 2), (2, nv))]
+    load = [
+        pltpu.make_async_copy(from_ref.at[t, vs], f_ref.at[t, vs], loads.at[n])
+        for n, (t, vs) in enumerate(pieces)
+    ]
+    for copy in load:
+        copy.start()
+    for copy, (t, vs) in zip(load, pieces):
+        copy.wait()
+
+        def run(layer_a, layer_b):
+            for v in range(vs.start, vs.stop):
+                a_ref[t, v] = f_ref[t, v, layer_a].astype(BF16)
+                b_ref[t, v] = f_ref[t, v, layer_b].astype(BF16)
+
+        by_parity(ids_ref, run)
     pack_rows(ids_ref, f_ref, outer_ref, inner_ref)
-    by_parity(ids_ref, functools.partial(pack_layers, f_ref, a_ref, b_ref))
 
 
 def rhs_kernel(ids_ref, f_ref, src_ref, pa_ref, pb_ref, out_ref):
@@ -413,8 +430,15 @@
                 lax.ppermute(b, "cell", odd),
             )
 
-    packed = call(
-        prepare_kernel, sends, (ids, start), [SMEM, VMEM], 4, 10**6, "prepare"
+    start, *packed = call(
+        prepare_kernel,
+        [field_like] + sends,
+        (ids, pltpu.with_memory_space_constraint(start, pltpu.HBM)),
+        [SMEM, pl.BlockSpec(memory_space=pl.ANY)],
+        8,
+        10**6,
+        "prepare",
+        scratch=[pltpu.SemaphoreType.DMA((2 * nt,))],
     )
     with jax.named_scope("other_times"):
         pa = lax.ppermute(packed[0], "tm", swap)

time: 53.5 us -> 53.6 us (level)
  local copies, waits for them, and re-layouts: 1.92 us -> 0.32 us
  Pallas kernels: 13.2 us -> 14.6 us
    unnamed x16 -> x12, local copies, waits for them, and re-layouts: 1.92 us -> 0.32 us
    pallas_call x11, Pallas kernels: 13.2 us -> 14.6 us  [call(): pl.pallas_call(kernel, out_shape=outs, in_specs=specs, out_specs=[VMEM] *...]
where the time goes in v10:
time: 53.6 us; the launch traced here: 53.4 us
  starting transfers between devices  27.3 us (51%)
  Pallas kernels  14.6 us (27%)
  waiting for transfers between devices  10.3 us (19%)
  between operations  0.81 us (2%)
    pallas_call x11, Pallas kernels, call(): pl.pallas_call(kernel, out_shape=outs, in_specs=specs, out_specs=[VMEM] *...  14.6 us
    ppermute x2, starting transfers between devices, exchange(): lax.ppermute(outer, 'passage', across)  13.5 us
    all_to_all x1, waiting for transfers between devices, body(): gathered = lax.all_to_all(sens, 'passage', 0, 0, tiled=True)  7.21 us
    all_to_all x1, starting transfers between devices, body(): gathered = lax.all_to_all(sens, 'passage', 0, 0, tiled=True)  6.29 us
    ppermute x2, starting transfers between devices, exchange(): lax.ppermute(b, 'cell', odd)  4.49 us
    ppermute x2, starting transfers between devices, exchange(): lax.ppermute(a, 'cell', even)  2.28 us
    ppermute x2, waiting for transfers between devices, exchange(): lax.ppermute(inner, 'passage', within)  1.91 us
    ppermute x1, waiting for transfers between devices, body(): other = lax.ppermute(sens, 'tm', swap)  1.14 us
  transfers between devices with their start and end apart: 12, of which 4 were waited for; matrix products, arithmetic and copies ran while one was open for 0% of the time, Pallas kernels for 16%

profile of v10, /device:TPU:8, one launch (start us, length us, event | category | flops | bytes accessed | tf_op | source)
XLA Modules:
  0.0 53.4 jit_solution(8851970946283104525)
XLA Ops:
  0.6 0.0 copy-start.3
  0.6 0.1 pad_add_fusion.ids_ref
  0.7 2.1 %prepare.1 = (f32[4,5,2,32,256]{4,3,2,1,0:T(8,128)S(1)}, bf16[4,5,32,256]{3,2,1,0:T(8,128)(2,1)S(1)}, bf16[4,5,32,256]{3,2,1,0:T(8,128)(2,1)S(1)}, f32[40,256]{1,0:T(8,128)S(1)}, f32[40,256]{1,0:T(8,128)S(1)}) custom-call(s32[2]{0:T(128)S(1)} %pad_add_fusion.ids_ref, f32[4,5,2,32,256]{4,3,2,1,0:T(8,128)} %from_ref.1), custom_call_target="tpu_custom_call" | custom-call | flops 1000000 | bytes 3358728 | tf_op jit(solution)/shard_map/prepare/pallas_call | solution.py:31
  2.8 0.1 collective-permute-start
  2.9 0.5 collective-permute-start.1
  3.4 2.2 %collective-permute-start.4 = (bf16[4,5,32,256]{3,2,1,0:T(8,128)(2,1)S(1)}, bf16[4,5,32,256]{3,2,1,0:T(8,128)(2,1)S(1)}, u32[]{:S(2)}, u32[]{:S(2)}) collective-permute-start(bf16[4,5,32,256]{3,2,1,0:T(8,128)(2,1)S(1)} %get-tuple-element.22), channel_id=1, source_target_pairs={{0,2},{2,0},{4,6},{6,4},{1,3},{3,1},{5,7},{7,5},{8,10},{10,8},{12,... | collective-permute-start | bytes 983048 | tf_op jit(solution)/shard_map/halos/ppermute | solution.py:429
  5.6 2.6 %collective-permute-start.5 = (bf16[4,5,32,256]{3,2,1,0:T(8,128)(2,1)S(1)}, bf16[4,5,32,256]{3,2,1,0:T(8,128)(2,1)S(1)}, u32[]{:S(2)}, u32[]{:S(2)}) collective-permute-start(bf16[4,5,32,256]{3,2,1,0:T(8,128)(2,1)S(1)} %get-tuple-element.23), channel_id=1, source_target_pairs={{2,4},{4,2},{3,5},{5,3},{10,12},{12,10},{11,13},{13,11},{18,20},{2... | collective-permute-start | bytes 983048 | tf_op jit(solution)/shard_map/halos/ppermute | solution.py:430
  8.1 8.1 %collective-permute-start.2 = (f32[40,256]{1,0:T(8,128)S(1)}, f32[40,256]{1,0:T(8,128)S(1)}, u32[]{:S(2)}, u32[]{:S(2)}) collective-permute-start(f32[40,256]{1,0:T(8,128)S(1)} %get-tuple-element.27), channel_id=1, source_target_pairs={{8,16},{24,32},{40,48},{56,64},{72,80},{88,96},{104,112},{120,128}... | collective-permute-start | bytes 122888 | tf_op jit(solution)/shard_map/halos/ppermute | solution.py:427
  16.3 0.0 collective-permute-done.pa_ref
  16.3 0.0 collective-permute-start.3
  16.3 0.0 collective-permute-done.1.pb_ref
  16.3 0.0 copy-done.3
  16.3 0.0 copy-start
  16.3 0.0 copy-start.1
  16.3 0.0 copy-start.2
  16.3 1.1 %rhs.1.refs_1_ = f32[4,5,2,32,256]{4,3,2,1,0:T(8,128)S(1)} custom-call(s32[2]{0:T(128)S(1)} %pad_add_fusion.ids_ref, f32[4,5,2,32,256]{4,3,2,1,0:T(8,128)S(1)} %get-tuple-element.21.f_ref.refs_0_, f32[4,5,2,32,256]{4,3,2,1,0:T(8,128)S(1)} %copy-done.3, bf16[4,5,32,256]{3,2,1,0:T(8,128)(2,1)S(1)} %collective-permute-done.pa_ref, ...), custom_call_target="tpu_custom_call" | custom-call | flops 10000000 | bytes 4587528 | tf_op jit(solution)/shard_map/rhs/pallas_call | solution.py:31
  17.4 0.3 copy-done
  17.7 0.0 copy-done.1
  17.7 0.0 copy-done.2
  17.7 1.8 %first_local.1 = (f32[4,5,2,32,256]{4,3,2,1,0:T(8,128)S(1)}, bf16[5,5,32,256]{3,2,1,0:T(8,128)(2,1)S(1)}, bf16[5,5,2,16,256]{4,3,2,1,0:T(8,128)(2,1)S(1)}) custom-call(f32[4,5,2,32,256]{4,3,2,1,0:T(8,128)S(1)} %get-tuple-element.21.f_ref.refs_0_, f32[4,5,2,32,256]{4,3,2,1,0:T(8,128)S(1)} %rhs.1.refs_1_, bf16[2,5,5,2,32,256]{5,4,3,2,1,0:T(8,128)(2,1)S(1)} %copy-done, ...), custom_call_target="tpu_custom_call" | custom-call | flops 20000000 | bytes 6520832 | tf_op jit(solution)/shard_map/first_local/pallas_call | solution.py:31
  19.6 0.0 collective-permute-done.2.refs_5_
  19.6 0.7 %collective-permute-done.3.refs_6_ = f32[40,256]{1,0:T(8,128)S(1)} collective-permute-done((f32[40,256]{1,0:T(8,128)S(1)}, f32[40,256]{1,0:T(8,128)S(1)}, u32[]{:S(2)}, u32[]{:S(2)}) %collective-permute-start.3) | collective-permute-done | bytes 40992 | tf_op jit(solution)/shard_map/halos/ppermute | solution.py:428
  20.3 0.0 collective-permute-done.4.refs_7_
  20.3 0.0 collective-permute-done.5.refs_8_
  20.3 0.0 copy-start.4
  20.3 0.0 copy-start.5
  20.3 1.4 %first_finish.1 = (f32[4,5,2,32,256]{4,3,2,1,0:T(8,128)S(1)}, bf16[4,5,32,256]{3,2,1,0:T(8,128)(2,1)S(1)}, bf16[4,5,32,256]{3,2,1,0:T(8,128)(2,1)S(1)}, f32[40,256]{1,0:T(8,128)S(1)}, f32[40,256]{1,0:T(8,128)S(1)}) custom-call(s32[2]{0:T(128)S(1)} %pad_add_fusion.ids_ref, f32[4,5,2,32,256]{4,3,2,1,0:T(8,128)S(1)} %get-tuple-element.24.refs_0_, ...), custom_call_target="tpu_custom_call" | custom-call | flops 10000000 | bytes 5046280 | tf_op jit(solution)/shard_map/first_finish/pallas_call | solution.py:31
  21.7 0.1 collective-permute-start.8
  21.8 1.9 %collective-permute-start.9 = (bf16[4,5,32,256]{3,2,1,0:T(8,128)(2,1)S(1)}, bf16[4,5,32,256]{3,2,1,0:T(8,128)(2,1)S(1)}, u32[]{:S(2)}, u32[]{:S(2)}) collective-permute-start(bf16[4,5,32,256]{3,2,1,0:T(8,128)(2,1)S(1)} %get-tuple-element.33), channel_id=1, source_target_pairs={{2,4},{4,2},{3,5},{5,3},{10,12},{12,10},{11,13},{13,11},{18,20},{2... | collective-permute-start | bytes 983048 | tf_op jit(solution)/shard_map/halos/ppermute | solution.py:430
  23.7 5.4 %collective-permute-start.6 = (f32[40,256]{1,0:T(8,128)S(1)}, f32[40,256]{1,0:T(8,128)S(1)}, u32[]{:S(2)}, u32[]{:S(2)}) collective-permute-start(f32[40,256]{1,0:T(8,128)S(1)} %get-tuple-element.30), channel_id=1, source_target_pairs={{8,16},{24,32},{40,48},{56,64},{72,80},{88,96},{104,112},{120,128}... | collective-permute-start | bytes 122888 | tf_op jit(solution)/shard_map/halos/ppermute | solution.py:427
  29.1 0.0 collective-permute-start.7
  29.1 0.0 copy-done.4
  29.1 0.0 copy-done.5
  29.1 1.0 %order.1.refs_9_ = f32[20,512]{1,0:T(8,128)S(1)} custom-call(s32[2]{0:T(128)S(1)} %pad_add_fusion.ids_ref, s32[1,1024]{1,0:T(1,128)S(1)} %copy-done.5, f32[5,4,1024]{2,1,0:T(4,128)S(1)} %bitcast.4), custom_call_target="tpu_custom_call" | custom-call | flops 1000000 | bytes 126984 | tf_op jit(solution)/shard_map/order/pallas_call | solution.py:31
  30.1 1.8 %second_local.1.refs_0_ = f32[4,5,2,32,256]{4,3,2,1,0:T(8,128)S(1)} custom-call(f32[4,5,2,32,256]{4,3,2,1,0:T(8,128)S(1)} %get-tuple-element.29.refs_0_, f32[4,5,2,32,256]{4,3,2,1,0:T(8,128)S(1)} %rhs.1.refs_1_, bf16[2,5,5,2,32,256]{5,4,3,2,1,0:T(8,128)(2,1)S(1)} %copy-done, f32[2,32,256]{2,1,0:T(8,128)S(1)} %copy-done.1, f32[2,32,256]{2,1,0:T(8,128)S(1)} %copy-done.2), custom_call_target="tpu_custom_call" | custom-call | flops 20000000 | bytes 5701632 | tf_op jit(solution)/shard_map/second_local/pallas_call | solution.py:31
  31.9 0.0 collective-permute-done.6.refs_5_
  31.9 1.2 %collective-permute-done.7.refs_6_ = f32[40,256]{1,0:T(8,128)S(1)} collective-permute-done((f32[40,256]{1,0:T(8,128)S(1)}, f32[40,256]{1,0:T(8,128)S(1)}, u32[]{:S(2)}, u32[]{:S(2)}) %collective-permute-start.7) | collective-permute-done | bytes 40992 | tf_op jit(solution)/shard_map/halos/ppermute | solution.py:428
  33.1 0.0 collective-permute-done.8.refs_7_
  33.1 0.0 collective-permute-done.9.refs_8_
  33.1 0.7 %surface.1.own_ref = f32[4,128]{1,0:T(4,128)S(1)} custom-call(s32[2]{0:T(128)S(1)} %pad_add_fusion.ids_ref, f32[4,5,2,32,256]{4,3,2,1,0:T(8,128)S(1)} %second_local.1.refs_0_, bf16[5,5,32,256]{3,2,1,0:T(8,128)(2,1)S(1)} %get-tuple-element.25.refs_1_, bf16[5,5,2,16,256]{4,3,2,1,0:T(8,128)(2,1)S(1)} %get-tuple-element.26.refs_2_, f32[2,32,256]{2,1,0:T(8,128)S(1)} %copy-done.1, ...), custom_call_target="tpu_custom_call" | custom-call | flops 10000000 | bytes 3041288 | tf_op jit(solution)/shard_map/surface/pallas_call | solution.py:31
  33.8 0.1 collective-permute-start.10
  33.9 1.1 %collective-permute-done.10.other_ref = f32[4,128]{1,0:T(4,128)S(1)} collective-permute-done((f32[4,128]{1,0:T(4,128)S(1)}, f32[4,128]{1,0:T(4,128)S(1)}, u32[]{:S(2)}, u32[]{:S(2)}) %collective-permute-start.10) | collective-permute-done | bytes 2080 | tf_op jit(solution)/shard_map/share_sensitivities/ppermute | solution.py:496
  35.1 0.6 %share.1 = (f32[32,4,128]{2,1,0:T(4,128)}, f32[8,128]{1,0:T(8,128)S(1)}) custom-call(f32[4,128]{1,0:T(4,128)S(1)} %surface.1.own_ref, f32[4,128]{1,0:T(4,128)S(1)} %collective-permute-done.10.other_ref), custom_call_target="tpu_custom_call" | custom-call | flops 10000 | bytes 73728 | tf_op jit(solution)/shard_map/share_sensitivities/share/pallas_call | solution.py:31
  35.7 6.3 %all-to-all-start = ((f32[32,4,128]{2,1,0:T(4,128)}), f32[32,4,128]{2,1,0:T(4,128)S(1)}, u32[]{:S(2)}, u32[]{:S(2)}) async-start(f32[32,4,128]{2,1,0:T(4,128)} %get-tuple-element.39), calls=%async_computation | async-start | bytes 131072 | tf_op jit(solution)/shard_map/share_sensitivities/all_to_all | solution.py:506
  42.0 2.3 %second_finish.1 = (f32[4,5,2,32,256]{4,3,2,1,0:T(8,128)}, f32[8,128]{1,0:T(8,128)S(1)}) custom-call(s32[2]{0:T(128)S(1)} %pad_add_fusion.ids_ref, f32[4,5,2,32,256]{4,3,2,1,0:T(8,128)S(1)} %second_local.1.refs_0_, bf16[5,5,32,256]{3,2,1,0:T(8,128)(2,1)S(1)} %get-tuple-element.25.refs_1_, bf16[5,5,2,16,256]{4,3,2,1,0:T(8,128)(2,1)S(1)} %get-tuple-element.26.refs_2_, ...), custom_call_target="tpu_custom_call" | custom-call | flops 10000000 | bytes 4317192 | tf_op jit(solution)/shard_map/second_finish/pallas_call | solution.py:31
  44.3 0.4 tables.1
  44.8 7.2 %all-to-all-done.sens_ref = f32[32,4,128]{2,1,0:T(4,128)S(1)} async-done(((f32[32,4,128]{2,1,0:T(4,128)}), f32[32,4,128]{2,1,0:T(4,128)S(1)}, u32[]{:S(2)}, u32[]{:S(2)}) %all-to-all-start) | async-done | bytes 65568 | tf_op jit(solution)/shard_map/share_sensitivities/all_to_all | solution.py:506
  52.0 1.4 %modes.1 = f32[32,1024]{1,0:T(8,128)} custom-call(bf16[1024,1024]{1,0:T(8,128)(2,1)S(1)} %get-tuple-element.37.chosen_ref, f32[64,32]{1,0:T(8,128)S(1)} %get-tuple-element.38.table_ref, f32[32,4,128]{2,1,0:T(4,128)S(1)} %all-to-all-done.sens_ref), custom_call_target="tpu_custom_call" | custom-call | flops 10000000 | bytes 2301952 | tf_op jit(solution)/shard_map/modes/pallas_call | solution.py:31
Async XLA Ops:
  0.6 15.7 %copy-start.3 = (f32[4,5,2,32,256]{4,3,2,1,0:T(8,128)S(1)}, f32[4,5,2,32,256]{4,3,2,1,0:T(8,128)}, u32[]{:S(2)}) copy-start(f32[4,5,2,32,256]{4,3,2,1,0:T(8,128)} %src_ref.1) | copy-start | bytes 3932164
  2.8 13.5 %collective-permute-start = (bf16[4,5,32,256]{3,2,1,0:T(8,128)(2,1)S(1)}, bf16[4,5,32,256]{3,2,1,0:T(8,128)(2,1)S(1)}, u32[]{:S(2)}, u32[]{:S(2)}) collective-permute-start(bf16[4,5,32,256]{3,2,1,0:T(8,128)(2,1)S(1)} %get-tuple-element.22), channel_id=1, source_target_pairs={{0,1},{1,0},{2,3},{3,2},{4,5},{5,4},{6,7},{7,6},{8,9},{9,8},{10,11... | collective-permute-start | bytes 983048 | tf_op jit(solution)/shard_map/other_times/ppermute | solution.py:444
  2.9 13.4 %collective-permute-start.1 = (bf16[4,5,32,256]{3,2,1,0:T(8,128)(2,1)S(1)}, bf16[4,5,32,256]{3,2,1,0:T(8,128)(2,1)S(1)}, u32[]{:S(2)}, u32[]{:S(2)}) collective-permute-start(bf16[4,5,32,256]{3,2,1,0:T(8,128)(2,1)S(1)} %get-tuple-element.23), channel_id=1, source_target_pairs={{0,1},{1,0},{2,3},{3,2},{4,5},{5,4},{6,7},{7,6},{8,9},{9,8},{10,11... | collective-permute-start | bytes 983048 | tf_op jit(solution)/shard_map/other_times/ppermute | solution.py:445
  3.4 16.9 %collective-permute-start.4 = (bf16[4,5,32,256]{3,2,1,0:T(8,128)(2,1)S(1)}, bf16[4,5,32,256]{3,2,1,0:T(8,128)(2,1)S(1)}, u32[]{:S(2)}, u32[]{:S(2)}) collective-permute-start(bf16[4,5,32,256]{3,2,1,0:T(8,128)(2,1)S(1)} %get-tuple-element.22), channel_id=1, source_target_pairs={{0,2},{2,0},{4,6},{6,4},{1,3},{3,1},{5,7},{7,5},{8,10},{10,8},{12,... | collective-permute-start | bytes 983048 | tf_op jit(solution)/shard_map/halos/ppermute | solution.py:429
  5.6 14.7 %collective-permute-start.5 = (bf16[4,5,32,256]{3,2,1,0:T(8,128)(2,1)S(1)}, bf16[4,5,32,256]{3,2,1,0:T(8,128)(2,1)S(1)}, u32[]{:S(2)}, u32[]{:S(2)}) collective-permute-start(bf16[4,5,32,256]{3,2,1,0:T(8,128)(2,1)S(1)} %get-tuple-element.23), channel_id=1, source_target_pairs={{2,4},{4,2},{3,5},{5,3},{10,12},{12,10},{11,13},{13,11},{18,20},{2... | collective-permute-start | bytes 983048 | tf_op jit(solution)/shard_map/halos/ppermute | solution.py:430
  8.1 11.4 %collective-permute-start.2 = (f32[40,256]{1,0:T(8,128)S(1)}, f32[40,256]{1,0:T(8,128)S(1)}, u32[]{:S(2)}, u32[]{:S(2)}) collective-permute-start(f32[40,256]{1,0:T(8,128)S(1)} %get-tuple-element.27), channel_id=1, source_target_pairs={{8,16},{24,32},{40,48},{56,64},{72,80},{88,96},{104,112},{120,128}... | collective-permute-start | bytes 122888 | tf_op jit(solution)/shard_map/halos/ppermute | solution.py:427
  16.3 4.0 %collective-permute-start.3 = (f32[40,256]{1,0:T(8,128)S(1)}, f32[40,256]{1,0:T(8,128)S(1)}, u32[]{:S(2)}, u32[]{:S(2)}) collective-permute-start(f32[40,256]{1,0:T(8,128)S(1)} %get-tuple-element.28), channel_id=1, source_target_pairs={{0,8},{8,0},{16,24},{24,16},{32,40},{40,32},{48,56},{56,48},{64,72... | collective-permute-start | bytes 122888 | tf_op jit(solution)/shard_map/halos/ppermute | solution.py:428
  16.3 1.4 %copy-start = (bf16[2,5,5,2,32,256]{5,4,3,2,1,0:T(8,128)(2,1)S(1)}, bf16[2,5,5,2,32,256]{5,4,3,2,1,0:T(8,128)(2,1)}, u32[]{:S(2)}) copy-start(bf16[2,5,5,2,32,256]{5,4,3,2,1,0:T(8,128)(2,1)} %refs_2_.3) | copy-start | bytes 4915204
  16.3 1.4 %copy-start.1 = (f32[2,32,256]{2,1,0:T(8,128)S(1)}, f32[2,32,256]{2,1,0:T(8,128)}, u32[]{:S(2)}) copy-start(f32[2,32,256]{2,1,0:T(8,128)} %refs_3_.9) | copy-start | bytes 196612
  16.3 1.4 %copy-start.2 = (f32[2,32,256]{2,1,0:T(8,128)S(1)}, f32[2,32,256]{2,1,0:T(8,128)}, u32[]{:S(2)}) copy-start(f32[2,32,256]{2,1,0:T(8,128)} %refs_4_.9) | copy-start | bytes 196612
  20.3 8.8 %copy-start.4 = (f32[4,5,1024]{2,0,1:T(4,128)S(1)}, f32[4,5,1024]{2,0,1:T(4,128)}, u32[]{:S(2)}) copy-start(f32[4,5,1024]{2,0,1:T(4,128)} %param.13) | copy-start | bytes 245764
  20.3 8.8 %copy-start.5 = (s32[1,1024]{1,0:T(1,128)S(1)}, s32[1,1024]{1,0:T(1,128)}, u32[]{:S(2)}) copy-start(s32[1,1024]{1,0:T(1,128)} %cells_ref.3) | copy-start | bytes 12292
  21.7 11.4 %collective-permute-start.8 = (bf16[4,5,32,256]{3,2,1,0:T(8,128)(2,1)S(1)}, bf16[4,5,32,256]{3,2,1,0:T(8,128)(2,1)S(1)}, u32[]{:S(2)}, u32[]{:S(2)}) collective-permute-start(bf16[4,5,32,256]{3,2,1,0:T(8,128)(2,1)S(1)} %get-tuple-element.32), channel_id=1, source_target_pairs={{0,2},{2,0},{4,6},{6,4},{1,3},{3,1},{5,7},{7,5},{8,10},{10,8},{12,... | collective-permute-start | bytes 983048 | tf_op jit(solution)/shard_map/halos/ppermute | solution.py:429
  21.8 11.3 %collective-permute-start.9 = (bf16[4,5,32,256]{3,2,1,0:T(8,128)(2,1)S(1)}, bf16[4,5,32,256]{3,2,1,0:T(8,128)(2,1)S(1)}, u32[]{:S(2)}, u32[]{:S(2)}) collective-permute-start(bf16[4,5,32,256]{3,2,1,0:T(8,128)(2,1)S(1)} %get-tuple-element.33), channel_id=1, source_target_pairs={{2,4},{4,2},{3,5},{5,3},{10,12},{12,10},{11,13},{13,11},{18,20},{2... | collective-permute-start | bytes 983048 | tf_op jit(solution)/shard_map/halos/ppermute | solution.py:430
  23.7 8.2 %collective-permute-start.6 = (f32[40,256]{1,0:T(8,128)S(1)}, f32[40,256]{1,0:T(8,128)S(1)}, u32[]{:S(2)}, u32[]{:S(2)}) collective-permute-start(f32[40,256]{1,0:T(8,128)S(1)} %get-tuple-element.30), channel_id=1, source_target_pairs={{8,16},{24,32},{40,48},{56,64},{72,80},{88,96},{104,112},{120,128}... | collective-permute-start | bytes 122888 | tf_op jit(solution)/shard_map/halos/ppermute | solution.py:427
  29.1 4.0 %collective-permute-start.7 = (f32[40,256]{1,0:T(8,128)S(1)}, f32[40,256]{1,0:T(8,128)S(1)}, u32[]{:S(2)}, u32[]{:S(2)}) collective-permute-start(f32[40,256]{1,0:T(8,128)S(1)} %get-tuple-element.31), channel_id=1, source_target_pairs={{0,8},{8,0},{16,24},{24,16},{32,40},{40,32},{48,56},{56,48},{64,72... | collective-permute-start | bytes 122888 | tf_op jit(solution)/shard_map/halos/ppermute | solution.py:428
  33.8 1.2 %collective-permute-start.10 = (f32[4,128]{1,0:T(4,128)S(1)}, f32[4,128]{1,0:T(4,128)S(1)}, u32[]{:S(2)}, u32[]{:S(2)}) collective-permute-start(f32[4,128]{1,0:T(4,128)S(1)} %surface.1.own_ref), channel_id=1, source_target_pairs={{0,1},{1,0},{2,3},{3,2},{4,5},{5,4},{6,7},{7,6},{8,9},{9,8},{10,11... | collective-permute-start | bytes 6152 | tf_op jit(solution)/shard_map/share_sensitivities/ppermute | solution.py:496
  35.7 16.3 %all-to-all-start = ((f32[32,4,128]{2,1,0:T(4,128)}), f32[32,4,128]{2,1,0:T(4,128)S(1)}, u32[]{:S(2)}, u32[]{:S(2)}) async-start(f32[32,4,128]{2,1,0:T(4,128)} %get-tuple-element.39), calls=%async_computation | async-start | bytes 131072 | tf_op jit(solution)/shard_map/share_sensitivities/all_to_all | solution.py:506

commit v11 on v10

--- a/solution.py
+++ b/solution.py
@@ -13,6 +13,7 @@
 F32 = jnp.float32
 BF16 = jnp.bfloat16
 VMEM = pl.BlockSpec(memory_space=pltpu.VMEM)
+ANY = pl.BlockSpec(memory_space=pl.ANY)
 SMEM = pl.BlockSpec(memory_space=pltpu.SMEM)
 
 
@@ -99,32 +100,35 @@
     pack_rows(ids_ref, f_ref, outer_ref, inner_ref)
 
 
-def rhs_kernel(ids_ref, f_ref, src_ref, pa_ref, pb_ref, out_ref):
+def rhs_kernel(ids_ref, f_ref, from_ref, pa_ref, pb_ref, out_ref, src_ref, loads):
     nt, nv, ni, nj, nk = f_ref.shape
-
-    def run(layer_a, layer_b):
+    load = [
+        pltpu.make_async_copy(from_ref.at[:, v], src_ref.at[:, v], loads.at[v])
+        for v in range(nv)
+    ]
+    for copy in load:
+        copy.start()
+
+    def run(v, layer_a, layer_b):
         for layer, other in ((layer_a, pa_ref), (layer_b, pb_ref)):
-
-            def one(v, carry):
-                for j in range(0, nj, 16):
-                    rows = slice(j, j + 16)
-                    own = [
-                        f_ref[t, v, layer, rows, :].astype(BF16).astype(F32)
-                        for t in range(nt)
-                    ]
-                    far = [other[t, v, rows, :].astype(F32) for t in range(nt)]
-                    times = own + far
-                    for b in range(nt):
-                        total = src_ref[b, v, layer, rows, :]
-                        for n in range(1, NT // 2):
-                            diff = times[(b + n) % NT] - times[(b - n) % NT]
-                            total = total - derivative(n) * diff
-                        out_ref[b, v, layer, rows, :] = total
-                return carry
-
-            lax.fori_loop(0, nv, one, 0)
-
-    by_parity(ids_ref, run)
+            for j in range(0, nj, 16):
+                rows = slice(j, j + 16)
+                own = [
+                    f_ref[t, v, layer, rows, :].astype(BF16).astype(F32)
+                    for t in range(nt)
+                ]
+                far = [other[t, v, rows, :].astype(F32) for t in range(nt)]
+                times = own + far
+                for b in range(nt):
+                    total = src_ref[b, v, layer, rows, :]
+                    for n in range(1, NT // 2):
+                        diff = times[(b + n) % NT] - times[(b - n) % NT]
+                        total = total - derivative(n) * diff
+                    out_ref[b, v, layer, rows, :] = total
+
+    for v in range(nv):
+        load[v].wait()
+        by_parity(ids_ref, functools.partial(run, v))
 
 
 def shifted(f_ref, t, u, i, j, lanes, rows_id):
@@ -430,11 +434,14 @@
                 lax.ppermute(b, "cell", odd),
             )
 
+    in_hbm = functools.partial(
+        pltpu.with_memory_space_constraint, memory_space=pltpu.HBM
+    )
     start, *packed = call(
         prepare_kernel,
         [field_like] + sends,
-        (ids, pltpu.with_memory_space_constraint(start, pltpu.HBM)),
-        [SMEM, pl.BlockSpec(memory_space=pl.ANY)],
+        (ids, in_hbm(start)),
+        [SMEM, ANY],
         8,
         10**6,
         "prepare",
@@ -447,11 +454,12 @@
     rhs = call(
         rhs_kernel,
         [field_like],
-        (ids, start, source, pa, pb),
-        [SMEM] + [VMEM] * 4,
-        4,
+        (ids, start, in_hbm(source), pa, pb),
+        [SMEM, VMEM, ANY, VMEM, VMEM],
+        8,
         10**7,
         "rhs",
+        scratch=[pltpu.VMEM(source.shape, F32), pltpu.SemaphoreType.DMA((nv,))],
     )[0]
     ordered = call(
         order_kernel,

time: 53.6 us -> 53.6 us (level)
  Pallas kernels: 14.6 us -> 15.6 us
  waiting for transfers between devices: 10.3 us -> 9.58 us
    pallas_call x11, Pallas kernels: 14.6 us -> 15.6 us  [call(): pl.pallas_call(kernel, out_shape=outs, in_specs=specs, out_specs=[VMEM] *...]
    ppermute x2, waiting for transfers between devices: 1.91 us -> 1.2 us  [exchange(): lax.ppermute(inner, 'passage', within)]
  transfers between devices with their start and end apart: 12 -> 12, of which waited for: 4 -> 3; matrix products, arithmetic and copies ran while one was open for 0% -> 0% of each run, Pallas kernels for 16% -> 18%
where the time goes in v11:
time: 53.6 us; the launch traced here: 53.3 us
  starting transfers between devices  27.2 us (51%)
  Pallas kernels  15.6 us (29%)
  waiting for transfers between devices  9.58 us (18%)
  between operations  0.85 us (2%)
    pallas_call x11, Pallas kernels, call(): pl.pallas_call(kernel, out_shape=outs, in_specs=specs, out_specs=[VMEM] *...  15.6 us
    ppermute x2, starting transfers between devices, exchange(): lax.ppermute(outer, 'passage', across)  13.5 us
    all_to_all x1, waiting for transfers between devices, body(): gathered = lax.all_to_all(sens, 'passage', 0, 0, tiled=True)  7.21 us
    all_to_all x1, starting transfers between devices, body(): gathered = lax.all_to_all(sens, 'passage', 0, 0, tiled=True)  6.29 us
    ppermute x2, starting transfers between devices, exchange(): lax.ppermute(b, 'cell', odd)  4.49 us
    ppermute x2, starting transfers between devices, exchange(): lax.ppermute(a, 'cell', even)  2.28 us
    ppermute x2, waiting for transfers between devices, exchange(): lax.ppermute(inner, 'passage', within)  1.2 us
    ppermute x1, waiting for transfers between devices, body(): other = lax.ppermute(sens, 'tm', swap)  1.14 us
  transfers between devices with their start and end apart: 12, of which 3 were waited for; matrix products, arithmetic and copies ran while one was open for 0% of the time, Pallas kernels for 18%

profile of v11, /device:TPU:8, one launch (start us, length us, event | category | flops | bytes accessed | tf_op | source)
XLA Modules:
  0.0 53.3 jit_solution(198923917079137681)
XLA Ops:
  0.6 0.1 pad_add_fusion.ids_ref
  0.7 2.1 %prepare.1 = (f32[4,5,2,32,256]{4,3,2,1,0:T(8,128)S(1)}, bf16[4,5,32,256]{3,2,1,0:T(8,128)(2,1)S(1)}, bf16[4,5,32,256]{3,2,1,0:T(8,128)(2,1)S(1)}, f32[40,256]{1,0:T(8,128)S(1)}, f32[40,256]{1,0:T(8,128)S(1)}) custom-call(s32[2]{0:T(128)S(1)} %pad_add_fusion.ids_ref, f32[4,5,2,32,256]{4,3,2,1,0:T(8,128)} %from_ref.2), custom_call_target="tpu_custom_call" | custom-call | flops 1000000 | bytes 3358728 | tf_op jit(solution)/shard_map/prepare/pallas_call | solution.py:32
  2.8 0.1 collective-permute-start
  2.9 0.5 collective-permute-start.1
  3.4 2.2 %collective-permute-start.4 = (bf16[4,5,32,256]{3,2,1,0:T(8,128)(2,1)S(1)}, bf16[4,5,32,256]{3,2,1,0:T(8,128)(2,1)S(1)}, u32[]{:S(2)}, u32[]{:S(2)}) collective-permute-start(bf16[4,5,32,256]{3,2,1,0:T(8,128)(2,1)S(1)} %get-tuple-element.22), channel_id=1, source_target_pairs={{0,2},{2,0},{4,6},{6,4},{1,3},{3,1},{5,7},{7,5},{8,10},{10,8},{12,... | collective-permute-start | bytes 983048 | tf_op jit(solution)/shard_map/halos/ppermute | solution.py:433
  5.6 2.6 %collective-permute-start.5 = (bf16[4,5,32,256]{3,2,1,0:T(8,128)(2,1)S(1)}, bf16[4,5,32,256]{3,2,1,0:T(8,128)(2,1)S(1)}, u32[]{:S(2)}, u32[]{:S(2)}) collective-permute-start(bf16[4,5,32,256]{3,2,1,0:T(8,128)(2,1)S(1)} %get-tuple-element.23), channel_id=1, source_target_pairs={{2,4},{4,2},{3,5},{5,3},{10,12},{12,10},{11,13},{13,11},{18,20},{2... | collective-permute-start | bytes 983048 | tf_op jit(solution)/shard_map/halos/ppermute | solution.py:434
  8.1 8.1 %collective-permute-start.2 = (f32[40,256]{1,0:T(8,128)S(1)}, f32[40,256]{1,0:T(8,128)S(1)}, u32[]{:S(2)}, u32[]{:S(2)}) collective-permute-start(f32[40,256]{1,0:T(8,128)S(1)} %get-tuple-element.27), channel_id=1, source_target_pairs={{8,16},{24,32},{40,48},{56,64},{72,80},{88,96},{104,112},{120,128}... | collective-permute-start | bytes 122888 | tf_op jit(solution)/shard_map/halos/ppermute | solution.py:431
  16.3 0.0 collective-permute-done.pa_ref
  16.3 0.0 collective-permute-start.3
  16.3 0.0 collective-permute-done.1.pb_ref
  16.3 0.0 copy-start
  16.3 0.0 copy-start.1
  16.3 0.0 copy-start.2
  16.3 2.1 %rhs.1.refs_1_ = f32[4,5,2,32,256]{4,3,2,1,0:T(8,128)S(1)} custom-call(s32[2]{0:T(128)S(1)} %pad_add_fusion.ids_ref, f32[4,5,2,32,256]{4,3,2,1,0:T(8,128)S(1)} %get-tuple-element.21.f_ref.refs_0_, f32[4,5,2,32,256]{4,3,2,1,0:T(8,128)} %from_ref.3, bf16[4,5,32,256]{3,2,1,0:T(8,128)(2,1)S(1)} %collective-permute-done.pa_ref, ...), custom_call_target="tpu_custom_call" | custom-call | flops 10000000 | bytes 4587528 | tf_op jit(solution)/shard_map/rhs/pallas_call | solution.py:32
  18.4 0.0 copy-done
  18.4 0.0 copy-done.1
  18.4 0.0 copy-done.2
  18.5 1.8 %first_local.1 = (f32[4,5,2,32,256]{4,3,2,1,0:T(8,128)S(1)}, bf16[5,5,32,256]{3,2,1,0:T(8,128)(2,1)S(1)}, bf16[5,5,2,16,256]{4,3,2,1,0:T(8,128)(2,1)S(1)}) custom-call(f32[4,5,2,32,256]{4,3,2,1,0:T(8,128)S(1)} %get-tuple-element.21.f_ref.refs_0_, f32[4,5,2,32,256]{4,3,2,1,0:T(8,128)S(1)} %rhs.1.refs_1_, bf16[2,5,5,2,32,256]{5,4,3,2,1,0:T(8,128)(2,1)S(1)} %copy-done, ...), custom_call_target="tpu_custom_call" | custom-call | flops 20000000 | bytes 6520832 | tf_op jit(solution)/shard_map/first_local/pallas_call | solution.py:32
  20.3 0.0 collective-permute-done.2.refs_5_
  20.3 0.0 collective-permute-done.3.refs_6_
  20.3 0.0 collective-permute-done.4.refs_7_
  20.3 0.0 collective-permute-done.5.refs_8_
  20.3 0.0 copy-start.3
  20.3 0.0 copy-start.4
  20.3 1.4 %first_finish.1 = (f32[4,5,2,32,256]{4,3,2,1,0:T(8,128)S(1)}, bf16[4,5,32,256]{3,2,1,0:T(8,128)(2,1)S(1)}, bf16[4,5,32,256]{3,2,1,0:T(8,128)(2,1)S(1)}, f32[40,256]{1,0:T(8,128)S(1)}, f32[40,256]{1,0:T(8,128)S(1)}) custom-call(s32[2]{0:T(128)S(1)} %pad_add_fusion.ids_ref, f32[4,5,2,32,256]{4,3,2,1,0:T(8,128)S(1)} %get-tuple-element.24.refs_0_, ...), custom_call_target="tpu_custom_call" | custom-call | flops 10000000 | bytes 5046280 | tf_op jit(solution)/shard_map/first_finish/pallas_call | solution.py:32
  21.7 0.1 collective-permute-start.8
  21.8 1.9 %collective-permute-start.9 = (bf16[4,5,32,256]{3,2,1,0:T(8,128)(2,1)S(1)}, bf16[4,5,32,256]{3,2,1,0:T(8,128)(2,1)S(1)}, u32[]{:S(2)}, u32[]{:S(2)}) collective-permute-start(bf16[4,5,32,256]{3,2,1,0:T(8,128)(2,1)S(1)} %get-tuple-element.33), channel_id=1, source_target_pairs={{2,4},{4,2},{3,5},{5,3},{10,12},{12,10},{11,13},{13,11},{18,20},{2... | collective-permute-start | bytes 983048 | tf_op jit(solution)/shard_map/halos/ppermute | solution.py:434
  23.7 5.3 %collective-permute-start.6 = (f32[40,256]{1,0:T(8,128)S(1)}, f32[40,256]{1,0:T(8,128)S(1)}, u32[]{:S(2)}, u32[]{:S(2)}) collective-permute-start(f32[40,256]{1,0:T(8,128)S(1)} %get-tuple-element.30), channel_id=1, source_target_pairs={{8,16},{24,32},{40,48},{56,64},{72,80},{88,96},{104,112},{120,128}... | collective-permute-start | bytes 122888 | tf_op jit(solution)/shard_map/halos/ppermute | solution.py:431
  29.1 0.0 collective-permute-start.7
  29.1 0.0 copy-done.3
  29.1 0.0 copy-done.4
  29.1 1.0 %order.1.refs_9_ = f32[20,512]{1,0:T(8,128)S(1)} custom-call(s32[2]{0:T(128)S(1)} %pad_add_fusion.ids_ref, s32[1,1024]{1,0:T(1,128)S(1)} %copy-done.4, f32[5,4,1024]{2,1,0:T(4,128)S(1)} %bitcast.4), custom_call_target="tpu_custom_call" | custom-call | flops 1000000 | bytes 126984 | tf_op jit(solution)/shard_map/order/pallas_call | solution.py:32
  30.1 1.8 %second_local.1.refs_0_ = f32[4,5,2,32,256]{4,3,2,1,0:T(8,128)S(1)} custom-call(f32[4,5,2,32,256]{4,3,2,1,0:T(8,128)S(1)} %get-tuple-element.29.refs_0_, f32[4,5,2,32,256]{4,3,2,1,0:T(8,128)S(1)} %rhs.1.refs_1_, bf16[2,5,5,2,32,256]{5,4,3,2,1,0:T(8,128)(2,1)S(1)} %copy-done, f32[2,32,256]{2,1,0:T(8,128)S(1)} %copy-done.1, f32[2,32,256]{2,1,0:T(8,128)S(1)} %copy-done.2), custom_call_target="tpu_custom_call" | custom-call | flops 20000000 | bytes 5701632 | tf_op jit(solution)/shard_map/second_local/pallas_call | solution.py:32
  31.9 0.0 collective-permute-done.6.refs_5_
  31.9 1.2 %collective-permute-done.7.refs_6_ = f32[40,256]{1,0:T(8,128)S(1)} collective-permute-done((f32[40,256]{1,0:T(8,128)S(1)}, f32[40,256]{1,0:T(8,128)S(1)}, u32[]{:S(2)}, u32[]{:S(2)}) %collective-permute-start.7) | collective-permute-done | bytes 40992 | tf_op jit(solution)/shard_map/halos/ppermute | solution.py:432
  33.1 0.0 collective-permute-done.8.refs_7_
  33.1 0.0 collective-permute-done.9.refs_8_
  33.1 0.7 %surface.1.own_ref = f32[4,128]{1,0:T(4,128)S(1)} custom-call(s32[2]{0:T(128)S(1)} %pad_add_fusion.ids_ref, f32[4,5,2,32,256]{4,3,2,1,0:T(8,128)S(1)} %second_local.1.refs_0_, bf16[5,5,32,256]{3,2,1,0:T(8,128)(2,1)S(1)} %get-tuple-element.25.refs_1_, bf16[5,5,2,16,256]{4,3,2,1,0:T(8,128)(2,1)S(1)} %get-tuple-element.26.refs_2_, f32[2,32,256]{2,1,0:T(8,128)S(1)} %copy-done.1, ...), custom_call_target="tpu_custom_call" | custom-call | flops 10000000 | bytes 3041288 | tf_op jit(solution)/shard_map/surface/pallas_call | solution.py:32
  33.8 0.1 collective-permute-start.10
  33.9 1.1 %collective-permute-done.10.other_ref = f32[4,128]{1,0:T(4,128)S(1)} collective-permute-done((f32[4,128]{1,0:T(4,128)S(1)}, f32[4,128]{1,0:T(4,128)S(1)}, u32[]{:S(2)}, u32[]{:S(2)}) %collective-permute-start.10) | collective-permute-done | bytes 2080 | tf_op jit(solution)/shard_map/share_sensitivities/ppermute | solution.py:504
  35.1 0.6 %share.1 = (f32[32,4,128]{2,1,0:T(4,128)}, f32[8,128]{1,0:T(8,128)S(1)}) custom-call(f32[4,128]{1,0:T(4,128)S(1)} %surface.1.own_ref, f32[4,128]{1,0:T(4,128)S(1)} %collective-permute-done.10.other_ref), custom_call_target="tpu_custom_call" | custom-call | flops 10000 | bytes 73728 | tf_op jit(solution)/shard_map/share_sensitivities/share/pallas_call | solution.py:32
  35.7 6.3 %all-to-all-start = ((f32[32,4,128]{2,1,0:T(4,128)}), f32[32,4,128]{2,1,0:T(4,128)S(1)}, u32[]{:S(2)}, u32[]{:S(2)}) async-start(f32[32,4,128]{2,1,0:T(4,128)} %get-tuple-element.39), calls=%async_computation | async-start | bytes 131072 | tf_op jit(solution)/shard_map/share_sensitivities/all_to_all | solution.py:514
  42.0 2.3 %second_finish.1 = (f32[4,5,2,32,256]{4,3,2,1,0:T(8,128)}, f32[8,128]{1,0:T(8,128)S(1)}) custom-call(s32[2]{0:T(128)S(1)} %pad_add_fusion.ids_ref, f32[4,5,2,32,256]{4,3,2,1,0:T(8,128)S(1)} %second_local.1.refs_0_, bf16[5,5,32,256]{3,2,1,0:T(8,128)(2,1)S(1)} %get-tuple-element.25.refs_1_, bf16[5,5,2,16,256]{4,3,2,1,0:T(8,128)(2,1)S(1)} %get-tuple-element.26.refs_2_, ...), custom_call_target="tpu_custom_call" | custom-call | flops 10000000 | bytes 4317192 | tf_op jit(solution)/shard_map/second_finish/pallas_call | solution.py:32
  44.3 0.4 tables.1
  44.8 7.2 %all-to-all-done.sens_ref = f32[32,4,128]{2,1,0:T(4,128)S(1)} async-done(((f32[32,4,128]{2,1,0:T(4,128)}), f32[32,4,128]{2,1,0:T(4,128)S(1)}, u32[]{:S(2)}, u32[]{:S(2)}) %all-to-all-start) | async-done | bytes 65568 | tf_op jit(solution)/shard_map/share_sensitivities/all_to_all | solution.py:514
  52.0 1.4 %modes.1 = f32[32,1024]{1,0:T(8,128)} custom-call(bf16[1024,1024]{1,0:T(8,128)(2,1)S(1)} %get-tuple-element.37.chosen_ref, f32[64,32]{1,0:T(8,128)S(1)} %get-tuple-element.38.table_ref, f32[32,4,128]{2,1,0:T(4,128)S(1)} %all-to-all-done.sens_ref), custom_call_target="tpu_custom_call" | custom-call | flops 10000000 | bytes 2301952 | tf_op jit(solution)/shard_map/modes/pallas_call | solution.py:32
Async XLA Ops:
  2.8 13.5 %collective-permute-start = (bf16[4,5,32,256]{3,2,1,0:T(8,128)(2,1)S(1)}, bf16[4,5,32,256]{3,2,1,0:T(8,128)(2,1)S(1)}, u32[]{:S(2)}, u32[]{:S(2)}) collective-permute-start(bf16[4,5,32,256]{3,2,1,0:T(8,128)(2,1)S(1)} %get-tuple-element.22), channel_id=1, source_target_pairs={{0,1},{1,0},{2,3},{3,2},{4,5},{5,4},{6,7},{7,6},{8,9},{9,8},{10,11... | collective-permute-start | bytes 983048 | tf_op jit(solution)/shard_map/other_times/ppermute | solution.py:451
  2.9 13.4 %collective-permute-start.1 = (bf16[4,5,32,256]{3,2,1,0:T(8,128)(2,1)S(1)}, bf16[4,5,32,256]{3,2,1,0:T(8,128)(2,1)S(1)}, u32[]{:S(2)}, u32[]{:S(2)}) collective-permute-start(bf16[4,5,32,256]{3,2,1,0:T(8,128)(2,1)S(1)} %get-tuple-element.23), channel_id=1, source_target_pairs={{0,1},{1,0},{2,3},{3,2},{4,5},{5,4},{6,7},{7,6},{8,9},{9,8},{10,11... | collective-permute-start | bytes 983048 | tf_op jit(solution)/shard_map/other_times/ppermute | solution.py:452
  3.4 16.9 %collective-permute-start.4 = (bf16[4,5,32,256]{3,2,1,0:T(8,128)(2,1)S(1)}, bf16[4,5,32,256]{3,2,1,0:T(8,128)(2,1)S(1)}, u32[]{:S(2)}, u32[]{:S(2)}) collective-permute-start(bf16[4,5,32,256]{3,2,1,0:T(8,128)(2,1)S(1)} %get-tuple-element.22), channel_id=1, source_target_pairs={{0,2},{2,0},{4,6},{6,4},{1,3},{3,1},{5,7},{7,5},{8,10},{10,8},{12,... | collective-permute-start | bytes 983048 | tf_op jit(solution)/shard_map/halos/ppermute | solution.py:433
  5.6 14.8 %collective-permute-start.5 = (bf16[4,5,32,256]{3,2,1,0:T(8,128)(2,1)S(1)}, bf16[4,5,32,256]{3,2,1,0:T(8,128)(2,1)S(1)}, u32[]{:S(2)}, u32[]{:S(2)}) collective-permute-start(bf16[4,5,32,256]{3,2,1,0:T(8,128)(2,1)S(1)} %get-tuple-element.23), channel_id=1, source_target_pairs={{2,4},{4,2},{3,5},{5,3},{10,12},{12,10},{11,13},{13,11},{18,20},{2... | collective-permute-start | bytes 983048 | tf_op jit(solution)/shard_map/halos/ppermute | solution.py:434
  8.1 12.1 %collective-permute-start.2 = (f32[40,256]{1,0:T(8,128)S(1)}, f32[40,256]{1,0:T(8,128)S(1)}, u32[]{:S(2)}, u32[]{:S(2)}) collective-permute-start(f32[40,256]{1,0:T(8,128)S(1)} %get-tuple-element.27), channel_id=1, source_target_pairs={{8,16},{24,32},{40,48},{56,64},{72,80},{88,96},{104,112},{120,128}... | collective-permute-start | bytes 122888 | tf_op jit(solution)/shard_map/halos/ppermute | solution.py:431
  16.3 4.0 %collective-permute-start.3 = (f32[40,256]{1,0:T(8,128)S(1)}, f32[40,256]{1,0:T(8,128)S(1)}, u32[]{:S(2)}, u32[]{:S(2)}) collective-permute-start(f32[40,256]{1,0:T(8,128)S(1)} %get-tuple-element.28), channel_id=1, source_target_pairs={{0,8},{8,0},{16,24},{24,16},{32,40},{40,32},{48,56},{56,48},{64,72... | collective-permute-start | bytes 122888 | tf_op jit(solution)/shard_map/halos/ppermute | solution.py:432
  16.3 2.1 %copy-start = (bf16[2,5,5,2,32,256]{5,4,3,2,1,0:T(8,128)(2,1)S(1)}, bf16[2,5,5,2,32,256]{5,4,3,2,1,0:T(8,128)(2,1)}, u32[]{:S(2)}) copy-start(bf16[2,5,5,2,32,256]{5,4,3,2,1,0:T(8,128)(2,1)} %refs_2_.3) | copy-start | bytes 4915204
  16.3 2.1 %copy-start.1 = (f32[2,32,256]{2,1,0:T(8,128)S(1)}, f32[2,32,256]{2,1,0:T(8,128)}, u32[]{:S(2)}) copy-start(f32[2,32,256]{2,1,0:T(8,128)} %refs_3_.9) | copy-start | bytes 196612
  16.3 2.1 %copy-start.2 = (f32[2,32,256]{2,1,0:T(8,128)S(1)}, f32[2,32,256]{2,1,0:T(8,128)}, u32[]{:S(2)}) copy-start(f32[2,32,256]{2,1,0:T(8,128)} %refs_4_.9) | copy-start | bytes 196612
  20.3 8.8 %copy-start.3 = (f32[4,5,1024]{2,0,1:T(4,128)S(1)}, f32[4,5,1024]{2,0,1:T(4,128)}, u32[]{:S(2)}) copy-start(f32[4,5,1024]{2,0,1:T(4,128)} %param.13) | copy-start | bytes 245764
  20.3 8.7 %copy-start.4 = (s32[1,1024]{1,0:T(1,128)S(1)}, s32[1,1024]{1,0:T(1,128)}, u32[]{:S(2)}) copy-start(s32[1,1024]{1,0:T(1,128)} %cells_ref.3) | copy-start | bytes 12292
  21.7 11.4 %collective-permute-start.8 = (bf16[4,5,32,256]{3,2,1,0:T(8,128)(2,1)S(1)}, bf16[4,5,32,256]{3,2,1,0:T(8,128)(2,1)S(1)}, u32[]{:S(2)}, u32[]{:S(2)}) collective-permute-start(bf16[4,5,32,256]{3,2,1,0:T(8,128)(2,1)S(1)} %get-tuple-element.32), channel_id=1, source_target_pairs={{0,2},{2,0},{4,6},{6,4},{1,3},{3,1},{5,7},{7,5},{8,10},{10,8},{12,... | collective-permute-start | bytes 983048 | tf_op jit(solution)/shard_map/halos/ppermute | solution.py:433
  21.8 11.3 %collective-permute-start.9 = (bf16[4,5,32,256]{3,2,1,0:T(8,128)(2,1)S(1)}, bf16[4,5,32,256]{3,2,1,0:T(8,128)(2,1)S(1)}, u32[]{:S(2)}, u32[]{:S(2)}) collective-permute-start(bf16[4,5,32,256]{3,2,1,0:T(8,128)(2,1)S(1)} %get-tuple-element.33), channel_id=1, source_target_pairs={{2,4},{4,2},{3,5},{5,3},{10,12},{12,10},{11,13},{13,11},{18,20},{2... | collective-permute-start | bytes 983048 | tf_op jit(solution)/shard_map/halos/ppermute | solution.py:434
  23.7 8.1 %collective-permute-start.6 = (f32[40,256]{1,0:T(8,128)S(1)}, f32[40,256]{1,0:T(8,128)S(1)}, u32[]{:S(2)}, u32[]{:S(2)}) collective-permute-start(f32[40,256]{1,0:T(8,128)S(1)} %get-tuple-element.30), channel_id=1, source_target_pairs={{8,16},{24,32},{40,48},{56,64},{72,80},{88,96},{104,112},{120,128}... | collective-permute-start | bytes 122888 | tf_op jit(solution)/shard_map/halos/ppermute | solution.py:431
  29.1 4.0 %collective-permute-start.7 = (f32[40,256]{1,0:T(8,128)S(1)}, f32[40,256]{1,0:T(8,128)S(1)}, u32[]{:S(2)}, u32[]{:S(2)}) collective-permute-start(f32[40,256]{1,0:T(8,128)S(1)} %get-tuple-element.31), channel_id=1, source_target_pairs={{0,8},{8,0},{16,24},{24,16},{32,40},{40,32},{48,56},{56,48},{64,72... | collective-permute-start | bytes 122888 | tf_op jit(solution)/shard_map/halos/ppermute | solution.py:432
  33.8 1.2 %collective-permute-start.10 = (f32[4,128]{1,0:T(4,128)S(1)}, f32[4,128]{1,0:T(4,128)S(1)}, u32[]{:S(2)}, u32[]{:S(2)}) collective-permute-start(f32[4,128]{1,0:T(4,128)S(1)} %surface.1.own_ref), channel_id=1, source_target_pairs={{0,1},{1,0},{2,3},{3,2},{4,5},{5,4},{6,7},{7,6},{8,9},{9,8},{10,11... | collective-permute-start | bytes 6152 | tf_op jit(solution)/shard_map/share_sensitivities/ppermute | solution.py:504
  35.7 16.3 %all-to-all-start = ((f32[32,4,128]{2,1,0:T(4,128)}), f32[32,4,128]{2,1,0:T(4,128)S(1)}, u32[]{:S(2)}, u32[]{:S(2)}) async-start(f32[32,4,128]{2,1,0:T(4,128)} %get-tuple-element.39), calls=%async_computation | async-start | bytes 131072 | tf_op jit(solution)/shard_map/share_sensitivities/all_to_all | solution.py:514

commit v12 on v7

--- a/solution.py
+++ b/solution.py
@@ -77,8 +77,7 @@
                 inner_ref[here, :] = edge_row(ids_ref, f_ref, t, v, i, False)
 
 
-def prepare_kernel(ids_ref, f_ref, a_ref, b_ref, outer_ref, inner_ref):
-    pack_rows(ids_ref, f_ref, outer_ref, inner_ref)
+def prepare_kernel(ids_ref, f_ref, a_ref, b_ref):
     by_parity(ids_ref, functools.partial(pack_layers, f_ref, a_ref, b_ref))
 
 
@@ -260,14 +259,13 @@
 
 def first_kernel(ids_ref, *refs):
     ins, ha_ref, hb_ref = refs[:7], refs[7], refs[8]
-    out_ref, a_ref, b_ref, no_ref, ni_ref = refs[9:]
+    out_ref, a_ref, b_ref = refs[9:]
 
     def run(layer_a, layer_b):
         finish_all(ids_ref, ins, out_ref, {layer_a: ha_ref, layer_b: hb_ref})
         pack_layers(out_ref, a_ref, b_ref, layer_a, layer_b)
 
     by_parity(ids_ref, run)
-    pack_rows(ids_ref, out_ref, no_ref, ni_ref)
 
 
 def surface_kernel(ids_ref, *refs):
@@ -402,9 +400,13 @@
     layer_like = jax.ShapeDtypeStruct((nt, nv, nj, nk), BF16)
     rows_like = jax.ShapeDtypeStruct((nt * nv * ni, nk), F32)
 
-    sends = [layer_like, layer_like, rows_like, rows_like]
-
-    def exchange(a, b, outer, inner):
+    sends = [layer_like, layer_like]
+
+    def exchange(field, a, b):
+        rows = [rows_like, rows_like]
+        outer, inner = call(
+            pack_rows, rows, (ids, field), [SMEM, VMEM], 4, 10**6, "rows"
+        )
         with jax.named_scope("halos"):
             return (
                 lax.ppermute(outer, "passage", across),
@@ -419,7 +421,7 @@
     with jax.named_scope("other_times"):
         pa = lax.ppermute(packed[0], "tm", swap)
         pb = lax.ppermute(packed[1], "tm", swap)
-    halos = exchange(*packed)
+    halos = exchange(start, *packed)
     rhs = call(
         rhs_kernel,
         [field_like],
@@ -462,7 +464,7 @@
         (),
         "first_finish",
     )
-    halos = exchange(*packed)
+    halos = exchange(field, *packed)
     part = local(field, [field_like], "second_local")[0]
     token_like = jax.ShapeDtypeStruct((8, 128), F32)
     pieces = ni * nk // 128

time: 53.5 us -> 53.5 us (level)
  Pallas kernels: 13.2 us -> 14.3 us
  starting transfers between devices: 27.2 us -> 26.1 us
    pallas_call x11 -> x13, Pallas kernels: 13.2 us -> 14.3 us  [call(): pl.pallas_call(kernel, out_shape=outs, in_specs=specs, out_specs=[VMEM] *...]
    all_to_all x1, starting transfers between devices: 6.29 us -> 5.7 us  [body(): gathered = lax.all_to_all(sens, 'passage', 0, 0, tiled=True)]
    ppermute x2, starting transfers between devices: 13.4 us -> 12.8 us  [exchange(): lax.ppermute(outer, 'passage', across)]
  transfers between devices with their start and end apart: 12 -> 12, of which waited for: 4 -> 4; matrix products, arithmetic and copies ran while one was open for 0% -> 0% of each run, Pallas kernels for 16% -> 18%
where the time goes in v12:
time: 53.5 us; the launch traced here: 53.2 us
  starting transfers between devices  26.1 us (49%)
  Pallas kernels  14.3 us (27%)
  waiting for transfers between devices  9.99 us (19%)
  local copies, waits for them, and re-layouts  1.92 us (4%)
  between operations  0.83 us (2%)
    pallas_call x13, Pallas kernels, call(): pl.pallas_call(kernel, out_shape=outs, in_specs=specs, out_specs=[VMEM] *...  14.3 us
    ppermute x2, starting transfers between devices, exchange(): lax.ppermute(outer, 'passage', across)  12.8 us
    all_to_all x1, waiting for transfers between devices, body(): gathered = lax.all_to_all(sens, 'passage', 0, 0, tiled=True)  7.21 us
    all_to_all x1, starting transfers between devices, body(): gathered = lax.all_to_all(sens, 'passage', 0, 0, tiled=True)  5.7 us
    ppermute x2, starting transfers between devices, exchange(): lax.ppermute(b, 'cell', odd)  4.49 us
    ppermute x2, starting transfers between devices, exchange(): lax.ppermute(a, 'cell', even)  2.28 us
    unnamed x16, local copies, waits for them, and re-layouts  1.92 us
    ppermute x2, waiting for transfers between devices, exchange(): lax.ppermute(inner, 'passage', within)  1.62 us
  transfers between devices with their start and end apart: 12, of which 4 were waited for; matrix products, arithmetic and copies ran while one was open for 0% of the time, Pallas kernels for 18%

profile of v12, /device:TPU:8, one launch (start us, length us, event | category | flops | bytes accessed | tf_op | source)
XLA Modules:
  0.0 53.2 jit_solution(15389536974386559424)
XLA Ops:
  0.6 0.1 pad_add_fusion.ids_ref
  0.7 0.0 copy-start
  0.7 1.3 %copy-done = f32[4,5,2,32,256]{4,3,2,1,0:T(8,128)S(1)} copy-done((f32[4,5,2,32,256]{4,3,2,1,0:T(8,128)S(1)}, f32[4,5,2,32,256]{4,3,2,1,0:T(8,128)}, u32[]{:S(2)}) %copy-start) | copy-done | bytes 1310744
  2.0 0.0 copy-start.5
  2.0 0.6 %prepare.1 = (bf16[4,5,32,256]{3,2,1,0:T(8,128)(2,1)S(1)}, bf16[4,5,32,256]{3,2,1,0:T(8,128)(2,1)S(1)}) custom-call(s32[2]{0:T(128)S(1)} %pad_add_fusion.ids_ref, f32[4,5,2,32,256]{4,3,2,1,0:T(8,128)S(1)} %copy-done), custom_call_target="tpu_custom_call" | custom-call | flops 1000000 | bytes 1966088 | tf_op jit(solution)/shard_map/prepare/pallas_call | solution.py:31
  2.7 0.1 collective-permute-start
  2.8 0.5 collective-permute-start.1
  3.3 2.2 %collective-permute-start.4 = (bf16[4,5,32,256]{3,2,1,0:T(8,128)(2,1)S(1)}, bf16[4,5,32,256]{3,2,1,0:T(8,128)(2,1)S(1)}, u32[]{:S(2)}, u32[]{:S(2)}) collective-permute-start(bf16[4,5,32,256]{3,2,1,0:T(8,128)(2,1)S(1)} %get-tuple-element.20), channel_id=1, source_target_pairs={{0,2},{2,0},{4,6},{6,4},{1,3},{3,1},{5,7},{7,5},{8,10},{10,8},{12,... | collective-permute-start | bytes 983048 | tf_op jit(solution)/shard_map/halos/ppermute | solution.py:414
  5.4 2.6 %collective-permute-start.5 = (bf16[4,5,32,256]{3,2,1,0:T(8,128)(2,1)S(1)}, bf16[4,5,32,256]{3,2,1,0:T(8,128)(2,1)S(1)}, u32[]{:S(2)}, u32[]{:S(2)}) collective-permute-start(bf16[4,5,32,256]{3,2,1,0:T(8,128)(2,1)S(1)} %get-tuple-element.21), channel_id=1, source_target_pairs={{2,4},{4,2},{3,5},{5,3},{10,12},{12,10},{11,13},{13,11},{18,20},{2... | collective-permute-start | bytes 983048 | tf_op jit(solution)/shard_map/halos/ppermute | solution.py:415
  8.0 0.6 %rows.2 = (f32[40,256]{1,0:T(8,128)S(1)}, f32[40,256]{1,0:T(8,128)S(1)}) custom-call(s32[2]{0:T(128)S(1)} %pad_add_fusion.ids_ref, f32[4,5,2,32,256]{4,3,2,1,0:T(8,128)S(1)} %copy-done), custom_call_target="tpu_custom_call" | custom-call | flops 1000000 | bytes 1392648 | tf_op jit(solution)/shard_map/rows/pallas_call | solution.py:31
  8.6 8.1 %collective-permute-start.2 = (f32[40,256]{1,0:T(8,128)S(1)}, f32[40,256]{1,0:T(8,128)S(1)}, u32[]{:S(2)}, u32[]{:S(2)}) collective-permute-start(f32[40,256]{1,0:T(8,128)S(1)} %get-tuple-element.25), channel_id=1, source_target_pairs={{8,16},{24,32},{40,48},{56,64},{72,80},{88,96},{104,112},{120,128}... | collective-permute-start | bytes 122888 | tf_op jit(solution)/shard_map/halos/ppermute | solution.py:412
  16.7 0.0 collective-permute-done.pa_ref
  16.8 0.0 copy-start.1
  16.8 0.0 copy-start.2
  16.8 0.0 copy-start.3
  16.8 0.0 copy-start.4
  16.8 0.1 collective-permute-start.3
  16.9 0.0 collective-permute-done.1.pb_ref
  16.9 0.0 copy-done.5
  16.9 1.1 %rhs.1.refs_1_ = f32[4,5,2,32,256]{4,3,2,1,0:T(8,128)S(1)} custom-call(s32[2]{0:T(128)S(1)} %pad_add_fusion.ids_ref, f32[4,5,2,32,256]{4,3,2,1,0:T(8,128)S(1)} %copy-done, f32[4,5,2,32,256]{4,3,2,1,0:T(8,128)S(1)} %copy-done.5, bf16[4,5,32,256]{3,2,1,0:T(8,128)(2,1)S(1)} %collective-permute-done.pa_ref, bf16[4,5,32,256]{3,2,1,0:T(8,128)(2,1)S(1)} %collective-permute-done.1.pb_ref), custom_call_target="tpu_custom_call" | custom-call | flops 10000000 | bytes 4587528 | tf_op jit(solution)/shard_map/rhs/pallas_call | solution.py:31
  18.0 0.1 copy-done.1
  18.1 0.5 copy-done.2
  18.6 0.0 copy-done.3
  18.6 0.0 copy-done.4
  18.6 1.8 %first_local.1 = (f32[4,5,2,32,256]{4,3,2,1,0:T(8,128)S(1)}, bf16[5,5,32,256]{3,2,1,0:T(8,128)(2,1)S(1)}, bf16[5,5,2,16,256]{4,3,2,1,0:T(8,128)(2,1)S(1)}) custom-call(f32[4,5,2,32,256]{4,3,2,1,0:T(8,128)S(1)} %copy-done.1, f32[4,5,2,32,256]{4,3,2,1,0:T(8,128)S(1)} %rhs.1.refs_1_, bf16[2,5,5,2,32,256]{5,4,3,2,1,0:T(8,128)(2,1)S(1)} %copy-done.2, ...), custom_call_target="tpu_custom_call" | custom-call | flops 20000000 | bytes 6520832 | tf_op jit(solution)/shard_map/first_local/pallas_call | solution.py:31
  20.4 0.0 collective-permute-done.2.refs_5_
  20.4 0.4 collective-permute-done.3.refs_6_
  20.9 0.0 collective-permute-done.4.refs_7_
  20.9 0.0 collective-permute-done.5.refs_8_
  20.9 1.3 %first_finish.1 = (f32[4,5,2,32,256]{4,3,2,1,0:T(8,128)S(1)}, bf16[4,5,32,256]{3,2,1,0:T(8,128)(2,1)S(1)}, bf16[4,5,32,256]{3,2,1,0:T(8,128)(2,1)S(1)}) custom-call(s32[2]{0:T(128)S(1)} %pad_add_fusion.ids_ref, f32[4,5,2,32,256]{4,3,2,1,0:T(8,128)S(1)} %get-tuple-element.22.refs_0_, bf16[5,5,32,256]{3,2,1,0:T(8,128)(2,1)S(1)} %get-tuple-element.23.refs_1_, ...), custom_call_target="tpu_custom_call" | custom-call | flops 10000000 | bytes 4964360 | tf_op jit(solution)/shard_map/first_finish/pallas_call | solution.py:31
  22.2 0.0 copy-start.6
  22.2 0.0 copy-start.7
  22.2 0.1 collective-permute-start.8
  22.3 1.9 %collective-permute-start.9 = (bf16[4,5,32,256]{3,2,1,0:T(8,128)(2,1)S(1)}, bf16[4,5,32,256]{3,2,1,0:T(8,128)(2,1)S(1)}, u32[]{:S(2)}, u32[]{:S(2)}) collective-permute-start(bf16[4,5,32,256]{3,2,1,0:T(8,128)(2,1)S(1)} %get-tuple-element.31), channel_id=1, source_target_pairs={{2,4},{4,2},{3,5},{5,3},{10,12},{12,10},{11,13},{13,11},{18,20},{2... | collective-permute-start | bytes 983048 | tf_op jit(solution)/shard_map/halos/ppermute | solution.py:415
  24.3 0.6 %rows.3 = (f32[40,256]{1,0:T(8,128)S(1)}, f32[40,256]{1,0:T(8,128)S(1)}) custom-call(s32[2]{0:T(128)S(1)} %pad_add_fusion.ids_ref, f32[4,5,2,32,256]{4,3,2,1,0:T(8,128)S(1)} %get-tuple-element.27.refs_0_.f_ref), custom_call_target="tpu_custom_call" | custom-call | flops 1000000 | bytes 1392648 | tf_op jit(solution)/shard_map/rows/pallas_call | solution.py:31
  24.9 4.7 %collective-permute-start.6 = (f32[40,256]{1,0:T(8,128)S(1)}, f32[40,256]{1,0:T(8,128)S(1)}, u32[]{:S(2)}, u32[]{:S(2)}) collective-permute-start(f32[40,256]{1,0:T(8,128)S(1)} %get-tuple-element.28), channel_id=1, source_target_pairs={{8,16},{24,32},{40,48},{56,64},{72,80},{88,96},{104,112},{120,128}... | collective-permute-start | bytes 122888 | tf_op jit(solution)/shard_map/halos/ppermute | solution.py:412
  29.5 0.0 collective-permute-start.7
  29.5 0.0 copy-done.6
  29.5 0.0 copy-done.7
  29.6 1.0 %order.1.refs_9_ = f32[20,512]{1,0:T(8,128)S(1)} custom-call(s32[2]{0:T(128)S(1)} %pad_add_fusion.ids_ref, s32[1,1024]{1,0:T(1,128)S(1)} %copy-done.7, f32[5,4,1024]{2,1,0:T(4,128)S(1)} %bitcast.4), custom_call_target="tpu_custom_call" | custom-call | flops 1000000 | bytes 126984 | tf_op jit(solution)/shard_map/order/pallas_call | solution.py:31
  30.6 1.8 %second_local.1.refs_0_ = f32[4,5,2,32,256]{4,3,2,1,0:T(8,128)S(1)} custom-call(f32[4,5,2,32,256]{4,3,2,1,0:T(8,128)S(1)} %get-tuple-element.27.refs_0_.f_ref, f32[4,5,2,32,256]{4,3,2,1,0:T(8,128)S(1)} %rhs.1.refs_1_, bf16[2,5,5,2,32,256]{5,4,3,2,1,0:T(8,128)(2,1)S(1)} %copy-done.2, f32[2,32,256]{2,1,0:T(8,128)S(1)} %copy-done.3, f32[2,32,256]{2,1,0:T(8,128)S(1)} %copy-done.4), custom_call_target="tpu_custom_call" | custom-call | flops 20000000 | bytes 5701632 | tf_op jit(solution)/shard_map/second_local/pallas_call | solution.py:31
  32.4 0.0 collective-permute-done.6.refs_5_
  32.4 1.2 %collective-permute-done.7.refs_6_ = f32[40,256]{1,0:T(8,128)S(1)} collective-permute-done((f32[40,256]{1,0:T(8,128)S(1)}, f32[40,256]{1,0:T(8,128)S(1)}, u32[]{:S(2)}, u32[]{:S(2)}) %collective-permute-start.7) | collective-permute-done | bytes 40992 | tf_op jit(solution)/shard_map/halos/ppermute | solution.py:413
  33.5 0.0 collective-permute-done.8.refs_7_
  33.5 0.0 collective-permute-done.9.refs_8_
  33.5 0.7 %surface.1.own_ref = f32[4,128]{1,0:T(4,128)S(1)} custom-call(s32[2]{0:T(128)S(1)} %pad_add_fusion.ids_ref, f32[4,5,2,32,256]{4,3,2,1,0:T(8,128)S(1)} %second_local.1.refs_0_, bf16[5,5,32,256]{3,2,1,0:T(8,128)(2,1)S(1)} %get-tuple-element.23.refs_1_, bf16[5,5,2,16,256]{4,3,2,1,0:T(8,128)(2,1)S(1)} %get-tuple-element.24.refs_2_, f32[2,32,256]{2,1,0:T(8,128)S(1)} %copy-done.3, ...), custom_call_target="tpu_custom_call" | custom-call | flops 10000000 | bytes 3041288 | tf_op jit(solution)/shard_map/surface/pallas_call | solution.py:31
  34.3 0.1 collective-permute-start.10
  34.4 1.1 %collective-permute-done.10.other_ref = f32[4,128]{1,0:T(4,128)S(1)} collective-permute-done((f32[4,128]{1,0:T(4,128)S(1)}, f32[4,128]{1,0:T(4,128)S(1)}, u32[]{:S(2)}, u32[]{:S(2)}) %collective-permute-start.10) | collective-permute-done | bytes 2080 | tf_op jit(solution)/shard_map/share_sensitivities/ppermute | solution.py:474
  35.5 0.6 %share.1 = (f32[32,4,128]{2,1,0:T(4,128)}, f32[8,128]{1,0:T(8,128)S(1)}) custom-call(f32[4,128]{1,0:T(4,128)S(1)} %surface.1.own_ref, f32[4,128]{1,0:T(4,128)S(1)} %collective-permute-done.10.other_ref), custom_call_target="tpu_custom_call" | custom-call | flops 10000 | bytes 73728 | tf_op jit(solution)/shard_map/share_sensitivities/share/pallas_call | solution.py:31
  36.2 5.7 %all-to-all-start = ((f32[32,4,128]{2,1,0:T(4,128)}), f32[32,4,128]{2,1,0:T(4,128)S(1)}, u32[]{:S(2)}, u32[]{:S(2)}) async-start(f32[32,4,128]{2,1,0:T(4,128)} %get-tuple-element.37), calls=%async_computation | async-start | bytes 131072 | tf_op jit(solution)/shard_map/share_sensitivities/all_to_all | solution.py:484
  41.9 2.3 %second_finish.1 = (f32[4,5,2,32,256]{4,3,2,1,0:T(8,128)}, f32[8,128]{1,0:T(8,128)S(1)}) custom-call(s32[2]{0:T(128)S(1)} %pad_add_fusion.ids_ref, f32[4,5,2,32,256]{4,3,2,1,0:T(8,128)S(1)} %second_local.1.refs_0_, bf16[5,5,32,256]{3,2,1,0:T(8,128)(2,1)S(1)} %get-tuple-element.23.refs_1_, bf16[5,5,2,16,256]{4,3,2,1,0:T(8,128)(2,1)S(1)} %get-tuple-element.24.refs_2_, ...), custom_call_target="tpu_custom_call" | custom-call | flops 10000000 | bytes 4317192 | tf_op jit(solution)/shard_map/second_finish/pallas_call | solution.py:31
  44.2 0.4 tables.1
  44.6 7.2 %all-to-all-done.sens_ref = f32[32,4,128]{2,1,0:T(4,128)S(1)} async-done(((f32[32,4,128]{2,1,0:T(4,128)}), f32[32,4,128]{2,1,0:T(4,128)S(1)}, u32[]{:S(2)}, u32[]{:S(2)}) %all-to-all-start) | async-done | bytes 65568 | tf_op jit(solution)/shard_map/share_sensitivities/all_to_all | solution.py:484
  51.9 1.4 %modes.1 = f32[32,1024]{1,0:T(8,128)} custom-call(bf16[1024,1024]{1,0:T(8,128)(2,1)S(1)} %get-tuple-element.35.chosen_ref, f32[64,32]{1,0:T(8,128)S(1)} %get-tuple-element.36.table_ref, f32[32,4,128]{2,1,0:T(4,128)S(1)} %all-to-all-done.sens_ref), custom_call_target="tpu_custom_call" | custom-call | flops 10000000 | bytes 2301952 | tf_op jit(solution)/shard_map/modes/pallas_call | solution.py:31
Async XLA Ops:
  0.7 1.3 %copy-start = (f32[4,5,2,32,256]{4,3,2,1,0:T(8,128)S(1)}, f32[4,5,2,32,256]{4,3,2,1,0:T(8,128)}, u32[]{:S(2)}) copy-start(f32[4,5,2,32,256]{4,3,2,1,0:T(8,128)} %f_ref.5) | copy-start | bytes 3932164
  2.0 14.9 %copy-start.5 = (f32[4,5,2,32,256]{4,3,2,1,0:T(8,128)S(1)}, f32[4,5,2,32,256]{4,3,2,1,0:T(8,128)}, u32[]{:S(2)}) copy-start(f32[4,5,2,32,256]{4,3,2,1,0:T(8,128)} %src_ref.1) | copy-start | bytes 3932164
  2.7 14.1 %collective-permute-start = (bf16[4,5,32,256]{3,2,1,0:T(8,128)(2,1)S(1)}, bf16[4,5,32,256]{3,2,1,0:T(8,128)(2,1)S(1)}, u32[]{:S(2)}, u32[]{:S(2)}) collective-permute-start(bf16[4,5,32,256]{3,2,1,0:T(8,128)(2,1)S(1)} %get-tuple-element.20), channel_id=1, source_target_pairs={{0,1},{1,0},{2,3},{3,2},{4,5},{5,4},{6,7},{7,6},{8,9},{9,8},{10,11... | collective-permute-start | bytes 983048 | tf_op jit(solution)/shard_map/other_times/ppermute | solution.py:422
  2.8 14.1 %collective-permute-start.1 = (bf16[4,5,32,256]{3,2,1,0:T(8,128)(2,1)S(1)}, bf16[4,5,32,256]{3,2,1,0:T(8,128)(2,1)S(1)}, u32[]{:S(2)}, u32[]{:S(2)}) collective-permute-start(bf16[4,5,32,256]{3,2,1,0:T(8,128)(2,1)S(1)} %get-tuple-element.21), channel_id=1, source_target_pairs={{0,1},{1,0},{2,3},{3,2},{4,5},{5,4},{6,7},{7,6},{8,9},{9,8},{10,11... | collective-permute-start | bytes 983048 | tf_op jit(solution)/shard_map/other_times/ppermute | solution.py:423
  3.3 17.6 %collective-permute-start.4 = (bf16[4,5,32,256]{3,2,1,0:T(8,128)(2,1)S(1)}, bf16[4,5,32,256]{3,2,1,0:T(8,128)(2,1)S(1)}, u32[]{:S(2)}, u32[]{:S(2)}) collective-permute-start(bf16[4,5,32,256]{3,2,1,0:T(8,128)(2,1)S(1)} %get-tuple-element.20), channel_id=1, source_target_pairs={{0,2},{2,0},{4,6},{6,4},{1,3},{3,1},{5,7},{7,5},{8,10},{10,8},{12,... | collective-permute-start | bytes 983048 | tf_op jit(solution)/shard_map/halos/ppermute | solution.py:414
  5.4 15.4 %collective-permute-start.5 = (bf16[4,5,32,256]{3,2,1,0:T(8,128)(2,1)S(1)}, bf16[4,5,32,256]{3,2,1,0:T(8,128)(2,1)S(1)}, u32[]{:S(2)}, u32[]{:S(2)}) collective-permute-start(bf16[4,5,32,256]{3,2,1,0:T(8,128)(2,1)S(1)} %get-tuple-element.21), channel_id=1, source_target_pairs={{2,4},{4,2},{3,5},{5,3},{10,12},{12,10},{11,13},{13,11},{18,20},{2... | collective-permute-start | bytes 983048 | tf_op jit(solution)/shard_map/halos/ppermute | solution.py:415
  8.6 11.8 %collective-permute-start.2 = (f32[40,256]{1,0:T(8,128)S(1)}, f32[40,256]{1,0:T(8,128)S(1)}, u32[]{:S(2)}, u32[]{:S(2)}) collective-permute-start(f32[40,256]{1,0:T(8,128)S(1)} %get-tuple-element.25), channel_id=1, source_target_pairs={{8,16},{24,32},{40,48},{56,64},{72,80},{88,96},{104,112},{120,128}... | collective-permute-start | bytes 122888 | tf_op jit(solution)/shard_map/halos/ppermute | solution.py:412
  16.8 1.3 %copy-start.1 = (f32[4,5,2,32,256]{4,3,2,1,0:T(8,128)S(1)}, f32[4,5,2,32,256]{4,3,2,1,0:T(8,128)}, u32[]{:S(2)}) copy-start(f32[4,5,2,32,256]{4,3,2,1,0:T(8,128)} %f_ref.5) | copy-start | bytes 3932164
  16.8 1.8 %copy-start.2 = (bf16[2,5,5,2,32,256]{5,4,3,2,1,0:T(8,128)(2,1)S(1)}, bf16[2,5,5,2,32,256]{5,4,3,2,1,0:T(8,128)(2,1)}, u32[]{:S(2)}) copy-start(bf16[2,5,5,2,32,256]{5,4,3,2,1,0:T(8,128)(2,1)} %refs_2_.3) | copy-start | bytes 4915204
  16.8 1.8 %copy-start.3 = (f32[2,32,256]{2,1,0:T(8,128)S(1)}, f32[2,32,256]{2,1,0:T(8,128)}, u32[]{:S(2)}) copy-start(f32[2,32,256]{2,1,0:T(8,128)} %refs_3_.9) | copy-start | bytes 196612
  16.8 1.8 %copy-start.4 = (f32[2,32,256]{2,1,0:T(8,128)S(1)}, f32[2,32,256]{2,1,0:T(8,128)}, u32[]{:S(2)}) copy-start(f32[2,32,256]{2,1,0:T(8,128)} %refs_4_.9) | copy-start | bytes 196612
  16.8 4.1 %collective-permute-start.3 = (f32[40,256]{1,0:T(8,128)S(1)}, f32[40,256]{1,0:T(8,128)S(1)}, u32[]{:S(2)}, u32[]{:S(2)}) collective-permute-start(f32[40,256]{1,0:T(8,128)S(1)} %get-tuple-element.26), channel_id=1, source_target_pairs={{0,8},{8,0},{16,24},{24,16},{32,40},{40,32},{48,56},{56,48},{64,72... | collective-permute-start | bytes 122888 | tf_op jit(solution)/shard_map/halos/ppermute | solution.py:413
  22.2 7.3 %copy-start.6 = (f32[4,5,1024]{2,0,1:T(4,128)S(1)}, f32[4,5,1024]{2,0,1:T(4,128)}, u32[]{:S(2)}) copy-start(f32[4,5,1024]{2,0,1:T(4,128)} %param.13) | copy-start | bytes 245764
  22.2 7.3 %copy-start.7 = (s32[1,1024]{1,0:T(1,128)S(1)}, s32[1,1024]{1,0:T(1,128)}, u32[]{:S(2)}) copy-start(s32[1,1024]{1,0:T(1,128)} %cells_ref.3) | copy-start | bytes 12292
  22.2 11.3 %collective-permute-start.8 = (bf16[4,5,32,256]{3,2,1,0:T(8,128)(2,1)S(1)}, bf16[4,5,32,256]{3,2,1,0:T(8,128)(2,1)S(1)}, u32[]{:S(2)}, u32[]{:S(2)}) collective-permute-start(bf16[4,5,32,256]{3,2,1,0:T(8,128)(2,1)S(1)} %get-tuple-element.30), channel_id=1, source_target_pairs={{0,2},{2,0},{4,6},{6,4},{1,3},{3,1},{5,7},{7,5},{8,10},{10,8},{12,... | collective-permute-start | bytes 983048 | tf_op jit(solution)/shard_map/halos/ppermute | solution.py:414
  22.3 11.2 %collective-permute-start.9 = (bf16[4,5,32,256]{3,2,1,0:T(8,128)(2,1)S(1)}, bf16[4,5,32,256]{3,2,1,0:T(8,128)(2,1)S(1)}, u32[]{:S(2)}, u32[]{:S(2)}) collective-permute-start(bf16[4,5,32,256]{3,2,1,0:T(8,128)(2,1)S(1)} %get-tuple-element.31), channel_id=1, source_target_pairs={{2,4},{4,2},{3,5},{5,3},{10,12},{12,10},{11,13},{13,11},{18,20},{2... | collective-permute-start | bytes 983048 | tf_op jit(solution)/shard_map/halos/ppermute | solution.py:415
  24.9 7.5 %collective-permute-start.6 = (f32[40,256]{1,0:T(8,128)S(1)}, f32[40,256]{1,0:T(8,128)S(1)}, u32[]{:S(2)}, u32[]{:S(2)}) collective-permute-start(f32[40,256]{1,0:T(8,128)S(1)} %get-tuple-element.28), channel_id=1, source_target_pairs={{8,16},{24,32},{40,48},{56,64},{72,80},{88,96},{104,112},{120,128}... | collective-permute-start | bytes 122888 | tf_op jit(solution)/shard_map/halos/ppermute | solution.py:412
  29.5 4.0 %collective-permute-start.7 = (f32[40,256]{1,0:T(8,128)S(1)}, f32[40,256]{1,0:T(8,128)S(1)}, u32[]{:S(2)}, u32[]{:S(2)}) collective-permute-start(f32[40,256]{1,0:T(8,128)S(1)} %get-tuple-element.29), channel_id=1, source_target_pairs={{0,8},{8,0},{16,24},{24,16},{32,40},{40,32},{48,56},{56,48},{64,72... | collective-permute-start | bytes 122888 | tf_op jit(solution)/shard_map/halos/ppermute | solution.py:413
  34.3 1.2 %collective-permute-start.10 = (f32[4,128]{1,0:T(4,128)S(1)}, f32[4,128]{1,0:T(4,128)S(1)}, u32[]{:S(2)}, u32[]{:S(2)}) collective-permute-start(f32[4,128]{1,0:T(4,128)S(1)} %surface.1.own_ref), channel_id=1, source_target_pairs={{0,1},{1,0},{2,3},{3,2},{4,5},{5,4},{6,7},{7,6},{8,9},{9,8},{10,11... | collective-permute-start | bytes 6152 | tf_op jit(solution)/shard_map/share_sensitivities/ppermute | solution.py:474
  36.2 15.7 %all-to-all-start = ((f32[32,4,128]{2,1,0:T(4,128)}), f32[32,4,128]{2,1,0:T(4,128)S(1)}, u32[]{:S(2)}, u32[]{:S(2)}) async-start(f32[32,4,128]{2,1,0:T(4,128)} %get-tuple-element.37), calls=%async_computation | async-start | bytes 131072 | tf_op jit(solution)/shard_map/share_sensitivities/all_to_all | solution.py:484

commit v13 on v12

--- a/solution.py
+++ b/solution.py
@@ -77,11 +77,16 @@
                 inner_ref[here, :] = edge_row(ids_ref, f_ref, t, v, i, False)
 
 
-def prepare_kernel(ids_ref, f_ref, a_ref, b_ref):
-    by_parity(ids_ref, functools.partial(pack_layers, f_ref, a_ref, b_ref))
-
-
-def rhs_kernel(ids_ref, f_ref, src_ref, pa_ref, pb_ref, out_ref):
+def prepare_kernel(ids_ref, f_ref, a_ref, b_ref, both_ref):
+    def run(layer_a, layer_b):
+        pack_layers(f_ref, a_ref, b_ref, layer_a, layer_b)
+        pack_layers(f_ref, both_ref.at[0], both_ref.at[1], layer_a, layer_b)
+
+    by_parity(ids_ref, run)
+
+
+def rhs_kernel(ids_ref, f_ref, src_ref, far_ref, out_ref):
+    pa_ref, pb_ref = far_ref.at[0], far_ref.at[1]
     nt, nv, ni, nj, nk = f_ref.shape
 
     def run(layer_a, layer_b):
@@ -415,18 +420,18 @@
                 lax.ppermute(b, "cell", odd),
             )
 
-    packed = call(
-        prepare_kernel, sends, (ids, start), [SMEM, VMEM], 4, 10**6, "prepare"
+    both_like = jax.ShapeDtypeStruct((2, *layer_like.shape), BF16)
+    *packed, both = call(
+        prepare_kernel, sends + [both_like], (ids, start), [SMEM, VMEM], 4, 10**6, "prepare"
     )
     with jax.named_scope("other_times"):
-        pa = lax.ppermute(packed[0], "tm", swap)
-        pb = lax.ppermute(packed[1], "tm", swap)
+        far = lax.ppermute(both, "tm", swap)
     halos = exchange(start, *packed)
     rhs = call(
         rhs_kernel,
         [field_like],
-        (ids, start, source, pa, pb),
-        [SMEM] + [VMEM] * 4,
+        (ids, start, source, far),
+        [SMEM] + [VMEM] * 3,
         4,
         10**7,
         "rhs",

time: 53.5 us -> 53.8 us (level)
  transfers between devices with their start and end apart: 12 -> 11, of which waited for: 4 -> 4; matrix products, arithmetic and copies ran while one was open for 0% -> 0% of each run, Pallas kernels for 18% -> 18%
where the time goes in v13:
time: 53.8 us; the launch traced here: 53.6 us
  starting transfers between devices  26.4 us (49%)
  Pallas kernels  14.4 us (27%)
  waiting for transfers between devices  9.98 us (19%)
  local copies, waits for them, and re-layouts  1.93 us (4%)
  between operations  0.82 us (2%)
    pallas_call x13, Pallas kernels, call(): pl.pallas_call(kernel, out_shape=outs, in_specs=specs, out_specs=[VMEM] *...  14.4 us
    ppermute x2, starting transfers between devices, exchange(): lax.ppermute(outer, 'passage', across)  13.2 us
    all_to_all x1, waiting for transfers between devices, body(): gathered = lax.all_to_all(sens, 'passage', 0, 0, tiled=True)  7.21 us
    all_to_all x1, starting transfers between devices, body(): gathered = lax.all_to_all(sens, 'passage', 0, 0, tiled=True)  6.07 us
    ppermute x2, starting transfers between devices, exchange(): lax.ppermute(b, 'cell', odd)  4.49 us
    ppermute x2, starting transfers between devices, exchange(): lax.ppermute(a, 'cell', even)  2.36 us
    unnamed x16, local copies, waits for them, and re-layouts  1.93 us
    ppermute x2, waiting for transfers between devices, exchange(): lax.ppermute(inner, 'passage', within)  1.61 us
  transfers between devices with their start and end apart: 11, of which 4 were waited for; matrix products, arithmetic and copies ran while one was open for 0% of the time, Pallas kernels for 18%

profile of v13, /device:TPU:8, one launch (start us, length us, event | category | flops | bytes accessed | tf_op | source)
XLA Modules:
  0.0 53.6 jit_solution(16046915019337133512)
XLA Ops:
  0.6 0.1 pad_add_fusion.ids_ref
  0.7 0.0 copy-start
  0.7 1.3 %copy-done = f32[4,5,2,32,256]{4,3,2,1,0:T(8,128)S(1)} copy-done((f32[4,5,2,32,256]{4,3,2,1,0:T(8,128)S(1)}, f32[4,5,2,32,256]{4,3,2,1,0:T(8,128)}, u32[]{:S(2)}) %copy-start) | copy-done | bytes 1310744
  2.0 0.0 copy-start.5
  2.0 0.7 %prepare.1 = (bf16[4,5,32,256]{3,2,1,0:T(8,128)(2,1)S(1)}, bf16[4,5,32,256]{3,2,1,0:T(8,128)(2,1)S(1)}, bf16[2,4,5,32,256]{4,3,2,1,0:T(8,128)(2,1)S(1)}) custom-call(s32[2]{0:T(128)S(1)} %pad_add_fusion.ids_ref, f32[4,5,2,32,256]{4,3,2,1,0:T(8,128)S(1)} %copy-done), custom_call_target="tpu_custom_call" | custom-call | flops 1000000 | bytes 2621448 | tf_op jit(solution)/shard_map/prepare/pallas_call | solution.py:31
  2.7 0.1 collective-permute-start
  2.8 2.3 %collective-permute-start.3 = (bf16[4,5,32,256]{3,2,1,0:T(8,128)(2,1)S(1)}, bf16[4,5,32,256]{3,2,1,0:T(8,128)(2,1)S(1)}, u32[]{:S(2)}, u32[]{:S(2)}) collective-permute-start(bf16[4,5,32,256]{3,2,1,0:T(8,128)(2,1)S(1)} %get-tuple-element.27), channel_id=1, source_target_pairs={{0,2},{2,0},{4,6},{6,4},{1,3},{3,1},{5,7},{7,5},{8,10},{10,8},{12,... | collective-permute-start | bytes 983048 | tf_op jit(solution)/shard_map/halos/ppermute | solution.py:419
  5.1 2.6 %collective-permute-start.4 = (bf16[4,5,32,256]{3,2,1,0:T(8,128)(2,1)S(1)}, bf16[4,5,32,256]{3,2,1,0:T(8,128)(2,1)S(1)}, u32[]{:S(2)}, u32[]{:S(2)}) collective-permute-start(bf16[4,5,32,256]{3,2,1,0:T(8,128)(2,1)S(1)} %get-tuple-element.28), channel_id=1, source_target_pairs={{2,4},{4,2},{3,5},{5,3},{10,12},{12,10},{11,13},{13,11},{18,20},{2... | collective-permute-start | bytes 983048 | tf_op jit(solution)/shard_map/halos/ppermute | solution.py:420
  7.7 0.6 %rows.2 = (f32[40,256]{1,0:T(8,128)S(1)}, f32[40,256]{1,0:T(8,128)S(1)}) custom-call(s32[2]{0:T(128)S(1)} %pad_add_fusion.ids_ref, f32[4,5,2,32,256]{4,3,2,1,0:T(8,128)S(1)} %copy-done), custom_call_target="tpu_custom_call" | custom-call | flops 1000000 | bytes 1392648 | tf_op jit(solution)/shard_map/rows/pallas_call | solution.py:31
  8.3 8.1 %collective-permute-start.1 = (f32[40,256]{1,0:T(8,128)S(1)}, f32[40,256]{1,0:T(8,128)S(1)}, u32[]{:S(2)}, u32[]{:S(2)}) collective-permute-start(f32[40,256]{1,0:T(8,128)S(1)} %get-tuple-element.25), channel_id=1, source_target_pairs={{8,16},{24,32},{40,48},{56,64},{72,80},{88,96},{104,112},{120,128}... | collective-permute-start | bytes 122888 | tf_op jit(solution)/shard_map/halos/ppermute | solution.py:417
  16.4 0.0 copy-start.1
  16.4 0.0 copy-start.2
  16.4 0.0 copy-start.3
  16.4 0.0 copy-start.4
  16.4 0.1 collective-permute-start.2
  16.5 0.0 collective-permute-done.far_ref
  16.5 0.0 copy-done.5
  16.5 1.1 %rhs.1.refs_1_ = f32[4,5,2,32,256]{4,3,2,1,0:T(8,128)S(1)} custom-call(s32[2]{0:T(128)S(1)} %pad_add_fusion.ids_ref, f32[4,5,2,32,256]{4,3,2,1,0:T(8,128)S(1)} %copy-done, f32[4,5,2,32,256]{4,3,2,1,0:T(8,128)S(1)} %copy-done.5, bf16[2,4,5,32,256]{4,3,2,1,0:T(8,128)(2,1)S(1)} %collective-permute-done.far_ref), custom_call_target="tpu_custom_call" | custom-call | flops 10000000 | bytes 4587528 | tf_op jit(solution)/shard_map/rhs/pallas_call | solution.py:31
  17.6 0.1 copy-done.1
  17.7 0.5 copy-done.2
  18.2 0.0 copy-done.3
  18.2 0.0 copy-done.4
  18.2 1.8 %first_local.1 = (f32[4,5,2,32,256]{4,3,2,1,0:T(8,128)S(1)}, bf16[5,5,32,256]{3,2,1,0:T(8,128)(2,1)S(1)}, bf16[5,5,2,16,256]{4,3,2,1,0:T(8,128)(2,1)S(1)}) custom-call(f32[4,5,2,32,256]{4,3,2,1,0:T(8,128)S(1)} %copy-done.1, f32[4,5,2,32,256]{4,3,2,1,0:T(8,128)S(1)} %rhs.1.refs_1_, bf16[2,5,5,2,32,256]{5,4,3,2,1,0:T(8,128)(2,1)S(1)} %copy-done.2, ...), custom_call_target="tpu_custom_call" | custom-call | flops 20000000 | bytes 6520832 | tf_op jit(solution)/shard_map/first_local/pallas_call | solution.py:31
  20.1 0.0 collective-permute-done.1.refs_5_
  20.1 0.4 collective-permute-done.2.refs_6_
  20.5 0.0 collective-permute-done.3.refs_7_
  20.5 0.0 collective-permute-done.4.refs_8_
  20.5 1.3 %first_finish.1 = (f32[4,5,2,32,256]{4,3,2,1,0:T(8,128)S(1)}, bf16[4,5,32,256]{3,2,1,0:T(8,128)(2,1)S(1)}, bf16[4,5,32,256]{3,2,1,0:T(8,128)(2,1)S(1)}) custom-call(s32[2]{0:T(128)S(1)} %pad_add_fusion.ids_ref, f32[4,5,2,32,256]{4,3,2,1,0:T(8,128)S(1)} %get-tuple-element.22.refs_0_, bf16[5,5,32,256]{3,2,1,0:T(8,128)(2,1)S(1)} %get-tuple-element.23.refs_1_, ...), custom_call_target="tpu_custom_call" | custom-call | flops 10000000 | bytes 4964360 | tf_op jit(solution)/shard_map/first_finish/pallas_call | solution.py:31
  21.8 0.0 copy-start.6
  21.9 0.0 copy-start.7
  21.9 0.1 collective-permute-start.7
  22.0 1.9 %collective-permute-start.8 = (bf16[4,5,32,256]{3,2,1,0:T(8,128)(2,1)S(1)}, bf16[4,5,32,256]{3,2,1,0:T(8,128)(2,1)S(1)}, u32[]{:S(2)}, u32[]{:S(2)}) collective-permute-start(bf16[4,5,32,256]{3,2,1,0:T(8,128)(2,1)S(1)} %get-tuple-element.33), channel_id=1, source_target_pairs={{2,4},{4,2},{3,5},{5,3},{10,12},{12,10},{11,13},{13,11},{18,20},{2... | collective-permute-start | bytes 983048 | tf_op jit(solution)/shard_map/halos/ppermute | solution.py:420
  23.9 0.6 %rows.3 = (f32[40,256]{1,0:T(8,128)S(1)}, f32[40,256]{1,0:T(8,128)S(1)}) custom-call(s32[2]{0:T(128)S(1)} %pad_add_fusion.ids_ref, f32[4,5,2,32,256]{4,3,2,1,0:T(8,128)S(1)} %get-tuple-element.29.refs_0_.f_ref), custom_call_target="tpu_custom_call" | custom-call | flops 1000000 | bytes 1392648 | tf_op jit(solution)/shard_map/rows/pallas_call | solution.py:31
  24.5 5.0 %collective-permute-start.5 = (f32[40,256]{1,0:T(8,128)S(1)}, f32[40,256]{1,0:T(8,128)S(1)}, u32[]{:S(2)}, u32[]{:S(2)}) collective-permute-start(f32[40,256]{1,0:T(8,128)S(1)} %get-tuple-element.30), channel_id=1, source_target_pairs={{8,16},{24,32},{40,48},{56,64},{72,80},{88,96},{104,112},{120,128}... | collective-permute-start | bytes 122888 | tf_op jit(solution)/shard_map/halos/ppermute | solution.py:417
  29.5 0.0 collective-permute-start.6
  29.5 0.0 copy-done.6
  29.5 0.0 copy-done.7
  29.5 1.0 %order.1.refs_9_ = f32[20,512]{1,0:T(8,128)S(1)} custom-call(s32[2]{0:T(128)S(1)} %pad_add_fusion.ids_ref, s32[1,1024]{1,0:T(1,128)S(1)} %copy-done.7, f32[5,4,1024]{2,1,0:T(4,128)S(1)} %bitcast.4), custom_call_target="tpu_custom_call" | custom-call | flops 1000000 | bytes 126984 | tf_op jit(solution)/shard_map/order/pallas_call | solution.py:31
  30.5 1.8 %second_local.1.refs_0_ = f32[4,5,2,32,256]{4,3,2,1,0:T(8,128)S(1)} custom-call(f32[4,5,2,32,256]{4,3,2,1,0:T(8,128)S(1)} %get-tuple-element.29.refs_0_.f_ref, f32[4,5,2,32,256]{4,3,2,1,0:T(8,128)S(1)} %rhs.1.refs_1_, bf16[2,5,5,2,32,256]{5,4,3,2,1,0:T(8,128)(2,1)S(1)} %copy-done.2, f32[2,32,256]{2,1,0:T(8,128)S(1)} %copy-done.3, f32[2,32,256]{2,1,0:T(8,128)S(1)} %copy-done.4), custom_call_target="tpu_custom_call" | custom-call | flops 20000000 | bytes 5701632 | tf_op jit(solution)/shard_map/second_local/pallas_call | solution.py:31
  32.3 0.0 collective-permute-done.5.refs_5_
  32.3 1.2 %collective-permute-done.6.refs_6_ = f32[40,256]{1,0:T(8,128)S(1)} collective-permute-done((f32[40,256]{1,0:T(8,128)S(1)}, f32[40,256]{1,0:T(8,128)S(1)}, u32[]{:S(2)}, u32[]{:S(2)}) %collective-permute-start.6) | collective-permute-done | bytes 40992 | tf_op jit(solution)/shard_map/halos/ppermute | solution.py:418
  33.5 0.0 collective-permute-done.7.refs_7_
  33.5 0.0 collective-permute-done.8.refs_8_
  33.5 0.7 %surface.1.own_ref = f32[4,128]{1,0:T(4,128)S(1)} custom-call(s32[2]{0:T(128)S(1)} %pad_add_fusion.ids_ref, f32[4,5,2,32,256]{4,3,2,1,0:T(8,128)S(1)} %second_local.1.refs_0_, bf16[5,5,32,256]{3,2,1,0:T(8,128)(2,1)S(1)} %get-tuple-element.23.refs_1_, bf16[5,5,2,16,256]{4,3,2,1,0:T(8,128)(2,1)S(1)} %get-tuple-element.24.refs_2_, f32[2,32,256]{2,1,0:T(8,128)S(1)} %copy-done.3, ...), custom_call_target="tpu_custom_call" | custom-call | flops 10000000 | bytes 3041288 | tf_op jit(solution)/shard_map/surface/pallas_call | solution.py:31
  34.3 0.1 collective-permute-start.9
  34.4 1.1 %collective-permute-done.9.other_ref = f32[4,128]{1,0:T(4,128)S(1)} collective-permute-done((f32[4,128]{1,0:T(4,128)S(1)}, f32[4,128]{1,0:T(4,128)S(1)}, u32[]{:S(2)}, u32[]{:S(2)}) %collective-permute-start.9) | collective-permute-done | bytes 2080 | tf_op jit(solution)/shard_map/share_sensitivities/ppermute | solution.py:479
  35.5 0.6 %share.1 = (f32[32,4,128]{2,1,0:T(4,128)}, f32[8,128]{1,0:T(8,128)S(1)}) custom-call(f32[4,128]{1,0:T(4,128)S(1)} %surface.1.own_ref, f32[4,128]{1,0:T(4,128)S(1)} %collective-permute-done.9.other_ref), custom_call_target="tpu_custom_call" | custom-call | flops 10000 | bytes 73728 | tf_op jit(solution)/shard_map/share_sensitivities/share/pallas_call | solution.py:31
  36.2 6.1 %all-to-all-start = ((f32[32,4,128]{2,1,0:T(4,128)}), f32[32,4,128]{2,1,0:T(4,128)S(1)}, u32[]{:S(2)}, u32[]{:S(2)}) async-start(f32[32,4,128]{2,1,0:T(4,128)} %get-tuple-element.39), calls=%async_computation | async-start | bytes 131072 | tf_op jit(solution)/shard_map/share_sensitivities/all_to_all | solution.py:489
  42.2 2.3 %second_finish.1 = (f32[4,5,2,32,256]{4,3,2,1,0:T(8,128)}, f32[8,128]{1,0:T(8,128)S(1)}) custom-call(s32[2]{0:T(128)S(1)} %pad_add_fusion.ids_ref, f32[4,5,2,32,256]{4,3,2,1,0:T(8,128)S(1)} %second_local.1.refs_0_, bf16[5,5,32,256]{3,2,1,0:T(8,128)(2,1)S(1)} %get-tuple-element.23.refs_1_, bf16[5,5,2,16,256]{4,3,2,1,0:T(8,128)(2,1)S(1)} %get-tuple-element.24.refs_2_, ...), custom_call_target="tpu_custom_call" | custom-call | flops 10000000 | bytes 4317192 | tf_op jit(solution)/shard_map/second_finish/pallas_call | solution.py:31
  44.6 0.4 tables.1
  45.0 7.2 %all-to-all-done.sens_ref = f32[32,4,128]{2,1,0:T(4,128)S(1)} async-done(((f32[32,4,128]{2,1,0:T(4,128)}), f32[32,4,128]{2,1,0:T(4,128)S(1)}, u32[]{:S(2)}, u32[]{:S(2)}) %all-to-all-start) | async-done | bytes 65568 | tf_op jit(solution)/shard_map/share_sensitivities/all_to_all | solution.py:489
  52.2 1.4 %modes.1 = f32[32,1024]{1,0:T(8,128)} custom-call(bf16[1024,1024]{1,0:T(8,128)(2,1)S(1)} %get-tuple-element.37.chosen_ref, f32[64,32]{1,0:T(8,128)S(1)} %get-tuple-element.38.table_ref, f32[32,4,128]{2,1,0:T(4,128)S(1)} %all-to-all-done.sens_ref), custom_call_target="tpu_custom_call" | custom-call | flops 10000000 | bytes 2301952 | tf_op jit(solution)/shard_map/modes/pallas_call | solution.py:31
Async XLA Ops:
  0.7 1.3 %copy-start = (f32[4,5,2,32,256]{4,3,2,1,0:T(8,128)S(1)}, f32[4,5,2,32,256]{4,3,2,1,0:T(8,128)}, u32[]{:S(2)}) copy-start(f32[4,5,2,32,256]{4,3,2,1,0:T(8,128)} %f_ref.5) | copy-start | bytes 3932164
  2.0 14.5 %copy-start.5 = (f32[4,5,2,32,256]{4,3,2,1,0:T(8,128)S(1)}, f32[4,5,2,32,256]{4,3,2,1,0:T(8,128)}, u32[]{:S(2)}) copy-start(f32[4,5,2,32,256]{4,3,2,1,0:T(8,128)} %src_ref.1) | copy-start | bytes 3932164
  2.7 13.8 %collective-permute-start = (bf16[2,4,5,32,256]{4,3,2,1,0:T(8,128)(2,1)S(1)}, bf16[2,4,5,32,256]{4,3,2,1,0:T(8,128)(2,1)S(1)}, u32[]{:S(2)}, u32[]{:S(2)}) collective-permute-start(bf16[2,4,5,32,256]{4,3,2,1,0:T(8,128)(2,1)S(1)} %get-tuple-element.21), channel_id=1, source_target_pairs={{0,1},{1,0},{2,3},{3,2},{4,5},{5,4},{6,7},{7,6},{8,9},{9,8},{10,11... | collective-permute-start | bytes 1966088 | tf_op jit(solution)/shard_map/other_times/ppermute | solution.py:428
  2.8 17.7 %collective-permute-start.3 = (bf16[4,5,32,256]{3,2,1,0:T(8,128)(2,1)S(1)}, bf16[4,5,32,256]{3,2,1,0:T(8,128)(2,1)S(1)}, u32[]{:S(2)}, u32[]{:S(2)}) collective-permute-start(bf16[4,5,32,256]{3,2,1,0:T(8,128)(2,1)S(1)} %get-tuple-element.27), channel_id=1, source_target_pairs={{0,2},{2,0},{4,6},{6,4},{1,3},{3,1},{5,7},{7,5},{8,10},{10,8},{12,... | collective-permute-start | bytes 983048 | tf_op jit(solution)/shard_map/halos/ppermute | solution.py:419
  5.1 15.4 %collective-permute-start.4 = (bf16[4,5,32,256]{3,2,1,0:T(8,128)(2,1)S(1)}, bf16[4,5,32,256]{3,2,1,0:T(8,128)(2,1)S(1)}, u32[]{:S(2)}, u32[]{:S(2)}) collective-permute-start(bf16[4,5,32,256]{3,2,1,0:T(8,128)(2,1)S(1)} %get-tuple-element.28), channel_id=1, source_target_pairs={{2,4},{4,2},{3,5},{5,3},{10,12},{12,10},{11,13},{13,11},{18,20},{2... | collective-permute-start | bytes 983048 | tf_op jit(solution)/shard_map/halos/ppermute | solution.py:420
  8.3 11.8 %collective-permute-start.1 = (f32[40,256]{1,0:T(8,128)S(1)}, f32[40,256]{1,0:T(8,128)S(1)}, u32[]{:S(2)}, u32[]{:S(2)}) collective-permute-start(f32[40,256]{1,0:T(8,128)S(1)} %get-tuple-element.25), channel_id=1, source_target_pairs={{8,16},{24,32},{40,48},{56,64},{72,80},{88,96},{104,112},{120,128}... | collective-permute-start | bytes 122888 | tf_op jit(solution)/shard_map/halos/ppermute | solution.py:417
  16.4 1.3 %copy-start.1 = (f32[4,5,2,32,256]{4,3,2,1,0:T(8,128)S(1)}, f32[4,5,2,32,256]{4,3,2,1,0:T(8,128)}, u32[]{:S(2)}) copy-start(f32[4,5,2,32,256]{4,3,2,1,0:T(8,128)} %f_ref.5) | copy-start | bytes 3932164
  16.4 1.8 %copy-start.2 = (bf16[2,5,5,2,32,256]{5,4,3,2,1,0:T(8,128)(2,1)S(1)}, bf16[2,5,5,2,32,256]{5,4,3,2,1,0:T(8,128)(2,1)}, u32[]{:S(2)}) copy-start(bf16[2,5,5,2,32,256]{5,4,3,2,1,0:T(8,128)(2,1)} %refs_2_.3) | copy-start | bytes 4915204
  16.4 1.8 %copy-start.3 = (f32[2,32,256]{2,1,0:T(8,128)S(1)}, f32[2,32,256]{2,1,0:T(8,128)}, u32[]{:S(2)}) copy-start(f32[2,32,256]{2,1,0:T(8,128)} %refs_3_.9) | copy-start | bytes 196612
  16.4 1.8 %copy-start.4 = (f32[2,32,256]{2,1,0:T(8,128)S(1)}, f32[2,32,256]{2,1,0:T(8,128)}, u32[]{:S(2)}) copy-start(f32[2,32,256]{2,1,0:T(8,128)} %refs_4_.9) | copy-start | bytes 196612
  16.4 4.1 %collective-permute-start.2 = (f32[40,256]{1,0:T(8,128)S(1)}, f32[40,256]{1,0:T(8,128)S(1)}, u32[]{:S(2)}, u32[]{:S(2)}) collective-permute-start(f32[40,256]{1,0:T(8,128)S(1)} %get-tuple-element.26), channel_id=1, source_target_pairs={{0,8},{8,0},{16,24},{24,16},{32,40},{40,32},{48,56},{56,48},{64,72... | collective-permute-start | bytes 122888 | tf_op jit(solution)/shard_map/halos/ppermute | solution.py:418
  21.8 7.7 %copy-start.6 = (f32[4,5,1024]{2,0,1:T(4,128)S(1)}, f32[4,5,1024]{2,0,1:T(4,128)}, u32[]{:S(2)}) copy-start(f32[4,5,1024]{2,0,1:T(4,128)} %param.13) | copy-start | bytes 245764
  21.9 7.7 %copy-start.7 = (s32[1,1024]{1,0:T(1,128)S(1)}, s32[1,1024]{1,0:T(1,128)}, u32[]{:S(2)}) copy-start(s32[1,1024]{1,0:T(1,128)} %cells_ref.3) | copy-start | bytes 12292
  21.9 11.7 %collective-permute-start.7 = (bf16[4,5,32,256]{3,2,1,0:T(8,128)(2,1)S(1)}, bf16[4,5,32,256]{3,2,1,0:T(8,128)(2,1)S(1)}, u32[]{:S(2)}, u32[]{:S(2)}) collective-permute-start(bf16[4,5,32,256]{3,2,1,0:T(8,128)(2,1)S(1)} %get-tuple-element.32), channel_id=1, source_target_pairs={{0,2},{2,0},{4,6},{6,4},{1,3},{3,1},{5,7},{7,5},{8,10},{10,8},{12,... | collective-permute-start | bytes 983048 | tf_op jit(solution)/shard_map/halos/ppermute | solution.py:419
  22.0 11.6 %collective-permute-start.8 = (bf16[4,5,32,256]{3,2,1,0:T(8,128)(2,1)S(1)}, bf16[4,5,32,256]{3,2,1,0:T(8,128)(2,1)S(1)}, u32[]{:S(2)}, u32[]{:S(2)}) collective-permute-start(bf16[4,5,32,256]{3,2,1,0:T(8,128)(2,1)S(1)} %get-tuple-element.33), channel_id=1, source_target_pairs={{2,4},{4,2},{3,5},{5,3},{10,12},{12,10},{11,13},{13,11},{18,20},{2... | collective-permute-start | bytes 983048 | tf_op jit(solution)/shard_map/halos/ppermute | solution.py:420
  24.5 7.8 %collective-permute-start.5 = (f32[40,256]{1,0:T(8,128)S(1)}, f32[40,256]{1,0:T(8,128)S(1)}, u32[]{:S(2)}, u32[]{:S(2)}) collective-permute-start(f32[40,256]{1,0:T(8,128)S(1)} %get-tuple-element.30), channel_id=1, source_target_pairs={{8,16},{24,32},{40,48},{56,64},{72,80},{88,96},{104,112},{120,128}... | collective-permute-start | bytes 122888 | tf_op jit(solution)/shard_map/halos/ppermute | solution.py:417
  29.5 4.0 %collective-permute-start.6 = (f32[40,256]{1,0:T(8,128)S(1)}, f32[40,256]{1,0:T(8,128)S(1)}, u32[]{:S(2)}, u32[]{:S(2)}) collective-permute-start(f32[40,256]{1,0:T(8,128)S(1)} %get-tuple-element.31), channel_id=1, source_target_pairs={{0,8},{8,0},{16,24},{24,16},{32,40},{40,32},{48,56},{56,48},{64,72... | collective-permute-start | bytes 122888 | tf_op jit(solution)/shard_map/halos/ppermute | solution.py:418
  34.3 1.2 %collective-permute-start.9 = (f32[4,128]{1,0:T(4,128)S(1)}, f32[4,128]{1,0:T(4,128)S(1)}, u32[]{:S(2)}, u32[]{:S(2)}) collective-permute-start(f32[4,128]{1,0:T(4,128)S(1)} %surface.1.own_ref), channel_id=1, source_target_pairs={{0,1},{1,0},{2,3},{3,2},{4,5},{5,4},{6,7},{7,6},{8,9},{9,8},{10,11... | collective-permute-start | bytes 6152 | tf_op jit(solution)/shard_map/share_sensitivities/ppermute | solution.py:479
  36.2 16.0 %all-to-all-start = ((f32[32,4,128]{2,1,0:T(4,128)}), f32[32,4,128]{2,1,0:T(4,128)S(1)}, u32[]{:S(2)}, u32[]{:S(2)}) async-start(f32[32,4,128]{2,1,0:T(4,128)} %get-tuple-element.39), calls=%async_computation | async-start | bytes 131072 | tf_op jit(solution)/shard_map/share_sensitivities/all_to_all | solution.py:489
